TPU v7x, 32 devices: a whole 2x2x4 slice. The times are simulated.
32 devices in a mesh: depth: 4 (over x, core), gx: 2 (over y), gy: 4 (over z).
Axes of the slice: x: 2, y: 2, z: 4, core: 2. Of those that a mesh axis runs over, the one named last changes fastest.
Arguments:
- arrival: bfloat16 [4, 192, 2, 4, 896], P('depth', None, 'gx', 'gy'), may hold values from -6 to 6
- source: bfloat16 [4, 4, 192, 2, 4, 896], P('depth', None, None, 'gx', 'gy'), may hold values from -6 to 6
- assignment: int32 [4, 192], replicated, may hold values from 0 to 191, each once within a row
- counts: int32 [7, 12, 2, 4], P(None, None, 'gx', 'gy'), may hold values from 1 to 16
- first_map: bfloat16 [4, 2, 4, 896, 896], P('depth', 'gx', 'gy'), may hold values from -0.1875 to 0.1875
- second_map: bfloat16 [4, 2, 4, 896, 896], P('depth', 'gx', 'gy'), may hold values from -0.1875 to 0.1875
- damping: float32 [4, 2, 4, 896], P('depth', 'gx', 'gy'), may hold values from 0.2 to 0.9
Outputs:
- final_traces: bfloat16 [4, 192, 2, 4, 896], P('depth', None, 'gx', 'gy')
Inputs may be any that keep to these rules, and one draw needn't show every extreme that they name: Each row of assignment is a permutation of the 192 shots.
All inputs are finite; a program needn't handle non-finite values.
Results may differ from a plain program's by a relative error of at most 0.017.
Values may be sent and summed in bfloat16 or wider, within the bound.
No kernel may reach another device: no remote copies, remote signals or barrier semaphores. Data moves between devices by JAX's collectives and lax.ppermute only.
A program may use at most 64 MiB of HBM per device.

v0:
```python
import jax
import jax.numpy as jnp
from jax import lax
from jax.sharding import PartitionSpec as P

FX = 32
FY = 28
SHOT_BATCH = 16


coupling_weight = 0.25


def extended(cells, sides, width):
    for axis, dim in sides:
        count = lax.axis_size(axis)
        ends = count - 1
        head = lax.slice_in_dim(cells, 0, width, axis=dim)
        tail = lax.slice_in_dim(cells, cells.shape[dim] - width, cells.shape[dim], axis=dim)
        cells = jnp.concatenate(
            [
                lax.ppermute(tail, axis, [(i, (i + 1) % count) for i in range(ends)]),
                cells,
                lax.ppermute(head, axis, [((i + 1) % count, i) for i in range(ends)]),
            ],
            axis=dim,
        )
    return cells


def shifted(x, axis, by):
    count = lax.axis_size(axis)
    pairs = [(i, i + by) for i in range(count) if 0 <= i + by < count]
    return lax.ppermute(x, axis, pairs)


def neighbour_sum(padded):
    widened = padded.astype(jnp.float32)
    return (
        widened[:, 2:, 1:-1] + widened[:, :-2, 1:-1] + widened[:, 1:-1, 2:] + widened[:, 1:-1, :-2]
    )


def advance(incoming, picked, active, map_first, map_second, damping_now, swap_faces):
    slot_count = incoming.shape[0]
    start_trace = (active * (picked.astype(jnp.float32) + incoming.astype(jnp.float32))).astype(
        jnp.bfloat16
    )
    mapped = jnp.dot(start_trace, map_first, preferred_element_type=jnp.float32).astype(
        jnp.bfloat16
    )
    face_grid = mapped.reshape(slot_count, FX, FY)
    padded = swap_faces(face_grid)
    coupled = (face_grid.astype(jnp.float32) + coupling_weight * neighbour_sum(padded)).astype(
        jnp.bfloat16
    )
    imaged = jnp.dot(
        coupled.reshape(slot_count, FX * FY), map_second, preferred_element_type=jnp.float32
    )
    blended = damping_now * imaged + (1.0 - damping_now) * start_trace.astype(jnp.float32)
    return (active * blended).astype(jnp.bfloat16)


def local(arrival, source, assignment, counts, first_map, second_map, damping):
    map_first = first_map[0, 0, 0]
    map_second = second_map[0, 0, 0]
    damping_now = damping[0, 0, 0][None, :]
    layer_index = lax.axis_index("depth")
    section_count = lax.axis_size("depth")
    slot_count = arrival.shape[1]
    round_count = source.shape[1]
    positions = jnp.arange(SHOT_BATCH, dtype=jnp.int32)
    live_table = counts[:, :, 0, 0]
    incoming = arrival[0, :, 0, 0, :]

    def faces_whole(face_grid):
        return extended(face_grid, (("gx", 1), ("gy", 2)), 1)

    for round_number in range(round_count):
        unit_index = round_number - layer_index + section_count - 1
        live_counts = lax.dynamic_index_in_dim(live_table, unit_index, 0, keepdims=False)
        active = (
            (positions[None, :] < live_counts[:, None]).reshape(slot_count, 1).astype(jnp.float32)
        )
        picked = jnp.take(source[0, round_number, :, 0, 0, :], assignment[round_number], axis=0)
        final_round = round_number == round_count - 1
        traces = advance(incoming, picked, active, map_first, map_second, damping_now, faces_whole)
        if not final_round:
            traces = shifted(traces, "depth", 1)
        incoming = traces
    return incoming.reshape(1, slot_count, 1, 1, incoming.shape[1])


def solution(mesh):
    return jax.shard_map(
        local,
        mesh=mesh,
        in_specs=(
            P("depth", None, "gx", "gy", None),
            P("depth", None, None, "gx", "gy", None),
            P(),
            P(None, None, "gx", "gy"),
            P("depth", "gx", "gy", None, None),
            P("depth", "gx", "gy", None, None),
            P("depth", "gx", "gy", None),
        ),
        out_specs=P("depth", None, "gx", "gy", None),
        check_vma=False,
    )
```

profile of v0, /device:TPU:2, one launch (start us, length us, event | category | flops | bytes accessed | tf_op | source)
XLA Modules:
  0.0 124.0 jit_solution(11939700112841209384)
XLA Ops:
  0.0 1.4 %fusion.97 = (s32[12]{0:T(128)}, s32[12]{0:T(128)}, s32[12]{0:T(128)S(1)}, s32[12]{0:T(128)}) fusion(s32[7,12,1,1]{1,3,2,0:T(1,128)} %param.12, s32[]{:T(128)S(6)} %select_n.20, s32[]{:T(128)S(6)} %select_n.21, s32[]{:T(128)S(6)} %select_n.23, s32[]{:T(128)S(6)} %select_n.22), kind=kLoop, calls=%fused_computation.116 | loop fusion | bytes 400 | tf_op jit(solution)/shard_map/lt | solution.py:83
  3.0 1.4 %slice_bitcast_fusion.3 = (bf16[192,896]{1,0:T(8,128)(2,1)S(1)}, bf16[192,896]{1,0:T(8,128)(2,1)S(1)}, bf16[192,896]{1,0:T(8,128)(2,1)S(1)}, bf16[192,896]{1,0:T(8,128)(2,1)S(1)}) fusion(bf16[1,4,192,1,1,896]{5,2,4,3,1,0:T(8,128)(2,1)} %param.10), kind=kLoop, calls=%fused_computation.78 | loop fusion | bytes 2752512 | tf_op jit(solution)/shard_map/squeeze | solution.py:85
  5.5 1.6 %fusion.64 = bf16[192,896]{1,0:T(8,128)(2,1)S(1)} fusion(bf16[1,1,1,896,896]{4,3,2,1,0:T(8,128)(2,1)S(1)} %copy-done, bf16[1,192,1,1,896]{4,1,3,2,0:T(8,128)(2,1)} %param.9, bf16[192,896]{1,0:T(8,128)(2,1)S(1)} %gather_fusion.3, f32[192]{0:T(256)S(1)} %reshape.142, pred[192]{0:T(512)(128)(4,1)S(1)} %compare_and_fusion), kind=kOutput, calls=%fused_computation.36 | convolution fusion | flops 309485568 | bytes 2638784 | tf_op jit(solution)/shard_map/dot_general | solution.py:49
  9.8 3.4 %collective-permute-start = (bf16[192,1,28]{0,2,1:T(8,128)(2,1)}, bf16[192,1,28]{0,2,1:T(8,128)(2,1)S(1)}, u32[]{:S(2)}, u32[]{:S(2)}) collective-permute-start(bf16[192,1,28]{0,2,1:T(8,128)(2,1)} %get-tuple-element.25), channel_id=1, source_target_pairs={{0,4},{1,5},{2,6},{3,7},{8,12},{9,13},{10,14},{11,15},{16,20},{17,... | collective-permute-start | bytes 32264 | tf_op jit(solution)/shard_map/ppermute | solution.py:22
  13.2 1.3 %collective-permute-start.1 = (bf16[192,1,28]{0,2,1:T(8,128)(2,1)}, bf16[192,1,28]{0,2,1:T(8,128)(2,1)S(1)}, u32[]{:S(2)}, u32[]{:S(2)}) collective-permute-start(bf16[192,1,28]{0,2,1:T(8,128)(2,1)} %get-tuple-element.24), channel_id=1, source_target_pairs={{4,0},{5,1},{6,2},{7,3},{12,8},{13,9},{14,10},{15,11},{20,16},{21,... | collective-permute-start | bytes 32264 | tf_op jit(solution)/shard_map/ppermute | solution.py:24
  15.3 3.8 %collective-permute-done.1 = bf16[192,1,28]{0,2,1:T(8,128)(2,1)S(1)} collective-permute-done((bf16[192,1,28]{0,2,1:T(8,128)(2,1)}, bf16[192,1,28]{0,2,1:T(8,128)(2,1)S(1)}, u32[]{:S(2)}, u32[]{:S(2)}) %collective-permute-start.1) | collective-permute-done | bytes 10784 | tf_op jit(solution)/shard_map/ppermute | solution.py:24
  19.2 3.5 %collective-permute-start.2 = (bf16[192,34,1]{0,2,1:T(2,128)(2,1)S(1)}, bf16[192,34,1]{0,2,1:T(2,128)(2,1)S(1)}, u32[]{:S(2)}, u32[]{:S(2)}) collective-permute-start(bf16[192,34,1]{0,2,1:T(2,128)(2,1)S(1)} %get-tuple-element.16), channel_id=1, source_target_pairs={{0,1},{1,2},{2,3},{4,5},{5,6},{6,7},{8,9},{9,10},{10,11},{12,13},{... | collective-permute-start | bytes 39176 | tf_op jit(solution)/shard_map/ppermute | solution.py:22
  22.6 1.3 %collective-permute-start.3 = (bf16[192,34,1]{0,2,1:T(2,128)(2,1)S(1)}, bf16[192,34,1]{0,2,1:T(2,128)(2,1)S(1)}, u32[]{:S(2)}, u32[]{:S(2)}) collective-permute-start(bf16[192,34,1]{0,2,1:T(2,128)(2,1)S(1)} %get-tuple-element.17), channel_id=1, source_target_pairs={{1,0},{2,1},{3,2},{5,4},{6,5},{7,6},{9,8},{10,9},{11,10},{13,12},{... | collective-permute-start | bytes 39176 | tf_op jit(solution)/shard_map/ppermute | solution.py:24
  24.2 4.2 %collective-permute-done.3 = bf16[192,34,1]{0,2,1:T(2,128)(2,1)S(1)} collective-permute-done((bf16[192,34,1]{0,2,1:T(2,128)(2,1)S(1)}, bf16[192,34,1]{0,2,1:T(2,128)(2,1)S(1)}, u32[]{:S(2)}, u32[]{:S(2)}) %collective-permute-start.3) | collective-permute-done | bytes 13088 | tf_op jit(solution)/shard_map/ppermute | solution.py:24
  31.2 2.9 %fusion.52 = bf16[192,896]{1,0:T(8,128)(2,1)} fusion(bf16[192,896]{0,1:T(8,128)(2,1)S(1)} %reshape.131, bf16[1,1,1,896,896]{4,3,2,1,0:T(8,128)(2,1)} %param.14, f32[896]{0:T(1024)S(1)} %broadcast_subtract_fusion, f32[192]{0:T(256)S(1)} %copy-done.8, f32[896]{0:T(1024)S(1)} %reduce, bf16[1,192,1,1,896]{4,1,3,2,0:T(8,128)(2,1)} %param.9, ...), kind=kOutput, calls=%fused_computation.32 | convolution fusion | flops 310345728 | bytes 2990016 | tf_op jit(solution)/shard_map/dot_general | solution.py:57
  34.1 1.9 %collective-permute-start.4 = (bf16[192,896]{1,0:T(8,128)(2,1)}, bf16[192,896]{1,0:T(8,128)(2,1)S(1)}, u32[]{:S(2)}, u32[]{:S(2)}) collective-permute-start(bf16[192,896]{1,0:T(8,128)(2,1)} %fusion.52), channel_id=1, source_target_pairs={{0,8},{8,16},{16,24},{1,9},{9,17},{17,25},{2,10},{10,18},{18,26},{... | collective-permute-start | bytes 1032200 | tf_op jit(solution)/shard_map/ppermute | solution.py:34
  37.2 5.6 %collective-permute-done.4 = bf16[192,896]{1,0:T(8,128)(2,1)S(1)} collective-permute-done((bf16[192,896]{1,0:T(8,128)(2,1)}, bf16[192,896]{1,0:T(8,128)(2,1)S(1)}, u32[]{:S(2)}, u32[]{:S(2)}) %collective-permute-start.4) | collective-permute-done | bytes 344096 | tf_op jit(solution)/shard_map/ppermute | solution.py:34
  44.6 1.6 %collective-permute-start.5 = (bf16[192,1,28]{0,2,1:T(8,128)(2,1)S(1)}, bf16[192,1,28]{0,2,1:T(8,128)(2,1)S(1)}, u32[]{:S(2)}, u32[]{:S(2)}) collective-permute-start(bf16[192,1,28]{0,2,1:T(8,128)(2,1)S(1)} %get-tuple-element.23), channel_id=1, source_target_pairs={{0,4},{1,5},{2,6},{3,7},{8,12},{9,13},{10,14},{11,15},{16,20},{17,... | collective-permute-start | bytes 32264 | tf_op jit(solution)/shard_map/ppermute | solution.py:22
  46.2 1.3 %collective-permute-start.6 = (bf16[192,1,28]{0,2,1:T(8,128)(2,1)S(1)}, bf16[192,1,28]{0,2,1:T(8,128)(2,1)S(1)}, u32[]{:S(2)}, u32[]{:S(2)}) collective-permute-start(bf16[192,1,28]{0,2,1:T(8,128)(2,1)S(1)} %get-tuple-element.22), channel_id=1, source_target_pairs={{4,0},{5,1},{6,2},{7,3},{12,8},{13,9},{14,10},{15,11},{20,16},{21,... | collective-permute-start | bytes 32264 | tf_op jit(solution)/shard_map/ppermute | solution.py:24
  47.7 4.2 %collective-permute-done.6 = bf16[192,1,28]{0,2,1:T(8,128)(2,1)S(1)} collective-permute-done((bf16[192,1,28]{0,2,1:T(8,128)(2,1)S(1)}, bf16[192,1,28]{0,2,1:T(8,128)(2,1)S(1)}, u32[]{:S(2)}, u32[]{:S(2)}) %collective-permute-start.6) | collective-permute-done | bytes 10784 | tf_op jit(solution)/shard_map/ppermute | solution.py:24
  51.9 3.5 %collective-permute-start.7 = (bf16[192,34,1]{0,2,1:T(2,128)(2,1)S(1)}, bf16[192,34,1]{0,2,1:T(2,128)(2,1)S(1)}, u32[]{:S(2)}, u32[]{:S(2)}) collective-permute-start(bf16[192,34,1]{0,2,1:T(2,128)(2,1)S(1)} %get-tuple-element.14), channel_id=1, source_target_pairs={{0,1},{1,2},{2,3},{4,5},{5,6},{6,7},{8,9},{9,10},{10,11},{12,13},{... | collective-permute-start | bytes 39176 | tf_op jit(solution)/shard_map/ppermute | solution.py:22
  57.0 4.2 %collective-permute-done.8 = bf16[192,34,1]{0,2,1:T(2,128)(2,1)S(1)} collective-permute-done((bf16[192,34,1]{0,2,1:T(2,128)(2,1)S(1)}, bf16[192,34,1]{0,2,1:T(2,128)(2,1)S(1)}, u32[]{:S(2)}, u32[]{:S(2)}) %collective-permute-start.8) | collective-permute-done | bytes 13088 | tf_op jit(solution)/shard_map/ppermute | solution.py:24
  62.1 3.0 %fusion.55 = bf16[192,896]{1,0:T(8,128)(2,1)} fusion(bf16[192,896]{0,1:T(8,128)(2,1)S(1)} %reshape.133, bf16[1,1,1,896,896]{4,3,2,1,0:T(8,128)(2,1)} %param.14, f32[896]{0:T(1024)S(1)} %broadcast_subtract_fusion, f32[192]{0:T(256)S(1)} %reshape.141, f32[896]{0:T(1024)S(1)} %reduce, bf16[192,896]{1,0:T(8,128)(2,1)} %copy-done.11, ...), kind=kOutput, calls=%fused_computation.33 | convolution fusion | flops 310345728 | bytes 2990016 | tf_op jit(solution)/shard_map/dot_general | solution.py:57
  65.0 1.9 %collective-permute-start.9 = (bf16[192,896]{1,0:T(8,128)(2,1)}, bf16[192,896]{1,0:T(8,128)(2,1)S(1)}, u32[]{:S(2)}, u32[]{:S(2)}) collective-permute-start(bf16[192,896]{1,0:T(8,128)(2,1)} %fusion.55), channel_id=1, source_target_pairs={{0,8},{8,16},{16,24},{1,9},{9,17},{17,25},{2,10},{10,18},{18,26},{... | collective-permute-start | bytes 1032200 | tf_op jit(solution)/shard_map/ppermute | solution.py:34
  68.1 5.7 %collective-permute-done.9 = bf16[192,896]{1,0:T(8,128)(2,1)S(1)} collective-permute-done((bf16[192,896]{1,0:T(8,128)(2,1)}, bf16[192,896]{1,0:T(8,128)(2,1)S(1)}, u32[]{:S(2)}, u32[]{:S(2)}) %collective-permute-start.9) | collective-permute-done | bytes 344096 | tf_op jit(solution)/shard_map/ppermute | solution.py:34
  75.5 1.6 %collective-permute-start.10 = (bf16[192,1,28]{0,2,1:T(8,128)(2,1)S(1)}, bf16[192,1,28]{0,2,1:T(8,128)(2,1)S(1)}, u32[]{:S(2)}, u32[]{:S(2)}) collective-permute-start(bf16[192,1,28]{0,2,1:T(8,128)(2,1)S(1)} %get-tuple-element.21), channel_id=1, source_target_pairs={{0,4},{1,5},{2,6},{3,7},{8,12},{9,13},{10,14},{11,15},{16,20},{17,... | collective-permute-start | bytes 32264 | tf_op jit(solution)/shard_map/ppermute | solution.py:22
  78.6 4.2 %collective-permute-done.11 = bf16[192,1,28]{0,2,1:T(8,128)(2,1)S(1)} collective-permute-done((bf16[192,1,28]{0,2,1:T(8,128)(2,1)S(1)}, bf16[192,1,28]{0,2,1:T(8,128)(2,1)S(1)}, u32[]{:S(2)}, u32[]{:S(2)}) %collective-permute-start.11) | collective-permute-done | bytes 10784 | tf_op jit(solution)/shard_map/ppermute | solution.py:24
  82.9 3.5 %collective-permute-start.12 = (bf16[192,34,1]{0,2,1:T(2,128)(2,1)S(1)}, bf16[192,34,1]{0,2,1:T(2,128)(2,1)S(1)}, u32[]{:S(2)}, u32[]{:S(2)}) collective-permute-start(bf16[192,34,1]{0,2,1:T(2,128)(2,1)S(1)} %get-tuple-element.12), channel_id=1, source_target_pairs={{0,1},{1,2},{2,3},{4,5},{5,6},{6,7},{8,9},{9,10},{10,11},{12,13},{... | collective-permute-start | bytes 39176 | tf_op jit(solution)/shard_map/ppermute | solution.py:22
  88.0 4.2 %collective-permute-done.13 = bf16[192,34,1]{0,2,1:T(2,128)(2,1)S(1)} collective-permute-done((bf16[192,34,1]{0,2,1:T(2,128)(2,1)S(1)}, bf16[192,34,1]{0,2,1:T(2,128)(2,1)S(1)}, u32[]{:S(2)}, u32[]{:S(2)}) %collective-permute-start.13) | collective-permute-done | bytes 13088 | tf_op jit(solution)/shard_map/ppermute | solution.py:24
  93.1 2.1 %fusion.58 = bf16[192,896]{1,0:T(8,128)(2,1)S(1)} fusion(bf16[192,896]{0,1:T(8,128)(2,1)S(1)} %reshape.135, bf16[1,1,1,896,896]{4,3,2,1,0:T(8,128)(2,1)} %param.14, f32[896]{0:T(1024)S(1)} %broadcast_subtract_fusion, f32[192]{0:T(256)S(1)} %reshape.140, f32[896]{0:T(1024)S(1)} %reduce, bf16[192,896]{1,0:T(8,128)(2,1)} %copy-done.12, ...), kind=kOutput, calls=%fused_computation.34 | convolution fusion | flops 310345728 | bytes 2990016 | tf_op jit(solution)/shard_map/dot_general | solution.py:57
  95.2 2.1 %collective-permute-start.14 = (bf16[192,896]{1,0:T(8,128)(2,1)S(1)}, bf16[192,896]{1,0:T(8,128)(2,1)S(1)}, u32[]{:S(2)}, u32[]{:S(2)}) collective-permute-start(bf16[192,896]{1,0:T(8,128)(2,1)S(1)} %fusion.58), channel_id=1, source_target_pairs={{0,8},{8,16},{16,24},{1,9},{9,17},{17,25},{2,10},{10,18},{18,26},{... | collective-permute-start | bytes 1032200 | tf_op jit(solution)/shard_map/ppermute | solution.py:34
  98.5 5.2 %collective-permute-done.14 = bf16[192,896]{1,0:T(8,128)(2,1)S(1)} collective-permute-done((bf16[192,896]{1,0:T(8,128)(2,1)S(1)}, bf16[192,896]{1,0:T(8,128)(2,1)S(1)}, u32[]{:S(2)}, u32[]{:S(2)}) %collective-permute-start.14) | collective-permute-done | bytes 344096 | tf_op jit(solution)/shard_map/ppermute | solution.py:34
  104.9 1.6 %collective-permute-start.15 = (bf16[192,1,28]{0,2,1:T(8,128)(2,1)S(1)}, bf16[192,1,28]{0,2,1:T(8,128)(2,1)S(1)}, u32[]{:S(2)}, u32[]{:S(2)}) collective-permute-start(bf16[192,1,28]{0,2,1:T(8,128)(2,1)S(1)} %get-tuple-element.19), channel_id=1, source_target_pairs={{0,4},{1,5},{2,6},{3,7},{8,12},{9,13},{10,14},{11,15},{16,20},{17,... | collective-permute-start | bytes 32264 | tf_op jit(solution)/shard_map/ppermute | solution.py:22
  108.0 4.2 %collective-permute-done.16 = bf16[192,1,28]{0,2,1:T(8,128)(2,1)S(1)} collective-permute-done((bf16[192,1,28]{0,2,1:T(8,128)(2,1)S(1)}, bf16[192,1,28]{0,2,1:T(8,128)(2,1)S(1)}, u32[]{:S(2)}, u32[]{:S(2)}) %collective-permute-start.16) | collective-permute-done | bytes 10784 | tf_op jit(solution)/shard_map/ppermute | solution.py:24
  112.2 1.9 %collective-permute-start.17 = (bf16[192,34,1]{0,2,1:T(2,128)(2,1)S(1)}, bf16[192,34,1]{0,2,1:T(2,128)(2,1)S(1)}, u32[]{:S(2)}, u32[]{:S(2)}) collective-permute-start(bf16[192,34,1]{0,2,1:T(2,128)(2,1)S(1)} %get-tuple-element.10), channel_id=1, source_target_pairs={{0,1},{1,2},{2,3},{4,5},{5,6},{6,7},{8,9},{9,10},{10,11},{12,13},{... | collective-permute-start | bytes 39176 | tf_op jit(solution)/shard_map/ppermute | solution.py:22
  115.7 4.2 %collective-permute-done.18 = bf16[192,34,1]{0,2,1:T(2,128)(2,1)S(1)} collective-permute-done((bf16[192,34,1]{0,2,1:T(2,128)(2,1)S(1)}, bf16[192,34,1]{0,2,1:T(2,128)(2,1)S(1)}, u32[]{:S(2)}, u32[]{:S(2)}) %collective-permute-start.18) | collective-permute-done | bytes 13088 | tf_op jit(solution)/shard_map/ppermute | solution.py:24
  121.2 2.8 %fusion.76 = bf16[1,192,1,1,896]{4,1,3,2,0:T(8,128)(2,1)} fusion(bf16[192,896]{0,1:T(8,128)(2,1)S(1)} %reshape.137, bf16[1,1,1,896,896]{4,3,2,1,0:T(8,128)(2,1)} %param.14, f32[896]{0:T(1024)S(1)} %broadcast_subtract_fusion, f32[896]{0:T(1024)S(1)} %reduce, f32[192]{0:T(256)S(1)} %reshape.139, bf16[192,896]{1,0:T(8,128)(2,1)S(1)} %copy-done.10, ...), kind=kOutput, calls=%fused_computation.40 | convolution fusion | flops 310345728 | bytes 2990016 | tf_op jit(solution)/shard_map/dot_general | solution.py:57
  (111 shorter events, 28.1 us)
Async XLA Ops:
  0.0 5.5 %copy-start = (bf16[1,1,1,896,896]{4,3,2,1,0:T(8,128)(2,1)S(1)}, bf16[1,1,1,896,896]{4,3,2,1,0:T(8,128)(2,1)}, u32[]{:S(2)}) copy-start(bf16[1,1,1,896,896]{4,3,2,1,0:T(8,128)(2,1)} %param.13) | copy-start | bytes 4816900
  1.6 3.9 %copy-start.7 = (f32[192]{0:T(256)}, f32[192]{0:T(256)S(1)}, u32[]{:S(2)}) copy-start(f32[192]{0:T(256)S(1)} %reshape.142) | copy-start | bytes 2308
  2.4 3.0 %copy-start.13 = (pred[192]{0:T(512)(128)(4,1)}, pred[192]{0:T(512)(128)(4,1)S(1)}, u32[]{:S(2)}) copy-start(pred[192]{0:T(512)(128)(4,1)S(1)} %compare_and_fusion) | copy-start | bytes 580
  9.8 5.4 %collective-permute-start = (bf16[192,1,28]{0,2,1:T(8,128)(2,1)}, bf16[192,1,28]{0,2,1:T(8,128)(2,1)S(1)}, u32[]{:S(2)}, u32[]{:S(2)}) collective-permute-start(bf16[192,1,28]{0,2,1:T(8,128)(2,1)} %get-tuple-element.25), channel_id=1, source_target_pairs={{0,4},{1,5},{2,6},{3,7},{8,12},{9,13},{10,14},{11,15},{16,20},{17,... | collective-permute-start | bytes 32264 | tf_op jit(solution)/shard_map/ppermute | solution.py:22
  13.2 5.8 %collective-permute-start.1 = (bf16[192,1,28]{0,2,1:T(8,128)(2,1)}, bf16[192,1,28]{0,2,1:T(8,128)(2,1)S(1)}, u32[]{:S(2)}, u32[]{:S(2)}) collective-permute-start(bf16[192,1,28]{0,2,1:T(8,128)(2,1)} %get-tuple-element.24), channel_id=1, source_target_pairs={{4,0},{5,1},{6,2},{7,3},{12,8},{13,9},{14,10},{15,11},{20,16},{21,... | collective-permute-start | bytes 32264 | tf_op jit(solution)/shard_map/ppermute | solution.py:24
  19.2 5.1 %collective-permute-start.2 = (bf16[192,34,1]{0,2,1:T(2,128)(2,1)S(1)}, bf16[192,34,1]{0,2,1:T(2,128)(2,1)S(1)}, u32[]{:S(2)}, u32[]{:S(2)}) collective-permute-start(bf16[192,34,1]{0,2,1:T(2,128)(2,1)S(1)} %get-tuple-element.16), channel_id=1, source_target_pairs={{0,1},{1,2},{2,3},{4,5},{5,6},{6,7},{8,9},{9,10},{10,11},{12,13},{... | collective-permute-start | bytes 39176 | tf_op jit(solution)/shard_map/ppermute | solution.py:22
  22.6 5.8 %collective-permute-start.3 = (bf16[192,34,1]{0,2,1:T(2,128)(2,1)S(1)}, bf16[192,34,1]{0,2,1:T(2,128)(2,1)S(1)}, u32[]{:S(2)}, u32[]{:S(2)}) collective-permute-start(bf16[192,34,1]{0,2,1:T(2,128)(2,1)S(1)} %get-tuple-element.17), channel_id=1, source_target_pairs={{1,0},{2,1},{3,2},{5,4},{6,5},{7,6},{9,8},{10,9},{11,10},{13,12},{... | collective-permute-start | bytes 39176 | tf_op jit(solution)/shard_map/ppermute | solution.py:24
  28.7 2.4 %copy-start.8 = (f32[192]{0:T(256)S(1)}, f32[192]{0:T(256)}, u32[]{:S(2)}) copy-start(f32[192]{0:T(256)} %copy-done.7) | copy-start | bytes 2308
  28.8 2.4 %copy-start.14 = (pred[192]{0:T(512)(128)(4,1)S(1)}, pred[192]{0:T(512)(128)(4,1)}, u32[]{:S(2)}) copy-start(pred[192]{0:T(512)(128)(4,1)} %copy-done.13) | copy-start | bytes 580
  31.2 4.8 %copy-start.6 = (s32[12]{0:T(128)S(1)}, s32[12]{0:T(128)}, u32[]{:S(2)}) copy-start(s32[12]{0:T(128)} %get-tuple-element.33) | copy-start | bytes 148
  34.1 8.8 %collective-permute-start.4 = (bf16[192,896]{1,0:T(8,128)(2,1)}, bf16[192,896]{1,0:T(8,128)(2,1)S(1)}, u32[]{:S(2)}, u32[]{:S(2)}) collective-permute-start(bf16[192,896]{1,0:T(8,128)(2,1)} %fusion.52), channel_id=1, source_target_pairs={{0,8},{8,16},{16,24},{1,9},{9,17},{17,25},{2,10},{10,18},{18,26},{... | collective-permute-start | bytes 1032200 | tf_op jit(solution)/shard_map/ppermute | solution.py:34
  36.2 1.1 copy-start.3
  37.2 5.6 %copy-start.1 = (bf16[192,896]{1,0:T(8,128)(2,1)}, bf16[192,896]{1,0:T(8,128)(2,1)S(1)}, u32[]{:S(2)}) copy-start(bf16[192,896]{1,0:T(8,128)(2,1)S(1)} %gather_fusion.2) | copy-start | bytes 1032196
  42.8 0.7 copy-start.11
  44.4 12.3 %copy-start.5 = (s32[12]{0:T(128)S(1)}, s32[12]{0:T(128)}, u32[]{:S(2)}) copy-start(s32[12]{0:T(128)} %get-tuple-element.31) | copy-start | bytes 148
  44.6 3.1 %collective-permute-start.5 = (bf16[192,1,28]{0,2,1:T(8,128)(2,1)S(1)}, bf16[192,1,28]{0,2,1:T(8,128)(2,1)S(1)}, u32[]{:S(2)}, u32[]{:S(2)}) collective-permute-start(bf16[192,1,28]{0,2,1:T(8,128)(2,1)S(1)} %get-tuple-element.23), channel_id=1, source_target_pairs={{0,4},{1,5},{2,6},{3,7},{8,12},{9,13},{10,14},{11,15},{16,20},{17,... | collective-permute-start | bytes 32264 | tf_op jit(solution)/shard_map/ppermute | solution.py:22
  46.2 5.6 %collective-permute-start.6 = (bf16[192,1,28]{0,2,1:T(8,128)(2,1)S(1)}, bf16[192,1,28]{0,2,1:T(8,128)(2,1)S(1)}, u32[]{:S(2)}, u32[]{:S(2)}) collective-permute-start(bf16[192,1,28]{0,2,1:T(8,128)(2,1)S(1)} %get-tuple-element.22), channel_id=1, source_target_pairs={{4,0},{5,1},{6,2},{7,3},{12,8},{13,9},{14,10},{15,11},{20,16},{21,... | collective-permute-start | bytes 32264 | tf_op jit(solution)/shard_map/ppermute | solution.py:24
  51.9 5.1 %collective-permute-start.7 = (bf16[192,34,1]{0,2,1:T(2,128)(2,1)S(1)}, bf16[192,34,1]{0,2,1:T(2,128)(2,1)S(1)}, u32[]{:S(2)}, u32[]{:S(2)}) collective-permute-start(bf16[192,34,1]{0,2,1:T(2,128)(2,1)S(1)} %get-tuple-element.14), channel_id=1, source_target_pairs={{0,1},{1,2},{2,3},{4,5},{5,6},{6,7},{8,9},{9,10},{10,11},{12,13},{... | collective-permute-start | bytes 39176 | tf_op jit(solution)/shard_map/ppermute | solution.py:22
  55.4 5.8 %collective-permute-start.8 = (bf16[192,34,1]{0,2,1:T(2,128)(2,1)S(1)}, bf16[192,34,1]{0,2,1:T(2,128)(2,1)S(1)}, u32[]{:S(2)}, u32[]{:S(2)}) collective-permute-start(bf16[192,34,1]{0,2,1:T(2,128)(2,1)S(1)} %get-tuple-element.15), channel_id=1, source_target_pairs={{1,0},{2,1},{3,2},{5,4},{6,5},{7,6},{9,8},{10,9},{11,10},{13,12},{... | collective-permute-start | bytes 39176 | tf_op jit(solution)/shard_map/ppermute | solution.py:24
  65.0 8.8 %collective-permute-start.9 = (bf16[192,896]{1,0:T(8,128)(2,1)}, bf16[192,896]{1,0:T(8,128)(2,1)S(1)}, u32[]{:S(2)}, u32[]{:S(2)}) collective-permute-start(bf16[192,896]{1,0:T(8,128)(2,1)} %fusion.55), channel_id=1, source_target_pairs={{0,8},{8,16},{16,24},{1,9},{9,17},{17,25},{2,10},{10,18},{18,26},{... | collective-permute-start | bytes 1032200 | tf_op jit(solution)/shard_map/ppermute | solution.py:34
  73.8 0.7 copy-start.12
  75.5 3.1 %collective-permute-start.10 = (bf16[192,1,28]{0,2,1:T(8,128)(2,1)S(1)}, bf16[192,1,28]{0,2,1:T(8,128)(2,1)S(1)}, u32[]{:S(2)}, u32[]{:S(2)}) collective-permute-start(bf16[192,1,28]{0,2,1:T(8,128)(2,1)S(1)} %get-tuple-element.21), channel_id=1, source_target_pairs={{0,4},{1,5},{2,6},{3,7},{8,12},{9,13},{10,14},{11,15},{16,20},{17,... | collective-permute-start | bytes 32264 | tf_op jit(solution)/shard_map/ppermute | solution.py:22
  77.2 5.6 %collective-permute-start.11 = (bf16[192,1,28]{0,2,1:T(8,128)(2,1)S(1)}, bf16[192,1,28]{0,2,1:T(8,128)(2,1)S(1)}, u32[]{:S(2)}, u32[]{:S(2)}) collective-permute-start(bf16[192,1,28]{0,2,1:T(8,128)(2,1)S(1)} %get-tuple-element.20), channel_id=1, source_target_pairs={{4,0},{5,1},{6,2},{7,3},{12,8},{13,9},{14,10},{15,11},{20,16},{21,... | collective-permute-start | bytes 32264 | tf_op jit(solution)/shard_map/ppermute | solution.py:24
  82.9 5.1 %collective-permute-start.12 = (bf16[192,34,1]{0,2,1:T(2,128)(2,1)S(1)}, bf16[192,34,1]{0,2,1:T(2,128)(2,1)S(1)}, u32[]{:S(2)}, u32[]{:S(2)}) collective-permute-start(bf16[192,34,1]{0,2,1:T(2,128)(2,1)S(1)} %get-tuple-element.12), channel_id=1, source_target_pairs={{0,1},{1,2},{2,3},{4,5},{5,6},{6,7},{8,9},{9,10},{10,11},{12,13},{... | collective-permute-start | bytes 39176 | tf_op jit(solution)/shard_map/ppermute | solution.py:22
  86.4 5.8 %collective-permute-start.13 = (bf16[192,34,1]{0,2,1:T(2,128)(2,1)S(1)}, bf16[192,34,1]{0,2,1:T(2,128)(2,1)S(1)}, u32[]{:S(2)}, u32[]{:S(2)}) collective-permute-start(bf16[192,34,1]{0,2,1:T(2,128)(2,1)S(1)} %get-tuple-element.13), channel_id=1, source_target_pairs={{1,0},{2,1},{3,2},{5,4},{6,5},{7,6},{9,8},{10,9},{11,10},{13,12},{... | collective-permute-start | bytes 39176 | tf_op jit(solution)/shard_map/ppermute | solution.py:24
  93.1 4.2 %copy-start.4 = (s32[12]{0:T(128)S(1)}, s32[12]{0:T(128)}, u32[]{:S(2)}) copy-start(s32[12]{0:T(128)} %get-tuple-element.30) | copy-start | bytes 148
  95.2 8.6 %collective-permute-start.14 = (bf16[192,896]{1,0:T(8,128)(2,1)S(1)}, bf16[192,896]{1,0:T(8,128)(2,1)S(1)}, u32[]{:S(2)}, u32[]{:S(2)}) collective-permute-start(bf16[192,896]{1,0:T(8,128)(2,1)S(1)} %fusion.58), channel_id=1, source_target_pairs={{0,8},{8,16},{16,24},{1,9},{9,17},{17,25},{2,10},{10,18},{18,26},{... | collective-permute-start | bytes 1032200 | tf_op jit(solution)/shard_map/ppermute | solution.py:34
  104.9 3.1 %collective-permute-start.15 = (bf16[192,1,28]{0,2,1:T(8,128)(2,1)S(1)}, bf16[192,1,28]{0,2,1:T(8,128)(2,1)S(1)}, u32[]{:S(2)}, u32[]{:S(2)}) collective-permute-start(bf16[192,1,28]{0,2,1:T(8,128)(2,1)S(1)} %get-tuple-element.19), channel_id=1, source_target_pairs={{0,4},{1,5},{2,6},{3,7},{8,12},{9,13},{10,14},{11,15},{16,20},{17,... | collective-permute-start | bytes 32264 | tf_op jit(solution)/shard_map/ppermute | solution.py:22
  106.5 5.6 %collective-permute-start.16 = (bf16[192,1,28]{0,2,1:T(8,128)(2,1)S(1)}, bf16[192,1,28]{0,2,1:T(8,128)(2,1)S(1)}, u32[]{:S(2)}, u32[]{:S(2)}) collective-permute-start(bf16[192,1,28]{0,2,1:T(8,128)(2,1)S(1)} %get-tuple-element.18), channel_id=1, source_target_pairs={{4,0},{5,1},{6,2},{7,3},{12,8},{13,9},{14,10},{15,11},{20,16},{21,... | collective-permute-start | bytes 32264 | tf_op jit(solution)/shard_map/ppermute | solution.py:24
  112.2 3.5 %collective-permute-start.17 = (bf16[192,34,1]{0,2,1:T(2,128)(2,1)S(1)}, bf16[192,34,1]{0,2,1:T(2,128)(2,1)S(1)}, u32[]{:S(2)}, u32[]{:S(2)}) collective-permute-start(bf16[192,34,1]{0,2,1:T(2,128)(2,1)S(1)} %get-tuple-element.10), channel_id=1, source_target_pairs={{0,1},{1,2},{2,3},{4,5},{5,6},{6,7},{8,9},{9,10},{10,11},{12,13},{... | collective-permute-start | bytes 39176 | tf_op jit(solution)/shard_map/ppermute | solution.py:22
  114.1 5.8 %collective-permute-start.18 = (bf16[192,34,1]{0,2,1:T(2,128)(2,1)S(1)}, bf16[192,34,1]{0,2,1:T(2,128)(2,1)S(1)}, u32[]{:S(2)}, u32[]{:S(2)}) collective-permute-start(bf16[192,34,1]{0,2,1:T(2,128)(2,1)S(1)} %get-tuple-element.11), channel_id=1, source_target_pairs={{1,0},{2,1},{3,2},{5,4},{6,5},{7,6},{9,8},{10,9},{11,10},{13,12},{... | collective-permute-start | bytes 39176 | tf_op jit(solution)/shard_map/ppermute | solution.py:24
  120.2 1.0 copy-start.10
  (2 other events, 1.3 us)
where the time goes:
time: 125 us; the launch traced here: 124 us
  waiting for transfers between devices  51.2 us (41%)
  starting transfers between devices  37 us (30%)
  local copies, waits for them, and re-layouts  16.6 us (13%)
  matrix products  14.2 us (11%)
  other arithmetic  4.5 us (4%)
    ppermute x8, waiting for transfers between devices, extended(): lax.ppermute(head, axis, [((i + 1) % count, i) for i in range(ends)])  33.2 us
    ppermute x8, starting transfers between devices, extended(): lax.ppermute(tail, axis, [(i, (i + 1) % count) for i in range(ends)])  20.7 us
    ppermute x3, waiting for transfers between devices, shifted(): return lax.ppermute(x, axis, pairs)  16.5 us
    dot_general x4, matrix products, advance(): jnp.dot(coupled.reshape(slot_count, FX * FY), map_second, preferred_eleme...  10.7 us
    ppermute x8, starting transfers between devices, extended(): lax.ppermute(head, axis, [((i + 1) % count, i) for i in range(ends)])  10.3 us
    ppermute x3, starting transfers between devices, shifted(): return lax.ppermute(x, axis, pairs)  5.92 us
    gather x4, local copies, waits for them, and re-layouts, local(): jnp.take(source[0, round_number, :, 0, 0, :], assignment[round_number], a...  4.16 us
    dot_general x4, matrix products, advance(): jnp.dot(start_trace, map_first, preferred_element_type=jnp.float32)  3.45 us
  transfers between devices with their start and end apart: 19, of which 18 were waited for; matrix products, arithmetic and copies ran while one was open for 4% of the time, Pallas kernels for 0%

commit v1 on v0

v1 whole, which is shorter than its diff:
```python
import functools

import jax
import jax.numpy as jnp
from jax import lax
from jax.experimental import pallas as pl
from jax.experimental.pallas import tpu as pltpu
from jax.sharding import PartitionSpec as P

FX = 32
FY = 28
SHOT_BATCH = 16

coupling_weight = 0.25

LANES = 128
GROUP = LANES // 4
EDGE_AXES = (("gx", 0), ("gy", 2))


def dot(a, b):
    return jnp.dot(a, b, preferred_element_type=jnp.float32)


def dot_t(a, b):
    return lax.dot_general(a, b, (((0,), (0,)), ((), ())), preferred_element_type=jnp.float32)


def edge_selector(cells):
    row = lax.broadcasted_iota(jnp.int32, (cells, LANES), 0)
    lane = lax.broadcasted_iota(jnp.int32, (cells, LANES), 1)
    group = lane // GROUP
    spot = lane % GROUP
    along_x = group < 2
    cell = jnp.where(
        along_x,
        jnp.where(group == 0, spot, (FX - 1) * FY + spot),
        jnp.where(group == 2, spot * FY, spot * FY + FY - 1),
    )
    length = jnp.where(along_x, FY, FX)
    return jnp.where((row == cell) & (spot < length), 1.0, 0.0).astype(jnp.bfloat16)


def exchanges():
    found = []
    for axis, base in EDGE_AXES:
        for parity in range(min(lax.axis_size(axis) - 1, 2)):
            found.append((axis, parity, base))
    return found


def group_of(axis, parity, base):
    ahead = lax.axis_index(axis) % 2 == parity
    return jnp.where(ahead, base + 1, base)


def pack(edges, group):
    rows = edges.shape[0] // 4
    lane_group = lax.broadcasted_iota(jnp.int32, (rows, LANES), 1) // GROUP
    packed = jnp.zeros((rows, LANES), jnp.float32)
    for part in range(4):
        piece = edges[part * rows : (part + 1) * rows]
        piece = pltpu.roll(piece, (part - group + 4) % 4 * GROUP, 1)
        packed = jnp.where(lane_group == part, piece, packed)
    return packed.astype(jnp.bfloat16)


def unpack(packed, group):
    lane_group = lax.broadcasted_iota(jnp.int32, packed.shape, 1) // GROUP
    pieces = []
    for part in range(4):
        piece = pltpu.roll(packed, (group - part + 4) % 4 * GROUP, 1)
        pieces.append(jnp.where(lane_group == group, piece, 0.0))
    return jnp.concatenate(pieces, axis=0)


def unit_of(round_number):
    return round_number - lax.axis_index("depth") + lax.axis_size("depth") - 1


def only_active(values, counts_ref, unit):
    position = lax.broadcasted_iota(jnp.int32, (SHOT_BATCH, values.shape[1]), 0)
    pieces = []
    for batch in range(values.shape[0] // SHOT_BATCH):
        piece = values[batch * SHOT_BATCH : (batch + 1) * SHOT_BATCH]
        pieces.append(jnp.where(position < counts_ref[unit, batch], piece, 0.0))
    return jnp.concatenate(pieces, axis=0)


def opening_kernel(swaps, arrival, source, assignment, counts, first_map, *outs):
    start0, later, edge_out = outs[0], outs[1], outs[2]
    messages = outs[3:]
    rounds, slots, cells = source.shape
    first_edge = dot(first_map[...], edge_selector(cells)).astype(jnp.bfloat16)
    edge_out[:cells] = first_edge
    shot = lax.broadcasted_iota(jnp.int32, (slots, slots), 0)
    slot = lax.broadcasted_iota(jnp.int32, (1, slots), 1)
    for round_number in range(rounds):
        unit = unit_of(round_number)
        live = jnp.zeros((1, slots), jnp.int32)
        for batch in range(slots // SHOT_BATCH):
            live = jnp.where(slot // SHOT_BATCH == batch, counts[unit, batch], live)
        wanted = jnp.where(
            slot % SHOT_BATCH < live, assignment[round_number : round_number + 1], -1
        )
        chosen = jnp.where(shot == wanted, 1.0, 0.0).astype(jnp.bfloat16)
        picked = dot_t(chosen, source[round_number])
        if round_number == 0:
            picked = picked + only_active(arrival[...].astype(jnp.float32), counts, unit)
        picked = picked.astype(jnp.bfloat16)
        edges = dot(picked, first_edge)
        if round_number == 0:
            start0[...] = picked
        else:
            later[round_number - 1] = picked
            at = cells + (round_number - 1) * slots
            edge_out[at : at + slots] = edges.astype(jnp.bfloat16)
            edges = jnp.where(lax.axis_index("depth") == 0, edges, 0.0)
        at = round_number * (slots // 4)
        for message, swap in zip(messages, swaps):
            message[at : at + slots // 4] = pack(edges, group_of(*swap))


def coupled_map_kernel(start0, first_map, second_map, mapped_out, second_ext, padded):
    cells = second_map.shape[0]
    margin = 32
    mapped_out[...] = dot(start0[...], first_map[...]).astype(jnp.bfloat16)
    width = second_map.shape[1]
    padded[:margin] = jnp.zeros((margin, width), jnp.float32)
    padded[margin + cells :] = jnp.zeros((margin, width), jnp.float32)
    padded[margin : margin + cells] = second_map[...].astype(jnp.float32)
    column = lax.broadcasted_iota(jnp.int32, (cells, 1), 0) % FY
    middle = padded[margin : margin + cells]
    sides = padded[margin - FY : margin - FY + cells] + padded[margin + FY : margin + FY + cells]
    sides += jnp.where(column > 0, padded[margin - 1 : margin - 1 + cells], 0.0)
    sides += jnp.where(column < FY - 1, padded[margin + 1 : margin + 1 + cells], 0.0)
    second_ext[:cells] = (middle + coupling_weight * sides).astype(jnp.bfloat16)
    edge_rows = dot_t(edge_selector(cells), second_map[...])
    second_ext[cells:] = (coupling_weight * edge_rows).astype(jnp.bfloat16)


def whole_map_kernel(first_map, second_ext, whole_ext):
    cells = first_map.shape[0]
    whole_ext[:cells] = dot(first_map[...], second_ext[:cells]).astype(jnp.bfloat16)
    whole_ext[cells:] = second_ext[cells:]


def step_kernel(swaps, round_number, last, *refs):
    refs = list(refs)
    traces, extra, map_ext, damping, counts = refs[:5]
    opened = refs[5 : 5 + len(swaps)]
    rest = refs[5 + len(swaps) :]
    received = [None] * len(swaps)
    if round_number > 0:
        received, rest = rest[: len(swaps)], rest[len(swaps) :]
    if not last:
        edge_next, rest = rest[0], rest[1:]
    traces_out = rest[0]
    messages = rest[1:]
    slots, cells = traces.shape
    unit = unit_of(round_number)
    halo = jnp.zeros((slots, LANES), jnp.float32)
    part = slots // 4
    for first, later, swap in zip(opened, received, swaps):
        message = first[round_number * part : (round_number + 1) * part].astype(jnp.float32)
        if later is not None:
            message = message + later[...].astype(jnp.float32)
        halo = halo + unpack(message, group_of(*swap))
    halo = only_active(halo, counts, unit).astype(jnp.bfloat16)
    if round_number == 0:
        start = extra[...].astype(jnp.float32)
        row = traces[...]
    else:
        row = (traces[...].astype(jnp.float32) + extra[...].astype(jnp.float32)).astype(
            jnp.bfloat16
        )
        start = row.astype(jnp.float32)
    image = dot(jnp.concatenate([row, halo], axis=1), map_ext[...])
    damp = damping[...]
    ended = (damp * image + (1.0 - damp) * start).astype(jnp.bfloat16)
    traces_out[...] = ended
    if not last:
        at = cells + round_number * slots
        edges = dot(ended, edge_next[:cells]) + edge_next[at : at + slots].astype(jnp.float32)
        for message, swap in zip(messages, swaps):
            message[...] = pack(edges, group_of(*swap))


def call(kernel, out_shape, operands, scalars=(), scratch=()):
    spaces = [pltpu.SMEM if i in scalars else pltpu.VMEM for i in range(len(operands))]
    return pl.pallas_call(
        kernel,
        out_shape=out_shape,
        in_specs=[pl.BlockSpec(memory_space=space) for space in spaces],
        out_specs=[pl.BlockSpec(memory_space=pltpu.VMEM)] * len(out_shape),
        scratch_shapes=scratch,
        compiler_params=pltpu.CompilerParams(vmem_limit_bytes=32 * 1024 * 1024),
    )(*operands)


MESH_AXES = ("depth", "gx", "gy")


def send(x, layers, down, swap=None):
    sizes = [lax.axis_size(axis) for axis in MESH_AXES]
    pairs = []
    for layer in layers:
        for i in range(sizes[1]):
            for j in range(sizes[2]):
                to = {"depth": layer + down, "gx": i, "gy": j}
                if swap is not None:
                    axis, parity, _ = swap
                    to[axis] += 1 if to[axis] % 2 == parity else -1
                spot = [to[axis] for axis in MESH_AXES]
                if all(0 <= s < size for s, size in zip(spot, sizes)):
                    here = (layer * sizes[1] + i) * sizes[2] + j
                    there = (spot[0] * sizes[1] + spot[1]) * sizes[2] + spot[2]
                    pairs.append((here, there))
    return lax.ppermute(x, MESH_AXES, pairs)


def local(arrival, source, assignment, counts, first_map, second_map, damping):
    layers = lax.axis_size("depth")
    slots, cells = arrival.shape[1], arrival.shape[4]
    rounds = source.shape[1]
    arrival = arrival[0, :, 0, 0, :]
    source = source[0, :, :, 0, 0, :]
    counts = counts[:, :, 0, 0]
    first_map = first_map[0, 0, 0]
    second_map = second_map[0, 0, 0]
    damping = damping[0, 0]
    swaps = exchanges()
    useful = [
        [layer for layer in range(layers) if layer - r <= layers - rounds] for r in range(rounds)
    ]

    def array(*shape):
        return jax.ShapeDtypeStruct(shape, jnp.bfloat16)

    message = array(slots // 4, LANES)
    opened = call(
        functools.partial(opening_kernel, swaps),
        [
            array(slots, cells),
            array(rounds - 1, slots, cells),
            array(cells + (rounds - 1) * slots, LANES),
        ]
        + [array(rounds * (slots // 4), LANES)] * len(swaps),
        [arrival, source, assignment, counts, first_map],
        scalars=(3,),
    )
    start0, later, edge = opened[:3]
    first_received = [send(m, useful[0], 0, swap) for m, swap in zip(opened[3:], swaps)]
    received = []
    edge_next = send(edge, range(1, layers), -1)
    mapped, second_ext = call(
        coupled_map_kernel,
        [array(slots, cells), array(cells + LANES, cells)],
        [start0, first_map, second_map],
        scratch=[pltpu.VMEM((cells + 64, cells), jnp.float32)],
    )
    traces, extra, map_ext = mapped, start0, second_ext
    for round_number in range(rounds):
        last = round_number == rounds - 1
        operands = [traces, extra, map_ext, damping, counts] + first_received + received
        outs = [array(slots, cells)]
        if not last:
            operands.append(edge_next)
            outs += [message] * len(swaps)
        ended = call(
            functools.partial(step_kernel, swaps, round_number, last), outs, operands, scalars=(4,)
        )
        traces = ended[0]
        if not last:
            traces = send(traces, useful[round_number], 1)
            received = [
                send(m, useful[round_number], 1, swap) for m, swap in zip(ended[1:], swaps)
            ]
            extra = later[round_number]
            if round_number == 0:
                (map_ext,) = call(
                    whole_map_kernel, [array(cells + LANES, cells)], [first_map, second_ext]
                )
    return traces.reshape(1, slots, 1, 1, cells)


def solution(mesh):
    return jax.shard_map(
        local,
        mesh=mesh,
        in_specs=(
            P("depth", None, "gx", "gy", None),
            P("depth", None, None, "gx", "gy", None),
            P(),
            P(None, None, "gx", "gy"),
            P("depth", "gx", "gy", None, None),
            P("depth", "gx", "gy", None, None),
            P("depth", "gx", "gy", None),
        ),
        out_specs=P("depth", None, "gx", "gy", None),
        check_vma=False,
    )
```

time: 125 us -> 59.2 us (0.47)
  the two profiles are of different devices: /device:TPU:2 before, /device:TPU:9 now
where the time goes in v1:
time: 59.2 us; the launch traced here: 58.7 us
  starting transfers between devices  26 us (44%)
  Pallas kernels  13.8 us (23%)
  waiting for transfers between devices  13.4 us (23%)
  local copies, waits for them, and re-layouts  5.21 us (9%)
    ppermute x16, starting transfers between devices, send(): return lax.ppermute(x, MESH_AXES, pairs)  26 us
    pallas_call x7, Pallas kernels, call(): pl.pallas_call(kernel, out_shape=out_shape, in_specs=[pl.BlockSpec(memory...  13.8 us
    ppermute x16, waiting for transfers between devices, send(): return lax.ppermute(x, MESH_AXES, pairs)  13.4 us
    unnamed x15, local copies, waits for them, and re-layouts  5.12 us
  transfers between devices with their start and end apart: 16, of which 7 were waited for; matrix products, arithmetic and copies ran while one was open for 0% of the time, Pallas kernels for 9%

profile of v1, /device:TPU:9, one launch (start us, length us, event | category | flops | bytes accessed | tf_op | source)
XLA Modules:
  0.0 58.7 jit_solution(13032837837712143902)
XLA Ops:
  0.0 0.7 %copy.10 = s32[7,12,1,1]{1,0,2,3:T(8,128)S(1)} copy(s32[7,12,1,1]{1,3,2,0:T(1,128)} %param.10) | data formatting | bytes 672
  0.7 1.4 %copy-done = bf16[1,1,1,896,896]{4,3,2,1,0:T(8,128)(2,1)S(1)} copy-done((bf16[1,1,1,896,896]{4,3,2,1,0:T(8,128)(2,1)S(1)}, bf16[1,1,1,896,896]{4,3,2,1,0:T(8,128)(2,1)}, u32[]{:S(2)}) %copy-start) | copy-done | bytes 1605656
  2.1 1.3 %copy-done.3 = bf16[1,4,192,1,1,896]{5,2,4,3,1,0:T(8,128)(2,1)S(1)} copy-done((bf16[1,4,192,1,1,896]{5,2,4,3,1,0:T(8,128)(2,1)S(1)}, bf16[1,4,192,1,1,896]{5,2,4,3,1,0:T(8,128)(2,1)}, u32[]{:S(2)}) %copy-start.3) | copy-done | bytes 1376280
  3.4 1.0 %copy-done.4 = bf16[1,192,1,1,896]{4,1,3,2,0:T(8,128)(2,1)S(1)} copy-done((bf16[1,192,1,1,896]{4,1,3,2,0:T(8,128)(2,1)S(1)}, bf16[1,192,1,1,896]{4,1,3,2,0:T(8,128)(2,1)}, u32[]{:S(2)}) %copy-start.4) | copy-done | bytes 344088
  4.4 0.7 %copy-done.6 = s32[4,192]{1,0:T(4,128)S(1)} copy-done((s32[4,192]{1,0:T(4,128)S(1)}, s32[4,192]{1,0:T(4,128)}, u32[]{:S(2)}) %copy-start.6) | copy-done | bytes 3096
  5.1 2.5 %shard_map.73 = (bf16[192,896]{1,0:T(8,128)(2,1)S(1)}, bf16[3,192,896]{2,1,0:T(8,128)(2,1)S(1)}, bf16[1472,128]{1,0:T(8,128)(2,1)S(1)}, bf16[192,128]{1,0:T(8,12...) custom-call(bf16[192,896]{1,0:T(8,128)(2,1)S(1)} %bitcast.20, bf16[4,192,896]{2,1,0:T(8,128)(2,1)S(1)} %bitcast.19, ...), custom_call_target="tpu_custom_call" | custom-call | tf_op jit(solution)/shard_map/pallas_call | solution.py:191
  7.6 2.6 %collective-permute-start.3 = (bf16[1472,128]{1,0:T(8,128)(2,1)S(1)}, bf16[1472,128]{1,0:T(8,128)(2,1)S(1)}, u32[]{:S(2)}, u32[]{:S(2)}) collective-permute-start(bf16[1472,128]{1,0:T(8,128)(2,1)S(1)} %get-tuple-element.31), channel_id=1, source_target_pairs={{8,0},{9,1},{10,2},{11,3},{12,4},{13,5},{14,6},{15,7},{16,8},{17,9... | collective-permute-start | bytes 1130504 | tf_op jit(solution)/shard_map/ppermute | solution.py:219
  12.2 3.1 %shard_map.74 = (bf16[192,896]{1,0:T(8,128)(2,1)S(1)}, bf16[1024,896]{1,0:T(8,128)(2,1)S(1)}) custom-call(bf16[192,896]{1,0:T(8,128)(2,1)S(1)} %get-tuple-element.25.start0.refs_1_, bf16[896,896]{1,0:T(8,128)(2,1)S(1)} %bitcast.16, bf16[896,896]{1,0:T(8,128)(2,1)S(1)} %bitcast.18), custom_call_target="tpu_custom_call" | custom-call | tf_op jit(solution)/shard_map/pallas_call | solution.py:191
  15.4 1.2 %collective-permute-done.3.refs_8_.refs_11_ = bf16[1472,128]{1,0:T(8,128)(2,1)S(1)} collective-permute-done((bf16[1472,128]{1,0:T(8,128)(2,1)S(1)}, bf16[1472,128]{1,0:T(8,128)(2,1)S(1)}, u32[]{:S(2)}, u32[]{:S(2)}) %collective-permute-start.3) | collective-permute-done | bytes 376864 | tf_op jit(solution)/shard_map/ppermute | solution.py:219
  16.6 1.4 %shard_map.75 = (bf16[192,896]{1,0:T(8,128)(2,1)S(1)}, bf16[48,128]{1,0:T(8,128)(2,1)S(1)}, bf16[48,128]{1,0:T(8,128)(2,1)S(1)}, bf16[48,128]{1,0:T(8,128)(2,1)S(1)}) custom-call(bf16[192,896]{1,0:T(8,128)(2,1)S(1)} %get-tuple-element.26.refs_0_, bf16[192,896]{1,0:T(8,128)(2,1)S(1)} %get-tuple-element.25.start0.refs_1_, ...), custom_call_target="tpu_custom_call" | custom-call | tf_op jit(solution)/shard_map/pallas_call | solution.py:191
  18.0 1.3 %collective-permute-start.4 = (bf16[192,896]{1,0:T(8,128)(2,1)S(1)}, bf16[192,896]{1,0:T(8,128)(2,1)S(1)}, u32[]{:S(2)}, u32[]{:S(2)}) collective-permute-start(bf16[192,896]{1,0:T(8,128)(2,1)S(1)} %get-tuple-element.32), channel_id=1, source_target_pairs={{0,8},{1,9},{2,10},{3,11},{4,12},{5,13},{6,14},{7,15}} | collective-permute-start | bytes 1032200 | tf_op jit(solution)/shard_map/ppermute | solution.py:219
  19.3 1.3 %collective-permute-start.5 = (bf16[48,128]{1,0:T(8,128)(2,1)S(1)}, bf16[48,128]{1,0:T(8,128)(2,1)S(1)}, u32[]{:S(2)}, u32[]{:S(2)}) collective-permute-start(bf16[48,128]{1,0:T(8,128)(2,1)S(1)} %get-tuple-element.34), channel_id=1, source_target_pairs={{0,12},{1,13},{2,14},{3,15},{4,8},{5,9},{6,10},{7,11}} | collective-permute-start | bytes 36872 | tf_op jit(solution)/shard_map/ppermute | solution.py:219
  20.6 1.3 %collective-permute-start.6 = (bf16[48,128]{1,0:T(8,128)(2,1)S(1)}, bf16[48,128]{1,0:T(8,128)(2,1)S(1)}, u32[]{:S(2)}, u32[]{:S(2)}) collective-permute-start(bf16[48,128]{1,0:T(8,128)(2,1)S(1)} %get-tuple-element.35), channel_id=1, source_target_pairs={{0,9},{1,8},{2,11},{3,10},{4,13},{5,12},{6,15},{7,14}} | collective-permute-start | bytes 36872 | tf_op jit(solution)/shard_map/ppermute | solution.py:219
  21.9 1.3 %collective-permute-start.7 = (bf16[48,128]{1,0:T(8,128)(2,1)S(1)}, bf16[48,128]{1,0:T(8,128)(2,1)S(1)}, u32[]{:S(2)}, u32[]{:S(2)}) collective-permute-start(bf16[48,128]{1,0:T(8,128)(2,1)S(1)} %get-tuple-element.36), channel_id=1, source_target_pairs={{1,10},{2,9},{5,14},{6,13}} | collective-permute-start | bytes 36872 | tf_op jit(solution)/shard_map/ppermute | solution.py:219
  23.3 2.0 %shard_map.76.refs_2_ = bf16[1024,896]{1,0:T(8,128)(2,1)S(1)} custom-call(bf16[896,896]{1,0:T(8,128)(2,1)S(1)} %bitcast.17, bf16[1024,896]{1,0:T(8,128)(2,1)S(1)} %get-tuple-element.27.refs_2_.second_ext), custom_call_target="tpu_custom_call" | custom-call | tf_op jit(solution)/shard_map/pallas_call | solution.py:191
  25.3 3.4 %collective-permute-done.5.refs_8_ = bf16[48,128]{1,0:T(8,128)(2,1)S(1)} collective-permute-done((bf16[48,128]{1,0:T(8,128)(2,1)S(1)}, bf16[48,128]{1,0:T(8,128)(2,1)S(1)}, u32[]{:S(2)}, u32[]{:S(2)}) %collective-permute-start.5) | collective-permute-done | bytes 12320 | tf_op jit(solution)/shard_map/ppermute | solution.py:219
  28.7 3.0 %collective-permute-done.7.refs_10_ = bf16[48,128]{1,0:T(8,128)(2,1)S(1)} collective-permute-done((bf16[48,128]{1,0:T(8,128)(2,1)S(1)}, bf16[48,128]{1,0:T(8,128)(2,1)S(1)}, u32[]{:S(2)}, u32[]{:S(2)}) %collective-permute-start.7) | collective-permute-done | bytes 12320 | tf_op jit(solution)/shard_map/ppermute | solution.py:219
  31.7 1.4 %shard_map.77 = (bf16[192,896]{1,0:T(8,128)(2,1)S(1)}, bf16[48,128]{1,0:T(8,128)(2,1)S(1)}, bf16[48,128]{1,0:T(8,128)(2,1)S(1)}, bf16[48,128]{1,0:T(8,128)(2,1)S(1)}) custom-call(bf16[192,896]{1,0:T(8,128)(2,1)S(1)} %collective-permute-done.4.refs_0_, bf16[192,896]{1,0:T(8,128)(2,1)S(1)} %get-tuple-element.47.refs_1_, ...), custom_call_target="tpu_custom_call" | custom-call | tf_op jit(solution)/shard_map/pallas_call | solution.py:191
  33.1 1.9 %collective-permute-start.8 = (bf16[192,896]{1,0:T(8,128)(2,1)S(1)}, bf16[192,896]{1,0:T(8,128)(2,1)S(1)}, u32[]{:S(2)}, u32[]{:S(2)}) collective-permute-start(bf16[192,896]{1,0:T(8,128)(2,1)S(1)} %get-tuple-element.37), channel_id=1, source_target_pairs={{0,8},{1,9},{2,10},{3,11},{4,12},{5,13},{6,14},{7,15},{8,16},{9,17... | collective-permute-start | bytes 1032200 | tf_op jit(solution)/shard_map/ppermute | solution.py:219
  35.0 1.9 %collective-permute-start.9 = (bf16[48,128]{1,0:T(8,128)(2,1)S(1)}, bf16[48,128]{1,0:T(8,128)(2,1)S(1)}, u32[]{:S(2)}, u32[]{:S(2)}) collective-permute-start(bf16[48,128]{1,0:T(8,128)(2,1)S(1)} %get-tuple-element.38), channel_id=1, source_target_pairs={{0,12},{1,13},{2,14},{3,15},{4,8},{5,9},{6,10},{7,11},{8,20},{9,21... | collective-permute-start | bytes 36872 | tf_op jit(solution)/shard_map/ppermute | solution.py:219
  37.0 1.9 %collective-permute-start.10 = (bf16[48,128]{1,0:T(8,128)(2,1)S(1)}, bf16[48,128]{1,0:T(8,128)(2,1)S(1)}, u32[]{:S(2)}, u32[]{:S(2)}) collective-permute-start(bf16[48,128]{1,0:T(8,128)(2,1)S(1)} %get-tuple-element.39), channel_id=1, source_target_pairs={{0,9},{1,8},{2,11},{3,10},{4,13},{5,12},{6,15},{7,14},{8,17},{9,16... | collective-permute-start | bytes 36872 | tf_op jit(solution)/shard_map/ppermute | solution.py:219
  38.9 1.9 %collective-permute-start.11 = (bf16[48,128]{1,0:T(8,128)(2,1)S(1)}, bf16[48,128]{1,0:T(8,128)(2,1)S(1)}, u32[]{:S(2)}, u32[]{:S(2)}) collective-permute-start(bf16[48,128]{1,0:T(8,128)(2,1)S(1)} %get-tuple-element.40), channel_id=1, source_target_pairs={{1,10},{2,9},{5,14},{6,13},{9,18},{10,17},{13,22},{14,21}} | collective-permute-start | bytes 36872 | tf_op jit(solution)/shard_map/ppermute | solution.py:219
  40.8 1.1 %collective-permute-done.10.refs_9_ = bf16[48,128]{1,0:T(8,128)(2,1)S(1)} collective-permute-done((bf16[48,128]{1,0:T(8,128)(2,1)S(1)}, bf16[48,128]{1,0:T(8,128)(2,1)S(1)}, u32[]{:S(2)}, u32[]{:S(2)}) %collective-permute-start.10) | collective-permute-done | bytes 12320 | tf_op jit(solution)/shard_map/ppermute | solution.py:219
  42.0 1.9 %collective-permute-done.11.refs_10_ = bf16[48,128]{1,0:T(8,128)(2,1)S(1)} collective-permute-done((bf16[48,128]{1,0:T(8,128)(2,1)S(1)}, bf16[48,128]{1,0:T(8,128)(2,1)S(1)}, u32[]{:S(2)}, u32[]{:S(2)}) %collective-permute-start.11) | collective-permute-done | bytes 12320 | tf_op jit(solution)/shard_map/ppermute | solution.py:219
  43.9 1.4 %shard_map.78 = (bf16[192,896]{1,0:T(8,128)(2,1)S(1)}, bf16[48,128]{1,0:T(8,128)(2,1)S(1)}, bf16[48,128]{1,0:T(8,128)(2,1)S(1)}, bf16[48,128]{1,0:T(8,128)(2,1)S(1)}) custom-call(bf16[192,896]{1,0:T(8,128)(2,1)S(1)} %collective-permute-done.8.refs_0_, bf16[192,896]{1,0:T(8,128)(2,1)S(1)} %get-tuple-element.46.refs_1_, ...), custom_call_target="tpu_custom_call" | custom-call | tf_op jit(solution)/shard_map/pallas_call | solution.py:191
  45.3 2.5 %collective-permute-start.12 = (bf16[192,896]{1,0:T(8,128)(2,1)S(1)}, bf16[192,896]{1,0:T(8,128)(2,1)S(1)}, u32[]{:S(2)}, u32[]{:S(2)}) collective-permute-start(bf16[192,896]{1,0:T(8,128)(2,1)S(1)} %get-tuple-element.41), channel_id=1, source_target_pairs={{0,8},{1,9},{2,10},{3,11},{4,12},{5,13},{6,14},{7,15},{8,16},{9,17... | collective-permute-start | bytes 1032200 | tf_op jit(solution)/shard_map/ppermute | solution.py:219
  47.8 1.9 %collective-permute-start.13 = (bf16[48,128]{1,0:T(8,128)(2,1)S(1)}, bf16[48,128]{1,0:T(8,128)(2,1)S(1)}, u32[]{:S(2)}, u32[]{:S(2)}) collective-permute-start(bf16[48,128]{1,0:T(8,128)(2,1)S(1)} %get-tuple-element.42), channel_id=1, source_target_pairs={{0,12},{1,13},{2,14},{3,15},{4,8},{5,9},{6,10},{7,11},{8,20},{9,21... | collective-permute-start | bytes 36872 | tf_op jit(solution)/shard_map/ppermute | solution.py:219
  49.8 1.9 %collective-permute-start.14 = (bf16[48,128]{1,0:T(8,128)(2,1)S(1)}, bf16[48,128]{1,0:T(8,128)(2,1)S(1)}, u32[]{:S(2)}, u32[]{:S(2)}) collective-permute-start(bf16[48,128]{1,0:T(8,128)(2,1)S(1)} %get-tuple-element.43), channel_id=1, source_target_pairs={{0,9},{1,8},{2,11},{3,10},{4,13},{5,12},{6,15},{7,14},{8,17},{9,16... | collective-permute-start | bytes 36872 | tf_op jit(solution)/shard_map/ppermute | solution.py:219
  51.7 2.2 %collective-permute-start.15 = (bf16[48,128]{1,0:T(8,128)(2,1)S(1)}, bf16[48,128]{1,0:T(8,128)(2,1)S(1)}, u32[]{:S(2)}, u32[]{:S(2)}) collective-permute-start(bf16[48,128]{1,0:T(8,128)(2,1)S(1)} %get-tuple-element.44), channel_id=1, source_target_pairs={{1,10},{2,9},{5,14},{6,13},{9,18},{10,17},{13,22},{14,21},{17,26},... | collective-permute-start | bytes 36872 | tf_op jit(solution)/shard_map/ppermute | solution.py:219
  54.0 0.8 %collective-permute-done.14.refs_9_ = bf16[48,128]{1,0:T(8,128)(2,1)S(1)} collective-permute-done((bf16[48,128]{1,0:T(8,128)(2,1)S(1)}, bf16[48,128]{1,0:T(8,128)(2,1)S(1)}, u32[]{:S(2)}, u32[]{:S(2)}) %collective-permute-start.14) | collective-permute-done | bytes 12320 | tf_op jit(solution)/shard_map/ppermute | solution.py:219
  54.8 1.9 %collective-permute-done.15.refs_10_ = bf16[48,128]{1,0:T(8,128)(2,1)S(1)} collective-permute-done((bf16[48,128]{1,0:T(8,128)(2,1)S(1)}, bf16[48,128]{1,0:T(8,128)(2,1)S(1)}, u32[]{:S(2)}, u32[]{:S(2)}) %collective-permute-start.15) | collective-permute-done | bytes 12320 | tf_op jit(solution)/shard_map/ppermute | solution.py:219
  56.7 1.9 %shard_map.79 = bf16[192,896]{1,0:T(8,128)(2,1)} custom-call(bf16[192,896]{1,0:T(8,128)(2,1)S(1)} %collective-permute-done.12.refs_0_, bf16[192,896]{1,0:T(8,128)(2,1)S(1)} %get-tuple-element.45.refs_1_, bf16[1024,896]{1,0:T(8,128)(2,1)S(1)} %shard_map.76.refs_2_, f32[1,896]{1,0:T(1,128)S(1)} %bitcast.29, s32[7,12]{1,0:T(8,128)S(1)} %bitcast.25, ...), custom_call_target="tpu_custom_call" | custom-call | tf_op jit(solution)/shard_map/pallas_call | solution.py:191
  (23 shorter events, 2.1 us)
Async XLA Ops:
  0.7 1.4 %copy-start = (bf16[1,1,1,896,896]{4,3,2,1,0:T(8,128)(2,1)S(1)}, bf16[1,1,1,896,896]{4,3,2,1,0:T(8,128)(2,1)}, u32[]{:S(2)}) copy-start(bf16[1,1,1,896,896]{4,3,2,1,0:T(8,128)(2,1)} %param.11) | copy-start | bytes 4816900
  2.1 1.3 %copy-start.3 = (bf16[1,4,192,1,1,896]{5,2,4,3,1,0:T(8,128)(2,1)S(1)}, bf16[1,4,192,1,1,896]{5,2,4,3,1,0:T(8,128)(2,1)}, u32[]{:S(2)}) copy-start(bf16[1,4,192,1,1,896]{5,2,4,3,1,0:T(8,128)(2,1)} %param.8) | copy-start | bytes 4128772
  3.4 1.0 %copy-start.4 = (bf16[1,192,1,1,896]{4,1,3,2,0:T(8,128)(2,1)S(1)}, bf16[1,192,1,1,896]{4,1,3,2,0:T(8,128)(2,1)}, u32[]{:S(2)}) copy-start(bf16[1,192,1,1,896]{4,1,3,2,0:T(8,128)(2,1)} %param.7) | copy-start | bytes 1032196
  4.4 0.7 %copy-start.6 = (s32[4,192]{1,0:T(4,128)S(1)}, s32[4,192]{1,0:T(4,128)}, u32[]{:S(2)}) copy-start(s32[4,192]{1,0:T(4,128)} %assignment.1) | copy-start | bytes 9220
  5.1 7.1 %copy-start.1 = (bf16[1,1,1,896,896]{4,3,2,1,0:T(8,128)(2,1)S(1)}, bf16[1,1,1,896,896]{4,3,2,1,0:T(8,128)(2,1)}, u32[]{:S(2)}) copy-start(bf16[1,1,1,896,896]{4,3,2,1,0:T(8,128)(2,1)} %param.11) | copy-start | bytes 4816900
  5.1 7.1 %copy-start.2 = (bf16[1,1,1,896,896]{4,3,2,1,0:T(8,128)(2,1)S(1)}, bf16[1,1,1,896,896]{4,3,2,1,0:T(8,128)(2,1)}, u32[]{:S(2)}) copy-start(bf16[1,1,1,896,896]{4,3,2,1,0:T(8,128)(2,1)} %param.12) | copy-start | bytes 4816900
  7.6 9.0 %collective-permute-start.3 = (bf16[1472,128]{1,0:T(8,128)(2,1)S(1)}, bf16[1472,128]{1,0:T(8,128)(2,1)S(1)}, u32[]{:S(2)}, u32[]{:S(2)}) collective-permute-start(bf16[1472,128]{1,0:T(8,128)(2,1)S(1)} %get-tuple-element.31), channel_id=1, source_target_pairs={{8,0},{9,1},{10,2},{11,3},{12,4},{13,5},{14,6},{15,7},{16,8},{17,9... | collective-permute-start | bytes 1130504 | tf_op jit(solution)/shard_map/ppermute | solution.py:219
  10.2 5.2 %collective-permute-start = (bf16[192,128]{1,0:T(8,128)(2,1)S(1)}, bf16[192,128]{1,0:T(8,128)(2,1)S(1)}, u32[]{:S(2)}, u32[]{:S(2)}) collective-permute-start(bf16[192,128]{1,0:T(8,128)(2,1)S(1)} %get-tuple-element.28), channel_id=1, source_target_pairs={{0,4},{1,5},{2,6},{3,7},{4,0},{5,1},{6,2},{7,3}} | collective-permute-start | bytes 147464 | tf_op jit(solution)/shard_map/ppermute | solution.py:219
  10.9 4.5 %collective-permute-start.1 = (bf16[192,128]{1,0:T(8,128)(2,1)S(1)}, bf16[192,128]{1,0:T(8,128)(2,1)S(1)}, u32[]{:S(2)}, u32[]{:S(2)}) collective-permute-start(bf16[192,128]{1,0:T(8,128)(2,1)S(1)} %get-tuple-element.29), channel_id=1, source_target_pairs={{0,1},{1,0},{2,3},{3,2},{4,5},{5,4},{6,7},{7,6}} | collective-permute-start | bytes 147464 | tf_op jit(solution)/shard_map/ppermute | solution.py:219
  11.5 3.8 %collective-permute-start.2 = (bf16[192,128]{1,0:T(8,128)(2,1)S(1)}, bf16[192,128]{1,0:T(8,128)(2,1)S(1)}, u32[]{:S(2)}, u32[]{:S(2)}) collective-permute-start(bf16[192,128]{1,0:T(8,128)(2,1)S(1)} %get-tuple-element.30), channel_id=1, source_target_pairs={{1,2},{2,1},{5,6},{6,5}} | collective-permute-start | bytes 147464 | tf_op jit(solution)/shard_map/ppermute | solution.py:219
  12.2 4.3 %copy-start.5 = (f32[1,1,1,896]{3,2,1,0:T(1,128)S(1)}, f32[1,1,1,896]{3,2,1,0:T(1,128)}, u32[]{:S(2)}) copy-start(f32[1,1,1,896]{3,2,1,0:T(1,128)} %param.13) | copy-start | bytes 10756
  18.0 13.7 %collective-permute-start.4 = (bf16[192,896]{1,0:T(8,128)(2,1)S(1)}, bf16[192,896]{1,0:T(8,128)(2,1)S(1)}, u32[]{:S(2)}, u32[]{:S(2)}) collective-permute-start(bf16[192,896]{1,0:T(8,128)(2,1)S(1)} %get-tuple-element.32), channel_id=1, source_target_pairs={{0,8},{1,9},{2,10},{3,11},{4,12},{5,13},{6,14},{7,15}} | collective-permute-start | bytes 1032200 | tf_op jit(solution)/shard_map/ppermute | solution.py:219
  19.3 9.4 %collective-permute-start.5 = (bf16[48,128]{1,0:T(8,128)(2,1)S(1)}, bf16[48,128]{1,0:T(8,128)(2,1)S(1)}, u32[]{:S(2)}, u32[]{:S(2)}) collective-permute-start(bf16[48,128]{1,0:T(8,128)(2,1)S(1)} %get-tuple-element.34), channel_id=1, source_target_pairs={{0,12},{1,13},{2,14},{3,15},{4,8},{5,9},{6,10},{7,11}} | collective-permute-start | bytes 36872 | tf_op jit(solution)/shard_map/ppermute | solution.py:219
  20.6 8.1 %collective-permute-start.6 = (bf16[48,128]{1,0:T(8,128)(2,1)S(1)}, bf16[48,128]{1,0:T(8,128)(2,1)S(1)}, u32[]{:S(2)}, u32[]{:S(2)}) collective-permute-start(bf16[48,128]{1,0:T(8,128)(2,1)S(1)} %get-tuple-element.35), channel_id=1, source_target_pairs={{0,9},{1,8},{2,11},{3,10},{4,13},{5,12},{6,15},{7,14}} | collective-permute-start | bytes 36872 | tf_op jit(solution)/shard_map/ppermute | solution.py:219
  21.9 9.8 %collective-permute-start.7 = (bf16[48,128]{1,0:T(8,128)(2,1)S(1)}, bf16[48,128]{1,0:T(8,128)(2,1)S(1)}, u32[]{:S(2)}, u32[]{:S(2)}) collective-permute-start(bf16[48,128]{1,0:T(8,128)(2,1)S(1)} %get-tuple-element.36), channel_id=1, source_target_pairs={{1,10},{2,9},{5,14},{6,13}} | collective-permute-start | bytes 36872 | tf_op jit(solution)/shard_map/ppermute | solution.py:219
  33.1 10.8 %collective-permute-start.8 = (bf16[192,896]{1,0:T(8,128)(2,1)S(1)}, bf16[192,896]{1,0:T(8,128)(2,1)S(1)}, u32[]{:S(2)}, u32[]{:S(2)}) collective-permute-start(bf16[192,896]{1,0:T(8,128)(2,1)S(1)} %get-tuple-element.37), channel_id=1, source_target_pairs={{0,8},{1,9},{2,10},{3,11},{4,12},{5,13},{6,14},{7,15},{8,16},{9,17... | collective-permute-start | bytes 1032200 | tf_op jit(solution)/shard_map/ppermute | solution.py:219
  35.0 5.8 %collective-permute-start.9 = (bf16[48,128]{1,0:T(8,128)(2,1)S(1)}, bf16[48,128]{1,0:T(8,128)(2,1)S(1)}, u32[]{:S(2)}, u32[]{:S(2)}) collective-permute-start(bf16[48,128]{1,0:T(8,128)(2,1)S(1)} %get-tuple-element.38), channel_id=1, source_target_pairs={{0,12},{1,13},{2,14},{3,15},{4,8},{5,9},{6,10},{7,11},{8,20},{9,21... | collective-permute-start | bytes 36872 | tf_op jit(solution)/shard_map/ppermute | solution.py:219
  37.0 5.0 %collective-permute-start.10 = (bf16[48,128]{1,0:T(8,128)(2,1)S(1)}, bf16[48,128]{1,0:T(8,128)(2,1)S(1)}, u32[]{:S(2)}, u32[]{:S(2)}) collective-permute-start(bf16[48,128]{1,0:T(8,128)(2,1)S(1)} %get-tuple-element.39), channel_id=1, source_target_pairs={{0,9},{1,8},{2,11},{3,10},{4,13},{5,12},{6,15},{7,14},{8,17},{9,16... | collective-permute-start | bytes 36872 | tf_op jit(solution)/shard_map/ppermute | solution.py:219
  38.9 5.0 %collective-permute-start.11 = (bf16[48,128]{1,0:T(8,128)(2,1)S(1)}, bf16[48,128]{1,0:T(8,128)(2,1)S(1)}, u32[]{:S(2)}, u32[]{:S(2)}) collective-permute-start(bf16[48,128]{1,0:T(8,128)(2,1)S(1)} %get-tuple-element.40), channel_id=1, source_target_pairs={{1,10},{2,9},{5,14},{6,13},{9,18},{10,17},{13,22},{14,21}} | collective-permute-start | bytes 36872 | tf_op jit(solution)/shard_map/ppermute | solution.py:219
  45.3 11.4 %collective-permute-start.12 = (bf16[192,896]{1,0:T(8,128)(2,1)S(1)}, bf16[192,896]{1,0:T(8,128)(2,1)S(1)}, u32[]{:S(2)}, u32[]{:S(2)}) collective-permute-start(bf16[192,896]{1,0:T(8,128)(2,1)S(1)} %get-tuple-element.41), channel_id=1, source_target_pairs={{0,8},{1,9},{2,10},{3,11},{4,12},{5,13},{6,14},{7,15},{8,16},{9,17... | collective-permute-start | bytes 1032200 | tf_op jit(solution)/shard_map/ppermute | solution.py:219
  47.8 6.1 %collective-permute-start.13 = (bf16[48,128]{1,0:T(8,128)(2,1)S(1)}, bf16[48,128]{1,0:T(8,128)(2,1)S(1)}, u32[]{:S(2)}, u32[]{:S(2)}) collective-permute-start(bf16[48,128]{1,0:T(8,128)(2,1)S(1)} %get-tuple-element.42), channel_id=1, source_target_pairs={{0,12},{1,13},{2,14},{3,15},{4,8},{5,9},{6,10},{7,11},{8,20},{9,21... | collective-permute-start | bytes 36872 | tf_op jit(solution)/shard_map/ppermute | solution.py:219
  49.8 5.0 %collective-permute-start.14 = (bf16[48,128]{1,0:T(8,128)(2,1)S(1)}, bf16[48,128]{1,0:T(8,128)(2,1)S(1)}, u32[]{:S(2)}, u32[]{:S(2)}) collective-permute-start(bf16[48,128]{1,0:T(8,128)(2,1)S(1)} %get-tuple-element.43), channel_id=1, source_target_pairs={{0,9},{1,8},{2,11},{3,10},{4,13},{5,12},{6,15},{7,14},{8,17},{9,16... | collective-permute-start | bytes 36872 | tf_op jit(solution)/shard_map/ppermute | solution.py:219
  51.7 5.0 %collective-permute-start.15 = (bf16[48,128]{1,0:T(8,128)(2,1)S(1)}, bf16[48,128]{1,0:T(8,128)(2,1)S(1)}, u32[]{:S(2)}, u32[]{:S(2)}) collective-permute-start(bf16[48,128]{1,0:T(8,128)(2,1)S(1)} %get-tuple-element.44), channel_id=1, source_target_pairs={{1,10},{2,9},{5,14},{6,13},{9,18},{10,17},{13,22},{14,21},{17,26},... | collective-permute-start | bytes 36872 | tf_op jit(solution)/shard_map/ppermute | solution.py:219

commit v2 on v1

v2 whole, which is shorter than its diff:
```python
import functools

import jax
import jax.numpy as jnp
from jax import lax
from jax.experimental import pallas as pl
from jax.experimental.pallas import tpu as pltpu
from jax.sharding import PartitionSpec as P

FX = 32
FY = 28
SHOT_BATCH = 16

coupling_weight = 0.25

LANES = 128
GROUP = LANES // 4
EDGE_AXES = (("gx", 0), ("gy", 2))


def dot(a, b):
    return jnp.dot(a, b, preferred_element_type=jnp.float32)


def dot_t(a, b):
    return lax.dot_general(a, b, (((0,), (0,)), ((), ())), preferred_element_type=jnp.float32)


def edge_selector(cells):
    row = lax.broadcasted_iota(jnp.int32, (cells, LANES), 0)
    lane = lax.broadcasted_iota(jnp.int32, (cells, LANES), 1)
    group = lane // GROUP
    spot = lane % GROUP
    along_x = group < 2
    cell = jnp.where(
        along_x,
        jnp.where(group == 0, spot, (FX - 1) * FY + spot),
        jnp.where(group == 2, spot * FY, spot * FY + FY - 1),
    )
    length = jnp.where(along_x, FY, FX)
    return jnp.where((row == cell) & (spot < length), 1.0, 0.0).astype(jnp.bfloat16)


def exchanges():
    found = []
    for axis, base in EDGE_AXES:
        for parity in range(min(lax.axis_size(axis) - 1, 2)):
            found.append((axis, parity, base))
    return found


def group_of(axis, parity, base):
    ahead = lax.axis_index(axis) % 2 == parity
    return jnp.where(ahead, base + 1, base)


def pack(edges, group):
    rows = edges.shape[0] // 4
    lane_group = lax.broadcasted_iota(jnp.int32, (rows, LANES), 1) // GROUP
    packed = jnp.zeros((rows, LANES), jnp.float32)
    for part in range(4):
        piece = edges[part * rows : (part + 1) * rows]
        piece = pltpu.roll(piece, (part - group + 4) % 4 * GROUP, 1)
        packed = jnp.where(lane_group == part, piece, packed)
    return packed.astype(jnp.bfloat16)


def unpack(packed, group):
    lane_group = lax.broadcasted_iota(jnp.int32, packed.shape, 1) // GROUP
    pieces = []
    for part in range(4):
        piece = pltpu.roll(packed, (group - part + 4) % 4 * GROUP, 1)
        pieces.append(jnp.where(lane_group == group, piece, 0.0))
    return jnp.concatenate(pieces, axis=0)


def unit_of(round_number):
    return round_number - lax.axis_index("depth") + lax.axis_size("depth") - 1


def opening_kernel(swaps, arrival, source, assignment, counts, first_map, *refs):
    starts_out, live_out, edge_out = refs[:3]
    messages = refs[3 : 3 + len(swaps)]
    arrival_in, source_in, assignment_in, counts_in, first_in, sems = refs[3 + len(swaps) :]
    rounds, slots, cells = source.shape
    pairs = [(counts, counts_in), (assignment, assignment_in), (first_map, first_in)]
    pairs += [(arrival, arrival_in)]
    pairs += [(source.at[r], source_in.at[r]) for r in range(rounds)]
    copies = [
        pltpu.make_async_copy(here, there, sems.at[i]) for i, (here, there) in enumerate(pairs)
    ]
    for copy in copies:
        copy.start()
    selector = edge_selector(cells)
    shot = lax.broadcasted_iota(jnp.int32, (slots, slots), 0)
    slot = lax.broadcasted_iota(jnp.int32, (1, slots), 1)
    position = lax.broadcasted_iota(jnp.int32, (SHOT_BATCH, LANES), 0)
    copies[0].wait()
    copies[1].wait()
    chosen = []
    for round_number in range(rounds):
        unit = unit_of(round_number)
        live = jnp.zeros((1, slots), jnp.int32)
        for batch in range(slots // SHOT_BATCH):
            count = counts_in[unit, 0, 0, batch]
            live = jnp.where(slot // SHOT_BATCH == batch, count, live)
            rows = slice(batch * SHOT_BATCH, (batch + 1) * SHOT_BATCH)
            live_out[round_number, rows] = jnp.where(position < count, 1.0, 0.0).astype(
                jnp.bfloat16
            )
        wanted = jnp.where(
            slot % SHOT_BATCH < live, assignment_in[round_number : round_number + 1], -1
        )
        chosen.append(jnp.where(shot == wanted, 1.0, 0.0).astype(jnp.bfloat16))
    copies[2].wait()
    first_edge = dot(first_in[...], selector).astype(jnp.bfloat16)
    edge_out[:cells] = first_edge
    copies[3].wait()
    for round_number in range(rounds):
        copies[4 + round_number].wait()
        picked = dot_t(chosen[round_number], source_in[round_number])
        if round_number == 0:
            live = live_out[0].astype(jnp.float32)
            live = jnp.concatenate([live] * (cells // LANES), axis=1)
            picked = picked + live * arrival_in[...].astype(jnp.float32)
        picked = picked.astype(jnp.bfloat16)
        starts_out[round_number] = picked
        edges = dot(picked, first_edge)
        if round_number > 0:
            at = cells + (round_number - 1) * slots
            edge_out[at : at + slots] = edges.astype(jnp.bfloat16)
            edges = jnp.where(lax.axis_index("depth") == 0, edges, 0.0)
        at = round_number * (slots // 4)
        for message, swap in zip(messages, swaps):
            message[at : at + slots // 4] = pack(edges, group_of(*swap))


def coupled_inside(mapped):
    cells = mapped.shape[1]
    lane = lax.broadcasted_iota(jnp.int32, (1, cells), 1)
    column = lane % FY
    around = jnp.where(lane >= FY, pltpu.roll(mapped, FY, 1), 0.0)
    around += jnp.where(lane < cells - FY, pltpu.roll(mapped, cells - FY, 1), 0.0)
    around += jnp.where(column > 0, pltpu.roll(mapped, 1, 1), 0.0)
    around += jnp.where(column < FY - 1, pltpu.roll(mapped, cells - 1, 1), 0.0)
    return mapped + coupling_weight * around


def fill_whole_map(first_map, second_map, whole_ext, padded):
    cells = second_map.shape[0]
    margin = 32
    width = second_map.shape[1]
    padded[:margin] = jnp.zeros((margin, width), jnp.float32)
    padded[margin + cells :] = jnp.zeros((margin, width), jnp.float32)
    padded[margin : margin + cells] = second_map[...].astype(jnp.float32)
    column = lax.broadcasted_iota(jnp.int32, (cells, 1), 0) % FY
    middle = padded[margin : margin + cells]
    sides = padded[margin - FY : margin - FY + cells] + padded[margin + FY : margin + FY + cells]
    sides += jnp.where(column > 0, padded[margin - 1 : margin - 1 + cells], 0.0)
    sides += jnp.where(column < FY - 1, padded[margin + 1 : margin + 1 + cells], 0.0)
    coupled = (middle + coupling_weight * sides).astype(jnp.bfloat16)
    whole_ext[:cells] = dot(first_map[...], coupled).astype(jnp.bfloat16)


def inside_kernel(early_layers, starts, first_map, second_map, image_out, whole_ext, padded):
    cells = second_map.shape[0]
    early = lax.axis_index("depth") < early_layers
    edge_rows = dot_t(edge_selector(cells), second_map[...])
    whole_ext[cells:] = (coupling_weight * edge_rows).astype(jnp.bfloat16)

    @pl.when(early)
    def _():
        slots = starts.shape[1]
        for chain in range(image_out.shape[0] // slots):
            mapped = dot(starts[chain], first_map[...]).astype(jnp.bfloat16).astype(jnp.float32)
            coupled = coupled_inside(mapped).astype(jnp.bfloat16)
            image_out[chain * slots : (chain + 1) * slots] = dot(coupled, second_map[...])

    @pl.when(jnp.logical_not(early))
    def _():
        fill_whole_map(first_map, second_map, whole_ext, padded)


def whole_map_kernel(early_layers, first_map, second_map, whole_in, whole_ext, padded):
    del whole_in

    @pl.when(lax.axis_index("depth") < early_layers)
    def _():
        fill_whole_map(first_map, second_map, whole_ext, padded)


def halo_of(messages, swaps, at, part, live):
    halo = 0.0
    for parts, swap in zip(messages, swaps):
        packed = 0.0
        for ref, row in zip(parts, at):
            packed = packed + ref[row : row + part].astype(jnp.float32)
        halo = halo + unpack(packed, group_of(*swap))
    return (halo * live.astype(jnp.float32)).astype(jnp.bfloat16)


def blend(image, start, damping):
    damp = damping[...]
    return (damp * image + (1.0 - damp) * start.astype(jnp.float32)).astype(jnp.bfloat16)


def step_kernel(swaps, step, chains, *refs):
    refs = list(refs)
    starts, live, map_ext, damping, edge_next, traces = refs[:6]
    received = refs[6 : 6 + len(swaps)]
    outs = refs[6 + len(swaps) :]
    slots, cells = starts.shape[1:]
    part = slots // 4
    for chain in range(chains):
        round_number = step + chain
        halo = halo_of(
            [[ref] for ref in received], swaps, [chain * part], part, live[round_number]
        )
        rows = slice(chain * slots, (chain + 1) * slots)
        start = starts[round_number]
        if step == 0:
            image = traces[rows] + dot(halo, map_ext[cells:])
        else:
            start = start.astype(jnp.float32) + traces[rows].astype(jnp.float32)
            start = start.astype(jnp.bfloat16)
            image = dot(jnp.concatenate([start, halo], axis=1), map_ext[...])
        ended = blend(image, start, damping)
        if chain < chains - 1:
            outs[0][rows] = ended
        else:
            outs[-1][...] = ended
        at = cells + round_number * slots
        edges = dot(ended, edge_next[:cells]) + edge_next[at : at + slots].astype(jnp.float32)
        messages = outs[len(outs) - 1 - len(swaps) : len(outs) - 1]
        for message, swap in zip(messages, swaps):
            message[chain * part : (chain + 1) * part] = pack(edges, group_of(*swap))


def final_kernel(swaps, starts, live, map_ext, damping, *refs):
    rounds, slots, cells = starts.shape
    phases = []
    refs = list(refs)
    for phase in range(rounds):
        traces = refs.pop(0) if phase > 0 else None
        phases.append((traces, refs[: len(swaps)]))
        refs = refs[len(swaps) :]
    traces_out, row = refs
    part = slots // 4
    layer = lax.axis_index("depth")
    for phase, (traces, messages) in enumerate(phases):
        here = layer >= phase if phase == rounds - 1 else layer == phase

        @pl.when(here)
        def _():
            at = [messages[0].shape[0] - part]
            halo = halo_of([[ref] for ref in messages], swaps, at, part, live[rounds - 1])
            start = starts[rounds - 1]
            if traces is not None:
                start = start.astype(jnp.float32) + traces[...].astype(jnp.float32)
                start = start.astype(jnp.bfloat16)
            row[:, :cells] = start
            row[:, cells:] = halo

    image = dot(row[...], map_ext[...])
    traces_out[...] = blend(image, row[:, :cells], damping)


def call(kernel, out_shape, operands, in_hbm=False, scratch=(), aliases=None):
    space = pl.ANY if in_hbm else pltpu.VMEM
    return pl.pallas_call(
        kernel,
        out_shape=out_shape,
        in_specs=[pl.BlockSpec(memory_space=space)] * len(operands),
        out_specs=[pl.BlockSpec(memory_space=pltpu.VMEM)] * len(out_shape),
        scratch_shapes=scratch,
        input_output_aliases=aliases or {},
        compiler_params=pltpu.CompilerParams(vmem_limit_bytes=32 * 1024 * 1024),
    )(*operands)


MESH_AXES = ("depth", "gx", "gy")


def send(x, layers, down, swap=None):
    sizes = [lax.axis_size(axis) for axis in MESH_AXES]
    pairs = []
    for layer in layers:
        for i in range(sizes[1]):
            for j in range(sizes[2]):
                to = {"depth": layer + down, "gx": i, "gy": j}
                if swap is not None:
                    axis, parity, _ = swap
                    to[axis] += 1 if to[axis] % 2 == parity else -1
                spot = [to[axis] for axis in MESH_AXES]
                if all(0 <= s < size for s, size in zip(spot, sizes)):
                    here = (layer * sizes[1] + i) * sizes[2] + j
                    there = (spot[0] * sizes[1] + spot[1]) * sizes[2] + spot[2]
                    pairs.append((here, there))
    return lax.ppermute(x, MESH_AXES, pairs)


def local(arrival, source, assignment, counts, first_map, second_map, damping):
    layers = lax.axis_size("depth")
    slots, cells = arrival.shape[1], arrival.shape[4]
    rounds = source.shape[1]
    arrival = arrival[0, :, 0, 0, :]
    source = source[0, :, :, 0, 0, :]
    counts = counts.transpose(0, 2, 3, 1)
    first_map = first_map[0, 0, 0]
    second_map = second_map[0, 0, 0]
    damping = damping[0, 0]
    swaps = exchanges()
    early_layers = layers - rounds + 1

    def array(*shape, kind=jnp.bfloat16):
        return jax.ShapeDtypeStruct(shape, kind)

    part = slots // 4
    opened = call(
        functools.partial(opening_kernel, swaps),
        [
            array(rounds, slots, cells),
            array(rounds, slots, LANES),
            array(cells + (rounds - 1) * slots, LANES),
        ]
        + [array(rounds * part, LANES)] * len(swaps),
        [arrival, source, assignment, counts, first_map],
        in_hbm=True,
        scratch=[
            pltpu.VMEM(arrival.shape, arrival.dtype),
            pltpu.VMEM(source.shape, source.dtype),
            pltpu.VMEM(assignment.shape, assignment.dtype),
            pltpu.SMEM(counts.shape, counts.dtype),
            pltpu.VMEM(first_map.shape, first_map.dtype),
            pltpu.SemaphoreType.DMA((4 + rounds,)),
        ],
    )
    starts, live, edge = opened[:3]
    received = [send(m, range(early_layers), 0, swap) for m, swap in zip(opened[3:], swaps)]
    edge_next = send(edge, range(1, layers), -1)
    padded = pltpu.VMEM((cells + 64, cells), jnp.float32)
    traces, map_ext = call(
        functools.partial(inside_kernel, early_layers),
        [array((rounds - 1) * slots, cells, kind=jnp.float32), array(cells + LANES, cells)],
        [starts, first_map, second_map],
        scratch=[padded],
    )
    arrived = [list(received)]
    for step in range(rounds - 1):
        chains = rounds - 1 - step
        outs = [array((chains - 1) * slots, cells)] if chains > 1 else []
        outs += [array(chains * part, LANES)] * len(swaps) + [array(slots, cells)]
        ended = call(
            functools.partial(step_kernel, swaps, step, chains),
            outs,
            [starts, live, map_ext, damping, edge_next, traces] + received,
        )
        below = range(step, step + early_layers)
        if chains > 1:
            traces = send(ended[0], below, 1)
        received = [send(m, below, 1, swap) for m, swap in zip(ended[-1 - len(swaps) : -1], swaps)]
        leaving = send(ended[-1], below if chains == 1 else [step], 1)
        arrived.append([leaving] + received)
        if step == 0:
            (map_ext,) = call(
                functools.partial(whole_map_kernel, early_layers),
                [array(cells + LANES, cells)],
                [first_map, second_map, map_ext],
                scratch=[padded],
                aliases={2: 0},
            )
    (ended,) = call(
        functools.partial(final_kernel, swaps),
        [array(slots, cells)],
        [starts, live, map_ext, damping] + [x for phase in arrived for x in phase],
        scratch=[pltpu.VMEM((slots, cells + LANES), jnp.bfloat16)],
    )
    return ended.reshape(1, slots, 1, 1, cells)


def solution(mesh):
    return jax.shard_map(
        local,
        mesh=mesh,
        in_specs=(
            P("depth", None, "gx", "gy", None),
            P("depth", None, None, "gx", "gy", None),
            P(),
            P(None, None, "gx", "gy"),
            P("depth", "gx", "gy", None, None),
            P("depth", "gx", "gy", None, None),
            P("depth", "gx", "gy", None),
        ),
        out_specs=P("depth", None, "gx", "gy", None),
        check_vma=False,
    )
```

time: 59.2 us -> 54.9 us (0.927)
  the two profiles are of different devices: /device:TPU:9 before, /device:TPU:11 now
where the time goes in v2:
time: 54.9 us; the launch traced here: 54.4 us
  waiting for transfers between devices  19.7 us (36%)
  starting transfers between devices  16.5 us (30%)
  Pallas kernels  12.8 us (23%)
  local copies, waits for them, and re-layouts  5.12 us (9%)
    ppermute x18, waiting for transfers between devices, send(): return lax.ppermute(x, MESH_AXES, pairs)  19.7 us
    ppermute x18, starting transfers between devices, send(): return lax.ppermute(x, MESH_AXES, pairs)  16.5 us
    pallas_call x7, Pallas kernels, call(): pl.pallas_call(kernel, out_shape=out_shape, in_specs=[pl.BlockSpec(memory...  12.8 us
    unnamed x16, local copies, waits for them, and re-layouts  5.12 us
  transfers between devices with their start and end apart: 18, of which 3 were waited for; matrix products, arithmetic and copies ran while one was open for 0% of the time, Pallas kernels for 8%

profile of v2, /device:TPU:11, one launch (start us, length us, event | category | flops | bytes accessed | tf_op | source)
XLA Modules:
  0.0 54.4 jit_solution(13849523401383433075)
XLA Ops:
  0.0 1.4 %copy-done = bf16[1,1,1,896,896]{4,3,2,1,0:T(8,128)(2,1)S(1)} copy-done((bf16[1,1,1,896,896]{4,3,2,1,0:T(8,128)(2,1)S(1)}, bf16[1,1,1,896,896]{4,3,2,1,0:T(8,128)(2,1)}, u32[]{:S(2)}) %copy-start) | copy-done | bytes 1605656
  1.4 1.3 %copy-done.3 = bf16[1,4,192,1,1,896]{5,2,4,3,1,0:T(8,128)(2,1)S(1)} copy-done((bf16[1,4,192,1,1,896]{5,2,4,3,1,0:T(8,128)(2,1)S(1)}, bf16[1,4,192,1,1,896]{5,2,4,3,1,0:T(8,128)(2,1)}, u32[]{:S(2)}) %copy-start.3) | copy-done | bytes 1376280
  2.8 1.0 %copy-done.4 = bf16[1,192,1,1,896]{4,1,3,2,0:T(8,128)(2,1)S(1)} copy-done((bf16[1,192,1,1,896]{4,1,3,2,0:T(8,128)(2,1)S(1)}, bf16[1,192,1,1,896]{4,1,3,2,0:T(8,128)(2,1)}, u32[]{:S(2)}) %copy-start.4) | copy-done | bytes 344088
  3.7 0.7 %copy-done.6 = s32[4,192]{1,0:T(4,128)S(1)} copy-done((s32[4,192]{1,0:T(4,128)S(1)}, s32[4,192]{1,0:T(4,128)}, u32[]{:S(2)}) %copy-start.6) | copy-done | bytes 3096
  4.4 0.7 %copy-done.7 = s32[7,12,1,1]{1,3,2,0:T(1,128)S(1)} copy-done((s32[7,12,1,1]{1,3,2,0:T(1,128)S(1)}, s32[7,12,1,1]{1,3,2,0:T(1,128)}, u32[]{:S(2)}) %copy-start.7) | copy-done | bytes 360
  5.1 4.2 %shard_map.73 = (bf16[4,192,896]{2,1,0:T(8,128)(2,1)S(1)}, bf16[4,192,128]{2,1,0:T(8,128)(2,1)S(1)}, bf16[1472,128]{1,0:T(8,128)(2,1)S(1)}, bf16[192,128]{1,0:T(...) custom-call(bf16[192,896]{1,0:T(8,128)(2,1)S(1)} %bitcast.15, ...), custom_call_target="tpu_custom_call" | custom-call | tf_op jit(solution)/shard_map/pallas_call | solution.py:270
  9.3 2.6 %collective-permute-start.3 = (bf16[1472,128]{1,0:T(8,128)(2,1)S(1)}, bf16[1472,128]{1,0:T(8,128)(2,1)S(1)}, u32[]{:S(2)}, u32[]{:S(2)}) collective-permute-start(bf16[1472,128]{1,0:T(8,128)(2,1)S(1)} %get-tuple-element.33), channel_id=1, source_target_pairs={{8,0},{9,1},{10,2},{11,3},{12,4},{13,5},{14,6},{15,7},{16,8},{17,9... | collective-permute-start | bytes 1130504 | tf_op jit(solution)/shard_map/ppermute | solution.py:299
  11.9 0.7 %collective-permute-start = (bf16[192,128]{1,0:T(8,128)(2,1)S(1)}, bf16[192,128]{1,0:T(8,128)(2,1)S(1)}, u32[]{:S(2)}, u32[]{:S(2)}) collective-permute-start(bf16[192,128]{1,0:T(8,128)(2,1)S(1)} %get-tuple-element.30), channel_id=1, source_target_pairs={{0,4},{1,5},{2,6},{3,7},{4,0},{5,1},{6,2},{7,3}} | collective-permute-start | bytes 147464 | tf_op jit(solution)/shard_map/ppermute | solution.py:299
  12.6 0.7 %collective-permute-start.1 = (bf16[192,128]{1,0:T(8,128)(2,1)S(1)}, bf16[192,128]{1,0:T(8,128)(2,1)S(1)}, u32[]{:S(2)}, u32[]{:S(2)}) collective-permute-start(bf16[192,128]{1,0:T(8,128)(2,1)S(1)} %get-tuple-element.31), channel_id=1, source_target_pairs={{0,1},{1,0},{2,3},{3,2},{4,5},{5,4},{6,7},{7,6}} | collective-permute-start | bytes 147464 | tf_op jit(solution)/shard_map/ppermute | solution.py:299
  13.3 0.7 %collective-permute-start.2 = (bf16[192,128]{1,0:T(8,128)(2,1)S(1)}, bf16[192,128]{1,0:T(8,128)(2,1)S(1)}, u32[]{:S(2)}, u32[]{:S(2)}) collective-permute-start(bf16[192,128]{1,0:T(8,128)(2,1)S(1)} %get-tuple-element.32), channel_id=1, source_target_pairs={{1,2},{2,1},{5,6},{6,5}} | collective-permute-start | bytes 147464 | tf_op jit(solution)/shard_map/ppermute | solution.py:299
  14.0 3.5 %shard_map.74 = (f32[576,896]{1,0:T(8,128)S(1)}, bf16[1024,896]{1,0:T(8,128)(2,1)S(1)}) custom-call(bf16[4,192,896]{2,1,0:T(8,128)(2,1)S(1)} %get-tuple-element.27.starts.refs_0_, bf16[896,896]{1,0:T(8,128)(2,1)S(1)} %bitcast.10, bf16[896,896]{1,0:T(8,128)(2,1)S(1)} %bitcast.12), custom_call_target="tpu_custom_call" | custom-call | tf_op jit(solution)/shard_map/pallas_call | solution.py:270
  17.5 1.1 %shard_map.76 = (bf16[384,896]{1,0:T(8,128)(2,1)S(1)}, bf16[144,128]{1,0:T(8,128)(2,1)S(1)}, bf16[144,128]{1,0:T(8,128)(2,1)S(1)}, bf16[144,128]{1,0:T(8,128)(2,1)S(1)}, bf16[192,896]{1,0:T(8,128)(2,1)S(1)}) custom-call(bf16[4,192,896]{2,1,0:T(8,128)(2,1)S(1)} %get-tuple-element.27.starts.refs_0_, bf16[4,192,128]{2,1,0:T(8,128)(2,1)S(1)} %get-tuple-element.28.refs_1_.live, ...), custom_call_target="tpu_custom_call" | custom-call | tf_op jit(solution)/shard_map/pallas_call | solution.py:270
  18.7 0.7 %collective-permute-start.8 = (bf16[384,896]{1,0:T(8,128)(2,1)S(1)}, bf16[384,896]{1,0:T(8,128)(2,1)S(1)}, u32[]{:S(2)}, u32[]{:S(2)}) collective-permute-start(bf16[384,896]{1,0:T(8,128)(2,1)S(1)} %get-tuple-element.39), channel_id=1, source_target_pairs={{0,8},{1,9},{2,10},{3,11},{4,12},{5,13},{6,14},{7,15}} | collective-permute-start | bytes 2064392 | tf_op jit(solution)/shard_map/ppermute | solution.py:299
  19.4 0.7 %collective-permute-start.5 = (bf16[144,128]{1,0:T(8,128)(2,1)S(1)}, bf16[144,128]{1,0:T(8,128)(2,1)S(1)}, u32[]{:S(2)}, u32[]{:S(2)}) collective-permute-start(bf16[144,128]{1,0:T(8,128)(2,1)S(1)} %get-tuple-element.36), channel_id=1, source_target_pairs={{0,12},{1,13},{2,14},{3,15},{4,8},{5,9},{6,10},{7,11}} | collective-permute-start | bytes 110600 | tf_op jit(solution)/shard_map/ppermute | solution.py:299
  20.1 0.7 %collective-permute-start.6 = (bf16[144,128]{1,0:T(8,128)(2,1)S(1)}, bf16[144,128]{1,0:T(8,128)(2,1)S(1)}, u32[]{:S(2)}, u32[]{:S(2)}) collective-permute-start(bf16[144,128]{1,0:T(8,128)(2,1)S(1)} %get-tuple-element.37), channel_id=1, source_target_pairs={{0,9},{1,8},{2,11},{3,10},{4,13},{5,12},{6,15},{7,14}} | collective-permute-start | bytes 110600 | tf_op jit(solution)/shard_map/ppermute | solution.py:299
  20.7 0.7 %collective-permute-start.7 = (bf16[144,128]{1,0:T(8,128)(2,1)S(1)}, bf16[144,128]{1,0:T(8,128)(2,1)S(1)}, u32[]{:S(2)}, u32[]{:S(2)}) collective-permute-start(bf16[144,128]{1,0:T(8,128)(2,1)S(1)} %get-tuple-element.38), channel_id=1, source_target_pairs={{1,10},{2,9},{5,14},{6,13}} | collective-permute-start | bytes 110600 | tf_op jit(solution)/shard_map/ppermute | solution.py:299
  21.7 1.4 %shard_map.77 = (bf16[192,896]{1,0:T(8,128)(2,1)S(1)}, bf16[96,128]{1,0:T(8,128)(2,1)S(1)}, bf16[96,128]{1,0:T(8,128)(2,1)S(1)}, bf16[96,128]{1,0:T(8,128)(2,1)S(1)}, bf16[192,896]{1,0:T(8,128)(2,1)S(1)}) custom-call(bf16[4,192,896]{2,1,0:T(8,128)(2,1)S(1)} %get-tuple-element.27.starts.refs_0_, bf16[4,192,128]{2,1,0:T(8,128)(2,1)S(1)} %get-tuple-element.28.refs_1_.live, ...), custom_call_target="tpu_custom_call" | custom-call | tf_op jit(solution)/shard_map/pallas_call | solution.py:270
  23.0 0.7 %collective-permute-start.13 = (bf16[192,896]{1,0:T(8,128)(2,1)S(1)}, bf16[192,896]{1,0:T(8,128)(2,1)S(1)}, u32[]{:S(2)}, u32[]{:S(2)}) collective-permute-start(bf16[192,896]{1,0:T(8,128)(2,1)S(1)} %get-tuple-element.44), channel_id=1, source_target_pairs={{8,16},{9,17},{10,18},{11,19},{12,20},{13,21},{14,22},{15,23}} | collective-permute-start | bytes 1032200 | tf_op jit(solution)/shard_map/ppermute | solution.py:299
  23.7 0.7 %collective-permute-start.10 = (bf16[96,128]{1,0:T(8,128)(2,1)S(1)}, bf16[96,128]{1,0:T(8,128)(2,1)S(1)}, u32[]{:S(2)}, u32[]{:S(2)}) collective-permute-start(bf16[96,128]{1,0:T(8,128)(2,1)S(1)} %get-tuple-element.41), channel_id=1, source_target_pairs={{8,20},{9,21},{10,22},{11,23},{12,16},{13,17},{14,18},{15,19}} | collective-permute-start | bytes 73736 | tf_op jit(solution)/shard_map/ppermute | solution.py:299
  24.4 0.7 %collective-permute-start.11 = (bf16[96,128]{1,0:T(8,128)(2,1)S(1)}, bf16[96,128]{1,0:T(8,128)(2,1)S(1)}, u32[]{:S(2)}, u32[]{:S(2)}) collective-permute-start(bf16[96,128]{1,0:T(8,128)(2,1)S(1)} %get-tuple-element.42), channel_id=1, source_target_pairs={{8,17},{9,16},{10,19},{11,18},{12,21},{13,20},{14,23},{15,22}} | collective-permute-start | bytes 73736 | tf_op jit(solution)/shard_map/ppermute | solution.py:299
  25.1 0.7 %collective-permute-start.12 = (bf16[96,128]{1,0:T(8,128)(2,1)S(1)}, bf16[96,128]{1,0:T(8,128)(2,1)S(1)}, u32[]{:S(2)}, u32[]{:S(2)}) collective-permute-start(bf16[96,128]{1,0:T(8,128)(2,1)S(1)} %get-tuple-element.43), channel_id=1, source_target_pairs={{9,18},{10,17},{13,22},{14,21}} | collective-permute-start | bytes 73736 | tf_op jit(solution)/shard_map/ppermute | solution.py:299
  25.7 0.7 %collective-permute-start.4 = (bf16[192,896]{1,0:T(8,128)(2,1)S(1)}, bf16[192,896]{1,0:T(8,128)(2,1)S(1)}, u32[]{:S(2)}, u32[]{:S(2)}) collective-permute-start(bf16[192,896]{1,0:T(8,128)(2,1)S(1)} %get-tuple-element.35), channel_id=1, source_target_pairs={{0,8},{1,9},{2,10},{3,11},{4,12},{5,13},{6,14},{7,15}} | collective-permute-start | bytes 1032200 | tf_op jit(solution)/shard_map/ppermute | solution.py:299
  26.4 0.7 %collective-permute-start.9 = (bf16[192,896]{1,0:T(8,128)(2,1)S(1)}, bf16[192,896]{1,0:T(8,128)(2,1)S(1)}, u32[]{:S(2)}, u32[]{:S(2)}) collective-permute-start(bf16[192,896]{1,0:T(8,128)(2,1)S(1)} %get-tuple-element.40), channel_id=1, source_target_pairs={{8,16},{9,17},{10,18},{11,19},{12,20},{13,21},{14,22},{15,23}} | collective-permute-start | bytes 1032200 | tf_op jit(solution)/shard_map/ppermute | solution.py:299
  27.1 0.8 %shard_map.78 = (bf16[48,128]{1,0:T(8,128)(2,1)S(1)}, bf16[48,128]{1,0:T(8,128)(2,1)S(1)}, bf16[48,128]{1,0:T(8,128)(2,1)S(1)}, bf16[192,896]{1,0:T(8,128)(2,1)S(1)}) custom-call(bf16[4,192,896]{2,1,0:T(8,128)(2,1)S(1)} %get-tuple-element.27.starts.refs_0_, bf16[4,192,128]{2,1,0:T(8,128)(2,1)S(1)} %get-tuple-element.28.refs_1_.live, ...), custom_call_target="tpu_custom_call" | custom-call | tf_op jit(solution)/shard_map/pallas_call | solution.py:270
  28.0 1.3 %collective-permute-start.14 = (bf16[192,896]{1,0:T(8,128)(2,1)S(1)}, bf16[192,896]{1,0:T(8,128)(2,1)S(1)}, u32[]{:S(2)}, u32[]{:S(2)}) collective-permute-start(bf16[192,896]{1,0:T(8,128)(2,1)S(1)} %get-tuple-element.45), channel_id=1, source_target_pairs={{16,24},{17,25},{18,26},{19,27},{20,28},{21,29},{22,30},{23,31}} | collective-permute-start | bytes 1032200 | tf_op jit(solution)/shard_map/ppermute | solution.py:299
  29.3 1.3 %collective-permute-start.15 = (bf16[48,128]{1,0:T(8,128)(2,1)S(1)}, bf16[48,128]{1,0:T(8,128)(2,1)S(1)}, u32[]{:S(2)}, u32[]{:S(2)}) collective-permute-start(bf16[48,128]{1,0:T(8,128)(2,1)S(1)} %get-tuple-element.46), channel_id=1, source_target_pairs={{16,28},{17,29},{18,30},{19,31},{20,24},{21,25},{22,26},{23,27}} | collective-permute-start | bytes 36872 | tf_op jit(solution)/shard_map/ppermute | solution.py:299
  30.6 1.3 %collective-permute-start.16 = (bf16[48,128]{1,0:T(8,128)(2,1)S(1)}, bf16[48,128]{1,0:T(8,128)(2,1)S(1)}, u32[]{:S(2)}, u32[]{:S(2)}) collective-permute-start(bf16[48,128]{1,0:T(8,128)(2,1)S(1)} %get-tuple-element.47), channel_id=1, source_target_pairs={{16,25},{17,24},{18,27},{19,26},{20,29},{21,28},{22,31},{23,30}} | collective-permute-start | bytes 36872 | tf_op jit(solution)/shard_map/ppermute | solution.py:299
  31.9 1.3 %collective-permute-start.17 = (bf16[48,128]{1,0:T(8,128)(2,1)S(1)}, bf16[48,128]{1,0:T(8,128)(2,1)S(1)}, u32[]{:S(2)}, u32[]{:S(2)}) collective-permute-start(bf16[48,128]{1,0:T(8,128)(2,1)S(1)} %get-tuple-element.48), channel_id=1, source_target_pairs={{17,26},{18,25},{21,30},{22,29}} | collective-permute-start | bytes 36872 | tf_op jit(solution)/shard_map/ppermute | solution.py:299
  33.2 16.6 %collective-permute-done.15.refs_12_ = bf16[48,128]{1,0:T(8,128)(2,1)S(1)} collective-permute-done((bf16[48,128]{1,0:T(8,128)(2,1)S(1)}, bf16[48,128]{1,0:T(8,128)(2,1)S(1)}, u32[]{:S(2)}, u32[]{:S(2)}) %collective-permute-start.15) | collective-permute-done | bytes 12320 | tf_op jit(solution)/shard_map/ppermute | solution.py:299
  49.8 0.5 collective-permute-done.16.refs_13_
  50.3 2.6 %collective-permute-done.17.refs_14_ = bf16[48,128]{1,0:T(8,128)(2,1)S(1)} collective-permute-done((bf16[48,128]{1,0:T(8,128)(2,1)S(1)}, bf16[48,128]{1,0:T(8,128)(2,1)S(1)}, u32[]{:S(2)}, u32[]{:S(2)}) %collective-permute-start.17) | collective-permute-done | bytes 12320 | tf_op jit(solution)/shard_map/ppermute | solution.py:299
  52.9 1.6 %shard_map.79 = bf16[192,896]{1,0:T(8,128)(2,1)} custom-call(bf16[4,192,896]{2,1,0:T(8,128)(2,1)S(1)} %get-tuple-element.27.starts.refs_0_, bf16[4,192,128]{2,1,0:T(8,128)(2,1)S(1)} %get-tuple-element.28.refs_1_.live, bf16[1024,896]{1,0:T(8,128)(2,1)S(1)} %shard_map.75.refs_2_.map_ext, f32[1,896]{1,0:T(1,128)S(1)} %bitcast.19, ...), custom_call_target="tpu_custom_call" | custom-call | tf_op jit(solution)/shard_map/pallas_call | solution.py:270
  (27 shorter events, 0.3 us)
Async XLA Ops:
  0.0 1.4 %copy-start = (bf16[1,1,1,896,896]{4,3,2,1,0:T(8,128)(2,1)S(1)}, bf16[1,1,1,896,896]{4,3,2,1,0:T(8,128)(2,1)}, u32[]{:S(2)}) copy-start(bf16[1,1,1,896,896]{4,3,2,1,0:T(8,128)(2,1)} %param.11) | copy-start | bytes 4816900
  1.4 1.3 %copy-start.3 = (bf16[1,4,192,1,1,896]{5,2,4,3,1,0:T(8,128)(2,1)S(1)}, bf16[1,4,192,1,1,896]{5,2,4,3,1,0:T(8,128)(2,1)}, u32[]{:S(2)}) copy-start(bf16[1,4,192,1,1,896]{5,2,4,3,1,0:T(8,128)(2,1)} %param.8) | copy-start | bytes 4128772
  2.8 1.0 %copy-start.4 = (bf16[1,192,1,1,896]{4,1,3,2,0:T(8,128)(2,1)S(1)}, bf16[1,192,1,1,896]{4,1,3,2,0:T(8,128)(2,1)}, u32[]{:S(2)}) copy-start(bf16[1,192,1,1,896]{4,1,3,2,0:T(8,128)(2,1)} %param.7) | copy-start | bytes 1032196
  3.7 0.7 %copy-start.6 = (s32[4,192]{1,0:T(4,128)S(1)}, s32[4,192]{1,0:T(4,128)}, u32[]{:S(2)}) copy-start(s32[4,192]{1,0:T(4,128)} %assignment.1) | copy-start | bytes 9220
  4.4 0.7 %copy-start.7 = (s32[7,12,1,1]{1,3,2,0:T(1,128)S(1)}, s32[7,12,1,1]{1,3,2,0:T(1,128)}, u32[]{:S(2)}) copy-start(s32[7,12,1,1]{1,3,2,0:T(1,128)} %param.10) | copy-start | bytes 1012
  5.1 8.8 %copy-start.1 = (bf16[1,1,1,896,896]{4,3,2,1,0:T(8,128)(2,1)S(1)}, bf16[1,1,1,896,896]{4,3,2,1,0:T(8,128)(2,1)}, u32[]{:S(2)}) copy-start(bf16[1,1,1,896,896]{4,3,2,1,0:T(8,128)(2,1)} %param.11) | copy-start | bytes 4816900
  5.1 8.8 %copy-start.2 = (bf16[1,1,1,896,896]{4,3,2,1,0:T(8,128)(2,1)S(1)}, bf16[1,1,1,896,896]{4,3,2,1,0:T(8,128)(2,1)}, u32[]{:S(2)}) copy-start(bf16[1,1,1,896,896]{4,3,2,1,0:T(8,128)(2,1)} %param.12) | copy-start | bytes 4816900
  9.3 8.2 %collective-permute-start.3 = (bf16[1472,128]{1,0:T(8,128)(2,1)S(1)}, bf16[1472,128]{1,0:T(8,128)(2,1)S(1)}, u32[]{:S(2)}, u32[]{:S(2)}) collective-permute-start(bf16[1472,128]{1,0:T(8,128)(2,1)S(1)} %get-tuple-element.33), channel_id=1, source_target_pairs={{8,0},{9,1},{10,2},{11,3},{12,4},{13,5},{14,6},{15,7},{16,8},{17,9... | collective-permute-start | bytes 1130504 | tf_op jit(solution)/shard_map/ppermute | solution.py:299
  11.9 5.6 %collective-permute-start = (bf16[192,128]{1,0:T(8,128)(2,1)S(1)}, bf16[192,128]{1,0:T(8,128)(2,1)S(1)}, u32[]{:S(2)}, u32[]{:S(2)}) collective-permute-start(bf16[192,128]{1,0:T(8,128)(2,1)S(1)} %get-tuple-element.30), channel_id=1, source_target_pairs={{0,4},{1,5},{2,6},{3,7},{4,0},{5,1},{6,2},{7,3}} | collective-permute-start | bytes 147464 | tf_op jit(solution)/shard_map/ppermute | solution.py:299
  12.6 4.9 %collective-permute-start.1 = (bf16[192,128]{1,0:T(8,128)(2,1)S(1)}, bf16[192,128]{1,0:T(8,128)(2,1)S(1)}, u32[]{:S(2)}, u32[]{:S(2)}) collective-permute-start(bf16[192,128]{1,0:T(8,128)(2,1)S(1)} %get-tuple-element.31), channel_id=1, source_target_pairs={{0,1},{1,0},{2,3},{3,2},{4,5},{5,4},{6,7},{7,6}} | collective-permute-start | bytes 147464 | tf_op jit(solution)/shard_map/ppermute | solution.py:299
  13.3 4.3 %collective-permute-start.2 = (bf16[192,128]{1,0:T(8,128)(2,1)S(1)}, bf16[192,128]{1,0:T(8,128)(2,1)S(1)}, u32[]{:S(2)}, u32[]{:S(2)}) collective-permute-start(bf16[192,128]{1,0:T(8,128)(2,1)S(1)} %get-tuple-element.32), channel_id=1, source_target_pairs={{1,2},{2,1},{5,6},{6,5}} | collective-permute-start | bytes 147464 | tf_op jit(solution)/shard_map/ppermute | solution.py:299
  13.9 3.6 %copy-start.5 = (f32[1,1,1,896]{3,2,1,0:T(1,128)S(1)}, f32[1,1,1,896]{3,2,1,0:T(1,128)}, u32[]{:S(2)}) copy-start(f32[1,1,1,896]{3,2,1,0:T(1,128)} %param.13) | copy-start | bytes 10756
  18.7 3.0 %collective-permute-start.8 = (bf16[384,896]{1,0:T(8,128)(2,1)S(1)}, bf16[384,896]{1,0:T(8,128)(2,1)S(1)}, u32[]{:S(2)}, u32[]{:S(2)}) collective-permute-start(bf16[384,896]{1,0:T(8,128)(2,1)S(1)} %get-tuple-element.39), channel_id=1, source_target_pairs={{0,8},{1,9},{2,10},{3,11},{4,12},{5,13},{6,14},{7,15}} | collective-permute-start | bytes 2064392 | tf_op jit(solution)/shard_map/ppermute | solution.py:299
  19.4 2.2 %collective-permute-start.5 = (bf16[144,128]{1,0:T(8,128)(2,1)S(1)}, bf16[144,128]{1,0:T(8,128)(2,1)S(1)}, u32[]{:S(2)}, u32[]{:S(2)}) collective-permute-start(bf16[144,128]{1,0:T(8,128)(2,1)S(1)} %get-tuple-element.36), channel_id=1, source_target_pairs={{0,12},{1,13},{2,14},{3,15},{4,8},{5,9},{6,10},{7,11}} | collective-permute-start | bytes 110600 | tf_op jit(solution)/shard_map/ppermute | solution.py:299
  20.1 1.6 %collective-permute-start.6 = (bf16[144,128]{1,0:T(8,128)(2,1)S(1)}, bf16[144,128]{1,0:T(8,128)(2,1)S(1)}, u32[]{:S(2)}, u32[]{:S(2)}) collective-permute-start(bf16[144,128]{1,0:T(8,128)(2,1)S(1)} %get-tuple-element.37), channel_id=1, source_target_pairs={{0,9},{1,8},{2,11},{3,10},{4,13},{5,12},{6,15},{7,14}} | collective-permute-start | bytes 110600 | tf_op jit(solution)/shard_map/ppermute | solution.py:299
  20.7 0.9 %collective-permute-start.7 = (bf16[144,128]{1,0:T(8,128)(2,1)S(1)}, bf16[144,128]{1,0:T(8,128)(2,1)S(1)}, u32[]{:S(2)}, u32[]{:S(2)}) collective-permute-start(bf16[144,128]{1,0:T(8,128)(2,1)S(1)} %get-tuple-element.38), channel_id=1, source_target_pairs={{1,10},{2,9},{5,14},{6,13}} | collective-permute-start | bytes 110600 | tf_op jit(solution)/shard_map/ppermute | solution.py:299
  23.0 4.1 %collective-permute-start.13 = (bf16[192,896]{1,0:T(8,128)(2,1)S(1)}, bf16[192,896]{1,0:T(8,128)(2,1)S(1)}, u32[]{:S(2)}, u32[]{:S(2)}) collective-permute-start(bf16[192,896]{1,0:T(8,128)(2,1)S(1)} %get-tuple-element.44), channel_id=1, source_target_pairs={{8,16},{9,17},{10,18},{11,19},{12,20},{13,21},{14,22},{15,23}} | collective-permute-start | bytes 1032200 | tf_op jit(solution)/shard_map/ppermute | solution.py:299
  23.7 2.7 %collective-permute-start.10 = (bf16[96,128]{1,0:T(8,128)(2,1)S(1)}, bf16[96,128]{1,0:T(8,128)(2,1)S(1)}, u32[]{:S(2)}, u32[]{:S(2)}) collective-permute-start(bf16[96,128]{1,0:T(8,128)(2,1)S(1)} %get-tuple-element.41), channel_id=1, source_target_pairs={{8,20},{9,21},{10,22},{11,23},{12,16},{13,17},{14,18},{15,19}} | collective-permute-start | bytes 73736 | tf_op jit(solution)/shard_map/ppermute | solution.py:299
  24.4 2.7 %collective-permute-start.11 = (bf16[96,128]{1,0:T(8,128)(2,1)S(1)}, bf16[96,128]{1,0:T(8,128)(2,1)S(1)}, u32[]{:S(2)}, u32[]{:S(2)}) collective-permute-start(bf16[96,128]{1,0:T(8,128)(2,1)S(1)} %get-tuple-element.42), channel_id=1, source_target_pairs={{8,17},{9,16},{10,19},{11,18},{12,21},{13,20},{14,23},{15,22}} | collective-permute-start | bytes 73736 | tf_op jit(solution)/shard_map/ppermute | solution.py:299
  25.1 2.1 %collective-permute-start.12 = (bf16[96,128]{1,0:T(8,128)(2,1)S(1)}, bf16[96,128]{1,0:T(8,128)(2,1)S(1)}, u32[]{:S(2)}, u32[]{:S(2)}) collective-permute-start(bf16[96,128]{1,0:T(8,128)(2,1)S(1)} %get-tuple-element.43), channel_id=1, source_target_pairs={{9,18},{10,17},{13,22},{14,21}} | collective-permute-start | bytes 73736 | tf_op jit(solution)/shard_map/ppermute | solution.py:299
  25.7 6.1 %collective-permute-start.4 = (bf16[192,896]{1,0:T(8,128)(2,1)S(1)}, bf16[192,896]{1,0:T(8,128)(2,1)S(1)}, u32[]{:S(2)}, u32[]{:S(2)}) collective-permute-start(bf16[192,896]{1,0:T(8,128)(2,1)S(1)} %get-tuple-element.35), channel_id=1, source_target_pairs={{0,8},{1,9},{2,10},{3,11},{4,12},{5,13},{6,14},{7,15}} | collective-permute-start | bytes 1032200 | tf_op jit(solution)/shard_map/ppermute | solution.py:299
  26.4 6.8 %collective-permute-start.9 = (bf16[192,896]{1,0:T(8,128)(2,1)S(1)}, bf16[192,896]{1,0:T(8,128)(2,1)S(1)}, u32[]{:S(2)}, u32[]{:S(2)}) collective-permute-start(bf16[192,896]{1,0:T(8,128)(2,1)S(1)} %get-tuple-element.40), channel_id=1, source_target_pairs={{8,16},{9,17},{10,18},{11,19},{12,20},{13,21},{14,22},{15,23}} | collective-permute-start | bytes 1032200 | tf_op jit(solution)/shard_map/ppermute | solution.py:299
  28.0 24.9 %collective-permute-start.14 = (bf16[192,896]{1,0:T(8,128)(2,1)S(1)}, bf16[192,896]{1,0:T(8,128)(2,1)S(1)}, u32[]{:S(2)}, u32[]{:S(2)}) collective-permute-start(bf16[192,896]{1,0:T(8,128)(2,1)S(1)} %get-tuple-element.45), channel_id=1, source_target_pairs={{16,24},{17,25},{18,26},{19,27},{20,28},{21,29},{22,30},{23,31}} | collective-permute-start | bytes 1032200 | tf_op jit(solution)/shard_map/ppermute | solution.py:299
  29.3 20.5 %collective-permute-start.15 = (bf16[48,128]{1,0:T(8,128)(2,1)S(1)}, bf16[48,128]{1,0:T(8,128)(2,1)S(1)}, u32[]{:S(2)}, u32[]{:S(2)}) collective-permute-start(bf16[48,128]{1,0:T(8,128)(2,1)S(1)} %get-tuple-element.46), channel_id=1, source_target_pairs={{16,28},{17,29},{18,30},{19,31},{20,24},{21,25},{22,26},{23,27}} | collective-permute-start | bytes 36872 | tf_op jit(solution)/shard_map/ppermute | solution.py:299
  30.6 19.7 %collective-permute-start.16 = (bf16[48,128]{1,0:T(8,128)(2,1)S(1)}, bf16[48,128]{1,0:T(8,128)(2,1)S(1)}, u32[]{:S(2)}, u32[]{:S(2)}) collective-permute-start(bf16[48,128]{1,0:T(8,128)(2,1)S(1)} %get-tuple-element.47), channel_id=1, source_target_pairs={{16,25},{17,24},{18,27},{19,26},{20,29},{21,28},{22,31},{23,30}} | collective-permute-start | bytes 36872 | tf_op jit(solution)/shard_map/ppermute | solution.py:299
  31.9 21.0 %collective-permute-start.17 = (bf16[48,128]{1,0:T(8,128)(2,1)S(1)}, bf16[48,128]{1,0:T(8,128)(2,1)S(1)}, u32[]{:S(2)}, u32[]{:S(2)}) collective-permute-start(bf16[48,128]{1,0:T(8,128)(2,1)S(1)} %get-tuple-element.48), channel_id=1, source_target_pairs={{17,26},{18,25},{21,30},{22,29}} | collective-permute-start | bytes 36872 | tf_op jit(solution)/shard_map/ppermute | solution.py:299

commit v3 on v2

--- a/solution.py
+++ b/solution.py
@@ -78,14 +78,15 @@
     return round_number - lax.axis_index("depth") + lax.axis_size("depth") - 1
 
 
-def opening_kernel(swaps, arrival, source, assignment, counts, first_map, *refs):
-    starts_out, live_out, edge_out = refs[:3]
-    messages = refs[3 : 3 + len(swaps)]
-    arrival_in, source_in, assignment_in, counts_in, first_in, sems = refs[3 + len(swaps) :]
+def opening_kernel(swaps, arrival, source, assignment, counts, first_map, second_map, *refs):
+    starts_out, live_out, edge_out, first_in, second_in = refs[:5]
+    messages = refs[5 : 5 + len(swaps)]
+    arrival_in, source_in, assignment_in, counts_in, sems = refs[5 + len(swaps) :]
     rounds, slots, cells = source.shape
     pairs = [(counts, counts_in), (assignment, assignment_in), (first_map, first_in)]
     pairs += [(arrival, arrival_in)]
     pairs += [(source.at[r], source_in.at[r]) for r in range(rounds)]
+    pairs += [(second_map, second_in)]
     copies = [
         pltpu.make_async_copy(here, there, sems.at[i]) for i, (here, there) in enumerate(pairs)
     ]
@@ -133,6 +134,7 @@
         at = round_number * (slots // 4)
         for message, swap in zip(messages, swaps):
             message[at : at + slots // 4] = pack(edges, group_of(*swap))
+    copies[-1].wait()
 
 
 def coupled_inside(mapped):
@@ -170,11 +172,10 @@
 
     @pl.when(early)
     def _():
-        slots = starts.shape[1]
-        for chain in range(image_out.shape[0] // slots):
-            mapped = dot(starts[chain], first_map[...]).astype(jnp.bfloat16).astype(jnp.float32)
-            coupled = coupled_inside(mapped).astype(jnp.bfloat16)
-            image_out[chain * slots : (chain + 1) * slots] = dot(coupled, second_map[...])
+        chains = image_out.shape[0] // starts.shape[1]
+        mapped = dot(starts[:chains].reshape(-1, cells), first_map[...]).astype(jnp.bfloat16)
+        coupled = coupled_inside(mapped.astype(jnp.float32)).astype(jnp.bfloat16)
+        image_out[...] = dot(coupled, second_map[...])
 
     @pl.when(jnp.logical_not(early))
     def _():
@@ -211,29 +212,33 @@
     outs = refs[6 + len(swaps) :]
     slots, cells = starts.shape[1:]
     part = slots // 4
-    for chain in range(chains):
-        round_number = step + chain
-        halo = halo_of(
-            [[ref] for ref in received], swaps, [chain * part], part, live[round_number]
-        )
-        rows = slice(chain * slots, (chain + 1) * slots)
-        start = starts[round_number]
-        if step == 0:
-            image = traces[rows] + dot(halo, map_ext[cells:])
-        else:
-            start = start.astype(jnp.float32) + traces[rows].astype(jnp.float32)
-            start = start.astype(jnp.bfloat16)
-            image = dot(jnp.concatenate([start, halo], axis=1), map_ext[...])
-        ended = blend(image, start, damping)
-        if chain < chains - 1:
-            outs[0][rows] = ended
-        else:
-            outs[-1][...] = ended
-        at = cells + round_number * slots
-        edges = dot(ended, edge_next[:cells]) + edge_next[at : at + slots].astype(jnp.float32)
-        messages = outs[len(outs) - 1 - len(swaps) : len(outs) - 1]
-        for message, swap in zip(messages, swaps):
-            message[chain * part : (chain + 1) * part] = pack(edges, group_of(*swap))
+    now = slice(step, step + chains)
+    halo = [
+        halo_of([[ref] for ref in received], swaps, [chain * part], part, live[step + chain])
+        for chain in range(chains)
+    ]
+    halo = jnp.concatenate(halo, axis=0)
+    start = starts[now].reshape(-1, cells)
+    if step == 0:
+        image = traces[...] + dot(halo, map_ext[cells:])
+    else:
+        start = start.astype(jnp.float32) + traces[...].astype(jnp.float32)
+        start = start.astype(jnp.bfloat16)
+        image = dot(jnp.concatenate([start, halo], axis=1), map_ext[...])
+    ended = blend(image, start, damping)
+    staying = (chains - 1) * slots
+    if chains > 1:
+        outs[0][...] = ended[:staying]
+    outs[-1][...] = ended[staying:]
+    at = cells + step * slots
+    edges = dot(ended, edge_next[:cells])
+    edges += edge_next[at : at + chains * slots].astype(jnp.float32)
+    messages = outs[len(outs) - 1 - len(swaps) : len(outs) - 1]
+    for message, swap in zip(messages, swaps):
+        for chain in range(chains):
+            message[chain * part : (chain + 1) * part] = pack(
+                edges[chain * slots : (chain + 1) * slots], group_of(*swap)
+            )
 
 
 def final_kernel(swaps, starts, live, map_ext, damping, *refs):
@@ -266,7 +271,9 @@
 
 
 def call(kernel, out_shape, operands, in_hbm=False, scratch=(), aliases=None):
-    space = pl.ANY if in_hbm else pltpu.VMEM
+    space = pltpu.HBM if in_hbm else pltpu.VMEM
+    if in_hbm:
+        operands = [pltpu.with_memory_space_constraint(x, pltpu.HBM) for x in operands]
     return pl.pallas_call(
         kernel,
         out_shape=out_shape,
@@ -322,21 +329,22 @@
             array(rounds, slots, cells),
             array(rounds, slots, LANES),
             array(cells + (rounds - 1) * slots, LANES),
+            array(*first_map.shape),
+            array(*second_map.shape),
         ]
         + [array(rounds * part, LANES)] * len(swaps),
-        [arrival, source, assignment, counts, first_map],
+        [arrival, source, assignment, counts, first_map, second_map],
         in_hbm=True,
         scratch=[
             pltpu.VMEM(arrival.shape, arrival.dtype),
             pltpu.VMEM(source.shape, source.dtype),
             pltpu.VMEM(assignment.shape, assignment.dtype),
             pltpu.SMEM(counts.shape, counts.dtype),
-            pltpu.VMEM(first_map.shape, first_map.dtype),
-            pltpu.SemaphoreType.DMA((4 + rounds,)),
+            pltpu.SemaphoreType.DMA((5 + rounds,)),
         ],
     )
-    starts, live, edge = opened[:3]
-    received = [send(m, range(early_layers), 0, swap) for m, swap in zip(opened[3:], swaps)]
+    starts, live, edge, first_map, second_map = opened[:5]
+    received = [send(m, range(early_layers), 0, swap) for m, swap in zip(opened[5:], swaps)]
     edge_next = send(edge, range(1, layers), -1)
     padded = pltpu.VMEM((cells + 64, cells), jnp.float32)
     traces, map_ext = call(

time: 54.9 us -> 49.5 us (0.902)
  local copies, waits for them, and re-layouts: 5.12 us -> 0.01 us
    unnamed x16 -> x2, local copies, waits for them, and re-layouts: 5.12 us -> 0.01 us
  transfers between devices with their start and end apart: 18 -> 18, of which waited for: 3 -> 3; matrix products, arithmetic and copies ran while one was open for 0% -> 0% of each run, Pallas kernels for 8% -> 9%
where the time goes in v3:
time: 49.5 us; the launch traced here: 49.2 us
  waiting for transfers between devices  19.5 us (39%)
  starting transfers between devices  16.5 us (33%)
  Pallas kernels  12.9 us (26%)
    ppermute x18, waiting for transfers between devices, send(): return lax.ppermute(x, MESH_AXES, pairs)  19.5 us
    ppermute x18, starting transfers between devices, send(): return lax.ppermute(x, MESH_AXES, pairs)  16.5 us
    pallas_call x7, Pallas kernels, call(): pl.pallas_call(kernel, out_shape=out_shape, in_specs=[pl.BlockSpec(memory...  12.9 us
  transfers between devices with their start and end apart: 18, of which 3 were waited for; matrix products, arithmetic and copies ran while one was open for 0% of the time, Pallas kernels for 9%

profile of v3, /device:TPU:11, one launch (start us, length us, event | category | flops | bytes accessed | tf_op | source)
XLA Modules:
  0.0 49.2 jit_solution(17852592382621011600)
XLA Ops:
  0.0 4.6 %shard_map.73 = (bf16[4,192,896]{2,1,0:T(8,128)(2,1)S(1)}, bf16[4,192,128]{2,1,0:T(8,128)(2,1)S(1)}, bf16[1472,128]{1,0:T(8,128)(2,1)S(1)}, bf16[896,896]{1,0:T(...) custom-call(bf16[192,896]{1,0:T(8,128)(2,1)} %bitcast.16, ...), custom_call_target="tpu_custom_call" | custom-call | tf_op jit(solution)/shard_map/pallas_call | solution.py:277
  4.6 2.6 %collective-permute-start.3 = (bf16[1472,128]{1,0:T(8,128)(2,1)S(1)}, bf16[1472,128]{1,0:T(8,128)(2,1)S(1)}, u32[]{:S(2)}, u32[]{:S(2)}) collective-permute-start(bf16[1472,128]{1,0:T(8,128)(2,1)S(1)} %get-tuple-element.37), channel_id=1, source_target_pairs={{8,0},{9,1},{10,2},{11,3},{12,4},{13,5},{14,6},{15,7},{16,8},{17,9... | collective-permute-start | bytes 1130504 | tf_op jit(solution)/shard_map/ppermute | solution.py:306
  7.2 0.7 %collective-permute-start = (bf16[192,128]{1,0:T(8,128)(2,1)S(1)}, bf16[192,128]{1,0:T(8,128)(2,1)S(1)}, u32[]{:S(2)}, u32[]{:S(2)}) collective-permute-start(bf16[192,128]{1,0:T(8,128)(2,1)S(1)} %get-tuple-element.34), channel_id=1, source_target_pairs={{0,4},{1,5},{2,6},{3,7},{4,0},{5,1},{6,2},{7,3}} | collective-permute-start | bytes 147464 | tf_op jit(solution)/shard_map/ppermute | solution.py:306
  7.9 0.7 %collective-permute-start.1 = (bf16[192,128]{1,0:T(8,128)(2,1)S(1)}, bf16[192,128]{1,0:T(8,128)(2,1)S(1)}, u32[]{:S(2)}, u32[]{:S(2)}) collective-permute-start(bf16[192,128]{1,0:T(8,128)(2,1)S(1)} %get-tuple-element.35), channel_id=1, source_target_pairs={{0,1},{1,0},{2,3},{3,2},{4,5},{5,4},{6,7},{7,6}} | collective-permute-start | bytes 147464 | tf_op jit(solution)/shard_map/ppermute | solution.py:306
  8.5 0.7 %collective-permute-start.2 = (bf16[192,128]{1,0:T(8,128)(2,1)S(1)}, bf16[192,128]{1,0:T(8,128)(2,1)S(1)}, u32[]{:S(2)}, u32[]{:S(2)}) collective-permute-start(bf16[192,128]{1,0:T(8,128)(2,1)S(1)} %get-tuple-element.36), channel_id=1, source_target_pairs={{1,2},{2,1},{5,6},{6,5}} | collective-permute-start | bytes 147464 | tf_op jit(solution)/shard_map/ppermute | solution.py:306
  9.2 0.0 copy-start
  9.2 3.5 %shard_map.74 = (f32[576,896]{1,0:T(8,128)S(1)}, bf16[1024,896]{1,0:T(8,128)(2,1)S(1)}) custom-call(bf16[4,192,896]{2,1,0:T(8,128)(2,1)S(1)} %get-tuple-element.29.starts.refs_0_, bf16[896,896]{1,0:T(8,128)(2,1)S(1)} %get-tuple-element.31.first_map, bf16[896,896]{1,0:T(8,128)(2,1)S(1)} %get-tuple-element.32.second_map), custom_call_target="tpu_custom_call" | custom-call | tf_op jit(solution)/shard_map/pallas_call | solution.py:277
  12.8 0.0 collective-permute-done.2.refs_8_.refs_2_
  12.8 0.9 %shard_map.76 = (bf16[384,896]{1,0:T(8,128)(2,1)S(1)}, bf16[144,128]{1,0:T(8,128)(2,1)S(1)}, bf16[144,128]{1,0:T(8,128)(2,1)S(1)}, bf16[144,128]{1,0:T(8,128)(2,1)S(1)}, bf16[192,896]{1,0:T(8,128)(2,1)S(1)}) custom-call(bf16[4,192,896]{2,1,0:T(8,128)(2,1)S(1)} %get-tuple-element.29.starts.refs_0_, bf16[4,192,128]{2,1,0:T(8,128)(2,1)S(1)} %get-tuple-element.30.refs_1_.live, ...), custom_call_target="tpu_custom_call" | custom-call | tf_op jit(solution)/shard_map/pallas_call | solution.py:277
  13.7 0.7 %collective-permute-start.8 = (bf16[384,896]{1,0:T(8,128)(2,1)S(1)}, bf16[384,896]{1,0:T(8,128)(2,1)S(1)}, u32[]{:S(2)}, u32[]{:S(2)}) collective-permute-start(bf16[384,896]{1,0:T(8,128)(2,1)S(1)} %get-tuple-element.43), channel_id=1, source_target_pairs={{0,8},{1,9},{2,10},{3,11},{4,12},{5,13},{6,14},{7,15}} | collective-permute-start | bytes 2064392 | tf_op jit(solution)/shard_map/ppermute | solution.py:306
  14.4 0.7 %collective-permute-start.5 = (bf16[144,128]{1,0:T(8,128)(2,1)S(1)}, bf16[144,128]{1,0:T(8,128)(2,1)S(1)}, u32[]{:S(2)}, u32[]{:S(2)}) collective-permute-start(bf16[144,128]{1,0:T(8,128)(2,1)S(1)} %get-tuple-element.40), channel_id=1, source_target_pairs={{0,12},{1,13},{2,14},{3,15},{4,8},{5,9},{6,10},{7,11}} | collective-permute-start | bytes 110600 | tf_op jit(solution)/shard_map/ppermute | solution.py:306
  15.1 0.7 %collective-permute-start.6 = (bf16[144,128]{1,0:T(8,128)(2,1)S(1)}, bf16[144,128]{1,0:T(8,128)(2,1)S(1)}, u32[]{:S(2)}, u32[]{:S(2)}) collective-permute-start(bf16[144,128]{1,0:T(8,128)(2,1)S(1)} %get-tuple-element.41), channel_id=1, source_target_pairs={{0,9},{1,8},{2,11},{3,10},{4,13},{5,12},{6,15},{7,14}} | collective-permute-start | bytes 110600 | tf_op jit(solution)/shard_map/ppermute | solution.py:306
  15.8 0.7 %collective-permute-start.7 = (bf16[144,128]{1,0:T(8,128)(2,1)S(1)}, bf16[144,128]{1,0:T(8,128)(2,1)S(1)}, u32[]{:S(2)}, u32[]{:S(2)}) collective-permute-start(bf16[144,128]{1,0:T(8,128)(2,1)S(1)} %get-tuple-element.42), channel_id=1, source_target_pairs={{1,10},{2,9},{5,14},{6,13}} | collective-permute-start | bytes 110600 | tf_op jit(solution)/shard_map/ppermute | solution.py:306
  16.4 0.2 shard_map.75.refs_2_.map_ext
  16.6 0.0 collective-permute-done.5.refs_6_.refs_4_
  16.7 0.0 collective-permute-done.7.refs_8_.refs_6_
  16.7 1.3 %shard_map.77 = (bf16[192,896]{1,0:T(8,128)(2,1)S(1)}, bf16[96,128]{1,0:T(8,128)(2,1)S(1)}, bf16[96,128]{1,0:T(8,128)(2,1)S(1)}, bf16[96,128]{1,0:T(8,128)(2,1)S(1)}, bf16[192,896]{1,0:T(8,128)(2,1)S(1)}) custom-call(bf16[4,192,896]{2,1,0:T(8,128)(2,1)S(1)} %get-tuple-element.29.starts.refs_0_, bf16[4,192,128]{2,1,0:T(8,128)(2,1)S(1)} %get-tuple-element.30.refs_1_.live, ...), custom_call_target="tpu_custom_call" | custom-call | tf_op jit(solution)/shard_map/pallas_call | solution.py:277
  18.0 0.7 %collective-permute-start.13 = (bf16[192,896]{1,0:T(8,128)(2,1)S(1)}, bf16[192,896]{1,0:T(8,128)(2,1)S(1)}, u32[]{:S(2)}, u32[]{:S(2)}) collective-permute-start(bf16[192,896]{1,0:T(8,128)(2,1)S(1)} %get-tuple-element.48), channel_id=1, source_target_pairs={{8,16},{9,17},{10,18},{11,19},{12,20},{13,21},{14,22},{15,23}} | collective-permute-start | bytes 1032200 | tf_op jit(solution)/shard_map/ppermute | solution.py:306
  18.7 0.7 %collective-permute-start.10 = (bf16[96,128]{1,0:T(8,128)(2,1)S(1)}, bf16[96,128]{1,0:T(8,128)(2,1)S(1)}, u32[]{:S(2)}, u32[]{:S(2)}) collective-permute-start(bf16[96,128]{1,0:T(8,128)(2,1)S(1)} %get-tuple-element.45), channel_id=1, source_target_pairs={{8,20},{9,21},{10,22},{11,23},{12,16},{13,17},{14,18},{15,19}} | collective-permute-start | bytes 73736 | tf_op jit(solution)/shard_map/ppermute | solution.py:306
  19.4 0.7 %collective-permute-start.11 = (bf16[96,128]{1,0:T(8,128)(2,1)S(1)}, bf16[96,128]{1,0:T(8,128)(2,1)S(1)}, u32[]{:S(2)}, u32[]{:S(2)}) collective-permute-start(bf16[96,128]{1,0:T(8,128)(2,1)S(1)} %get-tuple-element.46), channel_id=1, source_target_pairs={{8,17},{9,16},{10,19},{11,18},{12,21},{13,20},{14,23},{15,22}} | collective-permute-start | bytes 73736 | tf_op jit(solution)/shard_map/ppermute | solution.py:306
  20.0 0.7 %collective-permute-start.12 = (bf16[96,128]{1,0:T(8,128)(2,1)S(1)}, bf16[96,128]{1,0:T(8,128)(2,1)S(1)}, u32[]{:S(2)}, u32[]{:S(2)}) collective-permute-start(bf16[96,128]{1,0:T(8,128)(2,1)S(1)} %get-tuple-element.47), channel_id=1, source_target_pairs={{9,18},{10,17},{13,22},{14,21}} | collective-permute-start | bytes 73736 | tf_op jit(solution)/shard_map/ppermute | solution.py:306
  20.7 0.7 %collective-permute-start.4 = (bf16[192,896]{1,0:T(8,128)(2,1)S(1)}, bf16[192,896]{1,0:T(8,128)(2,1)S(1)}, u32[]{:S(2)}, u32[]{:S(2)}) collective-permute-start(bf16[192,896]{1,0:T(8,128)(2,1)S(1)} %get-tuple-element.39), channel_id=1, source_target_pairs={{0,8},{1,9},{2,10},{3,11},{4,12},{5,13},{6,14},{7,15}} | collective-permute-start | bytes 1032200 | tf_op jit(solution)/shard_map/ppermute | solution.py:306
  21.4 0.7 %collective-permute-start.9 = (bf16[192,896]{1,0:T(8,128)(2,1)S(1)}, bf16[192,896]{1,0:T(8,128)(2,1)S(1)}, u32[]{:S(2)}, u32[]{:S(2)}) collective-permute-start(bf16[192,896]{1,0:T(8,128)(2,1)S(1)} %get-tuple-element.44), channel_id=1, source_target_pairs={{8,16},{9,17},{10,18},{11,19},{12,20},{13,21},{14,22},{15,23}} | collective-permute-start | bytes 1032200 | tf_op jit(solution)/shard_map/ppermute | solution.py:306
  22.1 0.8 %shard_map.78 = (bf16[48,128]{1,0:T(8,128)(2,1)S(1)}, bf16[48,128]{1,0:T(8,128)(2,1)S(1)}, bf16[48,128]{1,0:T(8,128)(2,1)S(1)}, bf16[192,896]{1,0:T(8,128)(2,1)S(1)}) custom-call(bf16[4,192,896]{2,1,0:T(8,128)(2,1)S(1)} %get-tuple-element.29.starts.refs_0_, bf16[4,192,128]{2,1,0:T(8,128)(2,1)S(1)} %get-tuple-element.30.refs_1_.live, ...), custom_call_target="tpu_custom_call" | custom-call | tf_op jit(solution)/shard_map/pallas_call | solution.py:277
  22.9 1.3 %collective-permute-start.14 = (bf16[192,896]{1,0:T(8,128)(2,1)S(1)}, bf16[192,896]{1,0:T(8,128)(2,1)S(1)}, u32[]{:S(2)}, u32[]{:S(2)}) collective-permute-start(bf16[192,896]{1,0:T(8,128)(2,1)S(1)} %get-tuple-element.49), channel_id=1, source_target_pairs={{16,24},{17,25},{18,26},{19,27},{20,28},{21,29},{22,30},{23,31}} | collective-permute-start | bytes 1032200 | tf_op jit(solution)/shard_map/ppermute | solution.py:306
  24.2 1.3 %collective-permute-start.15 = (bf16[48,128]{1,0:T(8,128)(2,1)S(1)}, bf16[48,128]{1,0:T(8,128)(2,1)S(1)}, u32[]{:S(2)}, u32[]{:S(2)}) collective-permute-start(bf16[48,128]{1,0:T(8,128)(2,1)S(1)} %get-tuple-element.50), channel_id=1, source_target_pairs={{16,28},{17,29},{18,30},{19,31},{20,24},{21,25},{22,26},{23,27}} | collective-permute-start | bytes 36872 | tf_op jit(solution)/shard_map/ppermute | solution.py:306
  25.5 1.3 %collective-permute-start.16 = (bf16[48,128]{1,0:T(8,128)(2,1)S(1)}, bf16[48,128]{1,0:T(8,128)(2,1)S(1)}, u32[]{:S(2)}, u32[]{:S(2)}) collective-permute-start(bf16[48,128]{1,0:T(8,128)(2,1)S(1)} %get-tuple-element.51), channel_id=1, source_target_pairs={{16,25},{17,24},{18,27},{19,26},{20,29},{21,28},{22,31},{23,30}} | collective-permute-start | bytes 36872 | tf_op jit(solution)/shard_map/ppermute | solution.py:306
  26.9 1.3 %collective-permute-start.17 = (bf16[48,128]{1,0:T(8,128)(2,1)S(1)}, bf16[48,128]{1,0:T(8,128)(2,1)S(1)}, u32[]{:S(2)}, u32[]{:S(2)}) collective-permute-start(bf16[48,128]{1,0:T(8,128)(2,1)S(1)} %get-tuple-element.52), channel_id=1, source_target_pairs={{17,26},{18,25},{21,30},{22,29}} | collective-permute-start | bytes 36872 | tf_op jit(solution)/shard_map/ppermute | solution.py:306
  28.2 16.4 %collective-permute-done.15.refs_12_ = bf16[48,128]{1,0:T(8,128)(2,1)S(1)} collective-permute-done((bf16[48,128]{1,0:T(8,128)(2,1)S(1)}, bf16[48,128]{1,0:T(8,128)(2,1)S(1)}, u32[]{:S(2)}, u32[]{:S(2)}) %collective-permute-start.15) | collective-permute-done | bytes 12320 | tf_op jit(solution)/shard_map/ppermute | solution.py:306
  44.6 0.5 collective-permute-done.16.refs_13_
  45.0 2.6 %collective-permute-done.17.refs_14_ = bf16[48,128]{1,0:T(8,128)(2,1)S(1)} collective-permute-done((bf16[48,128]{1,0:T(8,128)(2,1)S(1)}, bf16[48,128]{1,0:T(8,128)(2,1)S(1)}, u32[]{:S(2)}, u32[]{:S(2)}) %collective-permute-start.17) | collective-permute-done | bytes 12320 | tf_op jit(solution)/shard_map/ppermute | solution.py:306
  47.6 1.6 %shard_map.79 = bf16[192,896]{1,0:T(8,128)(2,1)} custom-call(bf16[4,192,896]{2,1,0:T(8,128)(2,1)S(1)} %get-tuple-element.29.starts.refs_0_, bf16[4,192,128]{2,1,0:T(8,128)(2,1)S(1)} %get-tuple-element.30.refs_1_.live, bf16[1024,896]{1,0:T(8,128)(2,1)S(1)} %shard_map.75.refs_2_.map_ext, f32[1,896]{1,0:T(1,128)S(1)} %bitcast.12, ...), custom_call_target="tpu_custom_call" | custom-call | tf_op jit(solution)/shard_map/pallas_call | solution.py:277
  (13 shorter events, 0.0 us)
Async XLA Ops:
  4.6 8.2 %collective-permute-start.3 = (bf16[1472,128]{1,0:T(8,128)(2,1)S(1)}, bf16[1472,128]{1,0:T(8,128)(2,1)S(1)}, u32[]{:S(2)}, u32[]{:S(2)}) collective-permute-start(bf16[1472,128]{1,0:T(8,128)(2,1)S(1)} %get-tuple-element.37), channel_id=1, source_target_pairs={{8,0},{9,1},{10,2},{11,3},{12,4},{13,5},{14,6},{15,7},{16,8},{17,9... | collective-permute-start | bytes 1130504 | tf_op jit(solution)/shard_map/ppermute | solution.py:306
  7.2 5.6 %collective-permute-start = (bf16[192,128]{1,0:T(8,128)(2,1)S(1)}, bf16[192,128]{1,0:T(8,128)(2,1)S(1)}, u32[]{:S(2)}, u32[]{:S(2)}) collective-permute-start(bf16[192,128]{1,0:T(8,128)(2,1)S(1)} %get-tuple-element.34), channel_id=1, source_target_pairs={{0,4},{1,5},{2,6},{3,7},{4,0},{5,1},{6,2},{7,3}} | collective-permute-start | bytes 147464 | tf_op jit(solution)/shard_map/ppermute | solution.py:306
  7.9 4.9 %collective-permute-start.1 = (bf16[192,128]{1,0:T(8,128)(2,1)S(1)}, bf16[192,128]{1,0:T(8,128)(2,1)S(1)}, u32[]{:S(2)}, u32[]{:S(2)}) collective-permute-start(bf16[192,128]{1,0:T(8,128)(2,1)S(1)} %get-tuple-element.35), channel_id=1, source_target_pairs={{0,1},{1,0},{2,3},{3,2},{4,5},{5,4},{6,7},{7,6}} | collective-permute-start | bytes 147464 | tf_op jit(solution)/shard_map/ppermute | solution.py:306
  8.5 4.2 %collective-permute-start.2 = (bf16[192,128]{1,0:T(8,128)(2,1)S(1)}, bf16[192,128]{1,0:T(8,128)(2,1)S(1)}, u32[]{:S(2)}, u32[]{:S(2)}) collective-permute-start(bf16[192,128]{1,0:T(8,128)(2,1)S(1)} %get-tuple-element.36), channel_id=1, source_target_pairs={{1,2},{2,1},{5,6},{6,5}} | collective-permute-start | bytes 147464 | tf_op jit(solution)/shard_map/ppermute | solution.py:306
  9.2 3.6 %copy-start = (f32[1,1,1,896]{3,2,1,0:T(1,128)S(1)}, f32[1,1,1,896]{3,2,1,0:T(1,128)}, u32[]{:S(2)}) copy-start(f32[1,1,1,896]{3,2,1,0:T(1,128)} %param.13) | copy-start | bytes 10756
  13.7 3.0 %collective-permute-start.8 = (bf16[384,896]{1,0:T(8,128)(2,1)S(1)}, bf16[384,896]{1,0:T(8,128)(2,1)S(1)}, u32[]{:S(2)}, u32[]{:S(2)}) collective-permute-start(bf16[384,896]{1,0:T(8,128)(2,1)S(1)} %get-tuple-element.43), channel_id=1, source_target_pairs={{0,8},{1,9},{2,10},{3,11},{4,12},{5,13},{6,14},{7,15}} | collective-permute-start | bytes 2064392 | tf_op jit(solution)/shard_map/ppermute | solution.py:306
  14.4 2.2 %collective-permute-start.5 = (bf16[144,128]{1,0:T(8,128)(2,1)S(1)}, bf16[144,128]{1,0:T(8,128)(2,1)S(1)}, u32[]{:S(2)}, u32[]{:S(2)}) collective-permute-start(bf16[144,128]{1,0:T(8,128)(2,1)S(1)} %get-tuple-element.40), channel_id=1, source_target_pairs={{0,12},{1,13},{2,14},{3,15},{4,8},{5,9},{6,10},{7,11}} | collective-permute-start | bytes 110600 | tf_op jit(solution)/shard_map/ppermute | solution.py:306
  15.1 1.6 %collective-permute-start.6 = (bf16[144,128]{1,0:T(8,128)(2,1)S(1)}, bf16[144,128]{1,0:T(8,128)(2,1)S(1)}, u32[]{:S(2)}, u32[]{:S(2)}) collective-permute-start(bf16[144,128]{1,0:T(8,128)(2,1)S(1)} %get-tuple-element.41), channel_id=1, source_target_pairs={{0,9},{1,8},{2,11},{3,10},{4,13},{5,12},{6,15},{7,14}} | collective-permute-start | bytes 110600 | tf_op jit(solution)/shard_map/ppermute | solution.py:306
  15.8 0.9 %collective-permute-start.7 = (bf16[144,128]{1,0:T(8,128)(2,1)S(1)}, bf16[144,128]{1,0:T(8,128)(2,1)S(1)}, u32[]{:S(2)}, u32[]{:S(2)}) collective-permute-start(bf16[144,128]{1,0:T(8,128)(2,1)S(1)} %get-tuple-element.42), channel_id=1, source_target_pairs={{1,10},{2,9},{5,14},{6,13}} | collective-permute-start | bytes 110600 | tf_op jit(solution)/shard_map/ppermute | solution.py:306
  18.0 4.1 %collective-permute-start.13 = (bf16[192,896]{1,0:T(8,128)(2,1)S(1)}, bf16[192,896]{1,0:T(8,128)(2,1)S(1)}, u32[]{:S(2)}, u32[]{:S(2)}) collective-permute-start(bf16[192,896]{1,0:T(8,128)(2,1)S(1)} %get-tuple-element.48), channel_id=1, source_target_pairs={{8,16},{9,17},{10,18},{11,19},{12,20},{13,21},{14,22},{15,23}} | collective-permute-start | bytes 1032200 | tf_op jit(solution)/shard_map/ppermute | solution.py:306
  18.7 2.7 %collective-permute-start.10 = (bf16[96,128]{1,0:T(8,128)(2,1)S(1)}, bf16[96,128]{1,0:T(8,128)(2,1)S(1)}, u32[]{:S(2)}, u32[]{:S(2)}) collective-permute-start(bf16[96,128]{1,0:T(8,128)(2,1)S(1)} %get-tuple-element.45), channel_id=1, source_target_pairs={{8,20},{9,21},{10,22},{11,23},{12,16},{13,17},{14,18},{15,19}} | collective-permute-start | bytes 73736 | tf_op jit(solution)/shard_map/ppermute | solution.py:306
  19.4 2.7 %collective-permute-start.11 = (bf16[96,128]{1,0:T(8,128)(2,1)S(1)}, bf16[96,128]{1,0:T(8,128)(2,1)S(1)}, u32[]{:S(2)}, u32[]{:S(2)}) collective-permute-start(bf16[96,128]{1,0:T(8,128)(2,1)S(1)} %get-tuple-element.46), channel_id=1, source_target_pairs={{8,17},{9,16},{10,19},{11,18},{12,21},{13,20},{14,23},{15,22}} | collective-permute-start | bytes 73736 | tf_op jit(solution)/shard_map/ppermute | solution.py:306
  20.0 2.1 %collective-permute-start.12 = (bf16[96,128]{1,0:T(8,128)(2,1)S(1)}, bf16[96,128]{1,0:T(8,128)(2,1)S(1)}, u32[]{:S(2)}, u32[]{:S(2)}) collective-permute-start(bf16[96,128]{1,0:T(8,128)(2,1)S(1)} %get-tuple-element.47), channel_id=1, source_target_pairs={{9,18},{10,17},{13,22},{14,21}} | collective-permute-start | bytes 73736 | tf_op jit(solution)/shard_map/ppermute | solution.py:306
  20.7 6.1 %collective-permute-start.4 = (bf16[192,896]{1,0:T(8,128)(2,1)S(1)}, bf16[192,896]{1,0:T(8,128)(2,1)S(1)}, u32[]{:S(2)}, u32[]{:S(2)}) collective-permute-start(bf16[192,896]{1,0:T(8,128)(2,1)S(1)} %get-tuple-element.39), channel_id=1, source_target_pairs={{0,8},{1,9},{2,10},{3,11},{4,12},{5,13},{6,14},{7,15}} | collective-permute-start | bytes 1032200 | tf_op jit(solution)/shard_map/ppermute | solution.py:306
  21.4 6.8 %collective-permute-start.9 = (bf16[192,896]{1,0:T(8,128)(2,1)S(1)}, bf16[192,896]{1,0:T(8,128)(2,1)S(1)}, u32[]{:S(2)}, u32[]{:S(2)}) collective-permute-start(bf16[192,896]{1,0:T(8,128)(2,1)S(1)} %get-tuple-element.44), channel_id=1, source_target_pairs={{8,16},{9,17},{10,18},{11,19},{12,20},{13,21},{14,22},{15,23}} | collective-permute-start | bytes 1032200 | tf_op jit(solution)/shard_map/ppermute | solution.py:306
  22.9 24.7 %collective-permute-start.14 = (bf16[192,896]{1,0:T(8,128)(2,1)S(1)}, bf16[192,896]{1,0:T(8,128)(2,1)S(1)}, u32[]{:S(2)}, u32[]{:S(2)}) collective-permute-start(bf16[192,896]{1,0:T(8,128)(2,1)S(1)} %get-tuple-element.49), channel_id=1, source_target_pairs={{16,24},{17,25},{18,26},{19,27},{20,28},{21,29},{22,30},{23,31}} | collective-permute-start | bytes 1032200 | tf_op jit(solution)/shard_map/ppermute | solution.py:306
  24.2 20.3 %collective-permute-start.15 = (bf16[48,128]{1,0:T(8,128)(2,1)S(1)}, bf16[48,128]{1,0:T(8,128)(2,1)S(1)}, u32[]{:S(2)}, u32[]{:S(2)}) collective-permute-start(bf16[48,128]{1,0:T(8,128)(2,1)S(1)} %get-tuple-element.50), channel_id=1, source_target_pairs={{16,28},{17,29},{18,30},{19,31},{20,24},{21,25},{22,26},{23,27}} | collective-permute-start | bytes 36872 | tf_op jit(solution)/shard_map/ppermute | solution.py:306
  25.5 19.5 %collective-permute-start.16 = (bf16[48,128]{1,0:T(8,128)(2,1)S(1)}, bf16[48,128]{1,0:T(8,128)(2,1)S(1)}, u32[]{:S(2)}, u32[]{:S(2)}) collective-permute-start(bf16[48,128]{1,0:T(8,128)(2,1)S(1)} %get-tuple-element.51), channel_id=1, source_target_pairs={{16,25},{17,24},{18,27},{19,26},{20,29},{21,28},{22,31},{23,30}} | collective-permute-start | bytes 36872 | tf_op jit(solution)/shard_map/ppermute | solution.py:306
  26.9 20.8 %collective-permute-start.17 = (bf16[48,128]{1,0:T(8,128)(2,1)S(1)}, bf16[48,128]{1,0:T(8,128)(2,1)S(1)}, u32[]{:S(2)}, u32[]{:S(2)}) collective-permute-start(bf16[48,128]{1,0:T(8,128)(2,1)S(1)} %get-tuple-element.52), channel_id=1, source_target_pairs={{17,26},{18,25},{21,30},{22,29}} | collective-permute-start | bytes 36872 | tf_op jit(solution)/shard_map/ppermute | solution.py:306

commit v4 on v3

--- a/solution.py
+++ b/solution.py
@@ -2,6 +2,7 @@
 
 import jax
 import jax.numpy as jnp
+import numpy as np
 from jax import lax
 from jax.experimental import pallas as pl
 from jax.experimental.pallas import tpu as pltpu
@@ -46,7 +47,7 @@
     for axis, base in EDGE_AXES:
         for parity in range(min(lax.axis_size(axis) - 1, 2)):
             found.append((axis, parity, base))
-    return found
+    return found[::-1]
 
 
 def group_of(axis, parity, base):
@@ -78,15 +79,15 @@
     return round_number - lax.axis_index("depth") + lax.axis_size("depth") - 1
 
 
-def opening_kernel(swaps, arrival, source, assignment, counts, first_map, second_map, *refs):
-    starts_out, live_out, edge_out, first_in, second_in = refs[:5]
+def opening_kernel(swaps, arrival, source, assignment, counts, first_map, band, *refs):
+    starts_out, live_out, edge_out, first_in, band_in = refs[:5]
     messages = refs[5 : 5 + len(swaps)]
     arrival_in, source_in, assignment_in, counts_in, sems = refs[5 + len(swaps) :]
     rounds, slots, cells = source.shape
     pairs = [(counts, counts_in), (assignment, assignment_in), (first_map, first_in)]
     pairs += [(arrival, arrival_in)]
     pairs += [(source.at[r], source_in.at[r]) for r in range(rounds)]
-    pairs += [(second_map, second_in)]
+    pairs += [(band, band_in)]
     copies = [
         pltpu.make_async_copy(here, there, sems.at[i]) for i, (here, there) in enumerate(pairs)
     ]
@@ -137,57 +138,73 @@
     copies[-1].wait()
 
 
-def coupled_inside(mapped):
-    cells = mapped.shape[1]
-    lane = lax.broadcasted_iota(jnp.int32, (1, cells), 1)
-    column = lane % FY
-    around = jnp.where(lane >= FY, pltpu.roll(mapped, FY, 1), 0.0)
-    around += jnp.where(lane < cells - FY, pltpu.roll(mapped, cells - FY, 1), 0.0)
-    around += jnp.where(column > 0, pltpu.roll(mapped, 1, 1), 0.0)
-    around += jnp.where(column < FY - 1, pltpu.roll(mapped, cells - 1, 1), 0.0)
-    return mapped + coupling_weight * around
-
-
-def fill_whole_map(first_map, second_map, whole_ext, padded):
+def bands(cells):
+    found = []
+    for at in range(0, cells, 2 * LANES):
+        end = min(at + 2 * LANES, cells)
+        found.append((slice(max(at - LANES, 0), min(end + LANES, cells)), slice(at, end)))
+    return found
+
+
+def coupling_band(cells):
+    cell = np.arange(cells)
+    apart = np.abs(cell[:, None] - cell[None, :])
+    same_row = cell[:, None] // FY == cell[None, :] // FY
+    linked = (apart == FY) | ((apart == 1) & same_row)
+    coupling = np.eye(cells) + coupling_weight * linked
+    band = np.zeros((len(bands(cells)), 4 * LANES, 2 * LANES), np.float32)
+    for block, (rows, columns) in zip(band, bands(cells)):
+        piece = coupling[rows, columns]
+        block[: piece.shape[0], : piece.shape[1]] = piece
+    return jnp.asarray(band, jnp.bfloat16)
+
+
+def coupled(x, band):
+    pieces = []
+    for at, (rows, columns) in enumerate(bands(x.shape[1])):
+        height, width = rows.stop - rows.start, columns.stop - columns.start
+        pieces.append(dot(x[:, rows], band[at, :height, :width]).astype(jnp.bfloat16))
+    return jnp.concatenate(pieces, axis=1)
+
+
+def fill_whole_map(first_map, band, second_map, whole_ext):
     cells = second_map.shape[0]
-    margin = 32
-    width = second_map.shape[1]
-    padded[:margin] = jnp.zeros((margin, width), jnp.float32)
-    padded[margin + cells :] = jnp.zeros((margin, width), jnp.float32)
-    padded[margin : margin + cells] = second_map[...].astype(jnp.float32)
-    column = lax.broadcasted_iota(jnp.int32, (cells, 1), 0) % FY
-    middle = padded[margin : margin + cells]
-    sides = padded[margin - FY : margin - FY + cells] + padded[margin + FY : margin + FY + cells]
-    sides += jnp.where(column > 0, padded[margin - 1 : margin - 1 + cells], 0.0)
-    sides += jnp.where(column < FY - 1, padded[margin + 1 : margin + 1 + cells], 0.0)
-    coupled = (middle + coupling_weight * sides).astype(jnp.bfloat16)
-    whole_ext[:cells] = dot(first_map[...], coupled).astype(jnp.bfloat16)
-
-
-def inside_kernel(early_layers, starts, first_map, second_map, image_out, whole_ext, padded):
+    whole_ext[:cells] = dot(coupled(first_map[...], band), second_map[...]).astype(jnp.bfloat16)
+
+
+def inside_kernel(early_layers, starts, first_map, band, second_map, *refs):
+    image_out, whole_ext, second_in, sem = refs
     cells = second_map.shape[0]
     early = lax.axis_index("depth") < early_layers
-    edge_rows = dot_t(edge_selector(cells), second_map[...])
-    whole_ext[cells:] = (coupling_weight * edge_rows).astype(jnp.bfloat16)
+    copy = pltpu.make_async_copy(second_map, second_in, sem)
+    copy.start()
 
     @pl.when(early)
     def _():
         chains = image_out.shape[0] // starts.shape[1]
         mapped = dot(starts[:chains].reshape(-1, cells), first_map[...]).astype(jnp.bfloat16)
-        coupled = coupled_inside(mapped.astype(jnp.float32)).astype(jnp.bfloat16)
-        image_out[...] = dot(coupled, second_map[...])
+        image_out[...] = coupled(mapped, band).astype(jnp.float32)
+
+    copy.wait()
+
+    @pl.when(early)
+    def _():
+        image_out[...] = dot(image_out[...].astype(jnp.bfloat16), second_in[...])
 
     @pl.when(jnp.logical_not(early))
     def _():
-        fill_whole_map(first_map, second_map, whole_ext, padded)
-
-
-def whole_map_kernel(early_layers, first_map, second_map, whole_in, whole_ext, padded):
+        fill_whole_map(first_map, band, second_in, whole_ext)
+
+    edge_rows = dot_t(edge_selector(cells), second_in[...])
+    whole_ext[cells:] = (coupling_weight * edge_rows).astype(jnp.bfloat16)
+
+
+def whole_map_kernel(early_layers, first_map, band, second_map, whole_in, whole_ext):
     del whole_in
 
     @pl.when(lax.axis_index("depth") < early_layers)
     def _():
-        fill_whole_map(first_map, second_map, whole_ext, padded)
+        fill_whole_map(first_map, band, second_map, whole_ext)
 
 
 def halo_of(messages, swaps, at, part, live):
@@ -209,7 +226,9 @@
     refs = list(refs)
     starts, live, map_ext, damping, edge_next, traces = refs[:6]
     received = refs[6 : 6 + len(swaps)]
-    outs = refs[6 + len(swaps) :]
+    others, outs = refs[6 + len(swaps) : -len(swaps) - 1], refs[-len(swaps) - 1 :]
+    if chains > 1:
+        others, outs = others[:-1], others[-1:] + outs
     slots, cells = starts.shape[1:]
     part = slots // 4
     now = slice(step, step + chains)
@@ -230,6 +249,12 @@
     if chains > 1:
         outs[0][...] = ended[:staying]
     outs[-1][...] = ended[staying:]
+    for layer, other in enumerate(others):
+
+        @pl.when(lax.axis_index("depth") == layer)
+        def _():
+            outs[-1][...] = other[...]
+
     at = cells + step * slots
     edges = dot(ended, edge_next[:cells])
     edges += edge_next[at : at + chains * slots].astype(jnp.float32)
@@ -241,43 +266,35 @@
             )
 
 
-def final_kernel(swaps, starts, live, map_ext, damping, *refs):
+def final_kernel(swaps, starts, live, map_ext, damping, traces, *refs):
     rounds, slots, cells = starts.shape
-    phases = []
-    refs = list(refs)
-    for phase in range(rounds):
-        traces = refs.pop(0) if phase > 0 else None
-        phases.append((traces, refs[: len(swaps)]))
-        refs = refs[len(swaps) :]
-    traces_out, row = refs
+    received, (traces_out, row) = refs[:-2], refs[-2:]
     part = slots // 4
     layer = lax.axis_index("depth")
-    for phase, (traces, messages) in enumerate(phases):
-        here = layer >= phase if phase == rounds - 1 else layer == phase
-
-        @pl.when(here)
+    start = starts[rounds - 1].astype(jnp.float32) + traces[...].astype(jnp.float32)
+    row[:, :cells] = start.astype(jnp.bfloat16)
+    for phase in range(rounds):
+        messages = received[phase * len(swaps) : (phase + 1) * len(swaps)]
+
+        @pl.when(layer >= phase if phase == rounds - 1 else layer == phase)
         def _():
             at = [messages[0].shape[0] - part]
-            halo = halo_of([[ref] for ref in messages], swaps, at, part, live[rounds - 1])
-            start = starts[rounds - 1]
-            if traces is not None:
-                start = start.astype(jnp.float32) + traces[...].astype(jnp.float32)
-                start = start.astype(jnp.bfloat16)
-            row[:, :cells] = start
-            row[:, cells:] = halo
+            row[:, cells:] = halo_of([[ref] for ref in messages], swaps, at, part, live[rounds - 1])
 
     image = dot(row[...], map_ext[...])
     traces_out[...] = blend(image, row[:, :cells], damping)
 
 
-def call(kernel, out_shape, operands, in_hbm=False, scratch=(), aliases=None):
-    space = pltpu.HBM if in_hbm else pltpu.VMEM
-    if in_hbm:
-        operands = [pltpu.with_memory_space_constraint(x, pltpu.HBM) for x in operands]
+def call(kernel, out_shape, operands, in_hbm=(), scratch=(), aliases=None):
+    spaces = [pltpu.HBM if i in in_hbm else pltpu.VMEM for i in range(len(operands))]
+    operands = [
+        pltpu.with_memory_space_constraint(x, pltpu.HBM) if i in in_hbm else x
+        for i, x in enumerate(operands)
+    ]
     return pl.pallas_call(
         kernel,
         out_shape=out_shape,
-        in_specs=[pl.BlockSpec(memory_space=space)] * len(operands),
+        in_specs=[pl.BlockSpec(memory_space=space) for space in spaces],
         out_specs=[pl.BlockSpec(memory_space=pltpu.VMEM)] * len(out_shape),
         scratch_shapes=scratch,
         input_output_aliases=aliases or {},
@@ -323,6 +340,7 @@
         return jax.ShapeDtypeStruct(shape, kind)
 
     part = slots // 4
+    band = coupling_band(cells)
     opened = call(
         functools.partial(opening_kernel, swaps),
         [
@@ -330,11 +348,11 @@
             array(rounds, slots, LANES),
             array(cells + (rounds - 1) * slots, LANES),
             array(*first_map.shape),
-            array(*second_map.shape),
+            array(*band.shape),
         ]
         + [array(rounds * part, LANES)] * len(swaps),
-        [arrival, source, assignment, counts, first_map, second_map],
-        in_hbm=True,
+        [arrival, source, assignment, counts, first_map, band],
+        in_hbm=range(6),
         scratch=[
             pltpu.VMEM(arrival.shape, arrival.dtype),
             pltpu.VMEM(source.shape, source.dtype),
@@ -343,44 +361,48 @@
             pltpu.SemaphoreType.DMA((5 + rounds,)),
         ],
     )
-    starts, live, edge, first_map, second_map = opened[:5]
+    starts, live, edge, first_map, band = opened[:5]
     received = [send(m, range(early_layers), 0, swap) for m, swap in zip(opened[5:], swaps)]
     edge_next = send(edge, range(1, layers), -1)
-    padded = pltpu.VMEM((cells + 64, cells), jnp.float32)
-    traces, map_ext = call(
+    image = array((rounds - 1) * slots, cells, kind=jnp.float32)
+    traces, map_ext, second_map = call(
         functools.partial(inside_kernel, early_layers),
-        [array((rounds - 1) * slots, cells, kind=jnp.float32), array(cells + LANES, cells)],
-        [starts, first_map, second_map],
-        scratch=[padded],
+        [image, array(cells + LANES, cells), array(*second_map.shape)],
+        [starts, first_map, band, second_map],
+        in_hbm=(3,),
+        scratch=[pltpu.SemaphoreType.DMA],
     )
-    arrived = [list(received)]
+    arrived = list(received)
+    kept = []
     for step in range(rounds - 1):
         chains = rounds - 1 - step
         outs = [array((chains - 1) * slots, cells)] if chains > 1 else []
         outs += [array(chains * part, LANES)] * len(swaps) + [array(slots, cells)]
+        operands = [starts, live, map_ext, damping, edge_next, traces] + received
         ended = call(
             functools.partial(step_kernel, swaps, step, chains),
             outs,
-            [starts, live, map_ext, damping, edge_next, traces] + received,
+            operands + (kept if chains == 1 else []),
         )
         below = range(step, step + early_layers)
         if chains > 1:
             traces = send(ended[0], below, 1)
+            kept.append(ended[-1])
+        else:
+            traces = send(ended[-1], range(layers - 1), 1)
         received = [send(m, below, 1, swap) for m, swap in zip(ended[-1 - len(swaps) : -1], swaps)]
-        leaving = send(ended[-1], below if chains == 1 else [step], 1)
-        arrived.append([leaving] + received)
+        arrived += received
         if step == 0:
             (map_ext,) = call(
                 functools.partial(whole_map_kernel, early_layers),
                 [array(cells + LANES, cells)],
-                [first_map, second_map, map_ext],
-                scratch=[padded],
-                aliases={2: 0},
+                [first_map, band, second_map, map_ext],
+                aliases={3: 0},
             )
     (ended,) = call(
         functools.partial(final_kernel, swaps),
         [array(slots, cells)],
-        [starts, live, map_ext, damping] + [x for phase in arrived for x in phase],
+        [starts, live, map_ext, damping, traces] + arrived,
         scratch=[pltpu.VMEM((slots, cells + LANES), jnp.bfloat16)],
     )
     return ended.reshape(1, slots, 1, 1, cells)

time: 49.5 us -> 48.6 us (0.982)
  the two profiles are of different devices: /device:TPU:11 before, /device:TPU:1 now
where the time goes in v4:
time: 48.6 us; the launch traced here: 48.2 us
  starting transfers between devices  20.3 us (42%)
  Pallas kernels  14.2 us (29%)
  waiting for transfers between devices  13.3 us (27%)
    ppermute x16, starting transfers between devices, send(): return lax.ppermute(x, MESH_AXES, pairs)  20.3 us
    pallas_call x7, Pallas kernels, call(): pl.pallas_call(kernel, out_shape=out_shape, in_specs=[pl.BlockSpec(memory...  14.2 us
    ppermute x16, waiting for transfers between devices, send(): return lax.ppermute(x, MESH_AXES, pairs)  13.3 us
  transfers between devices with their start and end apart: 16, of which 5 were waited for; matrix products, arithmetic and copies ran while one was open for 0% of the time, Pallas kernels for 10%

profile of v4, /device:TPU:1, one launch (start us, length us, event | category | flops | bytes accessed | tf_op | source)
XLA Modules:
  0.0 48.2 jit_solution(13329692513000825458)
XLA Ops:
  0.0 4.6 %shard_map.82 = (bf16[4,192,896]{2,1,0:T(8,128)(2,1)S(1)}, bf16[4,192,128]{2,1,0:T(8,128)(2,1)S(1)}, bf16[1472,128]{1,0:T(8,128)(2,1)S(1)}, bf16[896,896]{1,0:T(...) custom-call(bf16[192,896]{1,0:T(8,128)(2,1)} %bitcast.16, ...), custom_call_target="tpu_custom_call" | custom-call | tf_op jit(solution)/shard_map/pallas_call | solution.py:294
  4.6 2.0 %collective-permute-start = (bf16[1472,128]{1,0:T(8,128)(2,1)S(1)}, bf16[1472,128]{1,0:T(8,128)(2,1)S(1)}, u32[]{:S(2)}, u32[]{:S(2)}) collective-permute-start(bf16[1472,128]{1,0:T(8,128)(2,1)S(1)} %get-tuple-element.36), channel_id=1, source_target_pairs={{8,0},{9,1},{10,2},{11,3},{12,4},{13,5},{14,6},{15,7},{16,8},{17,9... | collective-permute-start | bytes 1130504 | tf_op jit(solution)/shard_map/ppermute | solution.py:323
  6.5 0.7 %collective-permute-start.1 = (bf16[192,128]{1,0:T(8,128)(2,1)S(1)}, bf16[192,128]{1,0:T(8,128)(2,1)S(1)}, u32[]{:S(2)}, u32[]{:S(2)}) collective-permute-start(bf16[192,128]{1,0:T(8,128)(2,1)S(1)} %get-tuple-element.38), channel_id=1, source_target_pairs={{1,2},{2,1},{5,6},{6,5}} | collective-permute-start | bytes 147464 | tf_op jit(solution)/shard_map/ppermute | solution.py:323
  7.2 0.7 %collective-permute-start.2 = (bf16[192,128]{1,0:T(8,128)(2,1)S(1)}, bf16[192,128]{1,0:T(8,128)(2,1)S(1)}, u32[]{:S(2)}, u32[]{:S(2)}) collective-permute-start(bf16[192,128]{1,0:T(8,128)(2,1)S(1)} %get-tuple-element.39), channel_id=1, source_target_pairs={{0,1},{1,0},{2,3},{3,2},{4,5},{5,4},{6,7},{7,6}} | collective-permute-start | bytes 147464 | tf_op jit(solution)/shard_map/ppermute | solution.py:323
  7.9 0.7 %collective-permute-start.3 = (bf16[192,128]{1,0:T(8,128)(2,1)S(1)}, bf16[192,128]{1,0:T(8,128)(2,1)S(1)}, u32[]{:S(2)}, u32[]{:S(2)}) collective-permute-start(bf16[192,128]{1,0:T(8,128)(2,1)S(1)} %get-tuple-element.40), channel_id=1, source_target_pairs={{0,4},{1,5},{2,6},{3,7},{4,0},{5,1},{6,2},{7,3}} | collective-permute-start | bytes 147464 | tf_op jit(solution)/shard_map/ppermute | solution.py:323
  8.6 0.0 copy-start
  8.6 4.7 %shard_map.83 = (f32[576,896]{1,0:T(8,128)S(1)}, bf16[1024,896]{1,0:T(8,128)(2,1)S(1)}, bf16[896,896]{1,0:T(8,128)(2,1)S(1)}) custom-call(bf16[4,192,896]{2,1,0:T(8,128)(2,1)S(1)} %get-tuple-element.30.starts.refs_0_, bf16[896,896]{1,0:T(8,128)(2,1)S(1)} %get-tuple-element.32.first_map, bf16[4,512,256]{2,1,0:T(8,128)(2,1)S(1)} %get-tuple-element.33.band, ...), custom_call_target="tpu_custom_call" | custom-call | tf_op jit(solution)/shard_map/pallas_call | solution.py:294
  13.3 0.0 collective-permute-done.1.refs_6_.refs_0_
  13.3 0.0 collective-permute-done.3.refs_8_.refs_2_
  13.4 1.0 %collective-permute-done.refs_4_ = bf16[1472,128]{1,0:T(8,128)(2,1)S(1)} collective-permute-done((bf16[1472,128]{1,0:T(8,128)(2,1)S(1)}, bf16[1472,128]{1,0:T(8,128)(2,1)S(1)}, u32[]{:S(2)}, u32[]{:S(2)}) %collective-permute-start) | collective-permute-done | bytes 376864 | tf_op jit(solution)/shard_map/ppermute | solution.py:323
  14.4 0.9 %shard_map.85 = (bf16[384,896]{1,0:T(8,128)(2,1)S(1)}, bf16[144,128]{1,0:T(8,128)(2,1)S(1)}, bf16[144,128]{1,0:T(8,128)(2,1)S(1)}, bf16[144,128]{1,0:T(8,128)(2,1)S(1)}, bf16[192,896]{1,0:T(8,128)(2,1)S(1)}) custom-call(bf16[4,192,896]{2,1,0:T(8,128)(2,1)S(1)} %get-tuple-element.30.starts.refs_0_, bf16[4,192,128]{2,1,0:T(8,128)(2,1)S(1)} %get-tuple-element.31.refs_1_.live, ...), custom_call_target="tpu_custom_call" | custom-call | tf_op jit(solution)/shard_map/pallas_call | solution.py:294
  15.3 1.3 %collective-permute-start.4 = (bf16[384,896]{1,0:T(8,128)(2,1)S(1)}, bf16[384,896]{1,0:T(8,128)(2,1)S(1)}, u32[]{:S(2)}, u32[]{:S(2)}) collective-permute-start(bf16[384,896]{1,0:T(8,128)(2,1)S(1)} %get-tuple-element.41), channel_id=1, source_target_pairs={{0,8},{1,9},{2,10},{3,11},{4,12},{5,13},{6,14},{7,15}} | collective-permute-start | bytes 2064392 | tf_op jit(solution)/shard_map/ppermute | solution.py:323
  16.6 0.7 %collective-permute-start.5 = (bf16[144,128]{1,0:T(8,128)(2,1)S(1)}, bf16[144,128]{1,0:T(8,128)(2,1)S(1)}, u32[]{:S(2)}, u32[]{:S(2)}) collective-permute-start(bf16[144,128]{1,0:T(8,128)(2,1)S(1)} %get-tuple-element.42), channel_id=1, source_target_pairs={{1,10},{2,9},{5,14},{6,13}} | collective-permute-start | bytes 110600 | tf_op jit(solution)/shard_map/ppermute | solution.py:323
  17.3 1.3 %collective-permute-start.6 = (bf16[144,128]{1,0:T(8,128)(2,1)S(1)}, bf16[144,128]{1,0:T(8,128)(2,1)S(1)}, u32[]{:S(2)}, u32[]{:S(2)}) collective-permute-start(bf16[144,128]{1,0:T(8,128)(2,1)S(1)} %get-tuple-element.43), channel_id=1, source_target_pairs={{0,9},{1,8},{2,11},{3,10},{4,13},{5,12},{6,15},{7,14}} | collective-permute-start | bytes 110600 | tf_op jit(solution)/shard_map/ppermute | solution.py:323
  18.6 1.3 %collective-permute-start.7 = (bf16[144,128]{1,0:T(8,128)(2,1)S(1)}, bf16[144,128]{1,0:T(8,128)(2,1)S(1)}, u32[]{:S(2)}, u32[]{:S(2)}) collective-permute-start(bf16[144,128]{1,0:T(8,128)(2,1)S(1)} %get-tuple-element.44), channel_id=1, source_target_pairs={{0,12},{1,13},{2,14},{3,15},{4,8},{5,9},{6,10},{7,11}} | collective-permute-start | bytes 110600 | tf_op jit(solution)/shard_map/ppermute | solution.py:323
  19.9 0.2 shard_map.84.refs_2_.map_ext
  20.1 0.0 collective-permute-done.5.refs_6_.refs_3_
  20.1 7.6 %collective-permute-done.6.refs_7_.refs_4_ = bf16[144,128]{1,0:T(8,128)(2,1)S(1)} collective-permute-done((bf16[144,128]{1,0:T(8,128)(2,1)S(1)}, bf16[144,128]{1,0:T(8,128)(2,1)S(1)}, u32[]{:S(2)}, u32[]{:S(2)}) %collective-permute-start.6) | collective-permute-done | bytes 36896 | tf_op jit(solution)/shard_map/ppermute | solution.py:323
  27.7 1.2 %collective-permute-done.7.refs_8_.refs_5_ = bf16[144,128]{1,0:T(8,128)(2,1)S(1)} collective-permute-done((bf16[144,128]{1,0:T(8,128)(2,1)S(1)}, bf16[144,128]{1,0:T(8,128)(2,1)S(1)}, u32[]{:S(2)}, u32[]{:S(2)}) %collective-permute-start.7) | collective-permute-done | bytes 36896 | tf_op jit(solution)/shard_map/ppermute | solution.py:323
  28.9 1.3 %shard_map.86 = (bf16[192,896]{1,0:T(8,128)(2,1)S(1)}, bf16[96,128]{1,0:T(8,128)(2,1)S(1)}, bf16[96,128]{1,0:T(8,128)(2,1)S(1)}, bf16[96,128]{1,0:T(8,128)(2,1)S(1)}, bf16[192,896]{1,0:T(8,128)(2,1)S(1)}) custom-call(bf16[4,192,896]{2,1,0:T(8,128)(2,1)S(1)} %get-tuple-element.30.starts.refs_0_, bf16[4,192,128]{2,1,0:T(8,128)(2,1)S(1)} %get-tuple-element.31.refs_1_.live, ...), custom_call_target="tpu_custom_call" | custom-call | tf_op jit(solution)/shard_map/pallas_call | solution.py:294
  30.2 1.3 %collective-permute-start.8 = (bf16[192,896]{1,0:T(8,128)(2,1)S(1)}, bf16[192,896]{1,0:T(8,128)(2,1)S(1)}, u32[]{:S(2)}, u32[]{:S(2)}) collective-permute-start(bf16[192,896]{1,0:T(8,128)(2,1)S(1)} %get-tuple-element.45), channel_id=1, source_target_pairs={{8,16},{9,17},{10,18},{11,19},{12,20},{13,21},{14,22},{15,23}} | collective-permute-start | bytes 1032200 | tf_op jit(solution)/shard_map/ppermute | solution.py:323
  31.5 0.7 %collective-permute-start.9 = (bf16[96,128]{1,0:T(8,128)(2,1)S(1)}, bf16[96,128]{1,0:T(8,128)(2,1)S(1)}, u32[]{:S(2)}, u32[]{:S(2)}) collective-permute-start(bf16[96,128]{1,0:T(8,128)(2,1)S(1)} %get-tuple-element.46), channel_id=1, source_target_pairs={{9,18},{10,17},{13,22},{14,21}} | collective-permute-start | bytes 73736 | tf_op jit(solution)/shard_map/ppermute | solution.py:323
  32.2 1.3 %collective-permute-start.10 = (bf16[96,128]{1,0:T(8,128)(2,1)S(1)}, bf16[96,128]{1,0:T(8,128)(2,1)S(1)}, u32[]{:S(2)}, u32[]{:S(2)}) collective-permute-start(bf16[96,128]{1,0:T(8,128)(2,1)S(1)} %get-tuple-element.47), channel_id=1, source_target_pairs={{8,17},{9,16},{10,19},{11,18},{12,21},{13,20},{14,23},{15,22}} | collective-permute-start | bytes 73736 | tf_op jit(solution)/shard_map/ppermute | solution.py:323
  33.5 1.3 %collective-permute-start.11 = (bf16[96,128]{1,0:T(8,128)(2,1)S(1)}, bf16[96,128]{1,0:T(8,128)(2,1)S(1)}, u32[]{:S(2)}, u32[]{:S(2)}) collective-permute-start(bf16[96,128]{1,0:T(8,128)(2,1)S(1)} %get-tuple-element.48), channel_id=1, source_target_pairs={{8,20},{9,21},{10,22},{11,23},{12,16},{13,17},{14,18},{15,19}} | collective-permute-start | bytes 73736 | tf_op jit(solution)/shard_map/ppermute | solution.py:323
  34.8 1.4 %collective-permute-done.11.refs_8_ = bf16[96,128]{1,0:T(8,128)(2,1)S(1)} collective-permute-done((bf16[96,128]{1,0:T(8,128)(2,1)S(1)}, bf16[96,128]{1,0:T(8,128)(2,1)S(1)}, u32[]{:S(2)}, u32[]{:S(2)}) %collective-permute-start.11) | collective-permute-done | bytes 24608 | tf_op jit(solution)/shard_map/ppermute | solution.py:323
  36.2 1.0 %shard_map.87 = (bf16[48,128]{1,0:T(8,128)(2,1)S(1)}, bf16[48,128]{1,0:T(8,128)(2,1)S(1)}, bf16[48,128]{1,0:T(8,128)(2,1)S(1)}, bf16[192,896]{1,0:T(8,128)(2,1)S(1)}) custom-call(bf16[4,192,896]{2,1,0:T(8,128)(2,1)S(1)} %get-tuple-element.30.starts.refs_0_, bf16[4,192,128]{2,1,0:T(8,128)(2,1)S(1)} %get-tuple-element.31.refs_1_.live, ...), custom_call_target="tpu_custom_call" | custom-call | tf_op jit(solution)/shard_map/pallas_call | solution.py:294
  37.2 5.3 %collective-permute-start.12 = (bf16[192,896]{1,0:T(8,128)(2,1)S(1)}, bf16[192,896]{1,0:T(8,128)(2,1)S(1)}, u32[]{:S(2)}, u32[]{:S(2)}) collective-permute-start(bf16[192,896]{1,0:T(8,128)(2,1)S(1)} %get-tuple-element.51), channel_id=1, source_target_pairs={{0,8},{1,9},{2,10},{3,11},{4,12},{5,13},{6,14},{7,15},{8,16},{9,17... | collective-permute-start | bytes 1032200 | tf_op jit(solution)/shard_map/ppermute | solution.py:323
  42.5 0.7 %collective-permute-start.13 = (bf16[48,128]{1,0:T(8,128)(2,1)S(1)}, bf16[48,128]{1,0:T(8,128)(2,1)S(1)}, u32[]{:S(2)}, u32[]{:S(2)}) collective-permute-start(bf16[48,128]{1,0:T(8,128)(2,1)S(1)} %get-tuple-element.52), channel_id=1, source_target_pairs={{17,26},{18,25},{21,30},{22,29}} | collective-permute-start | bytes 36872 | tf_op jit(solution)/shard_map/ppermute | solution.py:323
  43.2 0.7 %collective-permute-start.14 = (bf16[48,128]{1,0:T(8,128)(2,1)S(1)}, bf16[48,128]{1,0:T(8,128)(2,1)S(1)}, u32[]{:S(2)}, u32[]{:S(2)}) collective-permute-start(bf16[48,128]{1,0:T(8,128)(2,1)S(1)} %get-tuple-element.53), channel_id=1, source_target_pairs={{16,25},{17,24},{18,27},{19,26},{20,29},{21,28},{22,31},{23,30}} | collective-permute-start | bytes 36872 | tf_op jit(solution)/shard_map/ppermute | solution.py:323
  43.8 0.7 %collective-permute-start.15 = (bf16[48,128]{1,0:T(8,128)(2,1)S(1)}, bf16[48,128]{1,0:T(8,128)(2,1)S(1)}, u32[]{:S(2)}, u32[]{:S(2)}) collective-permute-start(bf16[48,128]{1,0:T(8,128)(2,1)S(1)} %get-tuple-element.54), channel_id=1, source_target_pairs={{16,28},{17,29},{18,30},{19,31},{20,24},{21,25},{22,26},{23,27}} | collective-permute-start | bytes 36872 | tf_op jit(solution)/shard_map/ppermute | solution.py:323
  44.5 2.1 %collective-permute-done.12.traces = bf16[192,896]{1,0:T(8,128)(2,1)S(1)} collective-permute-done((bf16[192,896]{1,0:T(8,128)(2,1)S(1)}, bf16[192,896]{1,0:T(8,128)(2,1)S(1)}, u32[]{:S(2)}, u32[]{:S(2)}) %collective-permute-start.12) | collective-permute-done | bytes 344096 | tf_op jit(solution)/shard_map/ppermute | solution.py:323
  46.7 1.5 %shard_map.88 = bf16[192,896]{1,0:T(8,128)(2,1)} custom-call(bf16[4,192,896]{2,1,0:T(8,128)(2,1)S(1)} %get-tuple-element.30.starts.refs_0_, bf16[4,192,128]{2,1,0:T(8,128)(2,1)S(1)} %get-tuple-element.31.refs_1_.live, bf16[1024,896]{1,0:T(8,128)(2,1)S(1)} %shard_map.84.refs_2_.map_ext, f32[1,896]{1,0:T(1,128)S(1)} %bitcast.12, ...), custom_call_target="tpu_custom_call" | custom-call | tf_op jit(solution)/shard_map/pallas_call | solution.py:294
  (9 shorter events, 0.0 us)
Async XLA Ops:
  4.6 9.8 %collective-permute-start = (bf16[1472,128]{1,0:T(8,128)(2,1)S(1)}, bf16[1472,128]{1,0:T(8,128)(2,1)S(1)}, u32[]{:S(2)}, u32[]{:S(2)}) collective-permute-start(bf16[1472,128]{1,0:T(8,128)(2,1)S(1)} %get-tuple-element.36), channel_id=1, source_target_pairs={{8,0},{9,1},{10,2},{11,3},{12,4},{13,5},{14,6},{15,7},{16,8},{17,9... | collective-permute-start | bytes 1130504 | tf_op jit(solution)/shard_map/ppermute | solution.py:323
  6.5 6.8 %collective-permute-start.1 = (bf16[192,128]{1,0:T(8,128)(2,1)S(1)}, bf16[192,128]{1,0:T(8,128)(2,1)S(1)}, u32[]{:S(2)}, u32[]{:S(2)}) collective-permute-start(bf16[192,128]{1,0:T(8,128)(2,1)S(1)} %get-tuple-element.38), channel_id=1, source_target_pairs={{1,2},{2,1},{5,6},{6,5}} | collective-permute-start | bytes 147464 | tf_op jit(solution)/shard_map/ppermute | solution.py:323
  7.2 6.1 %collective-permute-start.2 = (bf16[192,128]{1,0:T(8,128)(2,1)S(1)}, bf16[192,128]{1,0:T(8,128)(2,1)S(1)}, u32[]{:S(2)}, u32[]{:S(2)}) collective-permute-start(bf16[192,128]{1,0:T(8,128)(2,1)S(1)} %get-tuple-element.39), channel_id=1, source_target_pairs={{0,1},{1,0},{2,3},{3,2},{4,5},{5,4},{6,7},{7,6}} | collective-permute-start | bytes 147464 | tf_op jit(solution)/shard_map/ppermute | solution.py:323
  7.9 5.5 %collective-permute-start.3 = (bf16[192,128]{1,0:T(8,128)(2,1)S(1)}, bf16[192,128]{1,0:T(8,128)(2,1)S(1)}, u32[]{:S(2)}, u32[]{:S(2)}) collective-permute-start(bf16[192,128]{1,0:T(8,128)(2,1)S(1)} %get-tuple-element.40), channel_id=1, source_target_pairs={{0,4},{1,5},{2,6},{3,7},{4,0},{5,1},{6,2},{7,3}} | collective-permute-start | bytes 147464 | tf_op jit(solution)/shard_map/ppermute | solution.py:323
  8.6 5.8 %copy-start = (f32[1,1,1,896]{3,2,1,0:T(1,128)S(1)}, f32[1,1,1,896]{3,2,1,0:T(1,128)}, u32[]{:S(2)}) copy-start(f32[1,1,1,896]{3,2,1,0:T(1,128)} %param.14) | copy-start | bytes 10756
  15.3 13.6 %collective-permute-start.4 = (bf16[384,896]{1,0:T(8,128)(2,1)S(1)}, bf16[384,896]{1,0:T(8,128)(2,1)S(1)}, u32[]{:S(2)}, u32[]{:S(2)}) collective-permute-start(bf16[384,896]{1,0:T(8,128)(2,1)S(1)} %get-tuple-element.41), channel_id=1, source_target_pairs={{0,8},{1,9},{2,10},{3,11},{4,12},{5,13},{6,14},{7,15}} | collective-permute-start | bytes 2064392 | tf_op jit(solution)/shard_map/ppermute | solution.py:323
  16.6 3.5 %collective-permute-start.5 = (bf16[144,128]{1,0:T(8,128)(2,1)S(1)}, bf16[144,128]{1,0:T(8,128)(2,1)S(1)}, u32[]{:S(2)}, u32[]{:S(2)}) collective-permute-start(bf16[144,128]{1,0:T(8,128)(2,1)S(1)} %get-tuple-element.42), channel_id=1, source_target_pairs={{1,10},{2,9},{5,14},{6,13}} | collective-permute-start | bytes 110600 | tf_op jit(solution)/shard_map/ppermute | solution.py:323
  17.3 10.4 %collective-permute-start.6 = (bf16[144,128]{1,0:T(8,128)(2,1)S(1)}, bf16[144,128]{1,0:T(8,128)(2,1)S(1)}, u32[]{:S(2)}, u32[]{:S(2)}) collective-permute-start(bf16[144,128]{1,0:T(8,128)(2,1)S(1)} %get-tuple-element.43), channel_id=1, source_target_pairs={{0,9},{1,8},{2,11},{3,10},{4,13},{5,12},{6,15},{7,14}} | collective-permute-start | bytes 110600 | tf_op jit(solution)/shard_map/ppermute | solution.py:323
  18.6 10.3 %collective-permute-start.7 = (bf16[144,128]{1,0:T(8,128)(2,1)S(1)}, bf16[144,128]{1,0:T(8,128)(2,1)S(1)}, u32[]{:S(2)}, u32[]{:S(2)}) collective-permute-start(bf16[144,128]{1,0:T(8,128)(2,1)S(1)} %get-tuple-element.44), channel_id=1, source_target_pairs={{0,12},{1,13},{2,14},{3,15},{4,8},{5,9},{6,10},{7,11}} | collective-permute-start | bytes 110600 | tf_op jit(solution)/shard_map/ppermute | solution.py:323
  30.2 6.0 %collective-permute-start.8 = (bf16[192,896]{1,0:T(8,128)(2,1)S(1)}, bf16[192,896]{1,0:T(8,128)(2,1)S(1)}, u32[]{:S(2)}, u32[]{:S(2)}) collective-permute-start(bf16[192,896]{1,0:T(8,128)(2,1)S(1)} %get-tuple-element.45), channel_id=1, source_target_pairs={{8,16},{9,17},{10,18},{11,19},{12,20},{13,21},{14,22},{15,23}} | collective-permute-start | bytes 1032200 | tf_op jit(solution)/shard_map/ppermute | solution.py:323
  31.5 3.3 %collective-permute-start.9 = (bf16[96,128]{1,0:T(8,128)(2,1)S(1)}, bf16[96,128]{1,0:T(8,128)(2,1)S(1)}, u32[]{:S(2)}, u32[]{:S(2)}) collective-permute-start(bf16[96,128]{1,0:T(8,128)(2,1)S(1)} %get-tuple-element.46), channel_id=1, source_target_pairs={{9,18},{10,17},{13,22},{14,21}} | collective-permute-start | bytes 73736 | tf_op jit(solution)/shard_map/ppermute | solution.py:323
  32.2 2.6 %collective-permute-start.10 = (bf16[96,128]{1,0:T(8,128)(2,1)S(1)}, bf16[96,128]{1,0:T(8,128)(2,1)S(1)}, u32[]{:S(2)}, u32[]{:S(2)}) collective-permute-start(bf16[96,128]{1,0:T(8,128)(2,1)S(1)} %get-tuple-element.47), channel_id=1, source_target_pairs={{8,17},{9,16},{10,19},{11,18},{12,21},{13,20},{14,23},{15,22}} | collective-permute-start | bytes 73736 | tf_op jit(solution)/shard_map/ppermute | solution.py:323
  33.5 2.7 %collective-permute-start.11 = (bf16[96,128]{1,0:T(8,128)(2,1)S(1)}, bf16[96,128]{1,0:T(8,128)(2,1)S(1)}, u32[]{:S(2)}, u32[]{:S(2)}) collective-permute-start(bf16[96,128]{1,0:T(8,128)(2,1)S(1)} %get-tuple-element.48), channel_id=1, source_target_pairs={{8,20},{9,21},{10,22},{11,23},{12,16},{13,17},{14,18},{15,19}} | collective-permute-start | bytes 73736 | tf_op jit(solution)/shard_map/ppermute | solution.py:323
  37.2 9.5 %collective-permute-start.12 = (bf16[192,896]{1,0:T(8,128)(2,1)S(1)}, bf16[192,896]{1,0:T(8,128)(2,1)S(1)}, u32[]{:S(2)}, u32[]{:S(2)}) collective-permute-start(bf16[192,896]{1,0:T(8,128)(2,1)S(1)} %get-tuple-element.51), channel_id=1, source_target_pairs={{0,8},{1,9},{2,10},{3,11},{4,12},{5,13},{6,14},{7,15},{8,16},{9,17... | collective-permute-start | bytes 1032200 | tf_op jit(solution)/shard_map/ppermute | solution.py:323
  42.5 2.0 %collective-permute-start.13 = (bf16[48,128]{1,0:T(8,128)(2,1)S(1)}, bf16[48,128]{1,0:T(8,128)(2,1)S(1)}, u32[]{:S(2)}, u32[]{:S(2)}) collective-permute-start(bf16[48,128]{1,0:T(8,128)(2,1)S(1)} %get-tuple-element.52), channel_id=1, source_target_pairs={{17,26},{18,25},{21,30},{22,29}} | collective-permute-start | bytes 36872 | tf_op jit(solution)/shard_map/ppermute | solution.py:323
  43.2 1.4 %collective-permute-start.14 = (bf16[48,128]{1,0:T(8,128)(2,1)S(1)}, bf16[48,128]{1,0:T(8,128)(2,1)S(1)}, u32[]{:S(2)}, u32[]{:S(2)}) collective-permute-start(bf16[48,128]{1,0:T(8,128)(2,1)S(1)} %get-tuple-element.53), channel_id=1, source_target_pairs={{16,25},{17,24},{18,27},{19,26},{20,29},{21,28},{22,31},{23,30}} | collective-permute-start | bytes 36872 | tf_op jit(solution)/shard_map/ppermute | solution.py:323
  43.8 0.7 %collective-permute-start.15 = (bf16[48,128]{1,0:T(8,128)(2,1)S(1)}, bf16[48,128]{1,0:T(8,128)(2,1)S(1)}, u32[]{:S(2)}, u32[]{:S(2)}) collective-permute-start(bf16[48,128]{1,0:T(8,128)(2,1)S(1)} %get-tuple-element.54), channel_id=1, source_target_pairs={{16,28},{17,29},{18,30},{19,31},{20,24},{21,25},{22,26},{23,27}} | collective-permute-start | bytes 36872 | tf_op jit(solution)/shard_map/ppermute | solution.py:323

commit v5 on v4

--- a/solution.py
+++ b/solution.py
@@ -79,46 +79,58 @@
     return round_number - lax.axis_index("depth") + lax.axis_size("depth") - 1
 
 
+def chosen_of(wanted, counts_in, round_number):
+    slots = wanted.shape[1]
+    shot = lax.broadcasted_iota(jnp.int32, (slots, slots), 0)
+    slot = lax.broadcasted_iota(jnp.int32, (1, slots), 1)
+    live = jnp.zeros((1, slots), jnp.int32)
+    for batch in range(slots // SHOT_BATCH):
+        count = counts_in[unit_of(round_number), 0, 0, batch]
+        live = jnp.where(slot // SHOT_BATCH == batch, count, live)
+    wanted = jnp.where(slot % SHOT_BATCH < live, wanted, -1)
+    return jnp.where(shot == wanted, 1.0, 0.0).astype(jnp.bfloat16)
+
+
 def opening_kernel(swaps, arrival, source, assignment, counts, first_map, band, *refs):
-    starts_out, live_out, edge_out, first_in, band_in = refs[:5]
-    messages = refs[5 : 5 + len(swaps)]
-    arrival_in, source_in, assignment_in, counts_in, sems = refs[5 + len(swaps) :]
+    first_out, later_out, live_out, edge_out, own_edge, first_in, band_in = refs[:7]
+    messages = refs[7 : 7 + len(swaps)]
+    arrival_in, source_in, assignment_in, counts_in, sems = refs[7 + len(swaps) :]
     rounds, slots, cells = source.shape
+    part = slots // 4
+    soon = first_out.shape[0]
+    upper = lax.axis_index("depth") == 0
     pairs = [(counts, counts_in), (assignment, assignment_in), (first_map, first_in)]
     pairs += [(arrival, arrival_in)]
-    pairs += [(source.at[r], source_in.at[r]) for r in range(rounds)]
-    pairs += [(band, band_in)]
+    pairs += [(source.at[r], source_in.at[r]) for r in range(soon)]
+    pairs += [(band, band_in), (source.at[pl.ds(soon, 2)], source_in.at[pl.ds(soon, 2)])]
     copies = [
         pltpu.make_async_copy(here, there, sems.at[i]) for i, (here, there) in enumerate(pairs)
     ]
-    for copy in copies:
+    for copy in copies[:-1]:
         copy.start()
+
+    @pl.when(jnp.logical_not(upper))
+    def _():
+        copies[-1].start()
+
     selector = edge_selector(cells)
-    shot = lax.broadcasted_iota(jnp.int32, (slots, slots), 0)
-    slot = lax.broadcasted_iota(jnp.int32, (1, slots), 1)
     position = lax.broadcasted_iota(jnp.int32, (SHOT_BATCH, LANES), 0)
     copies[0].wait()
-    copies[1].wait()
-    chosen = []
     for round_number in range(rounds):
-        unit = unit_of(round_number)
-        live = jnp.zeros((1, slots), jnp.int32)
         for batch in range(slots // SHOT_BATCH):
-            count = counts_in[unit, 0, 0, batch]
-            live = jnp.where(slot // SHOT_BATCH == batch, count, live)
+            count = counts_in[unit_of(round_number), 0, 0, batch]
             rows = slice(batch * SHOT_BATCH, (batch + 1) * SHOT_BATCH)
             live_out[round_number, rows] = jnp.where(position < count, 1.0, 0.0).astype(
                 jnp.bfloat16
             )
-        wanted = jnp.where(
-            slot % SHOT_BATCH < live, assignment_in[round_number : round_number + 1], -1
-        )
-        chosen.append(jnp.where(shot == wanted, 1.0, 0.0).astype(jnp.bfloat16))
+    copies[1].wait()
+    chosen = [chosen_of(assignment_in[r : r + 1], counts_in, r) for r in range(soon)]
     copies[2].wait()
     first_edge = dot(first_in[...], selector).astype(jnp.bfloat16)
     edge_out[:cells] = first_edge
+    own_edge[...] = first_edge
     copies[3].wait()
-    for round_number in range(rounds):
+    for round_number in range(soon):
         copies[4 + round_number].wait()
         picked = dot_t(chosen[round_number], source_in[round_number])
         if round_number == 0:
@@ -126,16 +138,24 @@
             live = jnp.concatenate([live] * (cells // LANES), axis=1)
             picked = picked + live * arrival_in[...].astype(jnp.float32)
         picked = picked.astype(jnp.bfloat16)
-        starts_out[round_number] = picked
+        first_out[round_number] = picked
         edges = dot(picked, first_edge)
         if round_number > 0:
             at = cells + (round_number - 1) * slots
             edge_out[at : at + slots] = edges.astype(jnp.bfloat16)
-            edges = jnp.where(lax.axis_index("depth") == 0, edges, 0.0)
-        at = round_number * (slots // 4)
         for message, swap in zip(messages, swaps):
-            message[at : at + slots // 4] = pack(edges, group_of(*swap))
-    copies[-1].wait()
+            message[round_number * part : (round_number + 1) * part] = pack(edges, group_of(*swap))
+    copies[4 + soon].wait()
+
+    @pl.when(jnp.logical_not(upper))
+    def _():
+        copies[-1].wait()
+        for at, round_number in enumerate(range(soon, rounds)):
+            chosen = chosen_of(assignment_in[round_number : round_number + 1], counts_in, round_number)
+            picked = dot_t(chosen, source_in[round_number]).astype(jnp.bfloat16)
+            later_out[at] = picked
+            row = cells + (round_number - 1) * slots
+            edge_out[row : row + slots] = dot(picked, own_edge[...]).astype(jnp.bfloat16)
 
 
 def bands(cells):
@@ -172,37 +192,65 @@
     whole_ext[:cells] = dot(coupled(first_map[...], band), second_map[...]).astype(jnp.bfloat16)
 
 
-def inside_kernel(early_layers, starts, first_map, band, second_map, *refs):
+def coupled_kernel(early_layers, first, first_map, band, edge_in, coupled_out, edge_out):
+    del edge_in, edge_out
+
+    @pl.when(lax.axis_index("depth") < early_layers)
+    def _():
+        cells = first_map.shape[0]
+        mapped = dot(first[...].reshape(-1, cells), first_map[...]).astype(jnp.bfloat16)
+        coupled_out[...] = coupled(mapped, band)
+
+
+def image_kernel(early_layers, inner, first_map, band, second_map, *refs):
     image_out, whole_ext, second_in, sem = refs
     cells = second_map.shape[0]
     early = lax.axis_index("depth") < early_layers
     copy = pltpu.make_async_copy(second_map, second_in, sem)
     copy.start()
+    selector = edge_selector(cells)
+    copy.wait()
 
     @pl.when(early)
     def _():
-        chains = image_out.shape[0] // starts.shape[1]
-        mapped = dot(starts[:chains].reshape(-1, cells), first_map[...]).astype(jnp.bfloat16)
-        image_out[...] = coupled(mapped, band).astype(jnp.float32)
-
-    copy.wait()
-
-    @pl.when(early)
-    def _():
-        image_out[...] = dot(image_out[...].astype(jnp.bfloat16), second_in[...])
+        image_out[...] = dot(inner[...], second_in[...])
 
     @pl.when(jnp.logical_not(early))
     def _():
         fill_whole_map(first_map, band, second_in, whole_ext)
 
-    edge_rows = dot_t(edge_selector(cells), second_in[...])
+    edge_rows = dot_t(selector, second_in[...])
     whole_ext[cells:] = (coupling_weight * edge_rows).astype(jnp.bfloat16)
 
 
-def whole_map_kernel(early_layers, first_map, band, second_map, whole_in, whole_ext):
-    del whole_in
-
-    @pl.when(lax.axis_index("depth") < early_layers)
+def late_kernel(early_layers, swaps, source, assignment, counts, *refs):
+    first_map, band, second_map, own_edge, _, _, whole_ext, later_out = refs[:8]
+    messages = refs[8 : 8 + len(swaps)]
+    source_in, assignment_in, counts_in, sems = refs[8 + len(swaps) :]
+    rounds, slots, cells = source.shape
+    part = slots // 4
+    layer = lax.axis_index("depth")
+    pairs = [(counts, counts_in), (assignment, assignment_in)]
+    pairs += [(source.at[pl.ds(rounds - 2, 2)], source_in)]
+    copies = [
+        pltpu.make_async_copy(here, there, sems.at[i]) for i, (here, there) in enumerate(pairs)
+    ]
+
+    @pl.when(layer == 0)
+    def _():
+        for copy in copies:
+            copy.start()
+        for copy in copies:
+            copy.wait()
+        for at, round_number in enumerate(range(rounds - 2, rounds)):
+            chosen = chosen_of(assignment_in[round_number : round_number + 1], counts_in, round_number)
+            picked = dot_t(chosen, source_in[at]).astype(jnp.bfloat16)
+            later_out[at] = picked
+            edges = dot(picked, own_edge[...])
+            for message, swap in zip(messages, swaps):
+                message[at * part : (at + 1) * part] = pack(edges, group_of(*swap))
+
+    @pl.when(layer < early_layers)
     def _():
         fill_whole_map(first_map, band, second_map, whole_ext)
 
@@ -222,22 +270,29 @@
     return (damp * image + (1.0 - damp) * start.astype(jnp.float32)).astype(jnp.bfloat16)
 
 
-def step_kernel(swaps, step, chains, *refs):
-    refs = list(refs)
-    starts, live, map_ext, damping, edge_next, traces = refs[:6]
-    received = refs[6 : 6 + len(swaps)]
-    others, outs = refs[6 + len(swaps) : -len(swaps) - 1], refs[-len(swaps) - 1 :]
-    if chains > 1:
-        others, outs = others[:-1], others[-1:] + outs
-    slots, cells = starts.shape[1:]
+def rounds_of(first, later, begin, end):
+    soon = first.shape[0]
+    found = [first[r] if r < soon else later[r - soon] for r in range(begin, end)]
+    return jnp.concatenate(found, axis=0)
+
+
+def step_kernel(swaps, step, chains, keeps, waiting, *refs):
+    first, later, live, map_ext, damping, edge_next, traces = refs[:7]
+    received = refs[7 : 7 + len(swaps)]
+    others = refs[7 + len(swaps) :]
+    messages, others = others[-len(swaps) :], others[: -len(swaps)]
+    kept_out = None
+    if keeps:
+        kept_out, others = others[-1], others[:-1]
+    traces_out, others = others[-1], others[:-1]
+    slots, cells = first.shape[1:]
     part = slots // 4
-    now = slice(step, step + chains)
     halo = [
         halo_of([[ref] for ref in received], swaps, [chain * part], part, live[step + chain])
         for chain in range(chains)
     ]
     halo = jnp.concatenate(halo, axis=0)
-    start = starts[now].reshape(-1, cells)
+    start = rounds_of(first, later, step, step + chains)
     if step == 0:
         image = traces[...] + dot(halo, map_ext[cells:])
     else:
@@ -245,42 +300,53 @@
         start = start.astype(jnp.bfloat16)
         image = dot(jnp.concatenate([start, halo], axis=1), map_ext[...])
     ended = blend(image, start, damping)
-    staying = (chains - 1) * slots
-    if chains > 1:
-        outs[0][...] = ended[:staying]
-    outs[-1][...] = ended[staying:]
-    for layer, other in enumerate(others):
-
-        @pl.when(lax.axis_index("depth") == layer)
-        def _():
-            outs[-1][...] = other[...]
-
+    going = (chains - 1 if keeps else chains) * slots
+    traces_out[...] = ended[:going]
+    if keeps:
+        kept_out[...] = ended[going:]
     at = cells + step * slots
     edges = dot(ended, edge_next[:cells])
     edges += edge_next[at : at + chains * slots].astype(jnp.float32)
-    messages = outs[len(outs) - 1 - len(swaps) : len(outs) - 1]
     for message, swap in zip(messages, swaps):
         for chain in range(chains):
             message[chain * part : (chain + 1) * part] = pack(
                 edges[chain * slots : (chain + 1) * slots], group_of(*swap)
             )
-
-
-def final_kernel(swaps, starts, live, map_ext, damping, traces, *refs):
-    rounds, slots, cells = starts.shape
+    layer = lax.axis_index("depth")
+    if waiting:
+
+        @pl.when(layer == 0)
+        def _():
+            for message, other in zip(messages, others):
+                message[...] = other[...]
+
+    else:
+        for at, other in enumerate(others):
+
+            @pl.when(layer == at + 1)
+            def _():
+                traces_out[...] = other[...]
+
+
+def final_kernel(swaps, picks, live, later, map_ext, damping, traces, *refs):
+    slots, cells = traces.shape
     received, (traces_out, row) = refs[:-2], refs[-2:]
     part = slots // 4
     layer = lax.axis_index("depth")
-    start = starts[rounds - 1].astype(jnp.float32) + traces[...].astype(jnp.float32)
+    start = later[later.shape[0] - 1].astype(jnp.float32) + traces[...].astype(jnp.float32)
     row[:, :cells] = start.astype(jnp.bfloat16)
-    for phase in range(rounds):
+
+    def take(phase):
         messages = received[phase * len(swaps) : (phase + 1) * len(swaps)]
-
-        @pl.when(layer >= phase if phase == rounds - 1 else layer == phase)
-        def _():
-            at = [messages[0].shape[0] - part]
-            row[:, cells:] = halo_of([[ref] for ref in messages], swaps, at, part, live[rounds - 1])
-
+        at = [messages[0].shape[0] - part]
+        mask = live[live.shape[0] - 1]
+        row[:, cells:] = halo_of([[ref] for ref in messages], swaps, at, part, mask)
+
+    by_rule = layer < 0
+    for at, phase in picks:
+        by_rule = by_rule | (layer == at)
+        pl.when(layer == at)(functools.partial(take, phase))
+    pl.when(jnp.logical_not(by_rule))(functools.partial(take, len(received) // len(swaps) - 1))
     image = dot(row[...], map_ext[...])
     traces_out[...] = blend(image, row[:, :cells], damping)
 
@@ -305,13 +371,13 @@
 MESH_AXES = ("depth", "gx", "gy")
 
 
-def send(x, layers, down, swap=None):
+def send(x, moves, swap=None):
     sizes = [lax.axis_size(axis) for axis in MESH_AXES]
     pairs = []
-    for layer in layers:
+    for layer, below in moves:
         for i in range(sizes[1]):
             for j in range(sizes[2]):
-                to = {"depth": layer + down, "gx": i, "gy": j}
+                to = {"depth": below, "gx": i, "gy": j}
                 if swap is not None:
                     axis, parity, _ = swap
                     to[axis] += 1 if to[axis] % 2 == parity else -1
@@ -335,74 +401,111 @@
     damping = damping[0, 0]
     swaps = exchanges()
     early_layers = layers - rounds + 1
+    soon = rounds - 2
 
     def array(*shape, kind=jnp.bfloat16):
         return jax.ShapeDtypeStruct(shape, kind)
 
+    def scratch(x):
+        return pltpu.VMEM(x.shape, x.dtype)
+
     part = slots // 4
     band = coupling_band(cells)
+    later = array(2, slots, cells)
+    whole = array(cells + LANES, cells)
+    counts_in = pltpu.SMEM(counts.shape, counts.dtype)
     opened = call(
         functools.partial(opening_kernel, swaps),
         [
-            array(rounds, slots, cells),
+            array(soon, slots, cells),
+            later,
             array(rounds, slots, LANES),
             array(cells + (rounds - 1) * slots, LANES),
+            array(cells, LANES),
             array(*first_map.shape),
             array(*band.shape),
         ]
-        + [array(rounds * part, LANES)] * len(swaps),
+        + [array(soon * part, LANES)] * len(swaps),
         [arrival, source, assignment, counts, first_map, band],
         in_hbm=range(6),
         scratch=[
-            pltpu.VMEM(arrival.shape, arrival.dtype),
-            pltpu.VMEM(source.shape, source.dtype),
-            pltpu.VMEM(assignment.shape, assignment.dtype),
-            pltpu.SMEM(counts.shape, counts.dtype),
-            pltpu.SemaphoreType.DMA((5 + rounds,)),
+            scratch(arrival),
+            scratch(source),
+            scratch(assignment),
+            counts_in,
+            pltpu.SemaphoreType.DMA((6 + soon,)),
         ],
     )
-    starts, live, edge, first_map, band = opened[:5]
-    received = [send(m, range(early_layers), 0, swap) for m, swap in zip(opened[5:], swaps)]
-    edge_next = send(edge, range(1, layers), -1)
-    image = array((rounds - 1) * slots, cells, kind=jnp.float32)
+    first, later, live, edge, own_edge, first_map, band = opened[:7]
+    received = [
+        send(m, [(layer, layer) for layer in range(early_layers)], swap)
+        for m, swap in zip(opened[7:], swaps)
+    ]
+    inner, edge = call(
+        functools.partial(coupled_kernel, early_layers),
+        [array(soon * slots, cells), array(*edge.shape)],
+        [first, first_map, band, edge],
+        aliases={3: 1},
+    )
+    edge_next = send(edge, [(layer, layer - 1) for layer in range(1, layers)])
     traces, map_ext, second_map = call(
-        functools.partial(inside_kernel, early_layers),
-        [image, array(cells + LANES, cells), array(*second_map.shape)],
-        [starts, first_map, band, second_map],
+        functools.partial(image_kernel, early_layers),
+        [array(soon * slots, cells, kind=jnp.float32), whole, array(*second_map.shape)],
+        [inner, first_map, band, second_map],
         in_hbm=(3,),
         scratch=[pltpu.SemaphoreType.DMA],
     )
-    arrived = list(received)
+    arrived = []
+    picks = []
     kept = []
     for step in range(rounds - 1):
-        chains = rounds - 1 - step
-        outs = [array((chains - 1) * slots, cells)] if chains > 1 else []
-        outs += [array(chains * part, LANES)] * len(swaps) + [array(slots, cells)]
-        operands = [starts, live, map_ext, damping, edge_next, traces] + received
+        chains = min(rounds - 1 - step, soon)
+        last = step == rounds - 2
+        before_last = step == rounds - 3
+        keeps = step + chains == rounds - 1 and not last
+        going = (chains - 1 if keeps else chains) * slots
+        outs = [array(going, cells)] + [array(slots, cells)] * keeps
+        outs += [array(chains * part, LANES)] * len(swaps)
+        operands = [first, later, live, map_ext, damping, edge_next, traces] + received
+        if last:
+            operands += kept
+        if before_last:
+            operands += waiting
         ended = call(
-            functools.partial(step_kernel, swaps, step, chains),
-            outs,
-            operands + (kept if chains == 1 else []),
+            functools.partial(step_kernel, swaps, step, chains, keeps, before_last), outs, operands
         )
-        below = range(step, step + early_layers)
-        if chains > 1:
-            traces = send(ended[0], below, 1)
-            kept.append(ended[-1])
-        else:
-            traces = send(ended[-1], range(layers - 1), 1)
-        received = [send(m, below, 1, swap) for m, swap in zip(ended[-1 - len(swaps) : -1], swaps)]
-        arrived += received
+        moves = [(layer, layer + 1) for layer in range(step, step + early_layers)]
+        traces = send(ended[0], [(layer, layer + 1) for layer in range(layers - 1)] if last else moves)
+        if keeps:
+            kept.append(ended[1])
+            picks.append((step + 1, len(arrived) // len(swaps)))
+        if before_last:
+            moves.append((0, 0))
+            picks.append((0, len(arrived) // len(swaps)))
+        if last:
+            moves.append((0, 1))
+        received = [send(m, moves, swap) for m, swap in zip(ended[-len(swaps) :], swaps)]
+        if step > 0:
+            arrived += received
         if step == 0:
-            (map_ext,) = call(
-                functools.partial(whole_map_kernel, early_layers),
-                [array(cells + LANES, cells)],
-                [first_map, band, second_map, map_ext],
-                aliases={3: 0},
+            late = call(
+                functools.partial(late_kernel, early_layers, swaps),
+                [whole, array(*later.shape)] + [array(2 * part, LANES)] * len(swaps),
+                [source, assignment, counts, first_map, band, second_map, own_edge, map_ext, later],
+                in_hbm=range(3),
+                scratch=[
+                    scratch(later),
+                    scratch(assignment),
+                    counts_in,
+                    pltpu.SemaphoreType.DMA((3,)),
+                ],
+                aliases={7: 0, 8: 1},
             )
+            map_ext, later, waiting = late[0], late[1], list(late[2:])
     (ended,) = call(
-        functools.partial(final_kernel, swaps),
+        functools.partial(final_kernel, swaps, picks),
         [array(slots, cells)],
-        [starts, live, map_ext, damping, traces] + arrived,
+        [live, later, map_ext, damping, traces] + arrived,
         scratch=[pltpu.VMEM((slots, cells + LANES), jnp.bfloat16)],
     )
     return ended.reshape(1, slots, 1, 1, cells)

time: 48.6 us -> 53.1 us (1.093)
  waiting for transfers between devices: 13.3 us -> 17.1 us
  starting transfers between devices: 20.3 us -> 21.9 us
  Pallas kernels: 14.2 us -> 13.5 us
    ppermute x16, waiting for transfers between devices: 13.3 us -> 17.1 us  [send(): return lax.ppermute(x, MESH_AXES, pairs)]
    ppermute x16, starting transfers between devices: 20.3 us -> 21.9 us  [send(): return lax.ppermute(x, MESH_AXES, pairs)]
    pallas_call x7 -> x8, Pallas kernels: 14.2 us -> 13.5 us  [call(): pl.pallas_call(kernel, out_shape=out_shape, in_specs=[pl.BlockSpec(memory...]
  transfers between devices with their start and end apart: 16 -> 16, of which waited for: 5 -> 6; matrix products, arithmetic and copies ran while one was open for 0% -> 0% of each run, Pallas kernels for 10% -> 9%
where the time goes in v5:
time: 53.1 us; the launch traced here: 52.7 us
  starting transfers between devices  21.9 us (41%)
  waiting for transfers between devices  17.1 us (32%)
  Pallas kernels  13.5 us (25%)
    ppermute x16, starting transfers between devices, send(): return lax.ppermute(x, MESH_AXES, pairs)  21.9 us
    ppermute x16, waiting for transfers between devices, send(): return lax.ppermute(x, MESH_AXES, pairs)  17.1 us
    pallas_call x8, Pallas kernels, call(): pl.pallas_call(kernel, out_shape=out_shape, in_specs=[pl.BlockSpec(memory...  13.5 us
  transfers between devices with their start and end apart: 16, of which 6 were waited for; matrix products, arithmetic and copies ran while one was open for 0% of the time, Pallas kernels for 9%

profile of v5, /device:TPU:1, one launch (start us, length us, event | category | flops | bytes accessed | tf_op | source)
XLA Modules:
  0.0 52.7 jit_solution(8711638056522214716)
XLA Ops:
  0.0 4.2 %shard_map.82 = (bf16[2,192,896]{2,1,0:T(8,128)(2,1)S(1)}, bf16[2,192,896]{2,1,0:T(8,128)(2,1)S(1)}, bf16[4,192,128]{2,1,0:T(8,128)(2,1)S(1)}, bf16[1472,128]{1,...) custom-call(bf16[192,896]{1,0:T(8,128)(2,1)} %bitcast.17, ...), custom_call_target="tpu_custom_call" | custom-call | tf_op jit(solution)/shard_map/pallas_call | solution.py:360
  4.3 2.6 %collective-permute-start = (bf16[1472,128]{1,0:T(8,128)(2,1)S(1)}, bf16[1472,128]{1,0:T(8,128)(2,1)S(1)}, u32[]{:S(2)}, u32[]{:S(2)}) collective-permute-start(bf16[1472,128]{1,0:T(8,128)(2,1)S(1)} %get-tuple-element.50), channel_id=1, source_target_pairs={{8,0},{9,1},{10,2},{11,3},{12,4},{13,5},{14,6},{15,7},{16,8},{17,9... | collective-permute-start | bytes 1130504 | tf_op jit(solution)/shard_map/ppermute | solution.py:389
  6.9 0.7 %collective-permute-start.1 = (bf16[96,128]{1,0:T(8,128)(2,1)S(1)}, bf16[96,128]{1,0:T(8,128)(2,1)S(1)}, u32[]{:S(2)}, u32[]{:S(2)}) collective-permute-start(bf16[96,128]{1,0:T(8,128)(2,1)S(1)} %get-tuple-element.52), channel_id=1, source_target_pairs={{1,2},{2,1},{5,6},{6,5}} | collective-permute-start | bytes 73736 | tf_op jit(solution)/shard_map/ppermute | solution.py:389
  7.6 0.7 %collective-permute-start.2 = (bf16[96,128]{1,0:T(8,128)(2,1)S(1)}, bf16[96,128]{1,0:T(8,128)(2,1)S(1)}, u32[]{:S(2)}, u32[]{:S(2)}) collective-permute-start(bf16[96,128]{1,0:T(8,128)(2,1)S(1)} %get-tuple-element.53), channel_id=1, source_target_pairs={{0,1},{1,0},{2,3},{3,2},{4,5},{5,4},{6,7},{7,6}} | collective-permute-start | bytes 73736 | tf_op jit(solution)/shard_map/ppermute | solution.py:389
  8.2 0.7 %collective-permute-start.3 = (bf16[96,128]{1,0:T(8,128)(2,1)S(1)}, bf16[96,128]{1,0:T(8,128)(2,1)S(1)}, u32[]{:S(2)}, u32[]{:S(2)}) collective-permute-start(bf16[96,128]{1,0:T(8,128)(2,1)S(1)} %get-tuple-element.54), channel_id=1, source_target_pairs={{0,4},{1,5},{2,6},{3,7},{4,0},{5,1},{6,2},{7,3}} | collective-permute-start | bytes 73736 | tf_op jit(solution)/shard_map/ppermute | solution.py:389
  8.9 0.0 copy-start
  8.9 4.7 %shard_map.84 = (f32[384,896]{1,0:T(8,128)S(1)}, bf16[1024,896]{1,0:T(8,128)(2,1)S(1)}, bf16[896,896]{1,0:T(8,128)(2,1)S(1)}) custom-call(bf16[384,896]{1,0:T(8,128)(2,1)S(1)} %get-tuple-element.43.inner, bf16[896,896]{1,0:T(8,128)(2,1)S(1)} %get-tuple-element.39.first_map.refs_0_, bf16[4,512,256]{2,1,0:T(8,128)(2,1)S(1)} %get-tuple-element.40.band.refs_1_, ...), custom_call_target="tpu_custom_call" | custom-call | tf_op jit(solution)/shard_map/pallas_call | solution.py:360
  13.7 0.0 collective-permute-done.2.refs_8_
  13.7 0.3 collective-permute-done.refs_5_
  14.1 0.7 %shard_map.86 = (bf16[384,896]{1,0:T(8,128)(2,1)S(1)}, bf16[96,128]{1,0:T(8,128)(2,1)S(1)}, bf16[96,128]{1,0:T(8,128)(2,1)S(1)}, bf16[96,128]{1,0:T(8,128)(2,1)S(1)}) custom-call(bf16[2,192,896]{2,1,0:T(8,128)(2,1)S(1)} %get-tuple-element.41.first.refs_0_, bf16[2,192,896]{2,1,0:T(8,128)(2,1)S(1)} %get-tuple-element.47.refs_5_.refs_1_, ...), custom_call_target="tpu_custom_call" | custom-call | tf_op jit(solution)/shard_map/pallas_call | solution.py:360
  14.8 1.3 %collective-permute-start.4 = (bf16[384,896]{1,0:T(8,128)(2,1)S(1)}, bf16[384,896]{1,0:T(8,128)(2,1)S(1)}, u32[]{:S(2)}, u32[]{:S(2)}) collective-permute-start(bf16[384,896]{1,0:T(8,128)(2,1)S(1)} %get-tuple-element.55), channel_id=1, source_target_pairs={{0,8},{1,9},{2,10},{3,11},{4,12},{5,13},{6,14},{7,15}} | collective-permute-start | bytes 2064392 | tf_op jit(solution)/shard_map/ppermute | solution.py:389
  16.1 0.7 %collective-permute-start.5 = (bf16[96,128]{1,0:T(8,128)(2,1)S(1)}, bf16[96,128]{1,0:T(8,128)(2,1)S(1)}, u32[]{:S(2)}, u32[]{:S(2)}) collective-permute-start(bf16[96,128]{1,0:T(8,128)(2,1)S(1)} %get-tuple-element.56), channel_id=1, source_target_pairs={{1,10},{2,9},{5,14},{6,13}} | collective-permute-start | bytes 73736 | tf_op jit(solution)/shard_map/ppermute | solution.py:389
  16.8 1.3 %collective-permute-start.6 = (bf16[96,128]{1,0:T(8,128)(2,1)S(1)}, bf16[96,128]{1,0:T(8,128)(2,1)S(1)}, u32[]{:S(2)}, u32[]{:S(2)}) collective-permute-start(bf16[96,128]{1,0:T(8,128)(2,1)S(1)} %get-tuple-element.57), channel_id=1, source_target_pairs={{0,9},{1,8},{2,11},{3,10},{4,13},{5,12},{6,15},{7,14}} | collective-permute-start | bytes 73736 | tf_op jit(solution)/shard_map/ppermute | solution.py:389
  18.1 1.3 %collective-permute-start.7 = (bf16[96,128]{1,0:T(8,128)(2,1)S(1)}, bf16[96,128]{1,0:T(8,128)(2,1)S(1)}, u32[]{:S(2)}, u32[]{:S(2)}) collective-permute-start(bf16[96,128]{1,0:T(8,128)(2,1)S(1)} %get-tuple-element.58), channel_id=1, source_target_pairs={{0,12},{1,13},{2,14},{3,15},{4,8},{5,9},{6,10},{7,11}} | collective-permute-start | bytes 73736 | tf_op jit(solution)/shard_map/ppermute | solution.py:389
  19.4 0.1 shard_map.85
  19.4 7.4 %collective-permute-done.6.refs_8_ = bf16[96,128]{1,0:T(8,128)(2,1)S(1)} collective-permute-done((bf16[96,128]{1,0:T(8,128)(2,1)S(1)}, bf16[96,128]{1,0:T(8,128)(2,1)S(1)}, u32[]{:S(2)}, u32[]{:S(2)}) %collective-permute-start.6) | collective-permute-done | bytes 24608 | tf_op jit(solution)/shard_map/ppermute | solution.py:389
  26.9 1.5 %collective-permute-done.7.refs_9_ = bf16[96,128]{1,0:T(8,128)(2,1)S(1)} collective-permute-done((bf16[96,128]{1,0:T(8,128)(2,1)S(1)}, bf16[96,128]{1,0:T(8,128)(2,1)S(1)}, u32[]{:S(2)}, u32[]{:S(2)}) %collective-permute-start.7) | collective-permute-done | bytes 24608 | tf_op jit(solution)/shard_map/ppermute | solution.py:389
  28.4 0.0 collective-permute-done.4.refs_6_
  28.4 1.3 %shard_map.87 = (bf16[192,896]{1,0:T(8,128)(2,1)S(1)}, bf16[192,896]{1,0:T(8,128)(2,1)S(1)}, bf16[96,128]{1,0:T(8,128)(2,1)S(1)}, bf16[96,128]{1,0:T(8,128)(2,1)S(1)}, bf16[96,128]{1,0:T(8,128)(2,1)S(1)}) custom-call(bf16[2,192,896]{2,1,0:T(8,128)(2,1)S(1)} %get-tuple-element.41.first.refs_0_, bf16[2,192,896]{2,1,0:T(8,128)(2,1)S(1)} %get-tuple-element.48.refs_1_.later, ...), custom_call_target="tpu_custom_call" | custom-call | tf_op jit(solution)/shard_map/pallas_call | solution.py:360
  29.7 1.3 %collective-permute-start.8 = (bf16[192,896]{1,0:T(8,128)(2,1)S(1)}, bf16[192,896]{1,0:T(8,128)(2,1)S(1)}, u32[]{:S(2)}, u32[]{:S(2)}) collective-permute-start(bf16[192,896]{1,0:T(8,128)(2,1)S(1)} %get-tuple-element.62), channel_id=1, source_target_pairs={{8,16},{9,17},{10,18},{11,19},{12,20},{13,21},{14,22},{15,23}} | collective-permute-start | bytes 1032200 | tf_op jit(solution)/shard_map/ppermute | solution.py:389
  31.1 0.7 %collective-permute-start.9 = (bf16[96,128]{1,0:T(8,128)(2,1)S(1)}, bf16[96,128]{1,0:T(8,128)(2,1)S(1)}, u32[]{:S(2)}, u32[]{:S(2)}) collective-permute-start(bf16[96,128]{1,0:T(8,128)(2,1)S(1)} %get-tuple-element.63), channel_id=1, source_target_pairs={{9,18},{10,17},{13,22},{14,21},{1,2},{2,1},{5,6},{6,5}} | collective-permute-start | bytes 73736 | tf_op jit(solution)/shard_map/ppermute | solution.py:389
  31.7 1.3 %collective-permute-start.10 = (bf16[96,128]{1,0:T(8,128)(2,1)S(1)}, bf16[96,128]{1,0:T(8,128)(2,1)S(1)}, u32[]{:S(2)}, u32[]{:S(2)}) collective-permute-start(bf16[96,128]{1,0:T(8,128)(2,1)S(1)} %get-tuple-element.64), channel_id=1, source_target_pairs={{8,17},{9,16},{10,19},{11,18},{12,21},{13,20},{14,23},{15,22},{0,1... | collective-permute-start | bytes 73736 | tf_op jit(solution)/shard_map/ppermute | solution.py:389
  33.0 1.3 %collective-permute-start.11 = (bf16[96,128]{1,0:T(8,128)(2,1)S(1)}, bf16[96,128]{1,0:T(8,128)(2,1)S(1)}, u32[]{:S(2)}, u32[]{:S(2)}) collective-permute-start(bf16[96,128]{1,0:T(8,128)(2,1)S(1)} %get-tuple-element.65), channel_id=1, source_target_pairs={{8,20},{9,21},{10,22},{11,23},{12,16},{13,17},{14,18},{15,19},{0,4... | collective-permute-start | bytes 73736 | tf_op jit(solution)/shard_map/ppermute | solution.py:389
  34.3 1.4 %collective-permute-done.11.refs_9_.refs_2_ = bf16[96,128]{1,0:T(8,128)(2,1)S(1)} collective-permute-done((bf16[96,128]{1,0:T(8,128)(2,1)S(1)}, bf16[96,128]{1,0:T(8,128)(2,1)S(1)}, u32[]{:S(2)}, u32[]{:S(2)}) %collective-permute-start.11) | collective-permute-done | bytes 24608 | tf_op jit(solution)/shard_map/ppermute | solution.py:389
  35.7 0.8 %shard_map.88 = (bf16[192,896]{1,0:T(8,128)(2,1)S(1)}, bf16[48,128]{1,0:T(8,128)(2,1)S(1)}, bf16[48,128]{1,0:T(8,128)(2,1)S(1)}, bf16[48,128]{1,0:T(8,128)(2,1)S(1)}) custom-call(bf16[2,192,896]{2,1,0:T(8,128)(2,1)S(1)} %get-tuple-element.41.first.refs_0_, bf16[2,192,896]{2,1,0:T(8,128)(2,1)S(1)} %get-tuple-element.48.refs_1_.later, ...), custom_call_target="tpu_custom_call" | custom-call | tf_op jit(solution)/shard_map/pallas_call | solution.py:360
  36.6 5.0 %collective-permute-start.12 = (bf16[192,896]{1,0:T(8,128)(2,1)S(1)}, bf16[192,896]{1,0:T(8,128)(2,1)S(1)}, u32[]{:S(2)}, u32[]{:S(2)}) collective-permute-start(bf16[192,896]{1,0:T(8,128)(2,1)S(1)} %get-tuple-element.67), channel_id=1, source_target_pairs={{0,8},{1,9},{2,10},{3,11},{4,12},{5,13},{6,14},{7,15},{8,16},{9,17... | collective-permute-start | bytes 1032200 | tf_op jit(solution)/shard_map/ppermute | solution.py:389
  41.5 0.7 %collective-permute-start.13 = (bf16[48,128]{1,0:T(8,128)(2,1)S(1)}, bf16[48,128]{1,0:T(8,128)(2,1)S(1)}, u32[]{:S(2)}, u32[]{:S(2)}) collective-permute-start(bf16[48,128]{1,0:T(8,128)(2,1)S(1)} %get-tuple-element.68), channel_id=1, source_target_pairs={{17,26},{18,25},{21,30},{22,29},{1,10},{2,9},{5,14},{6,13}} | collective-permute-start | bytes 36872 | tf_op jit(solution)/shard_map/ppermute | solution.py:389
  42.2 1.3 %collective-permute-start.14 = (bf16[48,128]{1,0:T(8,128)(2,1)S(1)}, bf16[48,128]{1,0:T(8,128)(2,1)S(1)}, u32[]{:S(2)}, u32[]{:S(2)}) collective-permute-start(bf16[48,128]{1,0:T(8,128)(2,1)S(1)} %get-tuple-element.69), channel_id=1, source_target_pairs={{16,25},{17,24},{18,27},{19,26},{20,29},{21,28},{22,31},{23,30},{0... | collective-permute-start | bytes 36872 | tf_op jit(solution)/shard_map/ppermute | solution.py:389
  43.5 1.3 %collective-permute-start.15 = (bf16[48,128]{1,0:T(8,128)(2,1)S(1)}, bf16[48,128]{1,0:T(8,128)(2,1)S(1)}, u32[]{:S(2)}, u32[]{:S(2)}) collective-permute-start(bf16[48,128]{1,0:T(8,128)(2,1)S(1)} %get-tuple-element.70), channel_id=1, source_target_pairs={{16,28},{17,29},{18,30},{19,31},{20,24},{21,25},{22,26},{23,27},{0... | collective-permute-start | bytes 36872 | tf_op jit(solution)/shard_map/ppermute | solution.py:389
  44.8 4.8 %collective-permute-done.14.refs_4_ = bf16[48,128]{1,0:T(8,128)(2,1)S(1)} collective-permute-done((bf16[48,128]{1,0:T(8,128)(2,1)S(1)}, bf16[48,128]{1,0:T(8,128)(2,1)S(1)}, u32[]{:S(2)}, u32[]{:S(2)}) %collective-permute-start.14) | collective-permute-done | bytes 12320 | tf_op jit(solution)/shard_map/ppermute | solution.py:389
  49.6 1.6 %collective-permute-done.15.refs_5_ = bf16[48,128]{1,0:T(8,128)(2,1)S(1)} collective-permute-done((bf16[48,128]{1,0:T(8,128)(2,1)S(1)}, bf16[48,128]{1,0:T(8,128)(2,1)S(1)}, u32[]{:S(2)}, u32[]{:S(2)}) %collective-permute-start.15) | collective-permute-done | bytes 12320 | tf_op jit(solution)/shard_map/ppermute | solution.py:389
  51.1 1.5 %shard_map.89 = bf16[192,896]{1,0:T(8,128)(2,1)} custom-call(bf16[4,192,128]{2,1,0:T(8,128)(2,1)S(1)} %get-tuple-element.38.refs_2_.live, bf16[2,192,896]{2,1,0:T(8,128)(2,1)S(1)} %get-tuple-element.48.refs_1_.later, bf16[1024,896]{1,0:T(8,128)(2,1)S(1)} %get-tuple-element.49.refs_3_.map_ext, f32[1,896]{1,0:T(1,128)S(1)} %bitcast.12, ...), custom_call_target="tpu_custom_call" | custom-call | tf_op jit(solution)/shard_map/pallas_call | solution.py:360
  (10 shorter events, 0.0 us)
Async XLA Ops:
  4.3 9.8 %collective-permute-start = (bf16[1472,128]{1,0:T(8,128)(2,1)S(1)}, bf16[1472,128]{1,0:T(8,128)(2,1)S(1)}, u32[]{:S(2)}, u32[]{:S(2)}) collective-permute-start(bf16[1472,128]{1,0:T(8,128)(2,1)S(1)} %get-tuple-element.50), channel_id=1, source_target_pairs={{8,0},{9,1},{10,2},{11,3},{12,4},{13,5},{14,6},{15,7},{16,8},{17,9... | collective-permute-start | bytes 1130504 | tf_op jit(solution)/shard_map/ppermute | solution.py:389
  6.9 6.8 %collective-permute-start.1 = (bf16[96,128]{1,0:T(8,128)(2,1)S(1)}, bf16[96,128]{1,0:T(8,128)(2,1)S(1)}, u32[]{:S(2)}, u32[]{:S(2)}) collective-permute-start(bf16[96,128]{1,0:T(8,128)(2,1)S(1)} %get-tuple-element.52), channel_id=1, source_target_pairs={{1,2},{2,1},{5,6},{6,5}} | collective-permute-start | bytes 73736 | tf_op jit(solution)/shard_map/ppermute | solution.py:389
  7.6 6.1 %collective-permute-start.2 = (bf16[96,128]{1,0:T(8,128)(2,1)S(1)}, bf16[96,128]{1,0:T(8,128)(2,1)S(1)}, u32[]{:S(2)}, u32[]{:S(2)}) collective-permute-start(bf16[96,128]{1,0:T(8,128)(2,1)S(1)} %get-tuple-element.53), channel_id=1, source_target_pairs={{0,1},{1,0},{2,3},{3,2},{4,5},{5,4},{6,7},{7,6}} | collective-permute-start | bytes 73736 | tf_op jit(solution)/shard_map/ppermute | solution.py:389
  8.2 5.5 %collective-permute-start.3 = (bf16[96,128]{1,0:T(8,128)(2,1)S(1)}, bf16[96,128]{1,0:T(8,128)(2,1)S(1)}, u32[]{:S(2)}, u32[]{:S(2)}) collective-permute-start(bf16[96,128]{1,0:T(8,128)(2,1)S(1)} %get-tuple-element.54), channel_id=1, source_target_pairs={{0,4},{1,5},{2,6},{3,7},{4,0},{5,1},{6,2},{7,3}} | collective-permute-start | bytes 73736 | tf_op jit(solution)/shard_map/ppermute | solution.py:389
  8.9 5.1 %copy-start = (f32[1,1,1,896]{3,2,1,0:T(1,128)S(1)}, f32[1,1,1,896]{3,2,1,0:T(1,128)}, u32[]{:S(2)}) copy-start(f32[1,1,1,896]{3,2,1,0:T(1,128)} %param.14) | copy-start | bytes 10756
  14.8 13.6 %collective-permute-start.4 = (bf16[384,896]{1,0:T(8,128)(2,1)S(1)}, bf16[384,896]{1,0:T(8,128)(2,1)S(1)}, u32[]{:S(2)}, u32[]{:S(2)}) collective-permute-start(bf16[384,896]{1,0:T(8,128)(2,1)S(1)} %get-tuple-element.55), channel_id=1, source_target_pairs={{0,8},{1,9},{2,10},{3,11},{4,12},{5,13},{6,14},{7,15}} | collective-permute-start | bytes 2064392 | tf_op jit(solution)/shard_map/ppermute | solution.py:389
  16.1 3.3 %collective-permute-start.5 = (bf16[96,128]{1,0:T(8,128)(2,1)S(1)}, bf16[96,128]{1,0:T(8,128)(2,1)S(1)}, u32[]{:S(2)}, u32[]{:S(2)}) collective-permute-start(bf16[96,128]{1,0:T(8,128)(2,1)S(1)} %get-tuple-element.56), channel_id=1, source_target_pairs={{1,10},{2,9},{5,14},{6,13}} | collective-permute-start | bytes 73736 | tf_op jit(solution)/shard_map/ppermute | solution.py:389
  16.8 10.1 %collective-permute-start.6 = (bf16[96,128]{1,0:T(8,128)(2,1)S(1)}, bf16[96,128]{1,0:T(8,128)(2,1)S(1)}, u32[]{:S(2)}, u32[]{:S(2)}) collective-permute-start(bf16[96,128]{1,0:T(8,128)(2,1)S(1)} %get-tuple-element.57), channel_id=1, source_target_pairs={{0,9},{1,8},{2,11},{3,10},{4,13},{5,12},{6,15},{7,14}} | collective-permute-start | bytes 73736 | tf_op jit(solution)/shard_map/ppermute | solution.py:389
  18.1 10.3 %collective-permute-start.7 = (bf16[96,128]{1,0:T(8,128)(2,1)S(1)}, bf16[96,128]{1,0:T(8,128)(2,1)S(1)}, u32[]{:S(2)}, u32[]{:S(2)}) collective-permute-start(bf16[96,128]{1,0:T(8,128)(2,1)S(1)} %get-tuple-element.58), channel_id=1, source_target_pairs={{0,12},{1,13},{2,14},{3,15},{4,8},{5,9},{6,10},{7,11}} | collective-permute-start | bytes 73736 | tf_op jit(solution)/shard_map/ppermute | solution.py:389
  29.7 6.0 %collective-permute-start.8 = (bf16[192,896]{1,0:T(8,128)(2,1)S(1)}, bf16[192,896]{1,0:T(8,128)(2,1)S(1)}, u32[]{:S(2)}, u32[]{:S(2)}) collective-permute-start(bf16[192,896]{1,0:T(8,128)(2,1)S(1)} %get-tuple-element.62), channel_id=1, source_target_pairs={{8,16},{9,17},{10,18},{11,19},{12,20},{13,21},{14,22},{15,23}} | collective-permute-start | bytes 1032200 | tf_op jit(solution)/shard_map/ppermute | solution.py:389
  31.1 3.3 %collective-permute-start.9 = (bf16[96,128]{1,0:T(8,128)(2,1)S(1)}, bf16[96,128]{1,0:T(8,128)(2,1)S(1)}, u32[]{:S(2)}, u32[]{:S(2)}) collective-permute-start(bf16[96,128]{1,0:T(8,128)(2,1)S(1)} %get-tuple-element.63), channel_id=1, source_target_pairs={{9,18},{10,17},{13,22},{14,21},{1,2},{2,1},{5,6},{6,5}} | collective-permute-start | bytes 73736 | tf_op jit(solution)/shard_map/ppermute | solution.py:389
  31.7 2.6 %collective-permute-start.10 = (bf16[96,128]{1,0:T(8,128)(2,1)S(1)}, bf16[96,128]{1,0:T(8,128)(2,1)S(1)}, u32[]{:S(2)}, u32[]{:S(2)}) collective-permute-start(bf16[96,128]{1,0:T(8,128)(2,1)S(1)} %get-tuple-element.64), channel_id=1, source_target_pairs={{8,17},{9,16},{10,19},{11,18},{12,21},{13,20},{14,23},{15,22},{0,1... | collective-permute-start | bytes 73736 | tf_op jit(solution)/shard_map/ppermute | solution.py:389
  33.0 2.7 %collective-permute-start.11 = (bf16[96,128]{1,0:T(8,128)(2,1)S(1)}, bf16[96,128]{1,0:T(8,128)(2,1)S(1)}, u32[]{:S(2)}, u32[]{:S(2)}) collective-permute-start(bf16[96,128]{1,0:T(8,128)(2,1)S(1)} %get-tuple-element.65), channel_id=1, source_target_pairs={{8,20},{9,21},{10,22},{11,23},{12,16},{13,17},{14,18},{15,19},{0,4... | collective-permute-start | bytes 73736 | tf_op jit(solution)/shard_map/ppermute | solution.py:389
  36.6 14.6 %collective-permute-start.12 = (bf16[192,896]{1,0:T(8,128)(2,1)S(1)}, bf16[192,896]{1,0:T(8,128)(2,1)S(1)}, u32[]{:S(2)}, u32[]{:S(2)}) collective-permute-start(bf16[192,896]{1,0:T(8,128)(2,1)S(1)} %get-tuple-element.67), channel_id=1, source_target_pairs={{0,8},{1,9},{2,10},{3,11},{4,12},{5,13},{6,14},{7,15},{8,16},{9,17... | collective-permute-start | bytes 1032200 | tf_op jit(solution)/shard_map/ppermute | solution.py:389
  41.5 3.3 %collective-permute-start.13 = (bf16[48,128]{1,0:T(8,128)(2,1)S(1)}, bf16[48,128]{1,0:T(8,128)(2,1)S(1)}, u32[]{:S(2)}, u32[]{:S(2)}) collective-permute-start(bf16[48,128]{1,0:T(8,128)(2,1)S(1)} %get-tuple-element.68), channel_id=1, source_target_pairs={{17,26},{18,25},{21,30},{22,29},{1,10},{2,9},{5,14},{6,13}} | collective-permute-start | bytes 36872 | tf_op jit(solution)/shard_map/ppermute | solution.py:389
  42.2 7.4 %collective-permute-start.14 = (bf16[48,128]{1,0:T(8,128)(2,1)S(1)}, bf16[48,128]{1,0:T(8,128)(2,1)S(1)}, u32[]{:S(2)}, u32[]{:S(2)}) collective-permute-start(bf16[48,128]{1,0:T(8,128)(2,1)S(1)} %get-tuple-element.69), channel_id=1, source_target_pairs={{16,25},{17,24},{18,27},{19,26},{20,29},{21,28},{22,31},{23,30},{0... | collective-permute-start | bytes 36872 | tf_op jit(solution)/shard_map/ppermute | solution.py:389
  43.5 7.6 %collective-permute-start.15 = (bf16[48,128]{1,0:T(8,128)(2,1)S(1)}, bf16[48,128]{1,0:T(8,128)(2,1)S(1)}, u32[]{:S(2)}, u32[]{:S(2)}) collective-permute-start(bf16[48,128]{1,0:T(8,128)(2,1)S(1)} %get-tuple-element.70), channel_id=1, source_target_pairs={{16,28},{17,29},{18,30},{19,31},{20,24},{21,25},{22,26},{23,27},{0... | collective-permute-start | bytes 36872 | tf_op jit(solution)/shard_map/ppermute | solution.py:389

commit v6 on v5

--- a/solution.py
+++ b/solution.py
@@ -30,6 +30,10 @@
 def edge_selector(cells):
     row = lax.broadcasted_iota(jnp.int32, (cells, LANES), 0)
     lane = lax.broadcasted_iota(jnp.int32, (cells, LANES), 1)
+    return select_edges(row, lane)
+
+
+def select_edges(row, lane):
     group = lane // GROUP
     spot = lane % GROUP
     along_x = group < 2
@@ -42,6 +46,12 @@
     return jnp.where((row == cell) & (spot < length), 1.0, 0.0).astype(jnp.bfloat16)
 
 
+def edge_rows_selector(cells):
+    lane = lax.broadcasted_iota(jnp.int32, (LANES, cells), 0)
+    row = lax.broadcasted_iota(jnp.int32, (LANES, cells), 1)
+    return select_edges(row, lane)
+
+
 def exchanges():
     found = []
     for axis, base in EDGE_AXES:
@@ -91,31 +101,18 @@
     return jnp.where(shot == wanted, 1.0, 0.0).astype(jnp.bfloat16)
 
 
-def opening_kernel(swaps, arrival, source, assignment, counts, first_map, band, *refs):
-    first_out, later_out, live_out, edge_out, own_edge, first_in, band_in = refs[:7]
-    messages = refs[7 : 7 + len(swaps)]
-    arrival_in, source_in, assignment_in, counts_in, sems = refs[7 + len(swaps) :]
-    rounds, slots, cells = source.shape
-    part = slots // 4
-    soon = first_out.shape[0]
-    upper = lax.axis_index("depth") == 0
-    pairs = [(counts, counts_in), (assignment, assignment_in), (first_map, first_in)]
-    pairs += [(arrival, arrival_in)]
-    pairs += [(source.at[r], source_in.at[r]) for r in range(soon)]
-    pairs += [(band, band_in), (source.at[pl.ds(soon, 2)], source_in.at[pl.ds(soon, 2)])]
+def started(pairs, sems):
     copies = [
         pltpu.make_async_copy(here, there, sems.at[i]) for i, (here, there) in enumerate(pairs)
     ]
-    for copy in copies[:-1]:
+    for copy in copies:
         copy.start()
-
-    @pl.when(jnp.logical_not(upper))
-    def _():
-        copies[-1].start()
-
-    selector = edge_selector(cells)
+    return copies
+
+
+def fill_live(live_out, counts_in):
     position = lax.broadcasted_iota(jnp.int32, (SHOT_BATCH, LANES), 0)
-    copies[0].wait()
+    rounds, slots = live_out.shape[:2]
     for round_number in range(rounds):
         for batch in range(slots // SHOT_BATCH):
             count = counts_in[unit_of(round_number), 0, 0, batch]
@@ -123,39 +120,86 @@
             live_out[round_number, rows] = jnp.where(position < count, 1.0, 0.0).astype(
                 jnp.bfloat16
             )
-    copies[1].wait()
-    chosen = [chosen_of(assignment_in[r : r + 1], counts_in, r) for r in range(soon)]
-    copies[2].wait()
-    first_edge = dot(first_in[...], selector).astype(jnp.bfloat16)
-    edge_out[:cells] = first_edge
-    own_edge[...] = first_edge
-    copies[3].wait()
-    for round_number in range(soon):
-        copies[4 + round_number].wait()
-        picked = dot_t(chosen[round_number], source_in[round_number])
-        if round_number == 0:
-            live = live_out[0].astype(jnp.float32)
-            live = jnp.concatenate([live] * (cells // LANES), axis=1)
-            picked = picked + live * arrival_in[...].astype(jnp.float32)
-        picked = picked.astype(jnp.bfloat16)
-        first_out[round_number] = picked
-        edges = dot(picked, first_edge)
-        if round_number > 0:
-            at = cells + (round_number - 1) * slots
-            edge_out[at : at + slots] = edges.astype(jnp.bfloat16)
-        for message, swap in zip(messages, swaps):
-            message[round_number * part : (round_number + 1) * part] = pack(edges, group_of(*swap))
-    copies[4 + soon].wait()
-
-    @pl.when(jnp.logical_not(upper))
-    def _():
+
+
+def edges_kernel(source, assignment, counts, first_map, band, second_map, *refs):
+    edge_out, first_out, later_out, live_out, first_in, band_in, second_in = refs[:7]
+    source_in, assignment_in, counts_in, sems = refs[7:]
+    rounds, slots, cells = source.shape
+    soon = first_out.shape[0]
+
+    @pl.when(lax.axis_index("depth") > 0)
+    def _():
+        pairs = [(counts, counts_in), (assignment, assignment_in), (first_map, first_in)]
+        pairs += [(source.at[r], source_in.at[r]) for r in range(1, rounds)]
+        pairs += [(band, band_in), (second_map, second_in)]
+        copies = started(pairs, sems)
+        selector = edge_selector(cells)
+        copies[0].wait()
+        fill_live(live_out, counts_in)
+        copies[1].wait()
+        copies[2].wait()
+        first_edge = dot(first_in[...], selector).astype(jnp.bfloat16)
+        edge_out[:cells] = first_edge
+        for r in range(1, rounds):
+            copies[2 + r].wait()
+            chosen = chosen_of(assignment_in[r : r + 1], counts_in, r)
+            picked = dot_t(chosen, source_in[r]).astype(jnp.bfloat16)
+            if r < soon:
+                first_out[r] = picked
+            else:
+                later_out[r - soon] = picked
+            at = cells + (r - 1) * slots
+            edge_out[at : at + slots] = dot(picked, first_edge).astype(jnp.bfloat16)
+        copies[-2].wait()
         copies[-1].wait()
-        for at, round_number in enumerate(range(soon, rounds)):
-            chosen = chosen_of(assignment_in[round_number : round_number + 1], counts_in, round_number)
-            picked = dot_t(chosen, source_in[round_number]).astype(jnp.bfloat16)
-            later_out[at] = picked
-            row = cells + (round_number - 1) * slots
-            edge_out[row : row + slots] = dot(picked, own_edge[...]).astype(jnp.bfloat16)
+
+
+def opening_kernel(early_layers, swaps, arrival, source, assignment, counts, *refs):
+    first_map, band, second_map = refs[:3]
+    first_out, live_out, first_in, band_in, second_in, own_edge, edge_cells = refs[8:15]
+    messages = refs[15 : 15 + len(swaps)]
+    arrival_in, source_in, assignment_in, counts_in, sems = refs[15 + len(swaps) :]
+    slots, cells = arrival.shape
+    part = slots // 4
+    soon = first_out.shape[0]
+    early = lax.axis_index("depth") < early_layers
+
+    @pl.when(jnp.logical_not(early))
+    def _():
+        edge_cells[...] = edge_rows_selector(cells)
+
+    @pl.when(early)
+    def _():
+        pairs = [(counts, counts_in), (assignment, assignment_in), (first_map, first_in)]
+        pairs += [(arrival, arrival_in)]
+        pairs += [(source.at[r], source_in.at[r]) for r in range(soon)]
+        pairs += [(band, band_in), (second_map, second_in)]
+        copies = started(pairs, sems)
+        edge_cells[...] = edge_rows_selector(cells)
+        selector = edge_selector(cells)
+        copies[0].wait()
+        fill_live(live_out, counts_in)
+        copies[1].wait()
+        chosen = [chosen_of(assignment_in[r : r + 1], counts_in, r) for r in range(soon)]
+        copies[2].wait()
+        first_edge = dot(first_in[...], selector).astype(jnp.bfloat16)
+        own_edge[...] = first_edge
+        copies[3].wait()
+        for r in range(soon):
+            copies[4 + r].wait()
+            picked = dot_t(chosen[r], source_in[r])
+            if r == 0:
+                live = live_out[0].astype(jnp.float32)
+                live = jnp.concatenate([live] * (cells // LANES), axis=1)
+                picked = picked + live * arrival_in[...].astype(jnp.float32)
+            picked = picked.astype(jnp.bfloat16)
+            first_out[r] = picked
+            edges = dot(picked, first_edge)
+            for message, swap in zip(messages, swaps):
+                message[r * part : (r + 1) * part] = pack(edges, group_of(*swap))
+        copies[-2].wait()
+        copies[-1].wait()
 
 
 def bands(cells):
@@ -192,65 +236,55 @@
     whole_ext[:cells] = dot(coupled(first_map[...], band), second_map[...]).astype(jnp.bfloat16)
 
 
-def coupled_kernel(early_layers, first, first_map, band, edge_in, coupled_out, edge_out):
-    del edge_in, edge_out
-
-    @pl.when(lax.axis_index("depth") < early_layers)
-    def _():
-        cells = first_map.shape[0]
-        mapped = dot(first[...].reshape(-1, cells), first_map[...]).astype(jnp.bfloat16)
-        coupled_out[...] = coupled(mapped, band)
-
-
-def image_kernel(early_layers, inner, first_map, band, second_map, *refs):
-    image_out, whole_ext, second_in, sem = refs
+def inside_kernel(early_layers, first, first_map, band, second_map, edge_cells, *refs):
+    image_out, whole_ext = refs
     cells = second_map.shape[0]
     early = lax.axis_index("depth") < early_layers
-    copy = pltpu.make_async_copy(second_map, second_in, sem)
-    copy.start()
-    selector = edge_selector(cells)
-    copy.wait()
 
     @pl.when(early)
     def _():
-        image_out[...] = dot(inner[...], second_in[...])
+        mapped = dot(first[...].reshape(-1, cells), first_map[...]).astype(jnp.bfloat16)
+        image_out[...] = dot(coupled(mapped, band), second_map[...])
 
     @pl.when(jnp.logical_not(early))
     def _():
-        fill_whole_map(first_map, band, second_in, whole_ext)
-
-    edge_rows = dot_t(selector, second_in[...])
+        fill_whole_map(first_map, band, second_map, whole_ext)
+
+    edge_rows = dot(edge_cells[...], second_map[...])
     whole_ext[cells:] = (coupling_weight * edge_rows).astype(jnp.bfloat16)
 
 
-def late_kernel(early_layers, swaps, source, assignment, counts, *refs):
+def waiting_kernel(early_layers, swaps, source, assignment, counts, *refs):
     first_map, band, second_map, own_edge, _, _, whole_ext, later_out = refs[:8]
     messages = refs[8 : 8 + len(swaps)]
     source_in, assignment_in, counts_in, sems = refs[8 + len(swaps) :]
-    rounds, slots, cells = source.shape
+    rounds, slots = source.shape[:2]
     part = slots // 4
     layer = lax.axis_index("depth")
-    pairs = [(counts, counts_in), (assignment, assignment_in)]
-    pairs += [(source.at[pl.ds(rounds - 2, 2)], source_in)]
-    copies = [
-        pltpu.make_async_copy(here, there, sems.at[i]) for i, (here, there) in enumerate(pairs)
-    ]
 
     @pl.when(layer == 0)
     def _():
-        for copy in copies:
-            copy.start()
-        for copy in copies:
+        pairs = [(counts, counts_in), (assignment, assignment_in)]
+        pairs += [(source.at[pl.ds(rounds - 2, 2)], source_in)]
+        for copy in started(pairs, sems):
             copy.wait()
-        for at, round_number in enumerate(range(rounds - 2, rounds)):
-            chosen = chosen_of(assignment_in[round_number : round_number + 1], counts_in, round_number)
+        for at, r in enumerate(range(rounds - 2, rounds)):
+            chosen = chosen_of(assignment_in[r : r + 1], counts_in, r)
             picked = dot_t(chosen, source_in[at]).astype(jnp.bfloat16)
             later_out[at] = picked
             edges = dot(picked, own_edge[...])
             for message, swap in zip(messages, swaps):
                 message[at * part : (at + 1) * part] = pack(edges, group_of(*swap))
 
-    @pl.when(layer < early_layers)
+    @pl.when((layer > 0) & (layer < early_layers))
+    def _():
+        fill_whole_map(first_map, band, second_map, whole_ext)
+
+
+def last_map_kernel(first_map, band, second_map, whole_in, whole_ext):
+    del whole_in
+
+    @pl.when(lax.axis_index("depth") == 0)
     def _():
         fill_whole_map(first_map, band, second_map, whole_ext)
 
@@ -276,7 +310,7 @@
     return jnp.concatenate(found, axis=0)
 
 
-def step_kernel(swaps, step, chains, keeps, waiting, *refs):
+def step_kernel(swaps, step, chains, keeps, waiting, early_layers, *refs):
     first, later, live, map_ext, damping, edge_next, traces = refs[:7]
     received = refs[7 : 7 + len(swaps)]
     others = refs[7 + len(swaps) :]
@@ -287,32 +321,39 @@
     traces_out, others = others[-1], others[:-1]
     slots, cells = first.shape[1:]
     part = slots // 4
-    halo = [
-        halo_of([[ref] for ref in received], swaps, [chain * part], part, live[step + chain])
-        for chain in range(chains)
-    ]
-    halo = jnp.concatenate(halo, axis=0)
-    start = rounds_of(first, later, step, step + chains)
-    if step == 0:
-        image = traces[...] + dot(halo, map_ext[cells:])
-    else:
-        start = start.astype(jnp.float32) + traces[...].astype(jnp.float32)
-        start = start.astype(jnp.bfloat16)
-        image = dot(jnp.concatenate([start, halo], axis=1), map_ext[...])
-    ended = blend(image, start, damping)
-    going = (chains - 1 if keeps else chains) * slots
-    traces_out[...] = ended[:going]
-    if keeps:
-        kept_out[...] = ended[going:]
-    at = cells + step * slots
-    edges = dot(ended, edge_next[:cells])
-    edges += edge_next[at : at + chains * slots].astype(jnp.float32)
-    for message, swap in zip(messages, swaps):
-        for chain in range(chains):
-            message[chain * part : (chain + 1) * part] = pack(
-                edges[chain * slots : (chain + 1) * slots], group_of(*swap)
-            )
     layer = lax.axis_index("depth")
+    here = (layer >= step) & (layer < step + early_layers)
+    if not keeps and step > 0:
+        here = here | (layer == 0)
+
+    @pl.when(here)
+    def _():
+        halo = [
+            halo_of([[ref] for ref in received], swaps, [chain * part], part, live[step + chain])
+            for chain in range(chains)
+        ]
+        halo = jnp.concatenate(halo, axis=0)
+        start = rounds_of(first, later, step, step + chains)
+        if step == 0:
+            image = traces[...] + dot(halo, map_ext[cells:])
+        else:
+            start = start.astype(jnp.float32) + traces[...].astype(jnp.float32)
+            start = start.astype(jnp.bfloat16)
+            image = dot(jnp.concatenate([start, halo], axis=1), map_ext[...])
+        ended = blend(image, start, damping)
+        going = (chains - 1 if keeps else chains) * slots
+        traces_out[...] = ended[:going]
+        if keeps:
+            kept_out[...] = ended[going:]
+        at = cells + step * slots
+        edges = dot(ended, edge_next[:cells])
+        edges += edge_next[at : at + chains * slots].astype(jnp.float32)
+        for message, swap in zip(messages, swaps):
+            for chain in range(chains):
+                message[chain * part : (chain + 1) * part] = pack(
+                    edges[chain * slots : (chain + 1) * slots], group_of(*swap)
+                )
+
     if waiting:
 
         @pl.when(layer == 0)
@@ -413,47 +454,37 @@
     band = coupling_band(cells)
     later = array(2, slots, cells)
     whole = array(cells + LANES, cells)
+    edge = array(cells + (rounds - 1) * slots, LANES)
     counts_in = pltpu.SMEM(counts.shape, counts.dtype)
+    maps = [first_map, band, second_map]
+    own = [array(soon, slots, cells), array(rounds, slots, LANES)]
+    own += [array(*x.shape) for x in maps]
+    copied = [scratch(source), scratch(assignment), counts_in]
+    edge, first, later, live, *maps_in = call(
+        edges_kernel,
+        [edge, own[0], later] + own[1:],
+        [source, assignment, counts] + maps,
+        in_hbm=range(6),
+        scratch=copied + [pltpu.SemaphoreType.DMA((4 + rounds,))],
+    )
+    edge_next = send(edge, [(layer, layer - 1) for layer in range(1, layers)])
     opened = call(
-        functools.partial(opening_kernel, swaps),
-        [
-            array(soon, slots, cells),
-            later,
-            array(rounds, slots, LANES),
-            array(cells + (rounds - 1) * slots, LANES),
-            array(cells, LANES),
-            array(*first_map.shape),
-            array(*band.shape),
-        ]
-        + [array(soon * part, LANES)] * len(swaps),
-        [arrival, source, assignment, counts, first_map, band],
-        in_hbm=range(6),
-        scratch=[
-            scratch(arrival),
-            scratch(source),
-            scratch(assignment),
-            counts_in,
-            pltpu.SemaphoreType.DMA((6 + soon,)),
-        ],
+        functools.partial(opening_kernel, early_layers, swaps),
+        own + [array(cells, LANES), array(LANES, cells)] + [array(soon * part, LANES)] * len(swaps),
+        [arrival, source, assignment, counts] + maps + [first, live] + maps_in,
+        in_hbm=range(7),
+        scratch=[scratch(arrival)] + copied + [pltpu.SemaphoreType.DMA((6 + soon,))],
+        aliases={7 + i: i for i in range(5)},
     )
-    first, later, live, edge, own_edge, first_map, band = opened[:7]
+    first, live, first_map, band, second_map, own_edge, edge_cells = opened[:7]
     received = [
         send(m, [(layer, layer) for layer in range(early_layers)], swap)
         for m, swap in zip(opened[7:], swaps)
     ]
-    inner, edge = call(
-        functools.partial(coupled_kernel, early_layers),
-        [array(soon * slots, cells), array(*edge.shape)],
-        [first, first_map, band, edge],
-        aliases={3: 1},
-    )
-    edge_next = send(edge, [(layer, layer - 1) for layer in range(1, layers)])
-    traces, map_ext, second_map = call(
-        functools.partial(image_kernel, early_layers),
-        [array(soon * slots, cells, kind=jnp.float32), whole, array(*second_map.shape)],
-        [inner, first_map, band, second_map],
-        in_hbm=(3,),
-        scratch=[pltpu.SemaphoreType.DMA],
+    traces, map_ext = call(
+        functools.partial(inside_kernel, early_layers),
+        [array(soon * slots, cells, kind=jnp.float32), whole],
+        [first, first_map, band, second_map, edge_cells],
     )
     arrived = []
     picks = []
@@ -472,7 +503,9 @@
         if before_last:
             operands += waiting
         ended = call(
-            functools.partial(step_kernel, swaps, step, chains, keeps, before_last), outs, operands
+            functools.partial(step_kernel, swaps, step, chains, keeps, before_last, early_layers),
+            outs,
+            operands,
         )
         moves = [(layer, layer + 1) for layer in range(step, step + early_layers)]
         traces = send(ended[0], [(layer, layer + 1) for layer in range(layers - 1)] if last else moves)
@@ -489,7 +522,7 @@
             arrived += received
         if step == 0:
             late = call(
-                functools.partial(late_kernel, early_layers, swaps),
+                functools.partial(waiting_kernel, early_layers, swaps),
                 [whole, array(*later.shape)] + [array(2 * part, LANES)] * len(swaps),
                 [source, assignment, counts, first_map, band, second_map, own_edge, map_ext, later],
                 in_hbm=range(3),
@@ -502,6 +535,13 @@
                 aliases={7: 0, 8: 1},
             )
             map_ext, later, waiting = late[0], late[1], list(late[2:])
+        if before_last:
+            (map_ext,) = call(
+                last_map_kernel,
+                [whole],
+                [first_map, band, second_map, map_ext],
+                aliases={3: 0},
+            )
     (ended,) = call(
         functools.partial(final_kernel, swaps, picks),
         [array(slots, cells)],

time: 53.1 us -> 49.7 us (0.936)
  Pallas kernels: 13.5 us -> 10.3 us
    pallas_call x8 -> x9, Pallas kernels: 13.5 us -> 10.3 us  [call(): pl.pallas_call(kernel, out_shape=out_shape, in_specs=[pl.BlockSpec(memory...]
  transfers between devices with their start and end apart: 16 -> 16, of which waited for: 6 -> 6; matrix products, arithmetic and copies ran while one was open for 0% -> 0% of each run, Pallas kernels for 9% -> 7%
where the time goes in v6:
time: 49.7 us; the launch traced here: 49.3 us
  starting transfers between devices  21.7 us (44%)
  waiting for transfers between devices  17 us (34%)
  Pallas kernels  10.3 us (21%)
    ppermute x16, starting transfers between devices, send(): return lax.ppermute(x, MESH_AXES, pairs)  21.7 us
    ppermute x16, waiting for transfers between devices, send(): return lax.ppermute(x, MESH_AXES, pairs)  17 us
    pallas_call x9, Pallas kernels, call(): pl.pallas_call(kernel, out_shape=out_shape, in_specs=[pl.BlockSpec(memory...  10.3 us
  transfers between devices with their start and end apart: 16, of which 6 were waited for; matrix products, arithmetic and copies ran while one was open for 0% of the time, Pallas kernels for 7%

profile of v6, /device:TPU:1, one launch (start us, length us, event | category | flops | bytes accessed | tf_op | source)
XLA Modules:
  0.0 49.3 jit_solution(6387502916097016223)
XLA Ops:
  0.0 3.9 %shard_map.82 = (bf16[1472,128]{1,0:T(8,128)(2,1)S(1)}, bf16[2,192,896]{2,1,0:T(8,128)(2,1)S(1)}, bf16[2,192,896]{2,1,0:T(8,128)(2,1)S(1)}, bf16[4,192,128]{2,1,...) custom-call(bf16[4,192,896]{2,1,0:T(8,128)(2,1)} %bitcast.13, ...), custom_call_target="tpu_custom_call" | custom-call | tf_op jit(solution)/shard_map/pallas_call | solution.py:401
  3.9 1.9 %collective-permute-start = (bf16[1472,128]{1,0:T(8,128)(2,1)S(1)}, bf16[1472,128]{1,0:T(8,128)(2,1)S(1)}, u32[]{:S(2)}, u32[]{:S(2)}) collective-permute-start(bf16[1472,128]{1,0:T(8,128)(2,1)S(1)} %get-tuple-element.58), channel_id=1, source_target_pairs={{8,0},{9,1},{10,2},{11,3},{12,4},{13,5},{14,6},{15,7},{16,8},{17,9... | collective-permute-start | bytes 1130504 | tf_op jit(solution)/shard_map/ppermute | solution.py:430
  5.8 0.1 shard_map.83
  6.0 0.7 %collective-permute-start.1 = (bf16[96,128]{1,0:T(8,128)(2,1)S(1)}, bf16[96,128]{1,0:T(8,128)(2,1)S(1)}, u32[]{:S(2)}, u32[]{:S(2)}) collective-permute-start(bf16[96,128]{1,0:T(8,128)(2,1)S(1)} %get-tuple-element.60), channel_id=1, source_target_pairs={{1,2},{2,1},{5,6},{6,5}} | collective-permute-start | bytes 73736 | tf_op jit(solution)/shard_map/ppermute | solution.py:430
  6.6 0.7 %collective-permute-start.2 = (bf16[96,128]{1,0:T(8,128)(2,1)S(1)}, bf16[96,128]{1,0:T(8,128)(2,1)S(1)}, u32[]{:S(2)}, u32[]{:S(2)}) collective-permute-start(bf16[96,128]{1,0:T(8,128)(2,1)S(1)} %get-tuple-element.61), channel_id=1, source_target_pairs={{0,1},{1,0},{2,3},{3,2},{4,5},{5,4},{6,7},{7,6}} | collective-permute-start | bytes 73736 | tf_op jit(solution)/shard_map/ppermute | solution.py:430
  7.3 0.7 %collective-permute-start.3 = (bf16[96,128]{1,0:T(8,128)(2,1)S(1)}, bf16[96,128]{1,0:T(8,128)(2,1)S(1)}, u32[]{:S(2)}, u32[]{:S(2)}) collective-permute-start(bf16[96,128]{1,0:T(8,128)(2,1)S(1)} %get-tuple-element.62), channel_id=1, source_target_pairs={{0,4},{1,5},{2,6},{3,7},{4,0},{5,1},{6,2},{7,3}} | collective-permute-start | bytes 73736 | tf_op jit(solution)/shard_map/ppermute | solution.py:430
  8.0 0.0 copy-start
  8.0 3.3 %shard_map.84 = (f32[384,896]{1,0:T(8,128)S(1)}, bf16[1024,896]{1,0:T(8,128)(2,1)S(1)}) custom-call(bf16[2,192,896]{2,1,0:T(8,128)(2,1)S(1)} %get-tuple-element.52.first.refs_0_, bf16[896,896]{1,0:T(8,128)(2,1)S(1)} %get-tuple-element.48.first_map.refs_0_, bf16[4,512,256]{2,1,0:T(8,128)(2,1)S(1)} %get-tuple-element.49.band.refs_1_, ...), custom_call_target="tpu_custom_call" | custom-call | tf_op jit(solution)/shard_map/pallas_call | solution.py:401
  11.3 0.0 collective-permute-done.1.refs_7_
  11.3 0.0 collective-permute-done.2.refs_8_
  11.3 2.3 %collective-permute-done.refs_5_ = bf16[1472,128]{1,0:T(8,128)(2,1)S(1)} collective-permute-done((bf16[1472,128]{1,0:T(8,128)(2,1)S(1)}, bf16[1472,128]{1,0:T(8,128)(2,1)S(1)}, u32[]{:S(2)}, u32[]{:S(2)}) %collective-permute-start) | collective-permute-done | bytes 376864 | tf_op jit(solution)/shard_map/ppermute | solution.py:430
  13.7 1.3 %collective-permute-start.4 = (bf16[384,896]{1,0:T(8,128)(2,1)S(1)}, bf16[384,896]{1,0:T(8,128)(2,1)S(1)}, u32[]{:S(2)}, u32[]{:S(2)}) collective-permute-start(bf16[384,896]{1,0:T(8,128)(2,1)S(1)} %get-tuple-element.63), channel_id=1, source_target_pairs={{0,8},{1,9},{2,10},{3,11},{4,12},{5,13},{6,14},{7,15}} | collective-permute-start | bytes 2064392 | tf_op jit(solution)/shard_map/ppermute | solution.py:430
  15.0 0.7 %collective-permute-start.5 = (bf16[96,128]{1,0:T(8,128)(2,1)S(1)}, bf16[96,128]{1,0:T(8,128)(2,1)S(1)}, u32[]{:S(2)}, u32[]{:S(2)}) collective-permute-start(bf16[96,128]{1,0:T(8,128)(2,1)S(1)} %get-tuple-element.64), channel_id=1, source_target_pairs={{1,10},{2,9},{5,14},{6,13}} | collective-permute-start | bytes 73736 | tf_op jit(solution)/shard_map/ppermute | solution.py:430
  15.6 1.3 %collective-permute-start.6 = (bf16[96,128]{1,0:T(8,128)(2,1)S(1)}, bf16[96,128]{1,0:T(8,128)(2,1)S(1)}, u32[]{:S(2)}, u32[]{:S(2)}) collective-permute-start(bf16[96,128]{1,0:T(8,128)(2,1)S(1)} %get-tuple-element.65), channel_id=1, source_target_pairs={{0,9},{1,8},{2,11},{3,10},{4,13},{5,12},{6,15},{7,14}} | collective-permute-start | bytes 73736 | tf_op jit(solution)/shard_map/ppermute | solution.py:430
  16.9 1.3 %collective-permute-start.7 = (bf16[96,128]{1,0:T(8,128)(2,1)S(1)}, bf16[96,128]{1,0:T(8,128)(2,1)S(1)}, u32[]{:S(2)}, u32[]{:S(2)}) collective-permute-start(bf16[96,128]{1,0:T(8,128)(2,1)S(1)} %get-tuple-element.66), channel_id=1, source_target_pairs={{0,12},{1,13},{2,14},{3,15},{4,8},{5,9},{6,10},{7,11}} | collective-permute-start | bytes 73736 | tf_op jit(solution)/shard_map/ppermute | solution.py:430
  18.2 0.1 shard_map.85
  18.3 0.0 collective-permute-done.5.refs_7_
  18.3 7.1 %collective-permute-done.6.refs_8_ = bf16[96,128]{1,0:T(8,128)(2,1)S(1)} collective-permute-done((bf16[96,128]{1,0:T(8,128)(2,1)S(1)}, bf16[96,128]{1,0:T(8,128)(2,1)S(1)}, u32[]{:S(2)}, u32[]{:S(2)}) %collective-permute-start.6) | collective-permute-done | bytes 24608 | tf_op jit(solution)/shard_map/ppermute | solution.py:430
  25.4 1.8 %collective-permute-done.7.refs_9_ = bf16[96,128]{1,0:T(8,128)(2,1)S(1)} collective-permute-done((bf16[96,128]{1,0:T(8,128)(2,1)S(1)}, bf16[96,128]{1,0:T(8,128)(2,1)S(1)}, u32[]{:S(2)}, u32[]{:S(2)}) %collective-permute-start.7) | collective-permute-done | bytes 24608 | tf_op jit(solution)/shard_map/ppermute | solution.py:430
  27.2 1.3 %shard_map.88 = (bf16[192,896]{1,0:T(8,128)(2,1)S(1)}, bf16[192,896]{1,0:T(8,128)(2,1)S(1)}, bf16[96,128]{1,0:T(8,128)(2,1)S(1)}, bf16[96,128]{1,0:T(8,128)(2,1)S(1)}, bf16[96,128]{1,0:T(8,128)(2,1)S(1)}) custom-call(bf16[2,192,896]{2,1,0:T(8,128)(2,1)S(1)} %get-tuple-element.52.first.refs_0_, bf16[2,192,896]{2,1,0:T(8,128)(2,1)S(1)} %get-tuple-element.56.refs_1_.later, ...), custom_call_target="tpu_custom_call" | custom-call | tf_op jit(solution)/shard_map/pallas_call | solution.py:401
  28.5 1.3 %collective-permute-start.8 = (bf16[192,896]{1,0:T(8,128)(2,1)S(1)}, bf16[192,896]{1,0:T(8,128)(2,1)S(1)}, u32[]{:S(2)}, u32[]{:S(2)}) collective-permute-start(bf16[192,896]{1,0:T(8,128)(2,1)S(1)} %get-tuple-element.70), channel_id=1, source_target_pairs={{8,16},{9,17},{10,18},{11,19},{12,20},{13,21},{14,22},{15,23}} | collective-permute-start | bytes 1032200 | tf_op jit(solution)/shard_map/ppermute | solution.py:430
  29.9 0.7 %collective-permute-start.9 = (bf16[96,128]{1,0:T(8,128)(2,1)S(1)}, bf16[96,128]{1,0:T(8,128)(2,1)S(1)}, u32[]{:S(2)}, u32[]{:S(2)}) collective-permute-start(bf16[96,128]{1,0:T(8,128)(2,1)S(1)} %get-tuple-element.71), channel_id=1, source_target_pairs={{9,18},{10,17},{13,22},{14,21},{1,2},{2,1},{5,6},{6,5}} | collective-permute-start | bytes 73736 | tf_op jit(solution)/shard_map/ppermute | solution.py:430
  30.5 1.3 %collective-permute-start.10 = (bf16[96,128]{1,0:T(8,128)(2,1)S(1)}, bf16[96,128]{1,0:T(8,128)(2,1)S(1)}, u32[]{:S(2)}, u32[]{:S(2)}) collective-permute-start(bf16[96,128]{1,0:T(8,128)(2,1)S(1)} %get-tuple-element.72), channel_id=1, source_target_pairs={{8,17},{9,16},{10,19},{11,18},{12,21},{13,20},{14,23},{15,22},{0,1... | collective-permute-start | bytes 73736 | tf_op jit(solution)/shard_map/ppermute | solution.py:430
  31.8 1.3 %collective-permute-start.11 = (bf16[96,128]{1,0:T(8,128)(2,1)S(1)}, bf16[96,128]{1,0:T(8,128)(2,1)S(1)}, u32[]{:S(2)}, u32[]{:S(2)}) collective-permute-start(bf16[96,128]{1,0:T(8,128)(2,1)S(1)} %get-tuple-element.73), channel_id=1, source_target_pairs={{8,20},{9,21},{10,22},{11,23},{12,16},{13,17},{14,18},{15,19},{0,4... | collective-permute-start | bytes 73736 | tf_op jit(solution)/shard_map/ppermute | solution.py:430
  33.2 1.4 %collective-permute-done.11.refs_9_.refs_2_ = bf16[96,128]{1,0:T(8,128)(2,1)S(1)} collective-permute-done((bf16[96,128]{1,0:T(8,128)(2,1)S(1)}, bf16[96,128]{1,0:T(8,128)(2,1)S(1)}, u32[]{:S(2)}, u32[]{:S(2)}) %collective-permute-start.11) | collective-permute-done | bytes 24608 | tf_op jit(solution)/shard_map/ppermute | solution.py:430
  34.6 5.5 %collective-permute-start.12 = (bf16[192,896]{1,0:T(8,128)(2,1)S(1)}, bf16[192,896]{1,0:T(8,128)(2,1)S(1)}, u32[]{:S(2)}, u32[]{:S(2)}) collective-permute-start(bf16[192,896]{1,0:T(8,128)(2,1)S(1)} %get-tuple-element.75), channel_id=1, source_target_pairs={{0,8},{1,9},{2,10},{3,11},{4,12},{5,13},{6,14},{7,15},{8,16},{9,17... | collective-permute-start | bytes 1032200 | tf_op jit(solution)/shard_map/ppermute | solution.py:430
  40.1 0.7 %collective-permute-start.13 = (bf16[48,128]{1,0:T(8,128)(2,1)S(1)}, bf16[48,128]{1,0:T(8,128)(2,1)S(1)}, u32[]{:S(2)}, u32[]{:S(2)}) collective-permute-start(bf16[48,128]{1,0:T(8,128)(2,1)S(1)} %get-tuple-element.76), channel_id=1, source_target_pairs={{17,26},{18,25},{21,30},{22,29},{1,10},{2,9},{5,14},{6,13}} | collective-permute-start | bytes 36872 | tf_op jit(solution)/shard_map/ppermute | solution.py:430
  40.8 1.3 %collective-permute-start.14 = (bf16[48,128]{1,0:T(8,128)(2,1)S(1)}, bf16[48,128]{1,0:T(8,128)(2,1)S(1)}, u32[]{:S(2)}, u32[]{:S(2)}) collective-permute-start(bf16[48,128]{1,0:T(8,128)(2,1)S(1)} %get-tuple-element.77), channel_id=1, source_target_pairs={{16,25},{17,24},{18,27},{19,26},{20,29},{21,28},{22,31},{23,30},{0... | collective-permute-start | bytes 36872 | tf_op jit(solution)/shard_map/ppermute | solution.py:430
  42.1 1.3 %collective-permute-start.15 = (bf16[48,128]{1,0:T(8,128)(2,1)S(1)}, bf16[48,128]{1,0:T(8,128)(2,1)S(1)}, u32[]{:S(2)}, u32[]{:S(2)}) collective-permute-start(bf16[48,128]{1,0:T(8,128)(2,1)S(1)} %get-tuple-element.78), channel_id=1, source_target_pairs={{16,28},{17,29},{18,30},{19,31},{20,24},{21,25},{22,26},{23,27},{0... | collective-permute-start | bytes 36872 | tf_op jit(solution)/shard_map/ppermute | solution.py:430
  43.4 2.4 %collective-permute-done.14.refs_4_ = bf16[48,128]{1,0:T(8,128)(2,1)S(1)} collective-permute-done((bf16[48,128]{1,0:T(8,128)(2,1)S(1)}, bf16[48,128]{1,0:T(8,128)(2,1)S(1)}, u32[]{:S(2)}, u32[]{:S(2)}) %collective-permute-start.14) | collective-permute-done | bytes 12320 | tf_op jit(solution)/shard_map/ppermute | solution.py:430
  45.8 2.0 %collective-permute-done.15.refs_5_ = bf16[48,128]{1,0:T(8,128)(2,1)S(1)} collective-permute-done((bf16[48,128]{1,0:T(8,128)(2,1)S(1)}, bf16[48,128]{1,0:T(8,128)(2,1)S(1)}, u32[]{:S(2)}, u32[]{:S(2)}) %collective-permute-start.15) | collective-permute-done | bytes 12320 | tf_op jit(solution)/shard_map/ppermute | solution.py:430
  47.7 1.6 %shard_map.90 = bf16[192,896]{1,0:T(8,128)(2,1)} custom-call(bf16[4,192,128]{2,1,0:T(8,128)(2,1)S(1)} %get-tuple-element.47.refs_2_.live, bf16[2,192,896]{2,1,0:T(8,128)(2,1)S(1)} %get-tuple-element.56.refs_1_.later, bf16[1024,896]{1,0:T(8,128)(2,1)S(1)} %shard_map.86.refs_3_.map_ext, f32[1,896]{1,0:T(1,128)S(1)} %bitcast.12, ...), custom_call_target="tpu_custom_call" | custom-call | tf_op jit(solution)/shard_map/pallas_call | solution.py:401
  (11 shorter events, 0.1 us)
Async XLA Ops:
  3.9 9.8 %collective-permute-start = (bf16[1472,128]{1,0:T(8,128)(2,1)S(1)}, bf16[1472,128]{1,0:T(8,128)(2,1)S(1)}, u32[]{:S(2)}, u32[]{:S(2)}) collective-permute-start(bf16[1472,128]{1,0:T(8,128)(2,1)S(1)} %get-tuple-element.58), channel_id=1, source_target_pairs={{8,0},{9,1},{10,2},{11,3},{12,4},{13,5},{14,6},{15,7},{16,8},{17,9... | collective-permute-start | bytes 1130504 | tf_op jit(solution)/shard_map/ppermute | solution.py:430
  6.0 5.3 %collective-permute-start.1 = (bf16[96,128]{1,0:T(8,128)(2,1)S(1)}, bf16[96,128]{1,0:T(8,128)(2,1)S(1)}, u32[]{:S(2)}, u32[]{:S(2)}) collective-permute-start(bf16[96,128]{1,0:T(8,128)(2,1)S(1)} %get-tuple-element.60), channel_id=1, source_target_pairs={{1,2},{2,1},{5,6},{6,5}} | collective-permute-start | bytes 73736 | tf_op jit(solution)/shard_map/ppermute | solution.py:430
  6.6 4.7 %collective-permute-start.2 = (bf16[96,128]{1,0:T(8,128)(2,1)S(1)}, bf16[96,128]{1,0:T(8,128)(2,1)S(1)}, u32[]{:S(2)}, u32[]{:S(2)}) collective-permute-start(bf16[96,128]{1,0:T(8,128)(2,1)S(1)} %get-tuple-element.61), channel_id=1, source_target_pairs={{0,1},{1,0},{2,3},{3,2},{4,5},{5,4},{6,7},{7,6}} | collective-permute-start | bytes 73736 | tf_op jit(solution)/shard_map/ppermute | solution.py:430
  7.3 4.0 %collective-permute-start.3 = (bf16[96,128]{1,0:T(8,128)(2,1)S(1)}, bf16[96,128]{1,0:T(8,128)(2,1)S(1)}, u32[]{:S(2)}, u32[]{:S(2)}) collective-permute-start(bf16[96,128]{1,0:T(8,128)(2,1)S(1)} %get-tuple-element.62), channel_id=1, source_target_pairs={{0,4},{1,5},{2,6},{3,7},{4,0},{5,1},{6,2},{7,3}} | collective-permute-start | bytes 73736 | tf_op jit(solution)/shard_map/ppermute | solution.py:430
  8.0 5.7 %copy-start = (f32[1,1,1,896]{3,2,1,0:T(1,128)S(1)}, f32[1,1,1,896]{3,2,1,0:T(1,128)}, u32[]{:S(2)}) copy-start(f32[1,1,1,896]{3,2,1,0:T(1,128)} %param.14) | copy-start | bytes 10756
  13.7 13.5 %collective-permute-start.4 = (bf16[384,896]{1,0:T(8,128)(2,1)S(1)}, bf16[384,896]{1,0:T(8,128)(2,1)S(1)}, u32[]{:S(2)}, u32[]{:S(2)}) collective-permute-start(bf16[384,896]{1,0:T(8,128)(2,1)S(1)} %get-tuple-element.63), channel_id=1, source_target_pairs={{0,8},{1,9},{2,10},{3,11},{4,12},{5,13},{6,14},{7,15}} | collective-permute-start | bytes 2064392 | tf_op jit(solution)/shard_map/ppermute | solution.py:430
  15.0 3.3 %collective-permute-start.5 = (bf16[96,128]{1,0:T(8,128)(2,1)S(1)}, bf16[96,128]{1,0:T(8,128)(2,1)S(1)}, u32[]{:S(2)}, u32[]{:S(2)}) collective-permute-start(bf16[96,128]{1,0:T(8,128)(2,1)S(1)} %get-tuple-element.64), channel_id=1, source_target_pairs={{1,10},{2,9},{5,14},{6,13}} | collective-permute-start | bytes 73736 | tf_op jit(solution)/shard_map/ppermute | solution.py:430
  15.6 9.8 %collective-permute-start.6 = (bf16[96,128]{1,0:T(8,128)(2,1)S(1)}, bf16[96,128]{1,0:T(8,128)(2,1)S(1)}, u32[]{:S(2)}, u32[]{:S(2)}) collective-permute-start(bf16[96,128]{1,0:T(8,128)(2,1)S(1)} %get-tuple-element.65), channel_id=1, source_target_pairs={{0,9},{1,8},{2,11},{3,10},{4,13},{5,12},{6,15},{7,14}} | collective-permute-start | bytes 73736 | tf_op jit(solution)/shard_map/ppermute | solution.py:430
  16.9 10.3 %collective-permute-start.7 = (bf16[96,128]{1,0:T(8,128)(2,1)S(1)}, bf16[96,128]{1,0:T(8,128)(2,1)S(1)}, u32[]{:S(2)}, u32[]{:S(2)}) collective-permute-start(bf16[96,128]{1,0:T(8,128)(2,1)S(1)} %get-tuple-element.66), channel_id=1, source_target_pairs={{0,12},{1,13},{2,14},{3,15},{4,8},{5,9},{6,10},{7,11}} | collective-permute-start | bytes 73736 | tf_op jit(solution)/shard_map/ppermute | solution.py:430
  28.5 6.0 %collective-permute-start.8 = (bf16[192,896]{1,0:T(8,128)(2,1)S(1)}, bf16[192,896]{1,0:T(8,128)(2,1)S(1)}, u32[]{:S(2)}, u32[]{:S(2)}) collective-permute-start(bf16[192,896]{1,0:T(8,128)(2,1)S(1)} %get-tuple-element.70), channel_id=1, source_target_pairs={{8,16},{9,17},{10,18},{11,19},{12,20},{13,21},{14,22},{15,23}} | collective-permute-start | bytes 1032200 | tf_op jit(solution)/shard_map/ppermute | solution.py:430
  29.9 3.3 %collective-permute-start.9 = (bf16[96,128]{1,0:T(8,128)(2,1)S(1)}, bf16[96,128]{1,0:T(8,128)(2,1)S(1)}, u32[]{:S(2)}, u32[]{:S(2)}) collective-permute-start(bf16[96,128]{1,0:T(8,128)(2,1)S(1)} %get-tuple-element.71), channel_id=1, source_target_pairs={{9,18},{10,17},{13,22},{14,21},{1,2},{2,1},{5,6},{6,5}} | collective-permute-start | bytes 73736 | tf_op jit(solution)/shard_map/ppermute | solution.py:430
  30.5 2.6 %collective-permute-start.10 = (bf16[96,128]{1,0:T(8,128)(2,1)S(1)}, bf16[96,128]{1,0:T(8,128)(2,1)S(1)}, u32[]{:S(2)}, u32[]{:S(2)}) collective-permute-start(bf16[96,128]{1,0:T(8,128)(2,1)S(1)} %get-tuple-element.72), channel_id=1, source_target_pairs={{8,17},{9,16},{10,19},{11,18},{12,21},{13,20},{14,23},{15,22},{0,1... | collective-permute-start | bytes 73736 | tf_op jit(solution)/shard_map/ppermute | solution.py:430
  31.8 2.7 %collective-permute-start.11 = (bf16[96,128]{1,0:T(8,128)(2,1)S(1)}, bf16[96,128]{1,0:T(8,128)(2,1)S(1)}, u32[]{:S(2)}, u32[]{:S(2)}) collective-permute-start(bf16[96,128]{1,0:T(8,128)(2,1)S(1)} %get-tuple-element.73), channel_id=1, source_target_pairs={{8,20},{9,21},{10,22},{11,23},{12,16},{13,17},{14,18},{15,19},{0,4... | collective-permute-start | bytes 73736 | tf_op jit(solution)/shard_map/ppermute | solution.py:430
  34.6 13.2 %collective-permute-start.12 = (bf16[192,896]{1,0:T(8,128)(2,1)S(1)}, bf16[192,896]{1,0:T(8,128)(2,1)S(1)}, u32[]{:S(2)}, u32[]{:S(2)}) collective-permute-start(bf16[192,896]{1,0:T(8,128)(2,1)S(1)} %get-tuple-element.75), channel_id=1, source_target_pairs={{0,8},{1,9},{2,10},{3,11},{4,12},{5,13},{6,14},{7,15},{8,16},{9,17... | collective-permute-start | bytes 1032200 | tf_op jit(solution)/shard_map/ppermute | solution.py:430
  40.1 3.3 %collective-permute-start.13 = (bf16[48,128]{1,0:T(8,128)(2,1)S(1)}, bf16[48,128]{1,0:T(8,128)(2,1)S(1)}, u32[]{:S(2)}, u32[]{:S(2)}) collective-permute-start(bf16[48,128]{1,0:T(8,128)(2,1)S(1)} %get-tuple-element.76), channel_id=1, source_target_pairs={{17,26},{18,25},{21,30},{22,29},{1,10},{2,9},{5,14},{6,13}} | collective-permute-start | bytes 36872 | tf_op jit(solution)/shard_map/ppermute | solution.py:430
  40.8 5.0 %collective-permute-start.14 = (bf16[48,128]{1,0:T(8,128)(2,1)S(1)}, bf16[48,128]{1,0:T(8,128)(2,1)S(1)}, u32[]{:S(2)}, u32[]{:S(2)}) collective-permute-start(bf16[48,128]{1,0:T(8,128)(2,1)S(1)} %get-tuple-element.77), channel_id=1, source_target_pairs={{16,25},{17,24},{18,27},{19,26},{20,29},{21,28},{22,31},{23,30},{0... | collective-permute-start | bytes 36872 | tf_op jit(solution)/shard_map/ppermute | solution.py:430
  42.1 5.7 %collective-permute-start.15 = (bf16[48,128]{1,0:T(8,128)(2,1)S(1)}, bf16[48,128]{1,0:T(8,128)(2,1)S(1)}, u32[]{:S(2)}, u32[]{:S(2)}) collective-permute-start(bf16[48,128]{1,0:T(8,128)(2,1)S(1)} %get-tuple-element.78), channel_id=1, source_target_pairs={{16,28},{17,29},{18,30},{19,31},{20,24},{21,25},{22,26},{23,27},{0... | collective-permute-start | bytes 36872 | tf_op jit(solution)/shard_map/ppermute | solution.py:430

commit v7 on v6

--- a/solution.py
+++ b/solution.py
@@ -361,20 +361,15 @@
             for message, other in zip(messages, others):
                 message[...] = other[...]
 
-    else:
-        for at, other in enumerate(others):
-
-            @pl.when(layer == at + 1)
-            def _():
-                traces_out[...] = other[...]
-
-
-def final_kernel(swaps, picks, live, later, map_ext, damping, traces, *refs):
+
+def final_kernel(swaps, picks, others, live, later, map_ext, damping, traces, *refs):
     slots, cells = traces.shape
-    received, (traces_out, row) = refs[:-2], refs[-2:]
+    kept, received, (traces_out, row) = refs[:others], refs[others:-2], refs[-2:]
     part = slots // 4
     layer = lax.axis_index("depth")
     start = later[later.shape[0] - 1].astype(jnp.float32) + traces[...].astype(jnp.float32)
+    for other in kept:
+        start = start + other[...].astype(jnp.float32)
     row[:, :cells] = start.astype(jnp.bfloat16)
 
     def take(phase):
@@ -498,8 +493,6 @@
         outs = [array(going, cells)] + [array(slots, cells)] * keeps
         outs += [array(chains * part, LANES)] * len(swaps)
         operands = [first, later, live, map_ext, damping, edge_next, traces] + received
-        if last:
-            operands += kept
         if before_last:
             operands += waiting
         ended = call(
@@ -508,9 +501,9 @@
             operands,
         )
         moves = [(layer, layer + 1) for layer in range(step, step + early_layers)]
-        traces = send(ended[0], [(layer, layer + 1) for layer in range(layers - 1)] if last else moves)
+        traces = send(ended[0], moves + [(0, 1)] if last else moves)
         if keeps:
-            kept.append(ended[1])
+            kept.append(send(ended[1], [(step, step + 1)]))
             picks.append((step + 1, len(arrived) // len(swaps)))
         if before_last:
             moves.append((0, 0))
@@ -543,9 +536,9 @@
                 aliases={3: 0},
             )
     (ended,) = call(
-        functools.partial(final_kernel, swaps, picks),
+        functools.partial(final_kernel, swaps, picks, len(kept)),
         [array(slots, cells)],
-        [live, later, map_ext, damping, traces] + arrived,
+        [live, later, map_ext, damping, traces] + kept + arrived,
         scratch=[pltpu.VMEM((slots, cells + LANES), jnp.bfloat16)],
     )
     return ended.reshape(1, slots, 1, 1, cells)

time: 49.7 us -> 48.7 us (0.980)
  starting transfers between devices: 21.7 us -> 18.8 us
  waiting for transfers between devices: 17 us -> 18.8 us
    ppermute x16 -> x17, starting transfers between devices: 21.7 us -> 18.8 us  [send(): return lax.ppermute(x, MESH_AXES, pairs)]
    ppermute x16 -> x17, waiting for transfers between devices: 17 us -> 18.8 us  [send(): return lax.ppermute(x, MESH_AXES, pairs)]
  transfers between devices with their start and end apart: 16 -> 17, of which waited for: 6 -> 5; matrix products, arithmetic and copies ran while one was open for 0% -> 0% of each run, Pallas kernels for 7% -> 7%
where the time goes in v7:
time: 48.7 us; the launch traced here: 48.3 us
  starting transfers between devices  18.8 us (39%)
  waiting for transfers between devices  18.8 us (39%)
  Pallas kernels  10.3 us (21%)
    ppermute x17, waiting for transfers between devices, send(): return lax.ppermute(x, MESH_AXES, pairs)  18.8 us
    ppermute x17, starting transfers between devices, send(): return lax.ppermute(x, MESH_AXES, pairs)  18.8 us
    pallas_call x9, Pallas kernels, call(): pl.pallas_call(kernel, out_shape=out_shape, in_specs=[pl.BlockSpec(memory...  10.3 us
  transfers between devices with their start and end apart: 17, of which 5 were waited for; matrix products, arithmetic and copies ran while one was open for 0% of the time, Pallas kernels for 7%

profile of v7, /device:TPU:1, one launch (start us, length us, event | category | flops | bytes accessed | tf_op | source)
XLA Modules:
  0.0 48.3 jit_solution(7772628708819219962)
XLA Ops:
  0.0 3.9 %shard_map.82 = (bf16[1472,128]{1,0:T(8,128)(2,1)S(1)}, bf16[2,192,896]{2,1,0:T(8,128)(2,1)S(1)}, bf16[2,192,896]{2,1,0:T(8,128)(2,1)S(1)}, bf16[4,192,128]{2,1,...) custom-call(bf16[4,192,896]{2,1,0:T(8,128)(2,1)} %bitcast.13, ...), custom_call_target="tpu_custom_call" | custom-call | tf_op jit(solution)/shard_map/pallas_call | solution.py:396
  3.9 1.9 %collective-permute-start = (bf16[1472,128]{1,0:T(8,128)(2,1)S(1)}, bf16[1472,128]{1,0:T(8,128)(2,1)S(1)}, u32[]{:S(2)}, u32[]{:S(2)}) collective-permute-start(bf16[1472,128]{1,0:T(8,128)(2,1)S(1)} %get-tuple-element.58), channel_id=1, source_target_pairs={{8,0},{9,1},{10,2},{11,3},{12,4},{13,5},{14,6},{15,7},{16,8},{17,9... | collective-permute-start | bytes 1130504 | tf_op jit(solution)/shard_map/ppermute | solution.py:425
  5.8 0.1 shard_map.83
  6.0 0.7 %collective-permute-start.1 = (bf16[96,128]{1,0:T(8,128)(2,1)S(1)}, bf16[96,128]{1,0:T(8,128)(2,1)S(1)}, u32[]{:S(2)}, u32[]{:S(2)}) collective-permute-start(bf16[96,128]{1,0:T(8,128)(2,1)S(1)} %get-tuple-element.60), channel_id=1, source_target_pairs={{1,2},{2,1},{5,6},{6,5}} | collective-permute-start | bytes 73736 | tf_op jit(solution)/shard_map/ppermute | solution.py:425
  6.6 0.7 %collective-permute-start.2 = (bf16[96,128]{1,0:T(8,128)(2,1)S(1)}, bf16[96,128]{1,0:T(8,128)(2,1)S(1)}, u32[]{:S(2)}, u32[]{:S(2)}) collective-permute-start(bf16[96,128]{1,0:T(8,128)(2,1)S(1)} %get-tuple-element.61), channel_id=1, source_target_pairs={{0,1},{1,0},{2,3},{3,2},{4,5},{5,4},{6,7},{7,6}} | collective-permute-start | bytes 73736 | tf_op jit(solution)/shard_map/ppermute | solution.py:425
  7.3 0.7 %collective-permute-start.3 = (bf16[96,128]{1,0:T(8,128)(2,1)S(1)}, bf16[96,128]{1,0:T(8,128)(2,1)S(1)}, u32[]{:S(2)}, u32[]{:S(2)}) collective-permute-start(bf16[96,128]{1,0:T(8,128)(2,1)S(1)} %get-tuple-element.62), channel_id=1, source_target_pairs={{0,4},{1,5},{2,6},{3,7},{4,0},{5,1},{6,2},{7,3}} | collective-permute-start | bytes 73736 | tf_op jit(solution)/shard_map/ppermute | solution.py:425
  8.0 0.0 copy-start
  8.0 3.3 %shard_map.84 = (f32[384,896]{1,0:T(8,128)S(1)}, bf16[1024,896]{1,0:T(8,128)(2,1)S(1)}) custom-call(bf16[2,192,896]{2,1,0:T(8,128)(2,1)S(1)} %get-tuple-element.52.first.refs_0_, bf16[896,896]{1,0:T(8,128)(2,1)S(1)} %get-tuple-element.48.first_map.refs_0_, bf16[4,512,256]{2,1,0:T(8,128)(2,1)S(1)} %get-tuple-element.49.band.refs_1_, ...), custom_call_target="tpu_custom_call" | custom-call | tf_op jit(solution)/shard_map/pallas_call | solution.py:396
  11.3 0.0 collective-permute-done.1.refs_7_
  11.3 0.0 collective-permute-done.3.refs_9_
  11.3 2.4 %collective-permute-done.refs_5_ = bf16[1472,128]{1,0:T(8,128)(2,1)S(1)} collective-permute-done((bf16[1472,128]{1,0:T(8,128)(2,1)S(1)}, bf16[1472,128]{1,0:T(8,128)(2,1)S(1)}, u32[]{:S(2)}, u32[]{:S(2)}) %collective-permute-start) | collective-permute-done | bytes 376864 | tf_op jit(solution)/shard_map/ppermute | solution.py:425
  13.7 1.3 %collective-permute-start.4 = (bf16[384,896]{1,0:T(8,128)(2,1)S(1)}, bf16[384,896]{1,0:T(8,128)(2,1)S(1)}, u32[]{:S(2)}, u32[]{:S(2)}) collective-permute-start(bf16[384,896]{1,0:T(8,128)(2,1)S(1)} %get-tuple-element.63), channel_id=1, source_target_pairs={{0,8},{1,9},{2,10},{3,11},{4,12},{5,13},{6,14},{7,15}} | collective-permute-start | bytes 2064392 | tf_op jit(solution)/shard_map/ppermute | solution.py:425
  15.0 0.7 %collective-permute-start.5 = (bf16[96,128]{1,0:T(8,128)(2,1)S(1)}, bf16[96,128]{1,0:T(8,128)(2,1)S(1)}, u32[]{:S(2)}, u32[]{:S(2)}) collective-permute-start(bf16[96,128]{1,0:T(8,128)(2,1)S(1)} %get-tuple-element.64), channel_id=1, source_target_pairs={{1,10},{2,9},{5,14},{6,13}} | collective-permute-start | bytes 73736 | tf_op jit(solution)/shard_map/ppermute | solution.py:425
  15.6 1.3 %collective-permute-start.6 = (bf16[96,128]{1,0:T(8,128)(2,1)S(1)}, bf16[96,128]{1,0:T(8,128)(2,1)S(1)}, u32[]{:S(2)}, u32[]{:S(2)}) collective-permute-start(bf16[96,128]{1,0:T(8,128)(2,1)S(1)} %get-tuple-element.65), channel_id=1, source_target_pairs={{0,9},{1,8},{2,11},{3,10},{4,13},{5,12},{6,15},{7,14}} | collective-permute-start | bytes 73736 | tf_op jit(solution)/shard_map/ppermute | solution.py:425
  16.9 1.3 %collective-permute-start.7 = (bf16[96,128]{1,0:T(8,128)(2,1)S(1)}, bf16[96,128]{1,0:T(8,128)(2,1)S(1)}, u32[]{:S(2)}, u32[]{:S(2)}) collective-permute-start(bf16[96,128]{1,0:T(8,128)(2,1)S(1)} %get-tuple-element.66), channel_id=1, source_target_pairs={{0,12},{1,13},{2,14},{3,15},{4,8},{5,9},{6,10},{7,11}} | collective-permute-start | bytes 73736 | tf_op jit(solution)/shard_map/ppermute | solution.py:425
  18.2 0.1 shard_map.85
  18.3 7.1 %collective-permute-done.6.refs_8_ = bf16[96,128]{1,0:T(8,128)(2,1)S(1)} collective-permute-done((bf16[96,128]{1,0:T(8,128)(2,1)S(1)}, bf16[96,128]{1,0:T(8,128)(2,1)S(1)}, u32[]{:S(2)}, u32[]{:S(2)}) %collective-permute-start.6) | collective-permute-done | bytes 24608 | tf_op jit(solution)/shard_map/ppermute | solution.py:425
  25.4 1.8 %collective-permute-done.7.refs_9_ = bf16[96,128]{1,0:T(8,128)(2,1)S(1)} collective-permute-done((bf16[96,128]{1,0:T(8,128)(2,1)S(1)}, bf16[96,128]{1,0:T(8,128)(2,1)S(1)}, u32[]{:S(2)}, u32[]{:S(2)}) %collective-permute-start.7) | collective-permute-done | bytes 24608 | tf_op jit(solution)/shard_map/ppermute | solution.py:425
  27.2 1.3 %shard_map.88 = (bf16[192,896]{1,0:T(8,128)(2,1)S(1)}, bf16[192,896]{1,0:T(8,128)(2,1)S(1)}, bf16[96,128]{1,0:T(8,128)(2,1)S(1)}, bf16[96,128]{1,0:T(8,128)(2,1)S(1)}, bf16[96,128]{1,0:T(8,128)(2,1)S(1)}) custom-call(bf16[2,192,896]{2,1,0:T(8,128)(2,1)S(1)} %get-tuple-element.52.first.refs_0_, bf16[2,192,896]{2,1,0:T(8,128)(2,1)S(1)} %get-tuple-element.56.refs_1_.later, ...), custom_call_target="tpu_custom_call" | custom-call | tf_op jit(solution)/shard_map/pallas_call | solution.py:396
  28.5 1.3 %collective-permute-start.8 = (bf16[192,896]{1,0:T(8,128)(2,1)S(1)}, bf16[192,896]{1,0:T(8,128)(2,1)S(1)}, u32[]{:S(2)}, u32[]{:S(2)}) collective-permute-start(bf16[192,896]{1,0:T(8,128)(2,1)S(1)} %get-tuple-element.70), channel_id=1, source_target_pairs={{8,16},{9,17},{10,18},{11,19},{12,20},{13,21},{14,22},{15,23}} | collective-permute-start | bytes 1032200 | tf_op jit(solution)/shard_map/ppermute | solution.py:425
  29.9 0.7 %collective-permute-start.9 = (bf16[96,128]{1,0:T(8,128)(2,1)S(1)}, bf16[96,128]{1,0:T(8,128)(2,1)S(1)}, u32[]{:S(2)}, u32[]{:S(2)}) collective-permute-start(bf16[96,128]{1,0:T(8,128)(2,1)S(1)} %get-tuple-element.71), channel_id=1, source_target_pairs={{9,18},{10,17},{13,22},{14,21},{1,2},{2,1},{5,6},{6,5}} | collective-permute-start | bytes 73736 | tf_op jit(solution)/shard_map/ppermute | solution.py:425
  30.5 1.3 %collective-permute-start.10 = (bf16[96,128]{1,0:T(8,128)(2,1)S(1)}, bf16[96,128]{1,0:T(8,128)(2,1)S(1)}, u32[]{:S(2)}, u32[]{:S(2)}) collective-permute-start(bf16[96,128]{1,0:T(8,128)(2,1)S(1)} %get-tuple-element.72), channel_id=1, source_target_pairs={{8,17},{9,16},{10,19},{11,18},{12,21},{13,20},{14,23},{15,22},{0,1... | collective-permute-start | bytes 73736 | tf_op jit(solution)/shard_map/ppermute | solution.py:425
  31.8 1.3 %collective-permute-start.11 = (bf16[96,128]{1,0:T(8,128)(2,1)S(1)}, bf16[96,128]{1,0:T(8,128)(2,1)S(1)}, u32[]{:S(2)}, u32[]{:S(2)}) collective-permute-start(bf16[96,128]{1,0:T(8,128)(2,1)S(1)} %get-tuple-element.73), channel_id=1, source_target_pairs={{8,20},{9,21},{10,22},{11,23},{12,16},{13,17},{14,18},{15,19},{0,4... | collective-permute-start | bytes 73736 | tf_op jit(solution)/shard_map/ppermute | solution.py:425
  33.2 1.3 %collective-permute-start.13 = (bf16[192,896]{1,0:T(8,128)(2,1)S(1)}, bf16[192,896]{1,0:T(8,128)(2,1)S(1)}, u32[]{:S(2)}, u32[]{:S(2)}) collective-permute-start(bf16[192,896]{1,0:T(8,128)(2,1)S(1)} %get-tuple-element.75), channel_id=1, source_target_pairs={{8,16},{9,17},{10,18},{11,19},{12,20},{13,21},{14,22},{15,23}} | collective-permute-start | bytes 1032200 | tf_op jit(solution)/shard_map/ppermute | solution.py:425
  34.5 0.0 collective-permute-done.11.refs_9_.refs_3_
  34.5 1.3 %collective-permute-start.12 = (bf16[192,896]{1,0:T(8,128)(2,1)S(1)}, bf16[192,896]{1,0:T(8,128)(2,1)S(1)}, u32[]{:S(2)}, u32[]{:S(2)}) collective-permute-start(bf16[192,896]{1,0:T(8,128)(2,1)S(1)} %get-tuple-element.74), channel_id=1, source_target_pairs={{16,24},{17,25},{18,26},{19,27},{20,28},{21,29},{22,30},{23,31},{0... | collective-permute-start | bytes 1032200 | tf_op jit(solution)/shard_map/ppermute | solution.py:425
  35.8 0.7 %collective-permute-start.14 = (bf16[48,128]{1,0:T(8,128)(2,1)S(1)}, bf16[48,128]{1,0:T(8,128)(2,1)S(1)}, u32[]{:S(2)}, u32[]{:S(2)}) collective-permute-start(bf16[48,128]{1,0:T(8,128)(2,1)S(1)} %get-tuple-element.76), channel_id=1, source_target_pairs={{17,26},{18,25},{21,30},{22,29},{1,10},{2,9},{5,14},{6,13}} | collective-permute-start | bytes 36872 | tf_op jit(solution)/shard_map/ppermute | solution.py:425
  36.5 1.3 %collective-permute-start.15 = (bf16[48,128]{1,0:T(8,128)(2,1)S(1)}, bf16[48,128]{1,0:T(8,128)(2,1)S(1)}, u32[]{:S(2)}, u32[]{:S(2)}) collective-permute-start(bf16[48,128]{1,0:T(8,128)(2,1)S(1)} %get-tuple-element.77), channel_id=1, source_target_pairs={{16,25},{17,24},{18,27},{19,26},{20,29},{21,28},{22,31},{23,30},{0... | collective-permute-start | bytes 36872 | tf_op jit(solution)/shard_map/ppermute | solution.py:425
  37.8 1.3 %collective-permute-start.16 = (bf16[48,128]{1,0:T(8,128)(2,1)S(1)}, bf16[48,128]{1,0:T(8,128)(2,1)S(1)}, u32[]{:S(2)}, u32[]{:S(2)}) collective-permute-start(bf16[48,128]{1,0:T(8,128)(2,1)S(1)} %get-tuple-element.78), channel_id=1, source_target_pairs={{16,28},{17,29},{18,30},{19,31},{20,24},{21,25},{22,26},{23,27},{0... | collective-permute-start | bytes 36872 | tf_op jit(solution)/shard_map/ppermute | solution.py:425
  39.1 6.0 %collective-permute-done.15.refs_5_ = bf16[48,128]{1,0:T(8,128)(2,1)S(1)} collective-permute-done((bf16[48,128]{1,0:T(8,128)(2,1)S(1)}, bf16[48,128]{1,0:T(8,128)(2,1)S(1)}, u32[]{:S(2)}, u32[]{:S(2)}) %collective-permute-start.15) | collective-permute-done | bytes 12320 | tf_op jit(solution)/shard_map/ppermute | solution.py:425
  45.1 1.5 %collective-permute-done.16.refs_6_ = bf16[48,128]{1,0:T(8,128)(2,1)S(1)} collective-permute-done((bf16[48,128]{1,0:T(8,128)(2,1)S(1)}, bf16[48,128]{1,0:T(8,128)(2,1)S(1)}, u32[]{:S(2)}, u32[]{:S(2)}) %collective-permute-start.16) | collective-permute-done | bytes 12320 | tf_op jit(solution)/shard_map/ppermute | solution.py:425
  46.7 1.6 %shard_map.90 = bf16[192,896]{1,0:T(8,128)(2,1)} custom-call(bf16[4,192,128]{2,1,0:T(8,128)(2,1)S(1)} %get-tuple-element.47.refs_2_.live, bf16[2,192,896]{2,1,0:T(8,128)(2,1)S(1)} %get-tuple-element.56.refs_1_.later, bf16[1024,896]{1,0:T(8,128)(2,1)S(1)} %shard_map.86.refs_3_.map_ext, f32[1,896]{1,0:T(1,128)S(1)} %bitcast.12, ...), custom_call_target="tpu_custom_call" | custom-call | tf_op jit(solution)/shard_map/pallas_call | solution.py:396
  (13 shorter events, 0.0 us)
Async XLA Ops:
  3.9 9.8 %collective-permute-start = (bf16[1472,128]{1,0:T(8,128)(2,1)S(1)}, bf16[1472,128]{1,0:T(8,128)(2,1)S(1)}, u32[]{:S(2)}, u32[]{:S(2)}) collective-permute-start(bf16[1472,128]{1,0:T(8,128)(2,1)S(1)} %get-tuple-element.58), channel_id=1, source_target_pairs={{8,0},{9,1},{10,2},{11,3},{12,4},{13,5},{14,6},{15,7},{16,8},{17,9... | collective-permute-start | bytes 1130504 | tf_op jit(solution)/shard_map/ppermute | solution.py:425
  6.0 5.3 %collective-permute-start.1 = (bf16[96,128]{1,0:T(8,128)(2,1)S(1)}, bf16[96,128]{1,0:T(8,128)(2,1)S(1)}, u32[]{:S(2)}, u32[]{:S(2)}) collective-permute-start(bf16[96,128]{1,0:T(8,128)(2,1)S(1)} %get-tuple-element.60), channel_id=1, source_target_pairs={{1,2},{2,1},{5,6},{6,5}} | collective-permute-start | bytes 73736 | tf_op jit(solution)/shard_map/ppermute | solution.py:425
  6.6 4.7 %collective-permute-start.2 = (bf16[96,128]{1,0:T(8,128)(2,1)S(1)}, bf16[96,128]{1,0:T(8,128)(2,1)S(1)}, u32[]{:S(2)}, u32[]{:S(2)}) collective-permute-start(bf16[96,128]{1,0:T(8,128)(2,1)S(1)} %get-tuple-element.61), channel_id=1, source_target_pairs={{0,1},{1,0},{2,3},{3,2},{4,5},{5,4},{6,7},{7,6}} | collective-permute-start | bytes 73736 | tf_op jit(solution)/shard_map/ppermute | solution.py:425
  7.3 4.0 %collective-permute-start.3 = (bf16[96,128]{1,0:T(8,128)(2,1)S(1)}, bf16[96,128]{1,0:T(8,128)(2,1)S(1)}, u32[]{:S(2)}, u32[]{:S(2)}) collective-permute-start(bf16[96,128]{1,0:T(8,128)(2,1)S(1)} %get-tuple-element.62), channel_id=1, source_target_pairs={{0,4},{1,5},{2,6},{3,7},{4,0},{5,1},{6,2},{7,3}} | collective-permute-start | bytes 73736 | tf_op jit(solution)/shard_map/ppermute | solution.py:425
  8.0 5.7 %copy-start = (f32[1,1,1,896]{3,2,1,0:T(1,128)S(1)}, f32[1,1,1,896]{3,2,1,0:T(1,128)}, u32[]{:S(2)}) copy-start(f32[1,1,1,896]{3,2,1,0:T(1,128)} %param.14) | copy-start | bytes 10756
  13.7 13.5 %collective-permute-start.4 = (bf16[384,896]{1,0:T(8,128)(2,1)S(1)}, bf16[384,896]{1,0:T(8,128)(2,1)S(1)}, u32[]{:S(2)}, u32[]{:S(2)}) collective-permute-start(bf16[384,896]{1,0:T(8,128)(2,1)S(1)} %get-tuple-element.63), channel_id=1, source_target_pairs={{0,8},{1,9},{2,10},{3,11},{4,12},{5,13},{6,14},{7,15}} | collective-permute-start | bytes 2064392 | tf_op jit(solution)/shard_map/ppermute | solution.py:425
  15.0 3.3 %collective-permute-start.5 = (bf16[96,128]{1,0:T(8,128)(2,1)S(1)}, bf16[96,128]{1,0:T(8,128)(2,1)S(1)}, u32[]{:S(2)}, u32[]{:S(2)}) collective-permute-start(bf16[96,128]{1,0:T(8,128)(2,1)S(1)} %get-tuple-element.64), channel_id=1, source_target_pairs={{1,10},{2,9},{5,14},{6,13}} | collective-permute-start | bytes 73736 | tf_op jit(solution)/shard_map/ppermute | solution.py:425
  15.6 9.7 %collective-permute-start.6 = (bf16[96,128]{1,0:T(8,128)(2,1)S(1)}, bf16[96,128]{1,0:T(8,128)(2,1)S(1)}, u32[]{:S(2)}, u32[]{:S(2)}) collective-permute-start(bf16[96,128]{1,0:T(8,128)(2,1)S(1)} %get-tuple-element.65), channel_id=1, source_target_pairs={{0,9},{1,8},{2,11},{3,10},{4,13},{5,12},{6,15},{7,14}} | collective-permute-start | bytes 73736 | tf_op jit(solution)/shard_map/ppermute | solution.py:425
  16.9 10.3 %collective-permute-start.7 = (bf16[96,128]{1,0:T(8,128)(2,1)S(1)}, bf16[96,128]{1,0:T(8,128)(2,1)S(1)}, u32[]{:S(2)}, u32[]{:S(2)}) collective-permute-start(bf16[96,128]{1,0:T(8,128)(2,1)S(1)} %get-tuple-element.66), channel_id=1, source_target_pairs={{0,12},{1,13},{2,14},{3,15},{4,8},{5,9},{6,10},{7,11}} | collective-permute-start | bytes 73736 | tf_op jit(solution)/shard_map/ppermute | solution.py:425
  28.5 6.0 %collective-permute-start.8 = (bf16[192,896]{1,0:T(8,128)(2,1)S(1)}, bf16[192,896]{1,0:T(8,128)(2,1)S(1)}, u32[]{:S(2)}, u32[]{:S(2)}) collective-permute-start(bf16[192,896]{1,0:T(8,128)(2,1)S(1)} %get-tuple-element.70), channel_id=1, source_target_pairs={{8,16},{9,17},{10,18},{11,19},{12,20},{13,21},{14,22},{15,23}} | collective-permute-start | bytes 1032200 | tf_op jit(solution)/shard_map/ppermute | solution.py:425
  29.9 4.6 %collective-permute-start.9 = (bf16[96,128]{1,0:T(8,128)(2,1)S(1)}, bf16[96,128]{1,0:T(8,128)(2,1)S(1)}, u32[]{:S(2)}, u32[]{:S(2)}) collective-permute-start(bf16[96,128]{1,0:T(8,128)(2,1)S(1)} %get-tuple-element.71), channel_id=1, source_target_pairs={{9,18},{10,17},{13,22},{14,21},{1,2},{2,1},{5,6},{6,5}} | collective-permute-start | bytes 73736 | tf_op jit(solution)/shard_map/ppermute | solution.py:425
  30.5 4.0 %collective-permute-start.10 = (bf16[96,128]{1,0:T(8,128)(2,1)S(1)}, bf16[96,128]{1,0:T(8,128)(2,1)S(1)}, u32[]{:S(2)}, u32[]{:S(2)}) collective-permute-start(bf16[96,128]{1,0:T(8,128)(2,1)S(1)} %get-tuple-element.72), channel_id=1, source_target_pairs={{8,17},{9,16},{10,19},{11,18},{12,21},{13,20},{14,23},{15,22},{0,1... | collective-permute-start | bytes 73736 | tf_op jit(solution)/shard_map/ppermute | solution.py:425
  31.8 2.7 %collective-permute-start.11 = (bf16[96,128]{1,0:T(8,128)(2,1)S(1)}, bf16[96,128]{1,0:T(8,128)(2,1)S(1)}, u32[]{:S(2)}, u32[]{:S(2)}) collective-permute-start(bf16[96,128]{1,0:T(8,128)(2,1)S(1)} %get-tuple-element.73), channel_id=1, source_target_pairs={{8,20},{9,21},{10,22},{11,23},{12,16},{13,17},{14,18},{15,19},{0,4... | collective-permute-start | bytes 73736 | tf_op jit(solution)/shard_map/ppermute | solution.py:425
  33.2 6.0 %collective-permute-start.13 = (bf16[192,896]{1,0:T(8,128)(2,1)S(1)}, bf16[192,896]{1,0:T(8,128)(2,1)S(1)}, u32[]{:S(2)}, u32[]{:S(2)}) collective-permute-start(bf16[192,896]{1,0:T(8,128)(2,1)S(1)} %get-tuple-element.75), channel_id=1, source_target_pairs={{8,16},{9,17},{10,18},{11,19},{12,20},{13,21},{14,22},{15,23}} | collective-permute-start | bytes 1032200 | tf_op jit(solution)/shard_map/ppermute | solution.py:425
  34.5 12.1 %collective-permute-start.12 = (bf16[192,896]{1,0:T(8,128)(2,1)S(1)}, bf16[192,896]{1,0:T(8,128)(2,1)S(1)}, u32[]{:S(2)}, u32[]{:S(2)}) collective-permute-start(bf16[192,896]{1,0:T(8,128)(2,1)S(1)} %get-tuple-element.74), channel_id=1, source_target_pairs={{16,24},{17,25},{18,26},{19,27},{20,28},{21,29},{22,30},{23,31},{0... | collective-permute-start | bytes 1032200 | tf_op jit(solution)/shard_map/ppermute | solution.py:425
  35.8 3.3 %collective-permute-start.14 = (bf16[48,128]{1,0:T(8,128)(2,1)S(1)}, bf16[48,128]{1,0:T(8,128)(2,1)S(1)}, u32[]{:S(2)}, u32[]{:S(2)}) collective-permute-start(bf16[48,128]{1,0:T(8,128)(2,1)S(1)} %get-tuple-element.76), channel_id=1, source_target_pairs={{17,26},{18,25},{21,30},{22,29},{1,10},{2,9},{5,14},{6,13}} | collective-permute-start | bytes 36872 | tf_op jit(solution)/shard_map/ppermute | solution.py:425
  36.5 8.6 %collective-permute-start.15 = (bf16[48,128]{1,0:T(8,128)(2,1)S(1)}, bf16[48,128]{1,0:T(8,128)(2,1)S(1)}, u32[]{:S(2)}, u32[]{:S(2)}) collective-permute-start(bf16[48,128]{1,0:T(8,128)(2,1)S(1)} %get-tuple-element.77), channel_id=1, source_target_pairs={{16,25},{17,24},{18,27},{19,26},{20,29},{21,28},{22,31},{23,30},{0... | collective-permute-start | bytes 36872 | tf_op jit(solution)/shard_map/ppermute | solution.py:425
  37.8 8.8 %collective-permute-start.16 = (bf16[48,128]{1,0:T(8,128)(2,1)S(1)}, bf16[48,128]{1,0:T(8,128)(2,1)S(1)}, u32[]{:S(2)}, u32[]{:S(2)}) collective-permute-start(bf16[48,128]{1,0:T(8,128)(2,1)S(1)} %get-tuple-element.78), channel_id=1, source_target_pairs={{16,28},{17,29},{18,30},{19,31},{20,24},{21,25},{22,26},{23,27},{0... | collective-permute-start | bytes 36872 | tf_op jit(solution)/shard_map/ppermute | solution.py:425

commit v8 on v7

--- a/solution.py
+++ b/solution.py
@@ -122,17 +122,14 @@
             )
 
 
-def edges_kernel(source, assignment, counts, first_map, band, second_map, *refs):
-    edge_out, first_out, later_out, live_out, first_in, band_in, second_in = refs[:7]
-    source_in, assignment_in, counts_in, sems = refs[7:]
+def edges_kernel(source, assignment, counts, first_map, edge_out, starts_out, live_out, *refs):
+    source_in, assignment_in, counts_in, first_in, sems = refs
     rounds, slots, cells = source.shape
-    soon = first_out.shape[0]
 
     @pl.when(lax.axis_index("depth") > 0)
     def _():
         pairs = [(counts, counts_in), (assignment, assignment_in), (first_map, first_in)]
         pairs += [(source.at[r], source_in.at[r]) for r in range(1, rounds)]
-        pairs += [(band, band_in), (second_map, second_in)]
         copies = started(pairs, sems)
         selector = edge_selector(cells)
         copies[0].wait()
@@ -144,25 +141,17 @@
         for r in range(1, rounds):
             copies[2 + r].wait()
             chosen = chosen_of(assignment_in[r : r + 1], counts_in, r)
-            picked = dot_t(chosen, source_in[r]).astype(jnp.bfloat16)
-            if r < soon:
-                first_out[r] = picked
-            else:
-                later_out[r - soon] = picked
-            at = cells + (r - 1) * slots
-            edge_out[at : at + slots] = dot(picked, first_edge).astype(jnp.bfloat16)
-        copies[-2].wait()
-        copies[-1].wait()
-
-
-def opening_kernel(early_layers, swaps, arrival, source, assignment, counts, *refs):
-    first_map, band, second_map = refs[:3]
-    first_out, live_out, first_in, band_in, second_in, own_edge, edge_cells = refs[8:15]
-    messages = refs[15 : 15 + len(swaps)]
-    arrival_in, source_in, assignment_in, counts_in, sems = refs[15 + len(swaps) :]
-    slots, cells = arrival.shape
+            starts_out[r] = dot_t(chosen, source_in[r]).astype(jnp.bfloat16)
+        edges = dot(starts_out[1:].reshape(-1, cells), first_edge)
+        edge_out[cells:] = edges.astype(jnp.bfloat16)
+
+
+def opening_kernel(early_layers, swaps, source, assignment, counts, arrival, first_map, *refs):
+    starts_out, live_out, edge_cells = refs[2:5]
+    messages = refs[5 : 5 + len(swaps)]
+    source_in, assignment_in, counts_in, sems = refs[5 + len(swaps) :]
+    rounds, slots, cells = source.shape
     part = slots // 4
-    soon = first_out.shape[0]
     early = lax.axis_index("depth") < early_layers
 
     @pl.when(jnp.logical_not(early))
@@ -171,35 +160,29 @@
 
     @pl.when(early)
     def _():
-        pairs = [(counts, counts_in), (assignment, assignment_in), (first_map, first_in)]
-        pairs += [(arrival, arrival_in)]
-        pairs += [(source.at[r], source_in.at[r]) for r in range(soon)]
-        pairs += [(band, band_in), (second_map, second_in)]
+        pairs = [(counts, counts_in), (assignment, assignment_in)]
+        pairs += [(source.at[r], source_in.at[r]) for r in range(rounds)]
         copies = started(pairs, sems)
         edge_cells[...] = edge_rows_selector(cells)
-        selector = edge_selector(cells)
+        first_edge = dot(first_map[...], edge_selector(cells)).astype(jnp.bfloat16)
         copies[0].wait()
         fill_live(live_out, counts_in)
         copies[1].wait()
-        chosen = [chosen_of(assignment_in[r : r + 1], counts_in, r) for r in range(soon)]
-        copies[2].wait()
-        first_edge = dot(first_in[...], selector).astype(jnp.bfloat16)
-        own_edge[...] = first_edge
-        copies[3].wait()
-        for r in range(soon):
-            copies[4 + r].wait()
-            picked = dot_t(chosen[r], source_in[r])
+        for r in range(rounds):
+            chosen = chosen_of(assignment_in[r : r + 1], counts_in, r)
+            copies[2 + r].wait()
+            picked = dot_t(chosen, source_in[r])
             if r == 0:
                 live = live_out[0].astype(jnp.float32)
                 live = jnp.concatenate([live] * (cells // LANES), axis=1)
-                picked = picked + live * arrival_in[...].astype(jnp.float32)
-            picked = picked.astype(jnp.bfloat16)
-            first_out[r] = picked
-            edges = dot(picked, first_edge)
-            for message, swap in zip(messages, swaps):
-                message[r * part : (r + 1) * part] = pack(edges, group_of(*swap))
-        copies[-2].wait()
-        copies[-1].wait()
+                picked = picked + live * arrival[...].astype(jnp.float32)
+            starts_out[r] = picked.astype(jnp.bfloat16)
+        edges = dot(starts_out[...].reshape(-1, cells), first_edge)
+        for message, swap in zip(messages, swaps):
+            for r in range(rounds):
+                message[r * part : (r + 1) * part] = pack(
+                    edges[r * slots : (r + 1) * slots], group_of(*swap)
+                )
 
 
 def bands(cells):
@@ -236,14 +219,15 @@
     whole_ext[:cells] = dot(coupled(first_map[...], band), second_map[...]).astype(jnp.bfloat16)
 
 
-def inside_kernel(early_layers, first, first_map, band, second_map, edge_cells, *refs):
+def inside_kernel(early_layers, starts, first_map, band, second_map, edge_cells, *refs):
     image_out, whole_ext = refs
-    cells = second_map.shape[0]
+    slots, cells = starts.shape[1:]
+    chains = image_out.shape[0] // slots
     early = lax.axis_index("depth") < early_layers
 
     @pl.when(early)
     def _():
-        mapped = dot(first[...].reshape(-1, cells), first_map[...]).astype(jnp.bfloat16)
+        mapped = dot(starts[:chains].reshape(-1, cells), first_map[...]).astype(jnp.bfloat16)
         image_out[...] = dot(coupled(mapped, band), second_map[...])
 
     @pl.when(jnp.logical_not(early))
@@ -254,48 +238,18 @@
     whole_ext[cells:] = (coupling_weight * edge_rows).astype(jnp.bfloat16)
 
 
-def waiting_kernel(early_layers, swaps, source, assignment, counts, *refs):
-    first_map, band, second_map, own_edge, _, _, whole_ext, later_out = refs[:8]
-    messages = refs[8 : 8 + len(swaps)]
-    source_in, assignment_in, counts_in, sems = refs[8 + len(swaps) :]
-    rounds, slots = source.shape[:2]
-    part = slots // 4
-    layer = lax.axis_index("depth")
-
-    @pl.when(layer == 0)
-    def _():
-        pairs = [(counts, counts_in), (assignment, assignment_in)]
-        pairs += [(source.at[pl.ds(rounds - 2, 2)], source_in)]
-        for copy in started(pairs, sems):
-            copy.wait()
-        for at, r in enumerate(range(rounds - 2, rounds)):
-            chosen = chosen_of(assignment_in[r : r + 1], counts_in, r)
-            picked = dot_t(chosen, source_in[at]).astype(jnp.bfloat16)
-            later_out[at] = picked
-            edges = dot(picked, own_edge[...])
-            for message, swap in zip(messages, swaps):
-                message[at * part : (at + 1) * part] = pack(edges, group_of(*swap))
-
-    @pl.when((layer > 0) & (layer < early_layers))
+def whole_map_kernel(early_layers, first_map, band, second_map, whole_in, whole_ext):
+    del whole_in
+
+    @pl.when(lax.axis_index("depth") < early_layers)
     def _():
         fill_whole_map(first_map, band, second_map, whole_ext)
 
 
-def last_map_kernel(first_map, band, second_map, whole_in, whole_ext):
-    del whole_in
-
-    @pl.when(lax.axis_index("depth") == 0)
-    def _():
-        fill_whole_map(first_map, band, second_map, whole_ext)
-
-
-def halo_of(messages, swaps, at, part, live):
+def halo_of(messages, swaps, live):
     halo = 0.0
-    for parts, swap in zip(messages, swaps):
-        packed = 0.0
-        for ref, row in zip(parts, at):
-            packed = packed + ref[row : row + part].astype(jnp.float32)
-        halo = halo + unpack(packed, group_of(*swap))
+    for message, swap in zip(messages, swaps):
+        halo = halo + unpack(message.astype(jnp.float32), group_of(*swap))
     return (halo * live.astype(jnp.float32)).astype(jnp.bfloat16)
 
 
@@ -304,36 +258,33 @@
     return (damp * image + (1.0 - damp) * start.astype(jnp.float32)).astype(jnp.bfloat16)
 
 
-def rounds_of(first, later, begin, end):
-    soon = first.shape[0]
-    found = [first[r] if r < soon else later[r - soon] for r in range(begin, end)]
-    return jnp.concatenate(found, axis=0)
-
-
-def step_kernel(swaps, step, chains, keeps, waiting, early_layers, *refs):
-    first, later, live, map_ext, damping, edge_next, traces = refs[:7]
-    received = refs[7 : 7 + len(swaps)]
-    others = refs[7 + len(swaps) :]
-    messages, others = others[-len(swaps) :], others[: -len(swaps)]
-    kept_out = None
-    if keeps:
-        kept_out, others = others[-1], others[:-1]
-    traces_out, others = others[-1], others[:-1]
-    slots, cells = first.shape[1:]
+def step_kernel(swaps, step, chains, keeps, early_layers, *refs):
+    starts, live, map_ext, damping, edge_next, traces = refs[:6]
+    received = refs[6 : 6 + len(swaps)]
+    opened = refs[6 + len(swaps) : -1 - len(swaps) - keeps]
+    outs = refs[-1 - len(swaps) - keeps :]
+    traces_out, messages = outs[0], outs[1 + keeps :]
+    slots, cells = starts.shape[1:]
     part = slots // 4
     layer = lax.axis_index("depth")
     here = (layer >= step) & (layer < step + early_layers)
-    if not keeps and step > 0:
+    if opened:
         here = here | (layer == 0)
 
     @pl.when(here)
     def _():
-        halo = [
-            halo_of([[ref] for ref in received], swaps, [chain * part], part, live[step + chain])
-            for chain in range(chains)
-        ]
+        halo = []
+        for chain in range(chains):
+            packed = [ref[chain * part : (chain + 1) * part] for ref in received]
+            if opened:
+                at = (step + chain) * part
+                packed = [
+                    jnp.where(layer == 0, ref[at : at + part].astype(jnp.float32), x)
+                    for ref, x in zip(opened, packed)
+                ]
+            halo.append(halo_of(packed, swaps, live[step + chain]))
         halo = jnp.concatenate(halo, axis=0)
-        start = rounds_of(first, later, step, step + chains)
+        start = starts[step : step + chains].reshape(-1, cells)
         if step == 0:
             image = traces[...] + dot(halo, map_ext[cells:])
         else:
@@ -341,10 +292,10 @@
             start = start.astype(jnp.bfloat16)
             image = dot(jnp.concatenate([start, halo], axis=1), map_ext[...])
         ended = blend(image, start, damping)
-        going = (chains - 1 if keeps else chains) * slots
+        going = traces_out.shape[0]
         traces_out[...] = ended[:going]
         if keeps:
-            kept_out[...] = ended[going:]
+            outs[1][...] = ended[going:]
         at = cells + step * slots
         edges = dot(ended, edge_next[:cells])
         edges += edge_next[at : at + chains * slots].astype(jnp.float32)
@@ -354,29 +305,21 @@
                     edges[chain * slots : (chain + 1) * slots], group_of(*swap)
                 )
 
-    if waiting:
-
-        @pl.when(layer == 0)
-        def _():
-            for message, other in zip(messages, others):
-                message[...] = other[...]
-
-
-def final_kernel(swaps, picks, others, live, later, map_ext, damping, traces, *refs):
+
+def final_kernel(swaps, picks, others, live, starts, map_ext, damping, traces, *refs):
     slots, cells = traces.shape
     kept, received, (traces_out, row) = refs[:others], refs[others:-2], refs[-2:]
     part = slots // 4
     layer = lax.axis_index("depth")
-    start = later[later.shape[0] - 1].astype(jnp.float32) + traces[...].astype(jnp.float32)
+    start = starts[starts.shape[0] - 1].astype(jnp.float32) + traces[...].astype(jnp.float32)
     for other in kept:
         start = start + other[...].astype(jnp.float32)
     row[:, :cells] = start.astype(jnp.bfloat16)
 
     def take(phase):
         messages = received[phase * len(swaps) : (phase + 1) * len(swaps)]
-        at = [messages[0].shape[0] - part]
-        mask = live[live.shape[0] - 1]
-        row[:, cells:] = halo_of([[ref] for ref in messages], swaps, at, part, mask)
+        messages = [ref[ref.shape[0] - part :] for ref in messages]
+        row[:, cells:] = halo_of(messages, swaps, live[live.shape[0] - 1])
 
     by_rule = layer < 0
     for at, phase in picks:
@@ -447,90 +390,65 @@
 
     part = slots // 4
     band = coupling_band(cells)
-    later = array(2, slots, cells)
     whole = array(cells + LANES, cells)
-    edge = array(cells + (rounds - 1) * slots, LANES)
-    counts_in = pltpu.SMEM(counts.shape, counts.dtype)
-    maps = [first_map, band, second_map]
-    own = [array(soon, slots, cells), array(rounds, slots, LANES)]
-    own += [array(*x.shape) for x in maps]
-    copied = [scratch(source), scratch(assignment), counts_in]
-    edge, first, later, live, *maps_in = call(
+    own = [array(rounds, slots, cells), array(rounds, slots, LANES)]
+    copied = [scratch(source), scratch(assignment), pltpu.SMEM(counts.shape, counts.dtype)]
+    edge, starts, live = call(
         edges_kernel,
-        [edge, own[0], later] + own[1:],
-        [source, assignment, counts] + maps,
-        in_hbm=range(6),
-        scratch=copied + [pltpu.SemaphoreType.DMA((4 + rounds,))],
+        [array(cells + (rounds - 1) * slots, LANES)] + own,
+        [source, assignment, counts, first_map],
+        in_hbm=range(4),
+        scratch=copied + [scratch(first_map), pltpu.SemaphoreType.DMA((2 + rounds,))],
     )
     edge_next = send(edge, [(layer, layer - 1) for layer in range(1, layers)])
     opened = call(
         functools.partial(opening_kernel, early_layers, swaps),
-        own + [array(cells, LANES), array(LANES, cells)] + [array(soon * part, LANES)] * len(swaps),
-        [arrival, source, assignment, counts] + maps + [first, live] + maps_in,
-        in_hbm=range(7),
-        scratch=[scratch(arrival)] + copied + [pltpu.SemaphoreType.DMA((6 + soon,))],
-        aliases={7 + i: i for i in range(5)},
-    )
-    first, live, first_map, band, second_map, own_edge, edge_cells = opened[:7]
+        own + [array(LANES, cells)] + [array(rounds * part, LANES)] * len(swaps),
+        [source, assignment, counts, arrival, first_map, starts, live],
+        in_hbm=range(3),
+        scratch=copied + [pltpu.SemaphoreType.DMA((2 + rounds,))],
+        aliases={5: 0, 6: 1},
+    )
+    starts, live, edge_cells = opened[:3]
     received = [
         send(m, [(layer, layer) for layer in range(early_layers)], swap)
-        for m, swap in zip(opened[7:], swaps)
+        for m, swap in zip(opened[3:], swaps)
     ]
     traces, map_ext = call(
         functools.partial(inside_kernel, early_layers),
         [array(soon * slots, cells, kind=jnp.float32), whole],
-        [first, first_map, band, second_map, edge_cells],
-    )
-    arrived = []
-    picks = []
+        [starts, first_map, band, second_map, edge_cells],
+    )
+    opened = received
+    arrived = list(opened)
+    picks = [(0, 0)]
     kept = []
     for step in range(rounds - 1):
         chains = min(rounds - 1 - step, soon)
         last = step == rounds - 2
-        before_last = step == rounds - 3
         keeps = step + chains == rounds - 1 and not last
         going = (chains - 1 if keeps else chains) * slots
         outs = [array(going, cells)] + [array(slots, cells)] * keeps
         outs += [array(chains * part, LANES)] * len(swaps)
-        operands = [first, later, live, map_ext, damping, edge_next, traces] + received
-        if before_last:
-            operands += waiting
+        operands = [starts, live, map_ext, damping, edge_next, traces] + received
         ended = call(
-            functools.partial(step_kernel, swaps, step, chains, keeps, before_last, early_layers),
+            functools.partial(step_kernel, swaps, step, chains, keeps, early_layers),
             outs,
-            operands,
+            operands + (opened if last else []),
         )
         moves = [(layer, layer + 1) for layer in range(step, step + early_layers)]
-        traces = send(ended[0], moves + [(0, 1)] if last else moves)
+        if last:
+            moves.append((0, 1))
+        traces = send(ended[0], moves)
         if keeps:
             kept.append(send(ended[1], [(step, step + 1)]))
             picks.append((step + 1, len(arrived) // len(swaps)))
-        if before_last:
-            moves.append((0, 0))
-            picks.append((0, len(arrived) // len(swaps)))
-        if last:
-            moves.append((0, 1))
         received = [send(m, moves, swap) for m, swap in zip(ended[-len(swaps) :], swaps)]
         if step > 0:
             arrived += received
         if step == 0:
-            late = call(
-                functools.partial(waiting_kernel, early_layers, swaps),
-                [whole, array(*later.shape)] + [array(2 * part, LANES)] * len(swaps),
-                [source, assignment, counts, first_map, band, second_map, own_edge, map_ext, later],
-                in_hbm=range(3),
-                scratch=[
-                    scratch(later),
-                    scratch(assignment),
-                    counts_in,
-                    pltpu.SemaphoreType.DMA((3,)),
-                ],
-                aliases={7: 0, 8: 1},
-            )
-            map_ext, later, waiting = late[0], late[1], list(late[2:])
-        if before_last:
             (map_ext,) = call(
-                last_map_kernel,
+                functools.partial(whole_map_kernel, early_layers),
                 [whole],
                 [first_map, band, second_map, map_ext],
                 aliases={3: 0},
@@ -538,7 +456,7 @@
     (ended,) = call(
         functools.partial(final_kernel, swaps, picks, len(kept)),
         [array(slots, cells)],
-        [live, later, map_ext, damping, traces] + kept + arrived,
+        [live, starts, map_ext, damping, traces] + kept + arrived,
         scratch=[pltpu.VMEM((slots, cells + LANES), jnp.bfloat16)],
     )
     return ended.reshape(1, slots, 1, 1, cells)

time: 48.7 us -> 46 us (0.945)
  waiting for transfers between devices: 18.8 us -> 16.2 us
    ppermute x17, waiting for transfers between devices: 18.8 us -> 16.2 us  [send(): return lax.ppermute(x, MESH_AXES, pairs)]
    pallas_call x9 -> x8, Pallas kernels: 10.3 us -> 10.1 us  [call(): pl.pallas_call(kernel, out_shape=out_shape, in_specs=[pl.BlockSpec(memory...]
  transfers between devices with their start and end apart: 17 -> 17, of which waited for: 5 -> 6; matrix products, arithmetic and copies ran while one was open for 0% -> 0% of each run, Pallas kernels for 7% -> 8%
where the time goes in v8:
time: 46 us; the launch traced here: 45.6 us
  starting transfers between devices  19 us (41%)
  waiting for transfers between devices  16.2 us (35%)
  Pallas kernels  10.1 us (22%)
    ppermute x17, starting transfers between devices, send(): return lax.ppermute(x, MESH_AXES, pairs)  19 us
    ppermute x17, waiting for transfers between devices, send(): return lax.ppermute(x, MESH_AXES, pairs)  16.2 us
    pallas_call x8, Pallas kernels, call(): pl.pallas_call(kernel, out_shape=out_shape, in_specs=[pl.BlockSpec(memory...  10.1 us
  transfers between devices with their start and end apart: 17, of which 6 were waited for; matrix products, arithmetic and copies ran while one was open for 0% of the time, Pallas kernels for 8%

profile of v8, /device:TPU:1, one launch (start us, length us, event | category | flops | bytes accessed | tf_op | source)
XLA Modules:
  0.0 45.6 jit_solution(5966855077117745760)
XLA Ops:
  0.0 3.8 %shard_map.82 = (bf16[1472,128]{1,0:T(8,128)(2,1)S(1)}, bf16[4,192,896]{2,1,0:T(8,128)(2,1)S(1)}, bf16[4,192,128]{2,1,0:T(8,128)(2,1)S(1)}) custom-call(bf16[4,192,896]{2,1,0:T(8,128)(2,1)} %bitcast.20, s32[4,192]{1,0:T(4,128)} %assignment.3, s32[7,1,1,12]{3,2,1,0:T(1,128)} %bitcast.22, bf16[896,896]{1,0:T(8,128)(2,1)} %bitcast.9), custom_call_target="tpu_custom_call" | custom-call | tf_op jit(solution)/shard_map/pallas_call | solution.py:339
  3.8 1.9 %collective-permute-start = (bf16[1472,128]{1,0:T(8,128)(2,1)S(1)}, bf16[1472,128]{1,0:T(8,128)(2,1)S(1)}, u32[]{:S(2)}, u32[]{:S(2)}) collective-permute-start(bf16[1472,128]{1,0:T(8,128)(2,1)S(1)} %get-tuple-element.35), channel_id=1, source_target_pairs={{8,0},{9,1},{10,2},{11,3},{12,4},{13,5},{14,6},{15,7},{16,8},{17,9... | collective-permute-start | bytes 1130504 | tf_op jit(solution)/shard_map/ppermute | solution.py:368
  5.8 0.0 copy-start.1
  5.8 0.0 copy-start.2
  5.8 0.1 shard_map.83
  5.9 0.8 %collective-permute-start.1 = (bf16[192,128]{1,0:T(8,128)(2,1)S(1)}, bf16[192,128]{1,0:T(8,128)(2,1)S(1)}, u32[]{:S(2)}, u32[]{:S(2)}) collective-permute-start(bf16[192,128]{1,0:T(8,128)(2,1)S(1)} %get-tuple-element.37), channel_id=1, source_target_pairs={{1,2},{2,1},{5,6},{6,5}} | collective-permute-start | bytes 147464 | tf_op jit(solution)/shard_map/ppermute | solution.py:368
  6.7 0.7 %collective-permute-start.2 = (bf16[192,128]{1,0:T(8,128)(2,1)S(1)}, bf16[192,128]{1,0:T(8,128)(2,1)S(1)}, u32[]{:S(2)}, u32[]{:S(2)}) collective-permute-start(bf16[192,128]{1,0:T(8,128)(2,1)S(1)} %get-tuple-element.38), channel_id=1, source_target_pairs={{0,1},{1,0},{2,3},{3,2},{4,5},{5,4},{6,7},{7,6}} | collective-permute-start | bytes 147464 | tf_op jit(solution)/shard_map/ppermute | solution.py:368
  7.4 0.7 %collective-permute-start.3 = (bf16[192,128]{1,0:T(8,128)(2,1)S(1)}, bf16[192,128]{1,0:T(8,128)(2,1)S(1)}, u32[]{:S(2)}, u32[]{:S(2)}) collective-permute-start(bf16[192,128]{1,0:T(8,128)(2,1)S(1)} %get-tuple-element.39), channel_id=1, source_target_pairs={{0,4},{1,5},{2,6},{3,7},{4,0},{5,1},{6,2},{7,3}} | collective-permute-start | bytes 147464 | tf_op jit(solution)/shard_map/ppermute | solution.py:368
  8.1 0.0 copy-start.4
  8.1 3.3 %shard_map.84 = (f32[384,896]{1,0:T(8,128)S(1)}, bf16[1024,896]{1,0:T(8,128)(2,1)S(1)}) custom-call(bf16[4,192,896]{2,1,0:T(8,128)(2,1)S(1)} %get-tuple-element.32.starts.refs_0_, bf16[896,896]{1,0:T(8,128)(2,1)S(1)} %bitcast.11, bf16[4,512,256]{2,1,0:T(8,128)(2,1)S(1)} %copy-done.2, bf16[896,896]{1,0:T(8,128)(2,1)S(1)} %bitcast.13, ...), custom_call_target="tpu_custom_call" | custom-call | tf_op jit(solution)/shard_map/pallas_call | solution.py:339
  11.4 0.0 collective-permute-done.1.refs_6_.refs_9_.refs_1_
  11.4 2.2 %collective-permute-done.refs_4_ = bf16[1472,128]{1,0:T(8,128)(2,1)S(1)} collective-permute-done((bf16[1472,128]{1,0:T(8,128)(2,1)S(1)}, bf16[1472,128]{1,0:T(8,128)(2,1)S(1)}, u32[]{:S(2)}, u32[]{:S(2)}) %collective-permute-start) | collective-permute-done | bytes 376864 | tf_op jit(solution)/shard_map/ppermute | solution.py:368
  13.6 1.3 %collective-permute-start.4 = (bf16[384,896]{1,0:T(8,128)(2,1)S(1)}, bf16[384,896]{1,0:T(8,128)(2,1)S(1)}, u32[]{:S(2)}, u32[]{:S(2)}) collective-permute-start(bf16[384,896]{1,0:T(8,128)(2,1)S(1)} %get-tuple-element.40), channel_id=1, source_target_pairs={{0,8},{1,9},{2,10},{3,11},{4,12},{5,13},{6,14},{7,15}} | collective-permute-start | bytes 2064392 | tf_op jit(solution)/shard_map/ppermute | solution.py:368
  14.9 0.7 %collective-permute-start.5 = (bf16[96,128]{1,0:T(8,128)(2,1)S(1)}, bf16[96,128]{1,0:T(8,128)(2,1)S(1)}, u32[]{:S(2)}, u32[]{:S(2)}) collective-permute-start(bf16[96,128]{1,0:T(8,128)(2,1)S(1)} %get-tuple-element.41), channel_id=1, source_target_pairs={{1,10},{2,9},{5,14},{6,13}} | collective-permute-start | bytes 73736 | tf_op jit(solution)/shard_map/ppermute | solution.py:368
  15.6 1.3 %collective-permute-start.6 = (bf16[96,128]{1,0:T(8,128)(2,1)S(1)}, bf16[96,128]{1,0:T(8,128)(2,1)S(1)}, u32[]{:S(2)}, u32[]{:S(2)}) collective-permute-start(bf16[96,128]{1,0:T(8,128)(2,1)S(1)} %get-tuple-element.42), channel_id=1, source_target_pairs={{0,9},{1,8},{2,11},{3,10},{4,13},{5,12},{6,15},{7,14}} | collective-permute-start | bytes 73736 | tf_op jit(solution)/shard_map/ppermute | solution.py:368
  16.9 1.3 %collective-permute-start.7 = (bf16[96,128]{1,0:T(8,128)(2,1)S(1)}, bf16[96,128]{1,0:T(8,128)(2,1)S(1)}, u32[]{:S(2)}, u32[]{:S(2)}) collective-permute-start(bf16[96,128]{1,0:T(8,128)(2,1)S(1)} %get-tuple-element.43), channel_id=1, source_target_pairs={{0,12},{1,13},{2,14},{3,15},{4,8},{5,9},{6,10},{7,11}} | collective-permute-start | bytes 73736 | tf_op jit(solution)/shard_map/ppermute | solution.py:368
  18.2 7.7 %collective-permute-done.6.refs_7_ = bf16[96,128]{1,0:T(8,128)(2,1)S(1)} collective-permute-done((bf16[96,128]{1,0:T(8,128)(2,1)S(1)}, bf16[96,128]{1,0:T(8,128)(2,1)S(1)}, u32[]{:S(2)}, u32[]{:S(2)}) %collective-permute-start.6) | collective-permute-done | bytes 24608 | tf_op jit(solution)/shard_map/ppermute | solution.py:368
  25.9 2.1 %collective-permute-done.7.refs_8_ = bf16[96,128]{1,0:T(8,128)(2,1)S(1)} collective-permute-done((bf16[96,128]{1,0:T(8,128)(2,1)S(1)}, bf16[96,128]{1,0:T(8,128)(2,1)S(1)}, u32[]{:S(2)}, u32[]{:S(2)}) %collective-permute-start.7) | collective-permute-done | bytes 24608 | tf_op jit(solution)/shard_map/ppermute | solution.py:368
  27.9 1.3 %shard_map.87 = (bf16[192,896]{1,0:T(8,128)(2,1)S(1)}, bf16[192,896]{1,0:T(8,128)(2,1)S(1)}, bf16[96,128]{1,0:T(8,128)(2,1)S(1)}, bf16[96,128]{1,0:T(8,128)(2,1)S(1)}, bf16[96,128]{1,0:T(8,128)(2,1)S(1)}) custom-call(bf16[4,192,896]{2,1,0:T(8,128)(2,1)S(1)} %get-tuple-element.32.starts.refs_0_, bf16[4,192,128]{2,1,0:T(8,128)(2,1)S(1)} %get-tuple-element.31.refs_1_.live, ...), custom_call_target="tpu_custom_call" | custom-call | tf_op jit(solution)/shard_map/pallas_call | solution.py:339
  29.3 1.3 %collective-permute-start.8 = (bf16[192,896]{1,0:T(8,128)(2,1)S(1)}, bf16[192,896]{1,0:T(8,128)(2,1)S(1)}, u32[]{:S(2)}, u32[]{:S(2)}) collective-permute-start(bf16[192,896]{1,0:T(8,128)(2,1)S(1)} %get-tuple-element.44), channel_id=1, source_target_pairs={{8,16},{9,17},{10,18},{11,19},{12,20},{13,21},{14,22},{15,23}} | collective-permute-start | bytes 1032200 | tf_op jit(solution)/shard_map/ppermute | solution.py:368
  30.6 1.3 %collective-permute-start.10 = (bf16[96,128]{1,0:T(8,128)(2,1)S(1)}, bf16[96,128]{1,0:T(8,128)(2,1)S(1)}, u32[]{:S(2)}, u32[]{:S(2)}) collective-permute-start(bf16[96,128]{1,0:T(8,128)(2,1)S(1)} %get-tuple-element.46), channel_id=1, source_target_pairs={{8,17},{9,16},{10,19},{11,18},{12,21},{13,20},{14,23},{15,22}} | collective-permute-start | bytes 73736 | tf_op jit(solution)/shard_map/ppermute | solution.py:368
  31.9 1.3 %collective-permute-start.11 = (bf16[96,128]{1,0:T(8,128)(2,1)S(1)}, bf16[96,128]{1,0:T(8,128)(2,1)S(1)}, u32[]{:S(2)}, u32[]{:S(2)}) collective-permute-start(bf16[96,128]{1,0:T(8,128)(2,1)S(1)} %get-tuple-element.47), channel_id=1, source_target_pairs={{8,20},{9,21},{10,22},{11,23},{12,16},{13,17},{14,18},{15,19}} | collective-permute-start | bytes 73736 | tf_op jit(solution)/shard_map/ppermute | solution.py:368
  33.2 0.7 %collective-permute-start.9 = (bf16[96,128]{1,0:T(8,128)(2,1)S(1)}, bf16[96,128]{1,0:T(8,128)(2,1)S(1)}, u32[]{:S(2)}, u32[]{:S(2)}) collective-permute-start(bf16[96,128]{1,0:T(8,128)(2,1)S(1)} %get-tuple-element.45), channel_id=1, source_target_pairs={{9,18},{10,17},{13,22},{14,21}} | collective-permute-start | bytes 73736 | tf_op jit(solution)/shard_map/ppermute | solution.py:368
  33.9 1.3 %collective-permute-start.13 = (bf16[192,896]{1,0:T(8,128)(2,1)S(1)}, bf16[192,896]{1,0:T(8,128)(2,1)S(1)}, u32[]{:S(2)}, u32[]{:S(2)}) collective-permute-start(bf16[192,896]{1,0:T(8,128)(2,1)S(1)} %get-tuple-element.49), channel_id=1, source_target_pairs={{8,16},{9,17},{10,18},{11,19},{12,20},{13,21},{14,22},{15,23}} | collective-permute-start | bytes 1032200 | tf_op jit(solution)/shard_map/ppermute | solution.py:368
  35.2 0.1 collective-permute-done.11.refs_8_.refs_6_
  35.3 1.3 %collective-permute-start.12 = (bf16[192,896]{1,0:T(8,128)(2,1)S(1)}, bf16[192,896]{1,0:T(8,128)(2,1)S(1)}, u32[]{:S(2)}, u32[]{:S(2)}) collective-permute-start(bf16[192,896]{1,0:T(8,128)(2,1)S(1)} %get-tuple-element.48), channel_id=1, source_target_pairs={{16,24},{17,25},{18,26},{19,27},{20,28},{21,29},{22,30},{23,31},{0... | collective-permute-start | bytes 1032200 | tf_op jit(solution)/shard_map/ppermute | solution.py:368
  36.6 0.7 %collective-permute-start.14 = (bf16[48,128]{1,0:T(8,128)(2,1)S(1)}, bf16[48,128]{1,0:T(8,128)(2,1)S(1)}, u32[]{:S(2)}, u32[]{:S(2)}) collective-permute-start(bf16[48,128]{1,0:T(8,128)(2,1)S(1)} %get-tuple-element.50), channel_id=1, source_target_pairs={{17,26},{18,25},{21,30},{22,29},{1,10},{2,9},{5,14},{6,13}} | collective-permute-start | bytes 36872 | tf_op jit(solution)/shard_map/ppermute | solution.py:368
  37.2 1.3 %collective-permute-start.15 = (bf16[48,128]{1,0:T(8,128)(2,1)S(1)}, bf16[48,128]{1,0:T(8,128)(2,1)S(1)}, u32[]{:S(2)}, u32[]{:S(2)}) collective-permute-start(bf16[48,128]{1,0:T(8,128)(2,1)S(1)} %get-tuple-element.51), channel_id=1, source_target_pairs={{16,25},{17,24},{18,27},{19,26},{20,29},{21,28},{22,31},{23,30},{0... | collective-permute-start | bytes 36872 | tf_op jit(solution)/shard_map/ppermute | solution.py:368
  38.5 1.3 %collective-permute-start.16 = (bf16[48,128]{1,0:T(8,128)(2,1)S(1)}, bf16[48,128]{1,0:T(8,128)(2,1)S(1)}, u32[]{:S(2)}, u32[]{:S(2)}) collective-permute-start(bf16[48,128]{1,0:T(8,128)(2,1)S(1)} %get-tuple-element.52), channel_id=1, source_target_pairs={{16,28},{17,29},{18,30},{19,31},{20,24},{21,25},{22,26},{23,27},{0... | collective-permute-start | bytes 36872 | tf_op jit(solution)/shard_map/ppermute | solution.py:368
  39.9 2.7 %collective-permute-done.15.refs_8_ = bf16[48,128]{1,0:T(8,128)(2,1)S(1)} collective-permute-done((bf16[48,128]{1,0:T(8,128)(2,1)S(1)}, bf16[48,128]{1,0:T(8,128)(2,1)S(1)}, u32[]{:S(2)}, u32[]{:S(2)}) %collective-permute-start.15) | collective-permute-done | bytes 12320 | tf_op jit(solution)/shard_map/ppermute | solution.py:368
  42.5 1.5 %collective-permute-done.16.refs_9_ = bf16[48,128]{1,0:T(8,128)(2,1)S(1)} collective-permute-done((bf16[48,128]{1,0:T(8,128)(2,1)S(1)}, bf16[48,128]{1,0:T(8,128)(2,1)S(1)}, u32[]{:S(2)}, u32[]{:S(2)}) %collective-permute-start.16) | collective-permute-done | bytes 12320 | tf_op jit(solution)/shard_map/ppermute | solution.py:368
  44.0 1.6 %shard_map.89 = bf16[192,896]{1,0:T(8,128)(2,1)} custom-call(bf16[4,192,128]{2,1,0:T(8,128)(2,1)S(1)} %get-tuple-element.31.refs_1_.live, bf16[4,192,896]{2,1,0:T(8,128)(2,1)S(1)} %get-tuple-element.32.starts.refs_0_, bf16[1024,896]{1,0:T(8,128)(2,1)S(1)} %shard_map.85.refs_2_.map_ext, f32[1,896]{1,0:T(1,128)S(1)} %bitcast.19, ...), custom_call_target="tpu_custom_call" | custom-call | tf_op jit(solution)/shard_map/pallas_call | solution.py:339
  (20 shorter events, 0.1 us)
Async XLA Ops:
  0.0 5.7 %copy-start = (bf16[1,1,1,896,896]{4,3,2,1,0:T(8,128)(2,1)S(1)}, bf16[1,1,1,896,896]{4,3,2,1,0:T(8,128)(2,1)}, u32[]{:S(2)}) copy-start(bf16[1,1,1,896,896]{4,3,2,1,0:T(8,128)(2,1)} %param.12) | copy-start | bytes 4816900
  0.0 5.8 %copy-start.3 = (bf16[1,192,1,1,896]{4,1,3,2,0:T(8,128)(2,1)S(1)}, bf16[1,192,1,1,896]{4,1,3,2,0:T(8,128)(2,1)}, u32[]{:S(2)}) copy-start(bf16[1,192,1,1,896]{4,1,3,2,0:T(8,128)(2,1)} %param.8) | copy-start | bytes 1032196
  3.8 9.8 %collective-permute-start = (bf16[1472,128]{1,0:T(8,128)(2,1)S(1)}, bf16[1472,128]{1,0:T(8,128)(2,1)S(1)}, u32[]{:S(2)}, u32[]{:S(2)}) collective-permute-start(bf16[1472,128]{1,0:T(8,128)(2,1)S(1)} %get-tuple-element.35), channel_id=1, source_target_pairs={{8,0},{9,1},{10,2},{11,3},{12,4},{13,5},{14,6},{15,7},{16,8},{17,9... | collective-permute-start | bytes 1130504 | tf_op jit(solution)/shard_map/ppermute | solution.py:368
  5.8 2.3 %copy-start.1 = (bf16[1,1,1,896,896]{4,3,2,1,0:T(8,128)(2,1)S(1)}, bf16[1,1,1,896,896]{4,3,2,1,0:T(8,128)(2,1)}, u32[]{:S(2)}) copy-start(bf16[1,1,1,896,896]{4,3,2,1,0:T(8,128)(2,1)} %param.13) | copy-start | bytes 4816900
  5.8 2.3 %copy-start.2 = (bf16[4,512,256]{2,1,0:T(8,128)(2,1)S(1)}, bf16[4,512,256]{2,1,0:T(8,128)(2,1)}, u32[]{:S(2)}) copy-start(bf16[4,512,256]{2,1,0:T(8,128)(2,1)} %constant.2.clone.band) | copy-start | bytes 3145732
  5.9 5.5 %collective-permute-start.1 = (bf16[192,128]{1,0:T(8,128)(2,1)S(1)}, bf16[192,128]{1,0:T(8,128)(2,1)S(1)}, u32[]{:S(2)}, u32[]{:S(2)}) collective-permute-start(bf16[192,128]{1,0:T(8,128)(2,1)S(1)} %get-tuple-element.37), channel_id=1, source_target_pairs={{1,2},{2,1},{5,6},{6,5}} | collective-permute-start | bytes 147464 | tf_op jit(solution)/shard_map/ppermute | solution.py:368
  6.7 4.7 %collective-permute-start.2 = (bf16[192,128]{1,0:T(8,128)(2,1)S(1)}, bf16[192,128]{1,0:T(8,128)(2,1)S(1)}, u32[]{:S(2)}, u32[]{:S(2)}) collective-permute-start(bf16[192,128]{1,0:T(8,128)(2,1)S(1)} %get-tuple-element.38), channel_id=1, source_target_pairs={{0,1},{1,0},{2,3},{3,2},{4,5},{5,4},{6,7},{7,6}} | collective-permute-start | bytes 147464 | tf_op jit(solution)/shard_map/ppermute | solution.py:368
  7.4 4.0 %collective-permute-start.3 = (bf16[192,128]{1,0:T(8,128)(2,1)S(1)}, bf16[192,128]{1,0:T(8,128)(2,1)S(1)}, u32[]{:S(2)}, u32[]{:S(2)}) collective-permute-start(bf16[192,128]{1,0:T(8,128)(2,1)S(1)} %get-tuple-element.39), channel_id=1, source_target_pairs={{0,4},{1,5},{2,6},{3,7},{4,0},{5,1},{6,2},{7,3}} | collective-permute-start | bytes 147464 | tf_op jit(solution)/shard_map/ppermute | solution.py:368
  8.1 5.5 %copy-start.4 = (f32[1,1,1,896]{3,2,1,0:T(1,128)S(1)}, f32[1,1,1,896]{3,2,1,0:T(1,128)}, u32[]{:S(2)}) copy-start(f32[1,1,1,896]{3,2,1,0:T(1,128)} %param.14) | copy-start | bytes 10756
  13.6 14.3 %collective-permute-start.4 = (bf16[384,896]{1,0:T(8,128)(2,1)S(1)}, bf16[384,896]{1,0:T(8,128)(2,1)S(1)}, u32[]{:S(2)}, u32[]{:S(2)}) collective-permute-start(bf16[384,896]{1,0:T(8,128)(2,1)S(1)} %get-tuple-element.40), channel_id=1, source_target_pairs={{0,8},{1,9},{2,10},{3,11},{4,12},{5,13},{6,14},{7,15}} | collective-permute-start | bytes 2064392 | tf_op jit(solution)/shard_map/ppermute | solution.py:368
  14.9 3.3 %collective-permute-start.5 = (bf16[96,128]{1,0:T(8,128)(2,1)S(1)}, bf16[96,128]{1,0:T(8,128)(2,1)S(1)}, u32[]{:S(2)}, u32[]{:S(2)}) collective-permute-start(bf16[96,128]{1,0:T(8,128)(2,1)S(1)} %get-tuple-element.41), channel_id=1, source_target_pairs={{1,10},{2,9},{5,14},{6,13}} | collective-permute-start | bytes 73736 | tf_op jit(solution)/shard_map/ppermute | solution.py:368
  15.6 10.3 %collective-permute-start.6 = (bf16[96,128]{1,0:T(8,128)(2,1)S(1)}, bf16[96,128]{1,0:T(8,128)(2,1)S(1)}, u32[]{:S(2)}, u32[]{:S(2)}) collective-permute-start(bf16[96,128]{1,0:T(8,128)(2,1)S(1)} %get-tuple-element.42), channel_id=1, source_target_pairs={{0,9},{1,8},{2,11},{3,10},{4,13},{5,12},{6,15},{7,14}} | collective-permute-start | bytes 73736 | tf_op jit(solution)/shard_map/ppermute | solution.py:368
  16.9 11.1 %collective-permute-start.7 = (bf16[96,128]{1,0:T(8,128)(2,1)S(1)}, bf16[96,128]{1,0:T(8,128)(2,1)S(1)}, u32[]{:S(2)}, u32[]{:S(2)}) collective-permute-start(bf16[96,128]{1,0:T(8,128)(2,1)S(1)} %get-tuple-element.43), channel_id=1, source_target_pairs={{0,12},{1,13},{2,14},{3,15},{4,8},{5,9},{6,10},{7,11}} | collective-permute-start | bytes 73736 | tf_op jit(solution)/shard_map/ppermute | solution.py:368
  29.3 6.0 %collective-permute-start.8 = (bf16[192,896]{1,0:T(8,128)(2,1)S(1)}, bf16[192,896]{1,0:T(8,128)(2,1)S(1)}, u32[]{:S(2)}, u32[]{:S(2)}) collective-permute-start(bf16[192,896]{1,0:T(8,128)(2,1)S(1)} %get-tuple-element.44), channel_id=1, source_target_pairs={{8,16},{9,17},{10,18},{11,19},{12,20},{13,21},{14,22},{15,23}} | collective-permute-start | bytes 1032200 | tf_op jit(solution)/shard_map/ppermute | solution.py:368
  30.6 4.6 %collective-permute-start.10 = (bf16[96,128]{1,0:T(8,128)(2,1)S(1)}, bf16[96,128]{1,0:T(8,128)(2,1)S(1)}, u32[]{:S(2)}, u32[]{:S(2)}) collective-permute-start(bf16[96,128]{1,0:T(8,128)(2,1)S(1)} %get-tuple-element.46), channel_id=1, source_target_pairs={{8,17},{9,16},{10,19},{11,18},{12,21},{13,20},{14,23},{15,22}} | collective-permute-start | bytes 73736 | tf_op jit(solution)/shard_map/ppermute | solution.py:368
  31.9 3.4 %collective-permute-start.11 = (bf16[96,128]{1,0:T(8,128)(2,1)S(1)}, bf16[96,128]{1,0:T(8,128)(2,1)S(1)}, u32[]{:S(2)}, u32[]{:S(2)}) collective-permute-start(bf16[96,128]{1,0:T(8,128)(2,1)S(1)} %get-tuple-element.47), channel_id=1, source_target_pairs={{8,20},{9,21},{10,22},{11,23},{12,16},{13,17},{14,18},{15,19}} | collective-permute-start | bytes 73736 | tf_op jit(solution)/shard_map/ppermute | solution.py:368
  33.2 2.1 %collective-permute-start.9 = (bf16[96,128]{1,0:T(8,128)(2,1)S(1)}, bf16[96,128]{1,0:T(8,128)(2,1)S(1)}, u32[]{:S(2)}, u32[]{:S(2)}) collective-permute-start(bf16[96,128]{1,0:T(8,128)(2,1)S(1)} %get-tuple-element.45), channel_id=1, source_target_pairs={{9,18},{10,17},{13,22},{14,21}} | collective-permute-start | bytes 73736 | tf_op jit(solution)/shard_map/ppermute | solution.py:368
  33.9 6.0 %collective-permute-start.13 = (bf16[192,896]{1,0:T(8,128)(2,1)S(1)}, bf16[192,896]{1,0:T(8,128)(2,1)S(1)}, u32[]{:S(2)}, u32[]{:S(2)}) collective-permute-start(bf16[192,896]{1,0:T(8,128)(2,1)S(1)} %get-tuple-element.49), channel_id=1, source_target_pairs={{8,16},{9,17},{10,18},{11,19},{12,20},{13,21},{14,22},{15,23}} | collective-permute-start | bytes 1032200 | tf_op jit(solution)/shard_map/ppermute | solution.py:368
  35.3 8.7 %collective-permute-start.12 = (bf16[192,896]{1,0:T(8,128)(2,1)S(1)}, bf16[192,896]{1,0:T(8,128)(2,1)S(1)}, u32[]{:S(2)}, u32[]{:S(2)}) collective-permute-start(bf16[192,896]{1,0:T(8,128)(2,1)S(1)} %get-tuple-element.48), channel_id=1, source_target_pairs={{16,24},{17,25},{18,26},{19,27},{20,28},{21,29},{22,30},{23,31},{0... | collective-permute-start | bytes 1032200 | tf_op jit(solution)/shard_map/ppermute | solution.py:368
  36.6 3.3 %collective-permute-start.14 = (bf16[48,128]{1,0:T(8,128)(2,1)S(1)}, bf16[48,128]{1,0:T(8,128)(2,1)S(1)}, u32[]{:S(2)}, u32[]{:S(2)}) collective-permute-start(bf16[48,128]{1,0:T(8,128)(2,1)S(1)} %get-tuple-element.50), channel_id=1, source_target_pairs={{17,26},{18,25},{21,30},{22,29},{1,10},{2,9},{5,14},{6,13}} | collective-permute-start | bytes 36872 | tf_op jit(solution)/shard_map/ppermute | solution.py:368
  37.2 5.3 %collective-permute-start.15 = (bf16[48,128]{1,0:T(8,128)(2,1)S(1)}, bf16[48,128]{1,0:T(8,128)(2,1)S(1)}, u32[]{:S(2)}, u32[]{:S(2)}) collective-permute-start(bf16[48,128]{1,0:T(8,128)(2,1)S(1)} %get-tuple-element.51), channel_id=1, source_target_pairs={{16,25},{17,24},{18,27},{19,26},{20,29},{21,28},{22,31},{23,30},{0... | collective-permute-start | bytes 36872 | tf_op jit(solution)/shard_map/ppermute | solution.py:368
  38.5 5.5 %collective-permute-start.16 = (bf16[48,128]{1,0:T(8,128)(2,1)S(1)}, bf16[48,128]{1,0:T(8,128)(2,1)S(1)}, u32[]{:S(2)}, u32[]{:S(2)}) collective-permute-start(bf16[48,128]{1,0:T(8,128)(2,1)S(1)} %get-tuple-element.52), channel_id=1, source_target_pairs={{16,28},{17,29},{18,30},{19,31},{20,24},{21,25},{22,26},{23,27},{0... | collective-permute-start | bytes 36872 | tf_op jit(solution)/shard_map/ppermute | solution.py:368

commit v9 on v8

--- a/solution.py
+++ b/solution.py
@@ -27,29 +27,28 @@
     return lax.dot_general(a, b, (((0,), (0,)), ((), ())), preferred_element_type=jnp.float32)
 
 
+def group_at(lane):
+    return lax.shift_right_logical(lane, GROUP.bit_length() - 1)
+
+
+def edge_cells_of(lane):
+    group, spot = group_at(lane), lane & (GROUP - 1)
+    along_y = jnp.where(group == 0, spot, spot + (FX - 1) * FY)
+    along_x = jnp.where(group == 2, spot * FY, spot * FY + FY - 1)
+    cell = jnp.where(group < 2, along_y, along_x)
+    return jnp.where(spot < jnp.where(group < 2, FY, FX), cell, -1)
+
+
 def edge_selector(cells):
+    cell = edge_cells_of(lax.broadcasted_iota(jnp.int32, (1, LANES), 1))
     row = lax.broadcasted_iota(jnp.int32, (cells, LANES), 0)
-    lane = lax.broadcasted_iota(jnp.int32, (cells, LANES), 1)
-    return select_edges(row, lane)
-
-
-def select_edges(row, lane):
-    group = lane // GROUP
-    spot = lane % GROUP
-    along_x = group < 2
-    cell = jnp.where(
-        along_x,
-        jnp.where(group == 0, spot, (FX - 1) * FY + spot),
-        jnp.where(group == 2, spot * FY, spot * FY + FY - 1),
-    )
-    length = jnp.where(along_x, FY, FX)
-    return jnp.where((row == cell) & (spot < length), 1.0, 0.0).astype(jnp.bfloat16)
+    return jnp.where(row == cell, 1.0, 0.0).astype(jnp.bfloat16)
 
 
 def edge_rows_selector(cells):
-    lane = lax.broadcasted_iota(jnp.int32, (LANES, cells), 0)
+    cell = edge_cells_of(lax.broadcasted_iota(jnp.int32, (LANES, 1), 0))
     row = lax.broadcasted_iota(jnp.int32, (LANES, cells), 1)
-    return select_edges(row, lane)
+    return jnp.where(row == cell, 1.0, 0.0).astype(jnp.bfloat16)
 
 
 def exchanges():
@@ -61,26 +60,26 @@
 
 
 def group_of(axis, parity, base):
-    ahead = lax.axis_index(axis) % 2 == parity
+    ahead = (lax.axis_index(axis) & 1) == parity
     return jnp.where(ahead, base + 1, base)
 
 
 def pack(edges, group):
     rows = edges.shape[0] // 4
-    lane_group = lax.broadcasted_iota(jnp.int32, (rows, LANES), 1) // GROUP
+    lane_group = group_at(lax.broadcasted_iota(jnp.int32, (rows, LANES), 1))
     packed = jnp.zeros((rows, LANES), jnp.float32)
     for part in range(4):
         piece = edges[part * rows : (part + 1) * rows]
-        piece = pltpu.roll(piece, (part - group + 4) % 4 * GROUP, 1)
+        piece = pltpu.roll(piece, ((part - group) & 3) * GROUP, 1)
         packed = jnp.where(lane_group == part, piece, packed)
     return packed.astype(jnp.bfloat16)
 
 
 def unpack(packed, group):
-    lane_group = lax.broadcasted_iota(jnp.int32, packed.shape, 1) // GROUP
+    lane_group = group_at(lax.broadcasted_iota(jnp.int32, packed.shape, 1))
     pieces = []
     for part in range(4):
-        piece = pltpu.roll(packed, (group - part + 4) % 4 * GROUP, 1)
+        piece = pltpu.roll(packed, ((group - part) & 3) * GROUP, 1)
         pieces.append(jnp.where(lane_group == group, piece, 0.0))
     return jnp.concatenate(pieces, axis=0)
 
@@ -96,8 +95,8 @@
     live = jnp.zeros((1, slots), jnp.int32)
     for batch in range(slots // SHOT_BATCH):
         count = counts_in[unit_of(round_number), 0, 0, batch]
-        live = jnp.where(slot // SHOT_BATCH == batch, count, live)
-    wanted = jnp.where(slot % SHOT_BATCH < live, wanted, -1)
+        live = jnp.where(slot >= batch * SHOT_BATCH, count + batch * SHOT_BATCH, live)
+    wanted = jnp.where(slot < live, wanted, -1)
     return jnp.where(shot == wanted, 1.0, 0.0).astype(jnp.bfloat16)
 
 
@@ -253,8 +252,7 @@
     return (halo * live.astype(jnp.float32)).astype(jnp.bfloat16)
 
 
-def blend(image, start, damping):
-    damp = damping[...]
+def blend(image, start, damp):
     return (damp * image + (1.0 - damp) * start.astype(jnp.float32)).astype(jnp.bfloat16)
 
 
@@ -291,7 +289,7 @@
             start = start.astype(jnp.float32) + traces[...].astype(jnp.float32)
             start = start.astype(jnp.bfloat16)
             image = dot(jnp.concatenate([start, halo], axis=1), map_ext[...])
-        ended = blend(image, start, damping)
+        ended = blend(image, start, damping[...])
         going = traces_out.shape[0]
         traces_out[...] = ended[:going]
         if keeps:
@@ -308,7 +306,8 @@
 
 def final_kernel(swaps, picks, others, live, starts, map_ext, damping, traces, *refs):
     slots, cells = traces.shape
-    kept, received, (traces_out, row) = refs[:others], refs[others:-2], refs[-2:]
+    kept, received = refs[:others], refs[others:-4]
+    traces_out, row, ended, sems = refs[-4:]
     part = slots // 4
     layer = lax.axis_index("depth")
     start = starts[starts.shape[0] - 1].astype(jnp.float32) + traces[...].astype(jnp.float32)
@@ -326,11 +325,20 @@
         by_rule = by_rule | (layer == at)
         pl.when(layer == at)(functools.partial(take, phase))
     pl.when(jnp.logical_not(by_rule))(functools.partial(take, len(received) // len(swaps) - 1))
-    image = dot(row[...], map_ext[...])
-    traces_out[...] = blend(image, row[:, :cells], damping)
-
-
-def call(kernel, out_shape, operands, in_hbm=(), scratch=(), aliases=None):
+    copies = []
+    half = cells // LANES // 2 * LANES
+    for at, columns in enumerate([slice(0, half), slice(half, cells)]):
+        image = dot(row[...], map_ext[:, columns])
+        ended[:, columns] = blend(image, row[:, columns], damping[:, columns])
+        copies.append(
+            pltpu.make_async_copy(ended.at[:, columns], traces_out.at[:, columns], sems.at[at])
+        )
+        copies[-1].start()
+    for copy in copies:
+        copy.wait()
+
+
+def call(kernel, out_shape, operands, in_hbm=(), scratch=(), aliases=None, to_hbm=False):
     spaces = [pltpu.HBM if i in in_hbm else pltpu.VMEM for i in range(len(operands))]
     operands = [
         pltpu.with_memory_space_constraint(x, pltpu.HBM) if i in in_hbm else x
@@ -340,7 +348,7 @@
         kernel,
         out_shape=out_shape,
         in_specs=[pl.BlockSpec(memory_space=space) for space in spaces],
-        out_specs=[pl.BlockSpec(memory_space=pltpu.VMEM)] * len(out_shape),
+        out_specs=[pl.BlockSpec(memory_space=pl.ANY if to_hbm else pltpu.VMEM)] * len(out_shape),
         scratch_shapes=scratch,
         input_output_aliases=aliases or {},
         compiler_params=pltpu.CompilerParams(vmem_limit_bytes=32 * 1024 * 1024),
@@ -457,7 +465,12 @@
         functools.partial(final_kernel, swaps, picks, len(kept)),
         [array(slots, cells)],
         [live, starts, map_ext, damping, traces] + kept + arrived,
-        scratch=[pltpu.VMEM((slots, cells + LANES), jnp.bfloat16)],
+        scratch=[
+            pltpu.VMEM((slots, cells + LANES), jnp.bfloat16),
+            scratch(arrival),
+            pltpu.SemaphoreType.DMA((2,)),
+        ],
+        to_hbm=True,
     )
     return ended.reshape(1, slots, 1, 1, cells)
 

time: 46 us -> 46.1 us (level)
  transfers between devices with their start and end apart: 17 -> 17, of which waited for: 6 -> 6; matrix products, arithmetic and copies ran while one was open for 0% -> 0% of each run, Pallas kernels for 8% -> 7%
where the time goes in v9:
time: 46.1 us; the launch traced here: 45.7 us
  starting transfers between devices  19 us (41%)
  waiting for transfers between devices  16.2 us (35%)
  Pallas kernels  10 us (22%)
    ppermute x17, starting transfers between devices, send(): return lax.ppermute(x, MESH_AXES, pairs)  19 us
    ppermute x17, waiting for transfers between devices, send(): return lax.ppermute(x, MESH_AXES, pairs)  16.2 us
    pallas_call x8, Pallas kernels, call(): pl.pallas_call(kernel, out_shape=out_shape, in_specs=[pl.BlockSpec(memory...  10 us
  transfers between devices with their start and end apart: 17, of which 6 were waited for; matrix products, arithmetic and copies ran while one was open for 0% of the time, Pallas kernels for 7%

profile of v9, /device:TPU:1, one launch (start us, length us, event | category | flops | bytes accessed | tf_op | source)
XLA Modules:
  0.0 45.7 jit_solution(16680358997213013658)
XLA Ops:
  0.0 3.8 %shard_map.82 = (bf16[1472,128]{1,0:T(8,128)(2,1)S(1)}, bf16[4,192,896]{2,1,0:T(8,128)(2,1)S(1)}, bf16[4,192,128]{2,1,0:T(8,128)(2,1)S(1)}) custom-call(bf16[4,192,896]{2,1,0:T(8,128)(2,1)} %bitcast.20, s32[4,192]{1,0:T(4,128)} %assignment.3, s32[7,1,1,12]{3,2,1,0:T(1,128)} %bitcast.22, bf16[896,896]{1,0:T(8,128)(2,1)} %bitcast.9), custom_call_target="tpu_custom_call" | custom-call | tf_op jit(solution)/shard_map/pallas_call | solution.py:347
  3.8 1.9 %collective-permute-start = (bf16[1472,128]{1,0:T(8,128)(2,1)S(1)}, bf16[1472,128]{1,0:T(8,128)(2,1)S(1)}, u32[]{:S(2)}, u32[]{:S(2)}) collective-permute-start(bf16[1472,128]{1,0:T(8,128)(2,1)S(1)} %get-tuple-element.35), channel_id=1, source_target_pairs={{8,0},{9,1},{10,2},{11,3},{12,4},{13,5},{14,6},{15,7},{16,8},{17,9... | collective-permute-start | bytes 1130504 | tf_op jit(solution)/shard_map/ppermute | solution.py:376
  5.8 0.0 copy-start.1
  5.8 0.0 copy-start.2
  5.8 0.1 shard_map.83
  5.9 0.8 %collective-permute-start.1 = (bf16[192,128]{1,0:T(8,128)(2,1)S(1)}, bf16[192,128]{1,0:T(8,128)(2,1)S(1)}, u32[]{:S(2)}, u32[]{:S(2)}) collective-permute-start(bf16[192,128]{1,0:T(8,128)(2,1)S(1)} %get-tuple-element.37), channel_id=1, source_target_pairs={{1,2},{2,1},{5,6},{6,5}} | collective-permute-start | bytes 147464 | tf_op jit(solution)/shard_map/ppermute | solution.py:376
  6.7 0.7 %collective-permute-start.2 = (bf16[192,128]{1,0:T(8,128)(2,1)S(1)}, bf16[192,128]{1,0:T(8,128)(2,1)S(1)}, u32[]{:S(2)}, u32[]{:S(2)}) collective-permute-start(bf16[192,128]{1,0:T(8,128)(2,1)S(1)} %get-tuple-element.38), channel_id=1, source_target_pairs={{0,1},{1,0},{2,3},{3,2},{4,5},{5,4},{6,7},{7,6}} | collective-permute-start | bytes 147464 | tf_op jit(solution)/shard_map/ppermute | solution.py:376
  7.4 0.7 %collective-permute-start.3 = (bf16[192,128]{1,0:T(8,128)(2,1)S(1)}, bf16[192,128]{1,0:T(8,128)(2,1)S(1)}, u32[]{:S(2)}, u32[]{:S(2)}) collective-permute-start(bf16[192,128]{1,0:T(8,128)(2,1)S(1)} %get-tuple-element.39), channel_id=1, source_target_pairs={{0,4},{1,5},{2,6},{3,7},{4,0},{5,1},{6,2},{7,3}} | collective-permute-start | bytes 147464 | tf_op jit(solution)/shard_map/ppermute | solution.py:376
  8.1 0.0 copy-start.4
  8.1 3.3 %shard_map.84 = (f32[384,896]{1,0:T(8,128)S(1)}, bf16[1024,896]{1,0:T(8,128)(2,1)S(1)}) custom-call(bf16[4,192,896]{2,1,0:T(8,128)(2,1)S(1)} %get-tuple-element.32.starts.refs_0_, bf16[896,896]{1,0:T(8,128)(2,1)S(1)} %bitcast.11, bf16[4,512,256]{2,1,0:T(8,128)(2,1)S(1)} %copy-done.2, bf16[896,896]{1,0:T(8,128)(2,1)S(1)} %bitcast.13, ...), custom_call_target="tpu_custom_call" | custom-call | tf_op jit(solution)/shard_map/pallas_call | solution.py:347
  11.4 0.0 collective-permute-done.1.refs_6_.refs_9_.refs_1_
  11.4 2.2 %collective-permute-done.refs_4_ = bf16[1472,128]{1,0:T(8,128)(2,1)S(1)} collective-permute-done((bf16[1472,128]{1,0:T(8,128)(2,1)S(1)}, bf16[1472,128]{1,0:T(8,128)(2,1)S(1)}, u32[]{:S(2)}, u32[]{:S(2)}) %collective-permute-start) | collective-permute-done | bytes 376864 | tf_op jit(solution)/shard_map/ppermute | solution.py:376
  13.6 1.3 %collective-permute-start.4 = (bf16[384,896]{1,0:T(8,128)(2,1)S(1)}, bf16[384,896]{1,0:T(8,128)(2,1)S(1)}, u32[]{:S(2)}, u32[]{:S(2)}) collective-permute-start(bf16[384,896]{1,0:T(8,128)(2,1)S(1)} %get-tuple-element.40), channel_id=1, source_target_pairs={{0,8},{1,9},{2,10},{3,11},{4,12},{5,13},{6,14},{7,15}} | collective-permute-start | bytes 2064392 | tf_op jit(solution)/shard_map/ppermute | solution.py:376
  14.9 0.7 %collective-permute-start.5 = (bf16[96,128]{1,0:T(8,128)(2,1)S(1)}, bf16[96,128]{1,0:T(8,128)(2,1)S(1)}, u32[]{:S(2)}, u32[]{:S(2)}) collective-permute-start(bf16[96,128]{1,0:T(8,128)(2,1)S(1)} %get-tuple-element.41), channel_id=1, source_target_pairs={{1,10},{2,9},{5,14},{6,13}} | collective-permute-start | bytes 73736 | tf_op jit(solution)/shard_map/ppermute | solution.py:376
  15.6 1.3 %collective-permute-start.6 = (bf16[96,128]{1,0:T(8,128)(2,1)S(1)}, bf16[96,128]{1,0:T(8,128)(2,1)S(1)}, u32[]{:S(2)}, u32[]{:S(2)}) collective-permute-start(bf16[96,128]{1,0:T(8,128)(2,1)S(1)} %get-tuple-element.42), channel_id=1, source_target_pairs={{0,9},{1,8},{2,11},{3,10},{4,13},{5,12},{6,15},{7,14}} | collective-permute-start | bytes 73736 | tf_op jit(solution)/shard_map/ppermute | solution.py:376
  16.9 1.3 %collective-permute-start.7 = (bf16[96,128]{1,0:T(8,128)(2,1)S(1)}, bf16[96,128]{1,0:T(8,128)(2,1)S(1)}, u32[]{:S(2)}, u32[]{:S(2)}) collective-permute-start(bf16[96,128]{1,0:T(8,128)(2,1)S(1)} %get-tuple-element.43), channel_id=1, source_target_pairs={{0,12},{1,13},{2,14},{3,15},{4,8},{5,9},{6,10},{7,11}} | collective-permute-start | bytes 73736 | tf_op jit(solution)/shard_map/ppermute | solution.py:376
  18.2 7.7 %collective-permute-done.6.refs_7_ = bf16[96,128]{1,0:T(8,128)(2,1)S(1)} collective-permute-done((bf16[96,128]{1,0:T(8,128)(2,1)S(1)}, bf16[96,128]{1,0:T(8,128)(2,1)S(1)}, u32[]{:S(2)}, u32[]{:S(2)}) %collective-permute-start.6) | collective-permute-done | bytes 24608 | tf_op jit(solution)/shard_map/ppermute | solution.py:376
  25.9 2.1 %collective-permute-done.7.refs_8_ = bf16[96,128]{1,0:T(8,128)(2,1)S(1)} collective-permute-done((bf16[96,128]{1,0:T(8,128)(2,1)S(1)}, bf16[96,128]{1,0:T(8,128)(2,1)S(1)}, u32[]{:S(2)}, u32[]{:S(2)}) %collective-permute-start.7) | collective-permute-done | bytes 24608 | tf_op jit(solution)/shard_map/ppermute | solution.py:376
  27.9 1.3 %shard_map.87 = (bf16[192,896]{1,0:T(8,128)(2,1)S(1)}, bf16[192,896]{1,0:T(8,128)(2,1)S(1)}, bf16[96,128]{1,0:T(8,128)(2,1)S(1)}, bf16[96,128]{1,0:T(8,128)(2,1)S(1)}, bf16[96,128]{1,0:T(8,128)(2,1)S(1)}) custom-call(bf16[4,192,896]{2,1,0:T(8,128)(2,1)S(1)} %get-tuple-element.32.starts.refs_0_, bf16[4,192,128]{2,1,0:T(8,128)(2,1)S(1)} %get-tuple-element.31.refs_1_.live, ...), custom_call_target="tpu_custom_call" | custom-call | tf_op jit(solution)/shard_map/pallas_call | solution.py:347
  29.3 1.3 %collective-permute-start.8 = (bf16[192,896]{1,0:T(8,128)(2,1)S(1)}, bf16[192,896]{1,0:T(8,128)(2,1)S(1)}, u32[]{:S(2)}, u32[]{:S(2)}) collective-permute-start(bf16[192,896]{1,0:T(8,128)(2,1)S(1)} %get-tuple-element.44), channel_id=1, source_target_pairs={{8,16},{9,17},{10,18},{11,19},{12,20},{13,21},{14,22},{15,23}} | collective-permute-start | bytes 1032200 | tf_op jit(solution)/shard_map/ppermute | solution.py:376
  30.6 1.3 %collective-permute-start.10 = (bf16[96,128]{1,0:T(8,128)(2,1)S(1)}, bf16[96,128]{1,0:T(8,128)(2,1)S(1)}, u32[]{:S(2)}, u32[]{:S(2)}) collective-permute-start(bf16[96,128]{1,0:T(8,128)(2,1)S(1)} %get-tuple-element.46), channel_id=1, source_target_pairs={{8,17},{9,16},{10,19},{11,18},{12,21},{13,20},{14,23},{15,22}} | collective-permute-start | bytes 73736 | tf_op jit(solution)/shard_map/ppermute | solution.py:376
  31.9 1.3 %collective-permute-start.11 = (bf16[96,128]{1,0:T(8,128)(2,1)S(1)}, bf16[96,128]{1,0:T(8,128)(2,1)S(1)}, u32[]{:S(2)}, u32[]{:S(2)}) collective-permute-start(bf16[96,128]{1,0:T(8,128)(2,1)S(1)} %get-tuple-element.47), channel_id=1, source_target_pairs={{8,20},{9,21},{10,22},{11,23},{12,16},{13,17},{14,18},{15,19}} | collective-permute-start | bytes 73736 | tf_op jit(solution)/shard_map/ppermute | solution.py:376
  33.2 0.7 %collective-permute-start.9 = (bf16[96,128]{1,0:T(8,128)(2,1)S(1)}, bf16[96,128]{1,0:T(8,128)(2,1)S(1)}, u32[]{:S(2)}, u32[]{:S(2)}) collective-permute-start(bf16[96,128]{1,0:T(8,128)(2,1)S(1)} %get-tuple-element.45), channel_id=1, source_target_pairs={{9,18},{10,17},{13,22},{14,21}} | collective-permute-start | bytes 73736 | tf_op jit(solution)/shard_map/ppermute | solution.py:376
  33.8 1.3 %collective-permute-start.13 = (bf16[192,896]{1,0:T(8,128)(2,1)S(1)}, bf16[192,896]{1,0:T(8,128)(2,1)S(1)}, u32[]{:S(2)}, u32[]{:S(2)}) collective-permute-start(bf16[192,896]{1,0:T(8,128)(2,1)S(1)} %get-tuple-element.49), channel_id=1, source_target_pairs={{8,16},{9,17},{10,18},{11,19},{12,20},{13,21},{14,22},{15,23}} | collective-permute-start | bytes 1032200 | tf_op jit(solution)/shard_map/ppermute | solution.py:376
  35.2 0.1 collective-permute-done.11.refs_8_.refs_6_
  35.3 1.3 %collective-permute-start.12 = (bf16[192,896]{1,0:T(8,128)(2,1)S(1)}, bf16[192,896]{1,0:T(8,128)(2,1)S(1)}, u32[]{:S(2)}, u32[]{:S(2)}) collective-permute-start(bf16[192,896]{1,0:T(8,128)(2,1)S(1)} %get-tuple-element.48), channel_id=1, source_target_pairs={{16,24},{17,25},{18,26},{19,27},{20,28},{21,29},{22,30},{23,31},{0... | collective-permute-start | bytes 1032200 | tf_op jit(solution)/shard_map/ppermute | solution.py:376
  36.6 0.7 %collective-permute-start.14 = (bf16[48,128]{1,0:T(8,128)(2,1)S(1)}, bf16[48,128]{1,0:T(8,128)(2,1)S(1)}, u32[]{:S(2)}, u32[]{:S(2)}) collective-permute-start(bf16[48,128]{1,0:T(8,128)(2,1)S(1)} %get-tuple-element.50), channel_id=1, source_target_pairs={{17,26},{18,25},{21,30},{22,29},{1,10},{2,9},{5,14},{6,13}} | collective-permute-start | bytes 36872 | tf_op jit(solution)/shard_map/ppermute | solution.py:376
  37.2 1.3 %collective-permute-start.15 = (bf16[48,128]{1,0:T(8,128)(2,1)S(1)}, bf16[48,128]{1,0:T(8,128)(2,1)S(1)}, u32[]{:S(2)}, u32[]{:S(2)}) collective-permute-start(bf16[48,128]{1,0:T(8,128)(2,1)S(1)} %get-tuple-element.51), channel_id=1, source_target_pairs={{16,25},{17,24},{18,27},{19,26},{20,29},{21,28},{22,31},{23,30},{0... | collective-permute-start | bytes 36872 | tf_op jit(solution)/shard_map/ppermute | solution.py:376
  38.5 1.3 %collective-permute-start.16 = (bf16[48,128]{1,0:T(8,128)(2,1)S(1)}, bf16[48,128]{1,0:T(8,128)(2,1)S(1)}, u32[]{:S(2)}, u32[]{:S(2)}) collective-permute-start(bf16[48,128]{1,0:T(8,128)(2,1)S(1)} %get-tuple-element.52), channel_id=1, source_target_pairs={{16,28},{17,29},{18,30},{19,31},{20,24},{21,25},{22,26},{23,27},{0... | collective-permute-start | bytes 36872 | tf_op jit(solution)/shard_map/ppermute | solution.py:376
  39.8 2.7 %collective-permute-done.15.refs_8_ = bf16[48,128]{1,0:T(8,128)(2,1)S(1)} collective-permute-done((bf16[48,128]{1,0:T(8,128)(2,1)S(1)}, bf16[48,128]{1,0:T(8,128)(2,1)S(1)}, u32[]{:S(2)}, u32[]{:S(2)}) %collective-permute-start.15) | collective-permute-done | bytes 12320 | tf_op jit(solution)/shard_map/ppermute | solution.py:376
  42.5 1.5 %collective-permute-done.16.refs_9_ = bf16[48,128]{1,0:T(8,128)(2,1)S(1)} collective-permute-done((bf16[48,128]{1,0:T(8,128)(2,1)S(1)}, bf16[48,128]{1,0:T(8,128)(2,1)S(1)}, u32[]{:S(2)}, u32[]{:S(2)}) %collective-permute-start.16) | collective-permute-done | bytes 12320 | tf_op jit(solution)/shard_map/ppermute | solution.py:376
  44.0 1.5 %shard_map.89 = bf16[192,896]{1,0:T(8,128)(2,1)} custom-call(bf16[4,192,128]{2,1,0:T(8,128)(2,1)S(1)} %get-tuple-element.31.refs_1_.live, bf16[4,192,896]{2,1,0:T(8,128)(2,1)S(1)} %get-tuple-element.32.starts.refs_0_, bf16[1024,896]{1,0:T(8,128)(2,1)S(1)} %shard_map.85.refs_2_.map_ext, f32[1,896]{1,0:T(1,128)S(1)} %bitcast.19, ...), custom_call_target="tpu_custom_call" | custom-call | tf_op jit(solution)/shard_map/pallas_call | solution.py:347
  (20 shorter events, 0.1 us)
Async XLA Ops:
  0.0 5.7 %copy-start = (bf16[1,1,1,896,896]{4,3,2,1,0:T(8,128)(2,1)S(1)}, bf16[1,1,1,896,896]{4,3,2,1,0:T(8,128)(2,1)}, u32[]{:S(2)}) copy-start(bf16[1,1,1,896,896]{4,3,2,1,0:T(8,128)(2,1)} %param.12) | copy-start | bytes 4816900
  0.0 5.8 %copy-start.3 = (bf16[1,192,1,1,896]{4,1,3,2,0:T(8,128)(2,1)S(1)}, bf16[1,192,1,1,896]{4,1,3,2,0:T(8,128)(2,1)}, u32[]{:S(2)}) copy-start(bf16[1,192,1,1,896]{4,1,3,2,0:T(8,128)(2,1)} %param.8) | copy-start | bytes 1032196
  3.8 9.8 %collective-permute-start = (bf16[1472,128]{1,0:T(8,128)(2,1)S(1)}, bf16[1472,128]{1,0:T(8,128)(2,1)S(1)}, u32[]{:S(2)}, u32[]{:S(2)}) collective-permute-start(bf16[1472,128]{1,0:T(8,128)(2,1)S(1)} %get-tuple-element.35), channel_id=1, source_target_pairs={{8,0},{9,1},{10,2},{11,3},{12,4},{13,5},{14,6},{15,7},{16,8},{17,9... | collective-permute-start | bytes 1130504 | tf_op jit(solution)/shard_map/ppermute | solution.py:376
  5.8 2.3 %copy-start.1 = (bf16[1,1,1,896,896]{4,3,2,1,0:T(8,128)(2,1)S(1)}, bf16[1,1,1,896,896]{4,3,2,1,0:T(8,128)(2,1)}, u32[]{:S(2)}) copy-start(bf16[1,1,1,896,896]{4,3,2,1,0:T(8,128)(2,1)} %param.13) | copy-start | bytes 4816900
  5.8 2.3 %copy-start.2 = (bf16[4,512,256]{2,1,0:T(8,128)(2,1)S(1)}, bf16[4,512,256]{2,1,0:T(8,128)(2,1)}, u32[]{:S(2)}) copy-start(bf16[4,512,256]{2,1,0:T(8,128)(2,1)} %constant.2.clone.band) | copy-start | bytes 3145732
  5.9 5.5 %collective-permute-start.1 = (bf16[192,128]{1,0:T(8,128)(2,1)S(1)}, bf16[192,128]{1,0:T(8,128)(2,1)S(1)}, u32[]{:S(2)}, u32[]{:S(2)}) collective-permute-start(bf16[192,128]{1,0:T(8,128)(2,1)S(1)} %get-tuple-element.37), channel_id=1, source_target_pairs={{1,2},{2,1},{5,6},{6,5}} | collective-permute-start | bytes 147464 | tf_op jit(solution)/shard_map/ppermute | solution.py:376
  6.7 4.7 %collective-permute-start.2 = (bf16[192,128]{1,0:T(8,128)(2,1)S(1)}, bf16[192,128]{1,0:T(8,128)(2,1)S(1)}, u32[]{:S(2)}, u32[]{:S(2)}) collective-permute-start(bf16[192,128]{1,0:T(8,128)(2,1)S(1)} %get-tuple-element.38), channel_id=1, source_target_pairs={{0,1},{1,0},{2,3},{3,2},{4,5},{5,4},{6,7},{7,6}} | collective-permute-start | bytes 147464 | tf_op jit(solution)/shard_map/ppermute | solution.py:376
  7.4 4.0 %collective-permute-start.3 = (bf16[192,128]{1,0:T(8,128)(2,1)S(1)}, bf16[192,128]{1,0:T(8,128)(2,1)S(1)}, u32[]{:S(2)}, u32[]{:S(2)}) collective-permute-start(bf16[192,128]{1,0:T(8,128)(2,1)S(1)} %get-tuple-element.39), channel_id=1, source_target_pairs={{0,4},{1,5},{2,6},{3,7},{4,0},{5,1},{6,2},{7,3}} | collective-permute-start | bytes 147464 | tf_op jit(solution)/shard_map/ppermute | solution.py:376
  8.1 5.5 %copy-start.4 = (f32[1,1,1,896]{3,2,1,0:T(1,128)S(1)}, f32[1,1,1,896]{3,2,1,0:T(1,128)}, u32[]{:S(2)}) copy-start(f32[1,1,1,896]{3,2,1,0:T(1,128)} %param.14) | copy-start | bytes 10756
  13.6 14.3 %collective-permute-start.4 = (bf16[384,896]{1,0:T(8,128)(2,1)S(1)}, bf16[384,896]{1,0:T(8,128)(2,1)S(1)}, u32[]{:S(2)}, u32[]{:S(2)}) collective-permute-start(bf16[384,896]{1,0:T(8,128)(2,1)S(1)} %get-tuple-element.40), channel_id=1, source_target_pairs={{0,8},{1,9},{2,10},{3,11},{4,12},{5,13},{6,14},{7,15}} | collective-permute-start | bytes 2064392 | tf_op jit(solution)/shard_map/ppermute | solution.py:376
  14.9 3.3 %collective-permute-start.5 = (bf16[96,128]{1,0:T(8,128)(2,1)S(1)}, bf16[96,128]{1,0:T(8,128)(2,1)S(1)}, u32[]{:S(2)}, u32[]{:S(2)}) collective-permute-start(bf16[96,128]{1,0:T(8,128)(2,1)S(1)} %get-tuple-element.41), channel_id=1, source_target_pairs={{1,10},{2,9},{5,14},{6,13}} | collective-permute-start | bytes 73736 | tf_op jit(solution)/shard_map/ppermute | solution.py:376
  15.6 10.3 %collective-permute-start.6 = (bf16[96,128]{1,0:T(8,128)(2,1)S(1)}, bf16[96,128]{1,0:T(8,128)(2,1)S(1)}, u32[]{:S(2)}, u32[]{:S(2)}) collective-permute-start(bf16[96,128]{1,0:T(8,128)(2,1)S(1)} %get-tuple-element.42), channel_id=1, source_target_pairs={{0,9},{1,8},{2,11},{3,10},{4,13},{5,12},{6,15},{7,14}} | collective-permute-start | bytes 73736 | tf_op jit(solution)/shard_map/ppermute | solution.py:376
  16.9 11.1 %collective-permute-start.7 = (bf16[96,128]{1,0:T(8,128)(2,1)S(1)}, bf16[96,128]{1,0:T(8,128)(2,1)S(1)}, u32[]{:S(2)}, u32[]{:S(2)}) collective-permute-start(bf16[96,128]{1,0:T(8,128)(2,1)S(1)} %get-tuple-element.43), channel_id=1, source_target_pairs={{0,12},{1,13},{2,14},{3,15},{4,8},{5,9},{6,10},{7,11}} | collective-permute-start | bytes 73736 | tf_op jit(solution)/shard_map/ppermute | solution.py:376
  29.3 6.0 %collective-permute-start.8 = (bf16[192,896]{1,0:T(8,128)(2,1)S(1)}, bf16[192,896]{1,0:T(8,128)(2,1)S(1)}, u32[]{:S(2)}, u32[]{:S(2)}) collective-permute-start(bf16[192,896]{1,0:T(8,128)(2,1)S(1)} %get-tuple-element.44), channel_id=1, source_target_pairs={{8,16},{9,17},{10,18},{11,19},{12,20},{13,21},{14,22},{15,23}} | collective-permute-start | bytes 1032200 | tf_op jit(solution)/shard_map/ppermute | solution.py:376
  30.6 4.6 %collective-permute-start.10 = (bf16[96,128]{1,0:T(8,128)(2,1)S(1)}, bf16[96,128]{1,0:T(8,128)(2,1)S(1)}, u32[]{:S(2)}, u32[]{:S(2)}) collective-permute-start(bf16[96,128]{1,0:T(8,128)(2,1)S(1)} %get-tuple-element.46), channel_id=1, source_target_pairs={{8,17},{9,16},{10,19},{11,18},{12,21},{13,20},{14,23},{15,22}} | collective-permute-start | bytes 73736 | tf_op jit(solution)/shard_map/ppermute | solution.py:376
  31.9 3.4 %collective-permute-start.11 = (bf16[96,128]{1,0:T(8,128)(2,1)S(1)}, bf16[96,128]{1,0:T(8,128)(2,1)S(1)}, u32[]{:S(2)}, u32[]{:S(2)}) collective-permute-start(bf16[96,128]{1,0:T(8,128)(2,1)S(1)} %get-tuple-element.47), channel_id=1, source_target_pairs={{8,20},{9,21},{10,22},{11,23},{12,16},{13,17},{14,18},{15,19}} | collective-permute-start | bytes 73736 | tf_op jit(solution)/shard_map/ppermute | solution.py:376
  33.2 2.1 %collective-permute-start.9 = (bf16[96,128]{1,0:T(8,128)(2,1)S(1)}, bf16[96,128]{1,0:T(8,128)(2,1)S(1)}, u32[]{:S(2)}, u32[]{:S(2)}) collective-permute-start(bf16[96,128]{1,0:T(8,128)(2,1)S(1)} %get-tuple-element.45), channel_id=1, source_target_pairs={{9,18},{10,17},{13,22},{14,21}} | collective-permute-start | bytes 73736 | tf_op jit(solution)/shard_map/ppermute | solution.py:376
  33.8 6.0 %collective-permute-start.13 = (bf16[192,896]{1,0:T(8,128)(2,1)S(1)}, bf16[192,896]{1,0:T(8,128)(2,1)S(1)}, u32[]{:S(2)}, u32[]{:S(2)}) collective-permute-start(bf16[192,896]{1,0:T(8,128)(2,1)S(1)} %get-tuple-element.49), channel_id=1, source_target_pairs={{8,16},{9,17},{10,18},{11,19},{12,20},{13,21},{14,22},{15,23}} | collective-permute-start | bytes 1032200 | tf_op jit(solution)/shard_map/ppermute | solution.py:376
  35.3 8.8 %collective-permute-start.12 = (bf16[192,896]{1,0:T(8,128)(2,1)S(1)}, bf16[192,896]{1,0:T(8,128)(2,1)S(1)}, u32[]{:S(2)}, u32[]{:S(2)}) collective-permute-start(bf16[192,896]{1,0:T(8,128)(2,1)S(1)} %get-tuple-element.48), channel_id=1, source_target_pairs={{16,24},{17,25},{18,26},{19,27},{20,28},{21,29},{22,30},{23,31},{0... | collective-permute-start | bytes 1032200 | tf_op jit(solution)/shard_map/ppermute | solution.py:376
  36.6 3.3 %collective-permute-start.14 = (bf16[48,128]{1,0:T(8,128)(2,1)S(1)}, bf16[48,128]{1,0:T(8,128)(2,1)S(1)}, u32[]{:S(2)}, u32[]{:S(2)}) collective-permute-start(bf16[48,128]{1,0:T(8,128)(2,1)S(1)} %get-tuple-element.50), channel_id=1, source_target_pairs={{17,26},{18,25},{21,30},{22,29},{1,10},{2,9},{5,14},{6,13}} | collective-permute-start | bytes 36872 | tf_op jit(solution)/shard_map/ppermute | solution.py:376
  37.2 5.3 %collective-permute-start.15 = (bf16[48,128]{1,0:T(8,128)(2,1)S(1)}, bf16[48,128]{1,0:T(8,128)(2,1)S(1)}, u32[]{:S(2)}, u32[]{:S(2)}) collective-permute-start(bf16[48,128]{1,0:T(8,128)(2,1)S(1)} %get-tuple-element.51), channel_id=1, source_target_pairs={{16,25},{17,24},{18,27},{19,26},{20,29},{21,28},{22,31},{23,30},{0... | collective-permute-start | bytes 36872 | tf_op jit(solution)/shard_map/ppermute | solution.py:376
  38.5 5.5 %collective-permute-start.16 = (bf16[48,128]{1,0:T(8,128)(2,1)S(1)}, bf16[48,128]{1,0:T(8,128)(2,1)S(1)}, u32[]{:S(2)}, u32[]{:S(2)}) collective-permute-start(bf16[48,128]{1,0:T(8,128)(2,1)S(1)} %get-tuple-element.52), channel_id=1, source_target_pairs={{16,28},{17,29},{18,30},{19,31},{20,24},{21,25},{22,26},{23,27},{0... | collective-permute-start | bytes 36872 | tf_op jit(solution)/shard_map/ppermute | solution.py:376

commit v10 on v9

--- a/solution.py
+++ b/solution.py
@@ -175,13 +175,11 @@
                 live = live_out[0].astype(jnp.float32)
                 live = jnp.concatenate([live] * (cells // LANES), axis=1)
                 picked = picked + live * arrival[...].astype(jnp.float32)
-            starts_out[r] = picked.astype(jnp.bfloat16)
-        edges = dot(starts_out[...].reshape(-1, cells), first_edge)
-        for message, swap in zip(messages, swaps):
-            for r in range(rounds):
-                message[r * part : (r + 1) * part] = pack(
-                    edges[r * slots : (r + 1) * slots], group_of(*swap)
-                )
+            picked = picked.astype(jnp.bfloat16)
+            starts_out[r] = picked
+            edges = dot(picked, first_edge)
+            for message, swap in zip(messages, swaps):
+                message[r * part : (r + 1) * part] = pack(edges, group_of(*swap))
 
 
 def bands(cells):
@@ -218,23 +216,26 @@
     whole_ext[:cells] = dot(coupled(first_map[...], band), second_map[...]).astype(jnp.bfloat16)
 
 
-def inside_kernel(early_layers, starts, first_map, band, second_map, edge_cells, *refs):
-    image_out, whole_ext = refs
+def inside_kernel(early_layers, starts, first_map, second_map, edge_cells, band, *refs):
+    image_out, whole_ext, band_in, sem = refs
     slots, cells = starts.shape[1:]
     chains = image_out.shape[0] // slots
     early = lax.axis_index("depth") < early_layers
-
-    @pl.when(early)
-    def _():
-        mapped = dot(starts[:chains].reshape(-1, cells), first_map[...]).astype(jnp.bfloat16)
-        image_out[...] = dot(coupled(mapped, band), second_map[...])
-
-    @pl.when(jnp.logical_not(early))
-    def _():
-        fill_whole_map(first_map, band, second_map, whole_ext)
-
+    copy = pltpu.make_async_copy(band, band_in, sem)
+    copy.start()
     edge_rows = dot(edge_cells[...], second_map[...])
     whole_ext[cells:] = (coupling_weight * edge_rows).astype(jnp.bfloat16)
+
+    @pl.when(early)
+    def _():
+        mapped = dot(starts[:chains].reshape(-1, cells), first_map[...]).astype(jnp.bfloat16)
+        copy.wait()
+        image_out[...] = dot(coupled(mapped, band_in), second_map[...])
+
+    @pl.when(jnp.logical_not(early))
+    def _():
+        copy.wait()
+        fill_whole_map(first_map, band_in, second_map, whole_ext)
 
 
 def whole_map_kernel(early_layers, first_map, band, second_map, whole_in, whole_ext):
@@ -422,10 +423,12 @@
         send(m, [(layer, layer) for layer in range(early_layers)], swap)
         for m, swap in zip(opened[3:], swaps)
     ]
-    traces, map_ext = call(
+    traces, map_ext, band = call(
         functools.partial(inside_kernel, early_layers),
-        [array(soon * slots, cells, kind=jnp.float32), whole],
-        [starts, first_map, band, second_map, edge_cells],
+        [array(soon * slots, cells, kind=jnp.float32), whole, array(*band.shape)],
+        [starts, first_map, second_map, edge_cells, band],
+        in_hbm=(4,),
+        scratch=[pltpu.SemaphoreType.DMA],
     )
     opened = received
     arrived = list(opened)

time: 46.1 us -> 46.4 us (level)
  Pallas kernels: 10 us -> 10.8 us
  waiting for transfers between devices: 16.2 us -> 15.7 us
    pallas_call x8, Pallas kernels: 10 us -> 10.8 us  [call(): pl.pallas_call(kernel, out_shape=out_shape, in_specs=[pl.BlockSpec(memory...]
    ppermute x17, waiting for transfers between devices: 16.2 us -> 15.7 us  [send(): return lax.ppermute(x, MESH_AXES, pairs)]
  transfers between devices with their start and end apart: 17 -> 17, of which waited for: 6 -> 6; matrix products, arithmetic and copies ran while one was open for 0% -> 0% of each run, Pallas kernels for 7% -> 9%
where the time goes in v10:
time: 46.4 us; the launch traced here: 46 us
  starting transfers between devices  19 us (41%)
  waiting for transfers between devices  15.7 us (34%)
  Pallas kernels  10.8 us (23%)
    ppermute x17, starting transfers between devices, send(): return lax.ppermute(x, MESH_AXES, pairs)  19 us
    ppermute x17, waiting for transfers between devices, send(): return lax.ppermute(x, MESH_AXES, pairs)  15.7 us
    pallas_call x8, Pallas kernels, call(): pl.pallas_call(kernel, out_shape=out_shape, in_specs=[pl.BlockSpec(memory...  10.8 us
  transfers between devices with their start and end apart: 17, of which 6 were waited for; matrix products, arithmetic and copies ran while one was open for 0% of the time, Pallas kernels for 9%

profile of v10, /device:TPU:1, one launch (start us, length us, event | category | flops | bytes accessed | tf_op | source)
XLA Modules:
  0.0 46.0 jit_solution(2059526296103749077)
XLA Ops:
  0.0 3.8 %shard_map.82 = (bf16[1472,128]{1,0:T(8,128)(2,1)S(1)}, bf16[4,192,896]{2,1,0:T(8,128)(2,1)S(1)}, bf16[4,192,128]{2,1,0:T(8,128)(2,1)S(1)}) custom-call(bf16[4,192,896]{2,1,0:T(8,128)(2,1)} %bitcast.20, s32[4,192]{1,0:T(4,128)} %assignment.3, s32[7,1,1,12]{3,2,1,0:T(1,128)} %bitcast.22, bf16[896,896]{1,0:T(8,128)(2,1)} %bitcast.9), custom_call_target="tpu_custom_call" | custom-call | tf_op jit(solution)/shard_map/pallas_call | solution.py:348
  3.8 1.9 %collective-permute-start = (bf16[1472,128]{1,0:T(8,128)(2,1)S(1)}, bf16[1472,128]{1,0:T(8,128)(2,1)S(1)}, u32[]{:S(2)}, u32[]{:S(2)}) collective-permute-start(bf16[1472,128]{1,0:T(8,128)(2,1)S(1)} %get-tuple-element.37), channel_id=1, source_target_pairs={{8,0},{9,1},{10,2},{11,3},{12,4},{13,5},{14,6},{15,7},{16,8},{17,9... | collective-permute-start | bytes 1130504 | tf_op jit(solution)/shard_map/ppermute | solution.py:377
  5.8 0.0 copy-start.1
  5.8 0.1 shard_map.83
  5.9 0.8 %collective-permute-start.1 = (bf16[192,128]{1,0:T(8,128)(2,1)S(1)}, bf16[192,128]{1,0:T(8,128)(2,1)S(1)}, u32[]{:S(2)}, u32[]{:S(2)}) collective-permute-start(bf16[192,128]{1,0:T(8,128)(2,1)S(1)} %get-tuple-element.39), channel_id=1, source_target_pairs={{1,2},{2,1},{5,6},{6,5}} | collective-permute-start | bytes 147464 | tf_op jit(solution)/shard_map/ppermute | solution.py:377
  6.7 0.7 %collective-permute-start.2 = (bf16[192,128]{1,0:T(8,128)(2,1)S(1)}, bf16[192,128]{1,0:T(8,128)(2,1)S(1)}, u32[]{:S(2)}, u32[]{:S(2)}) collective-permute-start(bf16[192,128]{1,0:T(8,128)(2,1)S(1)} %get-tuple-element.40), channel_id=1, source_target_pairs={{0,1},{1,0},{2,3},{3,2},{4,5},{5,4},{6,7},{7,6}} | collective-permute-start | bytes 147464 | tf_op jit(solution)/shard_map/ppermute | solution.py:377
  7.4 0.7 %collective-permute-start.3 = (bf16[192,128]{1,0:T(8,128)(2,1)S(1)}, bf16[192,128]{1,0:T(8,128)(2,1)S(1)}, u32[]{:S(2)}, u32[]{:S(2)}) collective-permute-start(bf16[192,128]{1,0:T(8,128)(2,1)S(1)} %get-tuple-element.41), channel_id=1, source_target_pairs={{0,4},{1,5},{2,6},{3,7},{4,0},{5,1},{6,2},{7,3}} | collective-permute-start | bytes 147464 | tf_op jit(solution)/shard_map/ppermute | solution.py:377
  8.1 0.0 copy-start.3
  8.1 4.1 %shard_map.84 = (f32[384,896]{1,0:T(8,128)S(1)}, bf16[1024,896]{1,0:T(8,128)(2,1)S(1)}, bf16[4,512,256]{2,1,0:T(8,128)(2,1)S(1)}) custom-call(bf16[4,192,896]{2,1,0:T(8,128)(2,1)S(1)} %get-tuple-element.33.starts.refs_0_, bf16[896,896]{1,0:T(8,128)(2,1)S(1)} %bitcast.11, bf16[896,896]{1,0:T(8,128)(2,1)S(1)} %bitcast.13, ...), custom_call_target="tpu_custom_call" | custom-call | tf_op jit(solution)/shard_map/pallas_call | solution.py:348
  12.2 0.0 collective-permute-done.2.refs_7_.refs_10_.refs_2_
  12.2 0.0 collective-permute-done.3.refs_8_.refs_11_.refs_3_
  12.2 1.4 %collective-permute-done.refs_4_ = bf16[1472,128]{1,0:T(8,128)(2,1)S(1)} collective-permute-done((bf16[1472,128]{1,0:T(8,128)(2,1)S(1)}, bf16[1472,128]{1,0:T(8,128)(2,1)S(1)}, u32[]{:S(2)}, u32[]{:S(2)}) %collective-permute-start) | collective-permute-done | bytes 376864 | tf_op jit(solution)/shard_map/ppermute | solution.py:377
  13.6 1.3 %collective-permute-start.4 = (bf16[384,896]{1,0:T(8,128)(2,1)S(1)}, bf16[384,896]{1,0:T(8,128)(2,1)S(1)}, u32[]{:S(2)}, u32[]{:S(2)}) collective-permute-start(bf16[384,896]{1,0:T(8,128)(2,1)S(1)} %get-tuple-element.42), channel_id=1, source_target_pairs={{0,8},{1,9},{2,10},{3,11},{4,12},{5,13},{6,14},{7,15}} | collective-permute-start | bytes 2064392 | tf_op jit(solution)/shard_map/ppermute | solution.py:377
  14.9 0.7 %collective-permute-start.5 = (bf16[96,128]{1,0:T(8,128)(2,1)S(1)}, bf16[96,128]{1,0:T(8,128)(2,1)S(1)}, u32[]{:S(2)}, u32[]{:S(2)}) collective-permute-start(bf16[96,128]{1,0:T(8,128)(2,1)S(1)} %get-tuple-element.43), channel_id=1, source_target_pairs={{1,10},{2,9},{5,14},{6,13}} | collective-permute-start | bytes 73736 | tf_op jit(solution)/shard_map/ppermute | solution.py:377
  15.6 1.3 %collective-permute-start.6 = (bf16[96,128]{1,0:T(8,128)(2,1)S(1)}, bf16[96,128]{1,0:T(8,128)(2,1)S(1)}, u32[]{:S(2)}, u32[]{:S(2)}) collective-permute-start(bf16[96,128]{1,0:T(8,128)(2,1)S(1)} %get-tuple-element.44), channel_id=1, source_target_pairs={{0,9},{1,8},{2,11},{3,10},{4,13},{5,12},{6,15},{7,14}} | collective-permute-start | bytes 73736 | tf_op jit(solution)/shard_map/ppermute | solution.py:377
  16.9 1.3 %collective-permute-start.7 = (bf16[96,128]{1,0:T(8,128)(2,1)S(1)}, bf16[96,128]{1,0:T(8,128)(2,1)S(1)}, u32[]{:S(2)}, u32[]{:S(2)}) collective-permute-start(bf16[96,128]{1,0:T(8,128)(2,1)S(1)} %get-tuple-element.45), channel_id=1, source_target_pairs={{0,12},{1,13},{2,14},{3,15},{4,8},{5,9},{6,10},{7,11}} | collective-permute-start | bytes 73736 | tf_op jit(solution)/shard_map/ppermute | solution.py:377
  18.2 8.0 %collective-permute-done.6.refs_7_ = bf16[96,128]{1,0:T(8,128)(2,1)S(1)} collective-permute-done((bf16[96,128]{1,0:T(8,128)(2,1)S(1)}, bf16[96,128]{1,0:T(8,128)(2,1)S(1)}, u32[]{:S(2)}, u32[]{:S(2)}) %collective-permute-start.6) | collective-permute-done | bytes 24608 | tf_op jit(solution)/shard_map/ppermute | solution.py:377
  26.2 1.8 %collective-permute-done.7.refs_8_ = bf16[96,128]{1,0:T(8,128)(2,1)S(1)} collective-permute-done((bf16[96,128]{1,0:T(8,128)(2,1)S(1)}, bf16[96,128]{1,0:T(8,128)(2,1)S(1)}, u32[]{:S(2)}, u32[]{:S(2)}) %collective-permute-start.7) | collective-permute-done | bytes 24608 | tf_op jit(solution)/shard_map/ppermute | solution.py:377
  28.0 1.3 %shard_map.87 = (bf16[192,896]{1,0:T(8,128)(2,1)S(1)}, bf16[192,896]{1,0:T(8,128)(2,1)S(1)}, bf16[96,128]{1,0:T(8,128)(2,1)S(1)}, bf16[96,128]{1,0:T(8,128)(2,1)S(1)}, bf16[96,128]{1,0:T(8,128)(2,1)S(1)}) custom-call(bf16[4,192,896]{2,1,0:T(8,128)(2,1)S(1)} %get-tuple-element.33.starts.refs_0_, bf16[4,192,128]{2,1,0:T(8,128)(2,1)S(1)} %get-tuple-element.32.refs_1_.live, ...), custom_call_target="tpu_custom_call" | custom-call | tf_op jit(solution)/shard_map/pallas_call | solution.py:348
  29.3 1.3 %collective-permute-start.8 = (bf16[192,896]{1,0:T(8,128)(2,1)S(1)}, bf16[192,896]{1,0:T(8,128)(2,1)S(1)}, u32[]{:S(2)}, u32[]{:S(2)}) collective-permute-start(bf16[192,896]{1,0:T(8,128)(2,1)S(1)} %get-tuple-element.46), channel_id=1, source_target_pairs={{8,16},{9,17},{10,18},{11,19},{12,20},{13,21},{14,22},{15,23}} | collective-permute-start | bytes 1032200 | tf_op jit(solution)/shard_map/ppermute | solution.py:377
  30.6 0.7 %collective-permute-start.9 = (bf16[96,128]{1,0:T(8,128)(2,1)S(1)}, bf16[96,128]{1,0:T(8,128)(2,1)S(1)}, u32[]{:S(2)}, u32[]{:S(2)}) collective-permute-start(bf16[96,128]{1,0:T(8,128)(2,1)S(1)} %get-tuple-element.47), channel_id=1, source_target_pairs={{9,18},{10,17},{13,22},{14,21}} | collective-permute-start | bytes 73736 | tf_op jit(solution)/shard_map/ppermute | solution.py:377
  31.3 1.3 %collective-permute-start.10 = (bf16[96,128]{1,0:T(8,128)(2,1)S(1)}, bf16[96,128]{1,0:T(8,128)(2,1)S(1)}, u32[]{:S(2)}, u32[]{:S(2)}) collective-permute-start(bf16[96,128]{1,0:T(8,128)(2,1)S(1)} %get-tuple-element.48), channel_id=1, source_target_pairs={{8,17},{9,16},{10,19},{11,18},{12,21},{13,20},{14,23},{15,22}} | collective-permute-start | bytes 73736 | tf_op jit(solution)/shard_map/ppermute | solution.py:377
  32.6 1.3 %collective-permute-start.11 = (bf16[96,128]{1,0:T(8,128)(2,1)S(1)}, bf16[96,128]{1,0:T(8,128)(2,1)S(1)}, u32[]{:S(2)}, u32[]{:S(2)}) collective-permute-start(bf16[96,128]{1,0:T(8,128)(2,1)S(1)} %get-tuple-element.49), channel_id=1, source_target_pairs={{8,20},{9,21},{10,22},{11,23},{12,16},{13,17},{14,18},{15,19}} | collective-permute-start | bytes 73736 | tf_op jit(solution)/shard_map/ppermute | solution.py:377
  33.9 1.3 %collective-permute-start.13 = (bf16[192,896]{1,0:T(8,128)(2,1)S(1)}, bf16[192,896]{1,0:T(8,128)(2,1)S(1)}, u32[]{:S(2)}, u32[]{:S(2)}) collective-permute-start(bf16[192,896]{1,0:T(8,128)(2,1)S(1)} %get-tuple-element.51), channel_id=1, source_target_pairs={{8,16},{9,17},{10,18},{11,19},{12,20},{13,21},{14,22},{15,23}} | collective-permute-start | bytes 1032200 | tf_op jit(solution)/shard_map/ppermute | solution.py:377
  35.2 0.1 collective-permute-done.11.refs_8_.refs_6_
  35.3 1.3 %collective-permute-start.12 = (bf16[192,896]{1,0:T(8,128)(2,1)S(1)}, bf16[192,896]{1,0:T(8,128)(2,1)S(1)}, u32[]{:S(2)}, u32[]{:S(2)}) collective-permute-start(bf16[192,896]{1,0:T(8,128)(2,1)S(1)} %get-tuple-element.50), channel_id=1, source_target_pairs={{16,24},{17,25},{18,26},{19,27},{20,28},{21,29},{22,30},{23,31},{0... | collective-permute-start | bytes 1032200 | tf_op jit(solution)/shard_map/ppermute | solution.py:377
  36.6 0.7 %collective-permute-start.14 = (bf16[48,128]{1,0:T(8,128)(2,1)S(1)}, bf16[48,128]{1,0:T(8,128)(2,1)S(1)}, u32[]{:S(2)}, u32[]{:S(2)}) collective-permute-start(bf16[48,128]{1,0:T(8,128)(2,1)S(1)} %get-tuple-element.52), channel_id=1, source_target_pairs={{17,26},{18,25},{21,30},{22,29},{1,10},{2,9},{5,14},{6,13}} | collective-permute-start | bytes 36872 | tf_op jit(solution)/shard_map/ppermute | solution.py:377
  37.3 1.3 %collective-permute-start.15 = (bf16[48,128]{1,0:T(8,128)(2,1)S(1)}, bf16[48,128]{1,0:T(8,128)(2,1)S(1)}, u32[]{:S(2)}, u32[]{:S(2)}) collective-permute-start(bf16[48,128]{1,0:T(8,128)(2,1)S(1)} %get-tuple-element.53), channel_id=1, source_target_pairs={{16,25},{17,24},{18,27},{19,26},{20,29},{21,28},{22,31},{23,30},{0... | collective-permute-start | bytes 36872 | tf_op jit(solution)/shard_map/ppermute | solution.py:377
  38.6 1.3 %collective-permute-start.16 = (bf16[48,128]{1,0:T(8,128)(2,1)S(1)}, bf16[48,128]{1,0:T(8,128)(2,1)S(1)}, u32[]{:S(2)}, u32[]{:S(2)}) collective-permute-start(bf16[48,128]{1,0:T(8,128)(2,1)S(1)} %get-tuple-element.54), channel_id=1, source_target_pairs={{16,28},{17,29},{18,30},{19,31},{20,24},{21,25},{22,26},{23,27},{0... | collective-permute-start | bytes 36872 | tf_op jit(solution)/shard_map/ppermute | solution.py:377
  39.9 2.7 %collective-permute-done.15.refs_8_ = bf16[48,128]{1,0:T(8,128)(2,1)S(1)} collective-permute-done((bf16[48,128]{1,0:T(8,128)(2,1)S(1)}, bf16[48,128]{1,0:T(8,128)(2,1)S(1)}, u32[]{:S(2)}, u32[]{:S(2)}) %collective-permute-start.15) | collective-permute-done | bytes 12320 | tf_op jit(solution)/shard_map/ppermute | solution.py:377
  42.6 1.7 %collective-permute-done.16.refs_9_ = bf16[48,128]{1,0:T(8,128)(2,1)S(1)} collective-permute-done((bf16[48,128]{1,0:T(8,128)(2,1)S(1)}, bf16[48,128]{1,0:T(8,128)(2,1)S(1)}, u32[]{:S(2)}, u32[]{:S(2)}) %collective-permute-start.16) | collective-permute-done | bytes 12320 | tf_op jit(solution)/shard_map/ppermute | solution.py:377
  44.3 1.5 %shard_map.89 = bf16[192,896]{1,0:T(8,128)(2,1)} custom-call(bf16[4,192,128]{2,1,0:T(8,128)(2,1)S(1)} %get-tuple-element.32.refs_1_.live, bf16[4,192,896]{2,1,0:T(8,128)(2,1)S(1)} %get-tuple-element.33.starts.refs_0_, bf16[1024,896]{1,0:T(8,128)(2,1)S(1)} %shard_map.85.refs_2_.map_ext, f32[1,896]{1,0:T(1,128)S(1)} %bitcast.19, ...), custom_call_target="tpu_custom_call" | custom-call | tf_op jit(solution)/shard_map/pallas_call | solution.py:348
  (18 shorter events, 0.1 us)
Async XLA Ops:
  0.0 5.7 %copy-start = (bf16[1,1,1,896,896]{4,3,2,1,0:T(8,128)(2,1)S(1)}, bf16[1,1,1,896,896]{4,3,2,1,0:T(8,128)(2,1)}, u32[]{:S(2)}) copy-start(bf16[1,1,1,896,896]{4,3,2,1,0:T(8,128)(2,1)} %param.12) | copy-start | bytes 4816900
  0.0 5.8 %copy-start.2 = (bf16[1,192,1,1,896]{4,1,3,2,0:T(8,128)(2,1)S(1)}, bf16[1,192,1,1,896]{4,1,3,2,0:T(8,128)(2,1)}, u32[]{:S(2)}) copy-start(bf16[1,192,1,1,896]{4,1,3,2,0:T(8,128)(2,1)} %param.8) | copy-start | bytes 1032196
  3.8 9.8 %collective-permute-start = (bf16[1472,128]{1,0:T(8,128)(2,1)S(1)}, bf16[1472,128]{1,0:T(8,128)(2,1)S(1)}, u32[]{:S(2)}, u32[]{:S(2)}) collective-permute-start(bf16[1472,128]{1,0:T(8,128)(2,1)S(1)} %get-tuple-element.37), channel_id=1, source_target_pairs={{8,0},{9,1},{10,2},{11,3},{12,4},{13,5},{14,6},{15,7},{16,8},{17,9... | collective-permute-start | bytes 1130504 | tf_op jit(solution)/shard_map/ppermute | solution.py:377
  5.8 2.3 %copy-start.1 = (bf16[1,1,1,896,896]{4,3,2,1,0:T(8,128)(2,1)S(1)}, bf16[1,1,1,896,896]{4,3,2,1,0:T(8,128)(2,1)}, u32[]{:S(2)}) copy-start(bf16[1,1,1,896,896]{4,3,2,1,0:T(8,128)(2,1)} %param.13) | copy-start | bytes 4816900
  5.9 6.3 %collective-permute-start.1 = (bf16[192,128]{1,0:T(8,128)(2,1)S(1)}, bf16[192,128]{1,0:T(8,128)(2,1)S(1)}, u32[]{:S(2)}, u32[]{:S(2)}) collective-permute-start(bf16[192,128]{1,0:T(8,128)(2,1)S(1)} %get-tuple-element.39), channel_id=1, source_target_pairs={{1,2},{2,1},{5,6},{6,5}} | collective-permute-start | bytes 147464 | tf_op jit(solution)/shard_map/ppermute | solution.py:377
  6.7 5.5 %collective-permute-start.2 = (bf16[192,128]{1,0:T(8,128)(2,1)S(1)}, bf16[192,128]{1,0:T(8,128)(2,1)S(1)}, u32[]{:S(2)}, u32[]{:S(2)}) collective-permute-start(bf16[192,128]{1,0:T(8,128)(2,1)S(1)} %get-tuple-element.40), channel_id=1, source_target_pairs={{0,1},{1,0},{2,3},{3,2},{4,5},{5,4},{6,7},{7,6}} | collective-permute-start | bytes 147464 | tf_op jit(solution)/shard_map/ppermute | solution.py:377
  7.4 4.8 %collective-permute-start.3 = (bf16[192,128]{1,0:T(8,128)(2,1)S(1)}, bf16[192,128]{1,0:T(8,128)(2,1)S(1)}, u32[]{:S(2)}, u32[]{:S(2)}) collective-permute-start(bf16[192,128]{1,0:T(8,128)(2,1)S(1)} %get-tuple-element.41), channel_id=1, source_target_pairs={{0,4},{1,5},{2,6},{3,7},{4,0},{5,1},{6,2},{7,3}} | collective-permute-start | bytes 147464 | tf_op jit(solution)/shard_map/ppermute | solution.py:377
  8.1 5.6 %copy-start.3 = (f32[1,1,1,896]{3,2,1,0:T(1,128)S(1)}, f32[1,1,1,896]{3,2,1,0:T(1,128)}, u32[]{:S(2)}) copy-start(f32[1,1,1,896]{3,2,1,0:T(1,128)} %param.14) | copy-start | bytes 10756
  13.6 14.4 %collective-permute-start.4 = (bf16[384,896]{1,0:T(8,128)(2,1)S(1)}, bf16[384,896]{1,0:T(8,128)(2,1)S(1)}, u32[]{:S(2)}, u32[]{:S(2)}) collective-permute-start(bf16[384,896]{1,0:T(8,128)(2,1)S(1)} %get-tuple-element.42), channel_id=1, source_target_pairs={{0,8},{1,9},{2,10},{3,11},{4,12},{5,13},{6,14},{7,15}} | collective-permute-start | bytes 2064392 | tf_op jit(solution)/shard_map/ppermute | solution.py:377
  14.9 3.3 %collective-permute-start.5 = (bf16[96,128]{1,0:T(8,128)(2,1)S(1)}, bf16[96,128]{1,0:T(8,128)(2,1)S(1)}, u32[]{:S(2)}, u32[]{:S(2)}) collective-permute-start(bf16[96,128]{1,0:T(8,128)(2,1)S(1)} %get-tuple-element.43), channel_id=1, source_target_pairs={{1,10},{2,9},{5,14},{6,13}} | collective-permute-start | bytes 73736 | tf_op jit(solution)/shard_map/ppermute | solution.py:377
  15.6 10.6 %collective-permute-start.6 = (bf16[96,128]{1,0:T(8,128)(2,1)S(1)}, bf16[96,128]{1,0:T(8,128)(2,1)S(1)}, u32[]{:S(2)}, u32[]{:S(2)}) collective-permute-start(bf16[96,128]{1,0:T(8,128)(2,1)S(1)} %get-tuple-element.44), channel_id=1, source_target_pairs={{0,9},{1,8},{2,11},{3,10},{4,13},{5,12},{6,15},{7,14}} | collective-permute-start | bytes 73736 | tf_op jit(solution)/shard_map/ppermute | solution.py:377
  16.9 11.1 %collective-permute-start.7 = (bf16[96,128]{1,0:T(8,128)(2,1)S(1)}, bf16[96,128]{1,0:T(8,128)(2,1)S(1)}, u32[]{:S(2)}, u32[]{:S(2)}) collective-permute-start(bf16[96,128]{1,0:T(8,128)(2,1)S(1)} %get-tuple-element.45), channel_id=1, source_target_pairs={{0,12},{1,13},{2,14},{3,15},{4,8},{5,9},{6,10},{7,11}} | collective-permute-start | bytes 73736 | tf_op jit(solution)/shard_map/ppermute | solution.py:377
  29.3 6.0 %collective-permute-start.8 = (bf16[192,896]{1,0:T(8,128)(2,1)S(1)}, bf16[192,896]{1,0:T(8,128)(2,1)S(1)}, u32[]{:S(2)}, u32[]{:S(2)}) collective-permute-start(bf16[192,896]{1,0:T(8,128)(2,1)S(1)} %get-tuple-element.46), channel_id=1, source_target_pairs={{8,16},{9,17},{10,18},{11,19},{12,20},{13,21},{14,22},{15,23}} | collective-permute-start | bytes 1032200 | tf_op jit(solution)/shard_map/ppermute | solution.py:377
  30.6 4.6 %collective-permute-start.9 = (bf16[96,128]{1,0:T(8,128)(2,1)S(1)}, bf16[96,128]{1,0:T(8,128)(2,1)S(1)}, u32[]{:S(2)}, u32[]{:S(2)}) collective-permute-start(bf16[96,128]{1,0:T(8,128)(2,1)S(1)} %get-tuple-element.47), channel_id=1, source_target_pairs={{9,18},{10,17},{13,22},{14,21}} | collective-permute-start | bytes 73736 | tf_op jit(solution)/shard_map/ppermute | solution.py:377
  31.3 3.9 %collective-permute-start.10 = (bf16[96,128]{1,0:T(8,128)(2,1)S(1)}, bf16[96,128]{1,0:T(8,128)(2,1)S(1)}, u32[]{:S(2)}, u32[]{:S(2)}) collective-permute-start(bf16[96,128]{1,0:T(8,128)(2,1)S(1)} %get-tuple-element.48), channel_id=1, source_target_pairs={{8,17},{9,16},{10,19},{11,18},{12,21},{13,20},{14,23},{15,22}} | collective-permute-start | bytes 73736 | tf_op jit(solution)/shard_map/ppermute | solution.py:377
  32.6 2.7 %collective-permute-start.11 = (bf16[96,128]{1,0:T(8,128)(2,1)S(1)}, bf16[96,128]{1,0:T(8,128)(2,1)S(1)}, u32[]{:S(2)}, u32[]{:S(2)}) collective-permute-start(bf16[96,128]{1,0:T(8,128)(2,1)S(1)} %get-tuple-element.49), channel_id=1, source_target_pairs={{8,20},{9,21},{10,22},{11,23},{12,16},{13,17},{14,18},{15,19}} | collective-permute-start | bytes 73736 | tf_op jit(solution)/shard_map/ppermute | solution.py:377
  33.9 6.0 %collective-permute-start.13 = (bf16[192,896]{1,0:T(8,128)(2,1)S(1)}, bf16[192,896]{1,0:T(8,128)(2,1)S(1)}, u32[]{:S(2)}, u32[]{:S(2)}) collective-permute-start(bf16[192,896]{1,0:T(8,128)(2,1)S(1)} %get-tuple-element.51), channel_id=1, source_target_pairs={{8,16},{9,17},{10,18},{11,19},{12,20},{13,21},{14,22},{15,23}} | collective-permute-start | bytes 1032200 | tf_op jit(solution)/shard_map/ppermute | solution.py:377
  35.3 9.0 %collective-permute-start.12 = (bf16[192,896]{1,0:T(8,128)(2,1)S(1)}, bf16[192,896]{1,0:T(8,128)(2,1)S(1)}, u32[]{:S(2)}, u32[]{:S(2)}) collective-permute-start(bf16[192,896]{1,0:T(8,128)(2,1)S(1)} %get-tuple-element.50), channel_id=1, source_target_pairs={{16,24},{17,25},{18,26},{19,27},{20,28},{21,29},{22,30},{23,31},{0... | collective-permute-start | bytes 1032200 | tf_op jit(solution)/shard_map/ppermute | solution.py:377
  36.6 3.3 %collective-permute-start.14 = (bf16[48,128]{1,0:T(8,128)(2,1)S(1)}, bf16[48,128]{1,0:T(8,128)(2,1)S(1)}, u32[]{:S(2)}, u32[]{:S(2)}) collective-permute-start(bf16[48,128]{1,0:T(8,128)(2,1)S(1)} %get-tuple-element.52), channel_id=1, source_target_pairs={{17,26},{18,25},{21,30},{22,29},{1,10},{2,9},{5,14},{6,13}} | collective-permute-start | bytes 36872 | tf_op jit(solution)/shard_map/ppermute | solution.py:377
  37.3 5.3 %collective-permute-start.15 = (bf16[48,128]{1,0:T(8,128)(2,1)S(1)}, bf16[48,128]{1,0:T(8,128)(2,1)S(1)}, u32[]{:S(2)}, u32[]{:S(2)}) collective-permute-start(bf16[48,128]{1,0:T(8,128)(2,1)S(1)} %get-tuple-element.53), channel_id=1, source_target_pairs={{16,25},{17,24},{18,27},{19,26},{20,29},{21,28},{22,31},{23,30},{0... | collective-permute-start | bytes 36872 | tf_op jit(solution)/shard_map/ppermute | solution.py:377
  38.6 5.7 %collective-permute-start.16 = (bf16[48,128]{1,0:T(8,128)(2,1)S(1)}, bf16[48,128]{1,0:T(8,128)(2,1)S(1)}, u32[]{:S(2)}, u32[]{:S(2)}) collective-permute-start(bf16[48,128]{1,0:T(8,128)(2,1)S(1)} %get-tuple-element.54), channel_id=1, source_target_pairs={{16,28},{17,29},{18,30},{19,31},{20,24},{21,25},{22,26},{23,27},{0... | collective-permute-start | bytes 36872 | tf_op jit(solution)/shard_map/ppermute | solution.py:377

commit v11 on v10

--- a/solution.py
+++ b/solution.py
@@ -59,9 +59,9 @@
     return found[::-1]
 
 
-def group_of(axis, parity, base):
-    ahead = (lax.axis_index(axis) & 1) == parity
-    return jnp.where(ahead, base + 1, base)
+def groups_of(swaps):
+    index = {axis: lax.axis_index(axis) & 1 for axis, _ in EDGE_AXES}
+    return [jnp.where(index[axis] == parity, base + 1, base) for axis, parity, base in swaps]
 
 
 def pack(edges, group):
@@ -84,17 +84,17 @@
     return jnp.concatenate(pieces, axis=0)
 
 
-def unit_of(round_number):
-    return round_number - lax.axis_index("depth") + lax.axis_size("depth") - 1
-
-
-def chosen_of(wanted, counts_in, round_number):
+def first_unit(layer):
+    return lax.axis_size("depth") - 1 - layer
+
+
+def chosen_of(wanted, counts_in, unit):
     slots = wanted.shape[1]
     shot = lax.broadcasted_iota(jnp.int32, (slots, slots), 0)
     slot = lax.broadcasted_iota(jnp.int32, (1, slots), 1)
     live = jnp.zeros((1, slots), jnp.int32)
     for batch in range(slots // SHOT_BATCH):
-        count = counts_in[unit_of(round_number), 0, 0, batch]
+        count = counts_in[unit, 0, 0, batch]
         live = jnp.where(slot >= batch * SHOT_BATCH, count + batch * SHOT_BATCH, live)
     wanted = jnp.where(slot < live, wanted, -1)
     return jnp.where(shot == wanted, 1.0, 0.0).astype(jnp.bfloat16)
@@ -109,12 +109,12 @@
     return copies
 
 
-def fill_live(live_out, counts_in):
+def fill_live(live_out, counts_in, unit):
     position = lax.broadcasted_iota(jnp.int32, (SHOT_BATCH, LANES), 0)
     rounds, slots = live_out.shape[:2]
     for round_number in range(rounds):
         for batch in range(slots // SHOT_BATCH):
-            count = counts_in[unit_of(round_number), 0, 0, batch]
+            count = counts_in[unit + round_number, 0, 0, batch]
             rows = slice(batch * SHOT_BATCH, (batch + 1) * SHOT_BATCH)
             live_out[round_number, rows] = jnp.where(position < count, 1.0, 0.0).astype(
                 jnp.bfloat16
@@ -124,22 +124,24 @@
 def edges_kernel(source, assignment, counts, first_map, edge_out, starts_out, live_out, *refs):
     source_in, assignment_in, counts_in, first_in, sems = refs
     rounds, slots, cells = source.shape
-
-    @pl.when(lax.axis_index("depth") > 0)
-    def _():
+    layer = lax.axis_index("depth")
+
+    @pl.when(layer > 0)
+    def _():
+        unit = first_unit(layer)
         pairs = [(counts, counts_in), (assignment, assignment_in), (first_map, first_in)]
         pairs += [(source.at[r], source_in.at[r]) for r in range(1, rounds)]
         copies = started(pairs, sems)
         selector = edge_selector(cells)
         copies[0].wait()
-        fill_live(live_out, counts_in)
+        fill_live(live_out, counts_in, unit)
         copies[1].wait()
         copies[2].wait()
         first_edge = dot(first_in[...], selector).astype(jnp.bfloat16)
         edge_out[:cells] = first_edge
         for r in range(1, rounds):
             copies[2 + r].wait()
-            chosen = chosen_of(assignment_in[r : r + 1], counts_in, r)
+            chosen = chosen_of(assignment_in[r : r + 1], counts_in, unit + r)
             starts_out[r] = dot_t(chosen, source_in[r]).astype(jnp.bfloat16)
         edges = dot(starts_out[1:].reshape(-1, cells), first_edge)
         edge_out[cells:] = edges.astype(jnp.bfloat16)
@@ -151,7 +153,8 @@
     source_in, assignment_in, counts_in, sems = refs[5 + len(swaps) :]
     rounds, slots, cells = source.shape
     part = slots // 4
-    early = lax.axis_index("depth") < early_layers
+    layer = lax.axis_index("depth")
+    early = layer < early_layers
 
     @pl.when(jnp.logical_not(early))
     def _():
@@ -159,16 +162,18 @@
 
     @pl.when(early)
     def _():
+        unit = first_unit(layer)
+        groups = groups_of(swaps)
         pairs = [(counts, counts_in), (assignment, assignment_in)]
         pairs += [(source.at[r], source_in.at[r]) for r in range(rounds)]
         copies = started(pairs, sems)
         edge_cells[...] = edge_rows_selector(cells)
         first_edge = dot(first_map[...], edge_selector(cells)).astype(jnp.bfloat16)
         copies[0].wait()
-        fill_live(live_out, counts_in)
+        fill_live(live_out, counts_in, unit)
         copies[1].wait()
         for r in range(rounds):
-            chosen = chosen_of(assignment_in[r : r + 1], counts_in, r)
+            chosen = chosen_of(assignment_in[r : r + 1], counts_in, unit + r)
             copies[2 + r].wait()
             picked = dot_t(chosen, source_in[r])
             if r == 0:
@@ -178,8 +183,8 @@
             picked = picked.astype(jnp.bfloat16)
             starts_out[r] = picked
             edges = dot(picked, first_edge)
-            for message, swap in zip(messages, swaps):
-                message[r * part : (r + 1) * part] = pack(edges, group_of(*swap))
+            for message, group in zip(messages, groups):
+                message[r * part : (r + 1) * part] = pack(edges, group)
 
 
 def bands(cells):
@@ -246,10 +251,10 @@
         fill_whole_map(first_map, band, second_map, whole_ext)
 
 
-def halo_of(messages, swaps, live):
+def halo_of(messages, groups, live):
     halo = 0.0
-    for message, swap in zip(messages, swaps):
-        halo = halo + unpack(message.astype(jnp.float32), group_of(*swap))
+    for message, group in zip(messages, groups):
+        halo = halo + unpack(message.astype(jnp.float32), group)
     return (halo * live.astype(jnp.float32)).astype(jnp.bfloat16)
 
 
@@ -272,6 +277,7 @@
 
     @pl.when(here)
     def _():
+        groups = groups_of(swaps)
         halo = []
         for chain in range(chains):
             packed = [ref[chain * part : (chain + 1) * part] for ref in received]
@@ -281,7 +287,7 @@
                     jnp.where(layer == 0, ref[at : at + part].astype(jnp.float32), x)
                     for ref, x in zip(opened, packed)
                 ]
-            halo.append(halo_of(packed, swaps, live[step + chain]))
+            halo.append(halo_of(packed, groups, live[step + chain]))
         halo = jnp.concatenate(halo, axis=0)
         start = starts[step : step + chains].reshape(-1, cells)
         if step == 0:
@@ -298,10 +304,10 @@
         at = cells + step * slots
         edges = dot(ended, edge_next[:cells])
         edges += edge_next[at : at + chains * slots].astype(jnp.float32)
-        for message, swap in zip(messages, swaps):
+        for message, group in zip(messages, groups):
             for chain in range(chains):
                 message[chain * part : (chain + 1) * part] = pack(
-                    edges[chain * slots : (chain + 1) * slots], group_of(*swap)
+                    edges[chain * slots : (chain + 1) * slots], group
                 )
 
 
@@ -316,10 +322,12 @@
         start = start + other[...].astype(jnp.float32)
     row[:, :cells] = start.astype(jnp.bfloat16)
 
+    groups = groups_of(swaps)
+
     def take(phase):
         messages = received[phase * len(swaps) : (phase + 1) * len(swaps)]
         messages = [ref[ref.shape[0] - part :] for ref in messages]
-        row[:, cells:] = halo_of(messages, swaps, live[live.shape[0] - 1])
+        row[:, cells:] = halo_of(messages, groups, live[live.shape[0] - 1])
 
     by_rule = layer < 0
     for at, phase in picks:

time: 46.4 us -> 46.4 us (level)
  no operation moved by 1% of the time
where the time goes in v11:
time: 46.4 us; the launch traced here: 46 us
  starting transfers between devices  19 us (41%)
  waiting for transfers between devices  15.7 us (34%)
  Pallas kernels  10.8 us (23%)
    ppermute x17, starting transfers between devices, send(): return lax.ppermute(x, MESH_AXES, pairs)  19 us
    ppermute x17, waiting for transfers between devices, send(): return lax.ppermute(x, MESH_AXES, pairs)  15.7 us
    pallas_call x8, Pallas kernels, call(): pl.pallas_call(kernel, out_shape=out_shape, in_specs=[pl.BlockSpec(memory...  10.8 us
  transfers between devices with their start and end apart: 17, of which 6 were waited for; matrix products, arithmetic and copies ran while one was open for 0% of the time, Pallas kernels for 9%

profile of v11, /device:TPU:1, one launch (start us, length us, event | category | flops | bytes accessed | tf_op | source)
XLA Modules:
  0.0 46.0 jit_solution(5279352960248579867)
XLA Ops:
  0.0 3.8 %shard_map.82 = (bf16[1472,128]{1,0:T(8,128)(2,1)S(1)}, bf16[4,192,896]{2,1,0:T(8,128)(2,1)S(1)}, bf16[4,192,128]{2,1,0:T(8,128)(2,1)S(1)}) custom-call(bf16[4,192,896]{2,1,0:T(8,128)(2,1)} %bitcast.20, s32[4,192]{1,0:T(4,128)} %assignment.3, s32[7,1,1,12]{3,2,1,0:T(1,128)} %bitcast.22, bf16[896,896]{1,0:T(8,128)(2,1)} %bitcast.9), custom_call_target="tpu_custom_call" | custom-call | tf_op jit(solution)/shard_map/pallas_call | solution.py:356
  3.8 1.9 %collective-permute-start = (bf16[1472,128]{1,0:T(8,128)(2,1)S(1)}, bf16[1472,128]{1,0:T(8,128)(2,1)S(1)}, u32[]{:S(2)}, u32[]{:S(2)}) collective-permute-start(bf16[1472,128]{1,0:T(8,128)(2,1)S(1)} %get-tuple-element.37), channel_id=1, source_target_pairs={{8,0},{9,1},{10,2},{11,3},{12,4},{13,5},{14,6},{15,7},{16,8},{17,9... | collective-permute-start | bytes 1130504 | tf_op jit(solution)/shard_map/ppermute | solution.py:385
  5.8 0.0 copy-start.1
  5.8 0.1 shard_map.83
  5.9 0.8 %collective-permute-start.1 = (bf16[192,128]{1,0:T(8,128)(2,1)S(1)}, bf16[192,128]{1,0:T(8,128)(2,1)S(1)}, u32[]{:S(2)}, u32[]{:S(2)}) collective-permute-start(bf16[192,128]{1,0:T(8,128)(2,1)S(1)} %get-tuple-element.39), channel_id=1, source_target_pairs={{1,2},{2,1},{5,6},{6,5}} | collective-permute-start | bytes 147464 | tf_op jit(solution)/shard_map/ppermute | solution.py:385
  6.7 0.7 %collective-permute-start.2 = (bf16[192,128]{1,0:T(8,128)(2,1)S(1)}, bf16[192,128]{1,0:T(8,128)(2,1)S(1)}, u32[]{:S(2)}, u32[]{:S(2)}) collective-permute-start(bf16[192,128]{1,0:T(8,128)(2,1)S(1)} %get-tuple-element.40), channel_id=1, source_target_pairs={{0,1},{1,0},{2,3},{3,2},{4,5},{5,4},{6,7},{7,6}} | collective-permute-start | bytes 147464 | tf_op jit(solution)/shard_map/ppermute | solution.py:385
  7.4 0.7 %collective-permute-start.3 = (bf16[192,128]{1,0:T(8,128)(2,1)S(1)}, bf16[192,128]{1,0:T(8,128)(2,1)S(1)}, u32[]{:S(2)}, u32[]{:S(2)}) collective-permute-start(bf16[192,128]{1,0:T(8,128)(2,1)S(1)} %get-tuple-element.41), channel_id=1, source_target_pairs={{0,4},{1,5},{2,6},{3,7},{4,0},{5,1},{6,2},{7,3}} | collective-permute-start | bytes 147464 | tf_op jit(solution)/shard_map/ppermute | solution.py:385
  8.1 0.0 copy-start.3
  8.1 4.1 %shard_map.84 = (f32[384,896]{1,0:T(8,128)S(1)}, bf16[1024,896]{1,0:T(8,128)(2,1)S(1)}, bf16[4,512,256]{2,1,0:T(8,128)(2,1)S(1)}) custom-call(bf16[4,192,896]{2,1,0:T(8,128)(2,1)S(1)} %get-tuple-element.33.starts.refs_0_, bf16[896,896]{1,0:T(8,128)(2,1)S(1)} %bitcast.11, bf16[896,896]{1,0:T(8,128)(2,1)S(1)} %bitcast.13, ...), custom_call_target="tpu_custom_call" | custom-call | tf_op jit(solution)/shard_map/pallas_call | solution.py:356
  12.2 0.0 collective-permute-done.3.refs_8_.refs_11_.refs_3_
  12.2 1.4 %collective-permute-done.refs_4_ = bf16[1472,128]{1,0:T(8,128)(2,1)S(1)} collective-permute-done((bf16[1472,128]{1,0:T(8,128)(2,1)S(1)}, bf16[1472,128]{1,0:T(8,128)(2,1)S(1)}, u32[]{:S(2)}, u32[]{:S(2)}) %collective-permute-start) | collective-permute-done | bytes 376864 | tf_op jit(solution)/shard_map/ppermute | solution.py:385
  13.6 1.3 %collective-permute-start.4 = (bf16[384,896]{1,0:T(8,128)(2,1)S(1)}, bf16[384,896]{1,0:T(8,128)(2,1)S(1)}, u32[]{:S(2)}, u32[]{:S(2)}) collective-permute-start(bf16[384,896]{1,0:T(8,128)(2,1)S(1)} %get-tuple-element.42), channel_id=1, source_target_pairs={{0,8},{1,9},{2,10},{3,11},{4,12},{5,13},{6,14},{7,15}} | collective-permute-start | bytes 2064392 | tf_op jit(solution)/shard_map/ppermute | solution.py:385
  14.9 0.7 %collective-permute-start.5 = (bf16[96,128]{1,0:T(8,128)(2,1)S(1)}, bf16[96,128]{1,0:T(8,128)(2,1)S(1)}, u32[]{:S(2)}, u32[]{:S(2)}) collective-permute-start(bf16[96,128]{1,0:T(8,128)(2,1)S(1)} %get-tuple-element.43), channel_id=1, source_target_pairs={{1,10},{2,9},{5,14},{6,13}} | collective-permute-start | bytes 73736 | tf_op jit(solution)/shard_map/ppermute | solution.py:385
  15.6 1.3 %collective-permute-start.6 = (bf16[96,128]{1,0:T(8,128)(2,1)S(1)}, bf16[96,128]{1,0:T(8,128)(2,1)S(1)}, u32[]{:S(2)}, u32[]{:S(2)}) collective-permute-start(bf16[96,128]{1,0:T(8,128)(2,1)S(1)} %get-tuple-element.44), channel_id=1, source_target_pairs={{0,9},{1,8},{2,11},{3,10},{4,13},{5,12},{6,15},{7,14}} | collective-permute-start | bytes 73736 | tf_op jit(solution)/shard_map/ppermute | solution.py:385
  16.9 1.3 %collective-permute-start.7 = (bf16[96,128]{1,0:T(8,128)(2,1)S(1)}, bf16[96,128]{1,0:T(8,128)(2,1)S(1)}, u32[]{:S(2)}, u32[]{:S(2)}) collective-permute-start(bf16[96,128]{1,0:T(8,128)(2,1)S(1)} %get-tuple-element.45), channel_id=1, source_target_pairs={{0,12},{1,13},{2,14},{3,15},{4,8},{5,9},{6,10},{7,11}} | collective-permute-start | bytes 73736 | tf_op jit(solution)/shard_map/ppermute | solution.py:385
  18.2 0.0 collective-permute-done.5.refs_6_
  18.2 8.0 %collective-permute-done.6.refs_7_ = bf16[96,128]{1,0:T(8,128)(2,1)S(1)} collective-permute-done((bf16[96,128]{1,0:T(8,128)(2,1)S(1)}, bf16[96,128]{1,0:T(8,128)(2,1)S(1)}, u32[]{:S(2)}, u32[]{:S(2)}) %collective-permute-start.6) | collective-permute-done | bytes 24608 | tf_op jit(solution)/shard_map/ppermute | solution.py:385
  26.2 1.8 %collective-permute-done.7.refs_8_ = bf16[96,128]{1,0:T(8,128)(2,1)S(1)} collective-permute-done((bf16[96,128]{1,0:T(8,128)(2,1)S(1)}, bf16[96,128]{1,0:T(8,128)(2,1)S(1)}, u32[]{:S(2)}, u32[]{:S(2)}) %collective-permute-start.7) | collective-permute-done | bytes 24608 | tf_op jit(solution)/shard_map/ppermute | solution.py:385
  28.0 1.3 %shard_map.87 = (bf16[192,896]{1,0:T(8,128)(2,1)S(1)}, bf16[192,896]{1,0:T(8,128)(2,1)S(1)}, bf16[96,128]{1,0:T(8,128)(2,1)S(1)}, bf16[96,128]{1,0:T(8,128)(2,1)S(1)}, bf16[96,128]{1,0:T(8,128)(2,1)S(1)}) custom-call(bf16[4,192,896]{2,1,0:T(8,128)(2,1)S(1)} %get-tuple-element.33.starts.refs_0_, bf16[4,192,128]{2,1,0:T(8,128)(2,1)S(1)} %get-tuple-element.32.refs_1_.live, ...), custom_call_target="tpu_custom_call" | custom-call | tf_op jit(solution)/shard_map/pallas_call | solution.py:356
  29.3 1.3 %collective-permute-start.8 = (bf16[192,896]{1,0:T(8,128)(2,1)S(1)}, bf16[192,896]{1,0:T(8,128)(2,1)S(1)}, u32[]{:S(2)}, u32[]{:S(2)}) collective-permute-start(bf16[192,896]{1,0:T(8,128)(2,1)S(1)} %get-tuple-element.46), channel_id=1, source_target_pairs={{8,16},{9,17},{10,18},{11,19},{12,20},{13,21},{14,22},{15,23}} | collective-permute-start | bytes 1032200 | tf_op jit(solution)/shard_map/ppermute | solution.py:385
  30.6 0.7 %collective-permute-start.9 = (bf16[96,128]{1,0:T(8,128)(2,1)S(1)}, bf16[96,128]{1,0:T(8,128)(2,1)S(1)}, u32[]{:S(2)}, u32[]{:S(2)}) collective-permute-start(bf16[96,128]{1,0:T(8,128)(2,1)S(1)} %get-tuple-element.47), channel_id=1, source_target_pairs={{9,18},{10,17},{13,22},{14,21}} | collective-permute-start | bytes 73736 | tf_op jit(solution)/shard_map/ppermute | solution.py:385
  31.3 1.3 %collective-permute-start.10 = (bf16[96,128]{1,0:T(8,128)(2,1)S(1)}, bf16[96,128]{1,0:T(8,128)(2,1)S(1)}, u32[]{:S(2)}, u32[]{:S(2)}) collective-permute-start(bf16[96,128]{1,0:T(8,128)(2,1)S(1)} %get-tuple-element.48), channel_id=1, source_target_pairs={{8,17},{9,16},{10,19},{11,18},{12,21},{13,20},{14,23},{15,22}} | collective-permute-start | bytes 73736 | tf_op jit(solution)/shard_map/ppermute | solution.py:385
  32.6 1.3 %collective-permute-start.11 = (bf16[96,128]{1,0:T(8,128)(2,1)S(1)}, bf16[96,128]{1,0:T(8,128)(2,1)S(1)}, u32[]{:S(2)}, u32[]{:S(2)}) collective-permute-start(bf16[96,128]{1,0:T(8,128)(2,1)S(1)} %get-tuple-element.49), channel_id=1, source_target_pairs={{8,20},{9,21},{10,22},{11,23},{12,16},{13,17},{14,18},{15,19}} | collective-permute-start | bytes 73736 | tf_op jit(solution)/shard_map/ppermute | solution.py:385
  33.9 1.3 %collective-permute-start.13 = (bf16[192,896]{1,0:T(8,128)(2,1)S(1)}, bf16[192,896]{1,0:T(8,128)(2,1)S(1)}, u32[]{:S(2)}, u32[]{:S(2)}) collective-permute-start(bf16[192,896]{1,0:T(8,128)(2,1)S(1)} %get-tuple-element.51), channel_id=1, source_target_pairs={{8,16},{9,17},{10,18},{11,19},{12,20},{13,21},{14,22},{15,23}} | collective-permute-start | bytes 1032200 | tf_op jit(solution)/shard_map/ppermute | solution.py:385
  35.3 0.1 collective-permute-done.11.refs_8_.refs_6_
  35.3 1.3 %collective-permute-start.12 = (bf16[192,896]{1,0:T(8,128)(2,1)S(1)}, bf16[192,896]{1,0:T(8,128)(2,1)S(1)}, u32[]{:S(2)}, u32[]{:S(2)}) collective-permute-start(bf16[192,896]{1,0:T(8,128)(2,1)S(1)} %get-tuple-element.50), channel_id=1, source_target_pairs={{16,24},{17,25},{18,26},{19,27},{20,28},{21,29},{22,30},{23,31},{0... | collective-permute-start | bytes 1032200 | tf_op jit(solution)/shard_map/ppermute | solution.py:385
  36.6 0.7 %collective-permute-start.14 = (bf16[48,128]{1,0:T(8,128)(2,1)S(1)}, bf16[48,128]{1,0:T(8,128)(2,1)S(1)}, u32[]{:S(2)}, u32[]{:S(2)}) collective-permute-start(bf16[48,128]{1,0:T(8,128)(2,1)S(1)} %get-tuple-element.52), channel_id=1, source_target_pairs={{17,26},{18,25},{21,30},{22,29},{1,10},{2,9},{5,14},{6,13}} | collective-permute-start | bytes 36872 | tf_op jit(solution)/shard_map/ppermute | solution.py:385
  37.3 1.3 %collective-permute-start.15 = (bf16[48,128]{1,0:T(8,128)(2,1)S(1)}, bf16[48,128]{1,0:T(8,128)(2,1)S(1)}, u32[]{:S(2)}, u32[]{:S(2)}) collective-permute-start(bf16[48,128]{1,0:T(8,128)(2,1)S(1)} %get-tuple-element.53), channel_id=1, source_target_pairs={{16,25},{17,24},{18,27},{19,26},{20,29},{21,28},{22,31},{23,30},{0... | collective-permute-start | bytes 36872 | tf_op jit(solution)/shard_map/ppermute | solution.py:385
  38.6 1.3 %collective-permute-start.16 = (bf16[48,128]{1,0:T(8,128)(2,1)S(1)}, bf16[48,128]{1,0:T(8,128)(2,1)S(1)}, u32[]{:S(2)}, u32[]{:S(2)}) collective-permute-start(bf16[48,128]{1,0:T(8,128)(2,1)S(1)} %get-tuple-element.54), channel_id=1, source_target_pairs={{16,28},{17,29},{18,30},{19,31},{20,24},{21,25},{22,26},{23,27},{0... | collective-permute-start | bytes 36872 | tf_op jit(solution)/shard_map/ppermute | solution.py:385
  39.9 2.7 %collective-permute-done.15.refs_8_ = bf16[48,128]{1,0:T(8,128)(2,1)S(1)} collective-permute-done((bf16[48,128]{1,0:T(8,128)(2,1)S(1)}, bf16[48,128]{1,0:T(8,128)(2,1)S(1)}, u32[]{:S(2)}, u32[]{:S(2)}) %collective-permute-start.15) | collective-permute-done | bytes 12320 | tf_op jit(solution)/shard_map/ppermute | solution.py:385
  42.6 1.7 %collective-permute-done.16.refs_9_ = bf16[48,128]{1,0:T(8,128)(2,1)S(1)} collective-permute-done((bf16[48,128]{1,0:T(8,128)(2,1)S(1)}, bf16[48,128]{1,0:T(8,128)(2,1)S(1)}, u32[]{:S(2)}, u32[]{:S(2)}) %collective-permute-start.16) | collective-permute-done | bytes 12320 | tf_op jit(solution)/shard_map/ppermute | solution.py:385
  44.3 1.5 %shard_map.89 = bf16[192,896]{1,0:T(8,128)(2,1)} custom-call(bf16[4,192,128]{2,1,0:T(8,128)(2,1)S(1)} %get-tuple-element.32.refs_1_.live, bf16[4,192,896]{2,1,0:T(8,128)(2,1)S(1)} %get-tuple-element.33.starts.refs_0_, bf16[1024,896]{1,0:T(8,128)(2,1)S(1)} %shard_map.85.refs_2_.map_ext, f32[1,896]{1,0:T(1,128)S(1)} %bitcast.19, ...), custom_call_target="tpu_custom_call" | custom-call | tf_op jit(solution)/shard_map/pallas_call | solution.py:356
  (18 shorter events, 0.1 us)
Async XLA Ops:
  0.0 5.7 %copy-start = (bf16[1,1,1,896,896]{4,3,2,1,0:T(8,128)(2,1)S(1)}, bf16[1,1,1,896,896]{4,3,2,1,0:T(8,128)(2,1)}, u32[]{:S(2)}) copy-start(bf16[1,1,1,896,896]{4,3,2,1,0:T(8,128)(2,1)} %param.12) | copy-start | bytes 4816900
  0.0 5.8 %copy-start.2 = (bf16[1,192,1,1,896]{4,1,3,2,0:T(8,128)(2,1)S(1)}, bf16[1,192,1,1,896]{4,1,3,2,0:T(8,128)(2,1)}, u32[]{:S(2)}) copy-start(bf16[1,192,1,1,896]{4,1,3,2,0:T(8,128)(2,1)} %param.8) | copy-start | bytes 1032196
  3.8 9.8 %collective-permute-start = (bf16[1472,128]{1,0:T(8,128)(2,1)S(1)}, bf16[1472,128]{1,0:T(8,128)(2,1)S(1)}, u32[]{:S(2)}, u32[]{:S(2)}) collective-permute-start(bf16[1472,128]{1,0:T(8,128)(2,1)S(1)} %get-tuple-element.37), channel_id=1, source_target_pairs={{8,0},{9,1},{10,2},{11,3},{12,4},{13,5},{14,6},{15,7},{16,8},{17,9... | collective-permute-start | bytes 1130504 | tf_op jit(solution)/shard_map/ppermute | solution.py:385
  5.8 2.3 %copy-start.1 = (bf16[1,1,1,896,896]{4,3,2,1,0:T(8,128)(2,1)S(1)}, bf16[1,1,1,896,896]{4,3,2,1,0:T(8,128)(2,1)}, u32[]{:S(2)}) copy-start(bf16[1,1,1,896,896]{4,3,2,1,0:T(8,128)(2,1)} %param.13) | copy-start | bytes 4816900
  5.9 6.3 %collective-permute-start.1 = (bf16[192,128]{1,0:T(8,128)(2,1)S(1)}, bf16[192,128]{1,0:T(8,128)(2,1)S(1)}, u32[]{:S(2)}, u32[]{:S(2)}) collective-permute-start(bf16[192,128]{1,0:T(8,128)(2,1)S(1)} %get-tuple-element.39), channel_id=1, source_target_pairs={{1,2},{2,1},{5,6},{6,5}} | collective-permute-start | bytes 147464 | tf_op jit(solution)/shard_map/ppermute | solution.py:385
  6.7 5.5 %collective-permute-start.2 = (bf16[192,128]{1,0:T(8,128)(2,1)S(1)}, bf16[192,128]{1,0:T(8,128)(2,1)S(1)}, u32[]{:S(2)}, u32[]{:S(2)}) collective-permute-start(bf16[192,128]{1,0:T(8,128)(2,1)S(1)} %get-tuple-element.40), channel_id=1, source_target_pairs={{0,1},{1,0},{2,3},{3,2},{4,5},{5,4},{6,7},{7,6}} | collective-permute-start | bytes 147464 | tf_op jit(solution)/shard_map/ppermute | solution.py:385
  7.4 4.8 %collective-permute-start.3 = (bf16[192,128]{1,0:T(8,128)(2,1)S(1)}, bf16[192,128]{1,0:T(8,128)(2,1)S(1)}, u32[]{:S(2)}, u32[]{:S(2)}) collective-permute-start(bf16[192,128]{1,0:T(8,128)(2,1)S(1)} %get-tuple-element.41), channel_id=1, source_target_pairs={{0,4},{1,5},{2,6},{3,7},{4,0},{5,1},{6,2},{7,3}} | collective-permute-start | bytes 147464 | tf_op jit(solution)/shard_map/ppermute | solution.py:385
  8.1 5.6 %copy-start.3 = (f32[1,1,1,896]{3,2,1,0:T(1,128)S(1)}, f32[1,1,1,896]{3,2,1,0:T(1,128)}, u32[]{:S(2)}) copy-start(f32[1,1,1,896]{3,2,1,0:T(1,128)} %param.14) | copy-start | bytes 10756
  13.6 14.4 %collective-permute-start.4 = (bf16[384,896]{1,0:T(8,128)(2,1)S(1)}, bf16[384,896]{1,0:T(8,128)(2,1)S(1)}, u32[]{:S(2)}, u32[]{:S(2)}) collective-permute-start(bf16[384,896]{1,0:T(8,128)(2,1)S(1)} %get-tuple-element.42), channel_id=1, source_target_pairs={{0,8},{1,9},{2,10},{3,11},{4,12},{5,13},{6,14},{7,15}} | collective-permute-start | bytes 2064392 | tf_op jit(solution)/shard_map/ppermute | solution.py:385
  14.9 3.3 %collective-permute-start.5 = (bf16[96,128]{1,0:T(8,128)(2,1)S(1)}, bf16[96,128]{1,0:T(8,128)(2,1)S(1)}, u32[]{:S(2)}, u32[]{:S(2)}) collective-permute-start(bf16[96,128]{1,0:T(8,128)(2,1)S(1)} %get-tuple-element.43), channel_id=1, source_target_pairs={{1,10},{2,9},{5,14},{6,13}} | collective-permute-start | bytes 73736 | tf_op jit(solution)/shard_map/ppermute | solution.py:385
  15.6 10.6 %collective-permute-start.6 = (bf16[96,128]{1,0:T(8,128)(2,1)S(1)}, bf16[96,128]{1,0:T(8,128)(2,1)S(1)}, u32[]{:S(2)}, u32[]{:S(2)}) collective-permute-start(bf16[96,128]{1,0:T(8,128)(2,1)S(1)} %get-tuple-element.44), channel_id=1, source_target_pairs={{0,9},{1,8},{2,11},{3,10},{4,13},{5,12},{6,15},{7,14}} | collective-permute-start | bytes 73736 | tf_op jit(solution)/shard_map/ppermute | solution.py:385
  16.9 11.2 %collective-permute-start.7 = (bf16[96,128]{1,0:T(8,128)(2,1)S(1)}, bf16[96,128]{1,0:T(8,128)(2,1)S(1)}, u32[]{:S(2)}, u32[]{:S(2)}) collective-permute-start(bf16[96,128]{1,0:T(8,128)(2,1)S(1)} %get-tuple-element.45), channel_id=1, source_target_pairs={{0,12},{1,13},{2,14},{3,15},{4,8},{5,9},{6,10},{7,11}} | collective-permute-start | bytes 73736 | tf_op jit(solution)/shard_map/ppermute | solution.py:385
  29.3 6.0 %collective-permute-start.8 = (bf16[192,896]{1,0:T(8,128)(2,1)S(1)}, bf16[192,896]{1,0:T(8,128)(2,1)S(1)}, u32[]{:S(2)}, u32[]{:S(2)}) collective-permute-start(bf16[192,896]{1,0:T(8,128)(2,1)S(1)} %get-tuple-element.46), channel_id=1, source_target_pairs={{8,16},{9,17},{10,18},{11,19},{12,20},{13,21},{14,22},{15,23}} | collective-permute-start | bytes 1032200 | tf_op jit(solution)/shard_map/ppermute | solution.py:385
  30.6 4.6 %collective-permute-start.9 = (bf16[96,128]{1,0:T(8,128)(2,1)S(1)}, bf16[96,128]{1,0:T(8,128)(2,1)S(1)}, u32[]{:S(2)}, u32[]{:S(2)}) collective-permute-start(bf16[96,128]{1,0:T(8,128)(2,1)S(1)} %get-tuple-element.47), channel_id=1, source_target_pairs={{9,18},{10,17},{13,22},{14,21}} | collective-permute-start | bytes 73736 | tf_op jit(solution)/shard_map/ppermute | solution.py:385
  31.3 3.9 %collective-permute-start.10 = (bf16[96,128]{1,0:T(8,128)(2,1)S(1)}, bf16[96,128]{1,0:T(8,128)(2,1)S(1)}, u32[]{:S(2)}, u32[]{:S(2)}) collective-permute-start(bf16[96,128]{1,0:T(8,128)(2,1)S(1)} %get-tuple-element.48), channel_id=1, source_target_pairs={{8,17},{9,16},{10,19},{11,18},{12,21},{13,20},{14,23},{15,22}} | collective-permute-start | bytes 73736 | tf_op jit(solution)/shard_map/ppermute | solution.py:385
  32.6 2.7 %collective-permute-start.11 = (bf16[96,128]{1,0:T(8,128)(2,1)S(1)}, bf16[96,128]{1,0:T(8,128)(2,1)S(1)}, u32[]{:S(2)}, u32[]{:S(2)}) collective-permute-start(bf16[96,128]{1,0:T(8,128)(2,1)S(1)} %get-tuple-element.49), channel_id=1, source_target_pairs={{8,20},{9,21},{10,22},{11,23},{12,16},{13,17},{14,18},{15,19}} | collective-permute-start | bytes 73736 | tf_op jit(solution)/shard_map/ppermute | solution.py:385
  33.9 6.0 %collective-permute-start.13 = (bf16[192,896]{1,0:T(8,128)(2,1)S(1)}, bf16[192,896]{1,0:T(8,128)(2,1)S(1)}, u32[]{:S(2)}, u32[]{:S(2)}) collective-permute-start(bf16[192,896]{1,0:T(8,128)(2,1)S(1)} %get-tuple-element.51), channel_id=1, source_target_pairs={{8,16},{9,17},{10,18},{11,19},{12,20},{13,21},{14,22},{15,23}} | collective-permute-start | bytes 1032200 | tf_op jit(solution)/shard_map/ppermute | solution.py:385
  35.3 9.0 %collective-permute-start.12 = (bf16[192,896]{1,0:T(8,128)(2,1)S(1)}, bf16[192,896]{1,0:T(8,128)(2,1)S(1)}, u32[]{:S(2)}, u32[]{:S(2)}) collective-permute-start(bf16[192,896]{1,0:T(8,128)(2,1)S(1)} %get-tuple-element.50), channel_id=1, source_target_pairs={{16,24},{17,25},{18,26},{19,27},{20,28},{21,29},{22,30},{23,31},{0... | collective-permute-start | bytes 1032200 | tf_op jit(solution)/shard_map/ppermute | solution.py:385
  36.6 3.3 %collective-permute-start.14 = (bf16[48,128]{1,0:T(8,128)(2,1)S(1)}, bf16[48,128]{1,0:T(8,128)(2,1)S(1)}, u32[]{:S(2)}, u32[]{:S(2)}) collective-permute-start(bf16[48,128]{1,0:T(8,128)(2,1)S(1)} %get-tuple-element.52), channel_id=1, source_target_pairs={{17,26},{18,25},{21,30},{22,29},{1,10},{2,9},{5,14},{6,13}} | collective-permute-start | bytes 36872 | tf_op jit(solution)/shard_map/ppermute | solution.py:385
  37.3 5.3 %collective-permute-start.15 = (bf16[48,128]{1,0:T(8,128)(2,1)S(1)}, bf16[48,128]{1,0:T(8,128)(2,1)S(1)}, u32[]{:S(2)}, u32[]{:S(2)}) collective-permute-start(bf16[48,128]{1,0:T(8,128)(2,1)S(1)} %get-tuple-element.53), channel_id=1, source_target_pairs={{16,25},{17,24},{18,27},{19,26},{20,29},{21,28},{22,31},{23,30},{0... | collective-permute-start | bytes 36872 | tf_op jit(solution)/shard_map/ppermute | solution.py:385
  38.6 5.7 %collective-permute-start.16 = (bf16[48,128]{1,0:T(8,128)(2,1)S(1)}, bf16[48,128]{1,0:T(8,128)(2,1)S(1)}, u32[]{:S(2)}, u32[]{:S(2)}) collective-permute-start(bf16[48,128]{1,0:T(8,128)(2,1)S(1)} %get-tuple-element.54), channel_id=1, source_target_pairs={{16,28},{17,29},{18,30},{19,31},{20,24},{21,25},{22,26},{23,27},{0... | collective-permute-start | bytes 36872 | tf_op jit(solution)/shard_map/ppermute | solution.py:385

commit v12 on v11

--- a/solution.py
+++ b/solution.py
@@ -88,13 +88,13 @@
     return lax.axis_size("depth") - 1 - layer
 
 
-def chosen_of(wanted, counts_in, unit):
+def chosen_of(wanted, counts):
     slots = wanted.shape[1]
     shot = lax.broadcasted_iota(jnp.int32, (slots, slots), 0)
     slot = lax.broadcasted_iota(jnp.int32, (1, slots), 1)
     live = jnp.zeros((1, slots), jnp.int32)
     for batch in range(slots // SHOT_BATCH):
-        count = counts_in[unit, 0, 0, batch]
+        count = jnp.broadcast_to(counts[:, batch : batch + 1], (1, slots))
         live = jnp.where(slot >= batch * SHOT_BATCH, count + batch * SHOT_BATCH, live)
     wanted = jnp.where(slot < live, wanted, -1)
     return jnp.where(shot == wanted, 1.0, 0.0).astype(jnp.bfloat16)
@@ -109,16 +109,13 @@
     return copies
 
 
-def fill_live(live_out, counts_in, unit):
+def fill_live(live_out, counts):
     position = lax.broadcasted_iota(jnp.int32, (SHOT_BATCH, LANES), 0)
-    rounds, slots = live_out.shape[:2]
-    for round_number in range(rounds):
-        for batch in range(slots // SHOT_BATCH):
-            count = counts_in[unit + round_number, 0, 0, batch]
+    for r, own in enumerate(counts):
+        for batch in range(own.shape[1]):
+            count = jnp.broadcast_to(own[:, batch : batch + 1], (SHOT_BATCH, LANES))
             rows = slice(batch * SHOT_BATCH, (batch + 1) * SHOT_BATCH)
-            live_out[round_number, rows] = jnp.where(position < count, 1.0, 0.0).astype(
-                jnp.bfloat16
-            )
+            live_out[r, rows] = jnp.where(position < count, 1.0, 0.0).astype(jnp.bfloat16)
 
 
 def edges_kernel(source, assignment, counts, first_map, edge_out, starts_out, live_out, *refs):
@@ -134,23 +131,24 @@
         copies = started(pairs, sems)
         selector = edge_selector(cells)
         copies[0].wait()
-        fill_live(live_out, counts_in, unit)
+        own = [counts_in[unit + r, 0] for r in range(rounds)]
+        fill_live(live_out, own)
         copies[1].wait()
         copies[2].wait()
         first_edge = dot(first_in[...], selector).astype(jnp.bfloat16)
         edge_out[:cells] = first_edge
         for r in range(1, rounds):
             copies[2 + r].wait()
-            chosen = chosen_of(assignment_in[r : r + 1], counts_in, unit + r)
+            chosen = chosen_of(assignment_in[r : r + 1], own[r])
             starts_out[r] = dot_t(chosen, source_in[r]).astype(jnp.bfloat16)
         edges = dot(starts_out[1:].reshape(-1, cells), first_edge)
         edge_out[cells:] = edges.astype(jnp.bfloat16)
 
 
-def opening_kernel(early_layers, swaps, source, assignment, counts, arrival, first_map, *refs):
+def opening_kernel(early_layers, swaps, source, assignment_in, counts_in, arrival, first_map, *refs):
     starts_out, live_out, edge_cells = refs[2:5]
     messages = refs[5 : 5 + len(swaps)]
-    source_in, assignment_in, counts_in, sems = refs[5 + len(swaps) :]
+    source_in, sems = refs[5 + len(swaps) :]
     rounds, slots, cells = source.shape
     part = slots // 4
     layer = lax.axis_index("depth")
@@ -164,17 +162,14 @@
     def _():
         unit = first_unit(layer)
         groups = groups_of(swaps)
-        pairs = [(counts, counts_in), (assignment, assignment_in)]
-        pairs += [(source.at[r], source_in.at[r]) for r in range(rounds)]
-        copies = started(pairs, sems)
+        copies = started([(source.at[r], source_in.at[r]) for r in range(rounds)], sems)
         edge_cells[...] = edge_rows_selector(cells)
         first_edge = dot(first_map[...], edge_selector(cells)).astype(jnp.bfloat16)
-        copies[0].wait()
-        fill_live(live_out, counts_in, unit)
-        copies[1].wait()
+        own = [counts_in[unit + r, 0] for r in range(rounds)]
+        fill_live(live_out, own)
         for r in range(rounds):
-            chosen = chosen_of(assignment_in[r : r + 1], counts_in, unit + r)
-            copies[2 + r].wait()
+            chosen = chosen_of(assignment_in[r : r + 1], own[r])
+            copies[r].wait()
             picked = dot_t(chosen, source_in[r])
             if r == 0:
                 live = live_out[0].astype(jnp.float32)
@@ -221,10 +216,10 @@
     whole_ext[:cells] = dot(coupled(first_map[...], band), second_map[...]).astype(jnp.bfloat16)
 
 
-def inside_kernel(early_layers, starts, first_map, second_map, edge_cells, band, *refs):
-    image_out, whole_ext, band_in, sem = refs
+def inside_kernel(early_layers, starts, first_map, second_map, edge_cells, damping, band, *refs):
+    traces_out, whole_ext, band_in, sem = refs
     slots, cells = starts.shape[1:]
-    chains = image_out.shape[0] // slots
+    chains = traces_out.shape[0] // slots
     early = lax.axis_index("depth") < early_layers
     copy = pltpu.make_async_copy(band, band_in, sem)
     copy.start()
@@ -233,9 +228,11 @@
 
     @pl.when(early)
     def _():
-        mapped = dot(starts[:chains].reshape(-1, cells), first_map[...]).astype(jnp.bfloat16)
+        start = starts[:chains].reshape(-1, cells)
+        mapped = dot(start, first_map[...]).astype(jnp.bfloat16)
         copy.wait()
-        image_out[...] = dot(coupled(mapped, band_in), second_map[...])
+        image = dot(coupled(mapped, band_in), second_map[...])
+        traces_out[...] = blend(image, start, damping[...])
 
     @pl.when(jnp.logical_not(early))
     def _():
@@ -259,44 +256,55 @@
 
 
 def blend(image, start, damp):
-    return (damp * image + (1.0 - damp) * start.astype(jnp.float32)).astype(jnp.bfloat16)
-
-
-def step_kernel(swaps, step, chains, keeps, early_layers, *refs):
-    starts, live, map_ext, damping, edge_next, traces = refs[:6]
-    received = refs[6 : 6 + len(swaps)]
-    opened = refs[6 + len(swaps) : -1 - len(swaps) - keeps]
+    return damp * image + (1.0 - damp) * start.astype(jnp.float32)
+
+
+def takes_part(step, last, early_layers):
+    layer = lax.axis_index("depth")
+    here = (layer >= step) & (layer < step + early_layers)
+    return here | (layer == 0) if last else here
+
+
+def inner_kernel(part_of, rounds, starts, map_ext, damping, *refs):
+    arrived, out = refs[:-1], refs[-1]
+    cells = out.shape[1]
+
+    @pl.when(part_of())
+    def _():
+        start = starts[rounds].reshape(-1, cells).astype(jnp.float32)
+        for traces in arrived:
+            start = start + traces[...].astype(jnp.float32)
+        start = start.astype(jnp.bfloat16)
+        out[...] = blend(dot(start, map_ext[:cells]), start, damping[...])
+
+
+def step_kernel(swaps, step, chains, keeps, part_of, *refs):
+    live, map_ext, damping, edge_next, inner = refs[:5]
+    received = refs[5 : 5 + len(swaps)]
+    opened = refs[5 + len(swaps) : -1 - len(swaps) - keeps]
     outs = refs[-1 - len(swaps) - keeps :]
     traces_out, messages = outs[0], outs[1 + keeps :]
-    slots, cells = starts.shape[1:]
+    cells = inner.shape[1]
+    slots = inner.shape[0] // chains
     part = slots // 4
-    layer = lax.axis_index("depth")
-    here = (layer >= step) & (layer < step + early_layers)
-    if opened:
-        here = here | (layer == 0)
-
-    @pl.when(here)
+
+    @pl.when(part_of())
     def _():
         groups = groups_of(swaps)
+        upper = lax.axis_index("depth") == 0
         halo = []
         for chain in range(chains):
             packed = [ref[chain * part : (chain + 1) * part] for ref in received]
             if opened:
                 at = (step + chain) * part
                 packed = [
-                    jnp.where(layer == 0, ref[at : at + part].astype(jnp.float32), x)
+                    jnp.where(upper, ref[at : at + part].astype(jnp.float32), x)
                     for ref, x in zip(opened, packed)
                 ]
             halo.append(halo_of(packed, groups, live[step + chain]))
         halo = jnp.concatenate(halo, axis=0)
-        start = starts[step : step + chains].reshape(-1, cells)
-        if step == 0:
-            image = traces[...] + dot(halo, map_ext[cells:])
-        else:
-            start = start.astype(jnp.float32) + traces[...].astype(jnp.float32)
-            start = start.astype(jnp.bfloat16)
-            image = dot(jnp.concatenate([start, halo], axis=1), map_ext[...])
-        ended = blend(image, start, damping[...])
+        ended = inner[...] + damping[...] * dot(halo, map_ext[cells:])
+        ended = ended.astype(jnp.bfloat16)
         going = traces_out.shape[0]
         traces_out[...] = ended[:going]
         if keeps:
@@ -311,23 +319,18 @@
                 )
 
 
-def final_kernel(swaps, picks, others, live, starts, map_ext, damping, traces, *refs):
-    slots, cells = traces.shape
-    kept, received = refs[:others], refs[others:-4]
-    traces_out, row, ended, sems = refs[-4:]
+def final_kernel(swaps, picks, live, map_ext, damping, inner, *refs):
+    slots, cells = inner.shape
+    received = refs[:-4]
+    traces_out, halo, ended, sems = refs[-4:]
     part = slots // 4
     layer = lax.axis_index("depth")
-    start = starts[starts.shape[0] - 1].astype(jnp.float32) + traces[...].astype(jnp.float32)
-    for other in kept:
-        start = start + other[...].astype(jnp.float32)
-    row[:, :cells] = start.astype(jnp.bfloat16)
-
     groups = groups_of(swaps)
 
     def take(phase):
         messages = received[phase * len(swaps) : (phase + 1) * len(swaps)]
         messages = [ref[ref.shape[0] - part :] for ref in messages]
-        row[:, cells:] = halo_of(messages, groups, live[live.shape[0] - 1])
+        halo[...] = halo_of(messages, groups, live[live.shape[0] - 1])
 
     by_rule = layer < 0
     for at, phase in picks:
@@ -337,8 +340,8 @@
     copies = []
     half = cells // LANES // 2 * LANES
     for at, columns in enumerate([slice(0, half), slice(half, cells)]):
-        image = dot(row[...], map_ext[:, columns])
-        ended[:, columns] = blend(image, row[:, columns], damping[:, columns])
+        image = dot(halo[...], map_ext[cells:, columns])
+        ended[:, columns] = (inner[:, columns] + damping[:, columns] * image).astype(jnp.bfloat16)
         copies.append(
             pltpu.make_async_copy(ended.at[:, columns], traces_out.at[:, columns], sems.at[at])
         )
@@ -409,7 +412,7 @@
     band = coupling_band(cells)
     whole = array(cells + LANES, cells)
     own = [array(rounds, slots, cells), array(rounds, slots, LANES)]
-    copied = [scratch(source), scratch(assignment), pltpu.SMEM(counts.shape, counts.dtype)]
+    copied = [scratch(source), scratch(assignment), scratch(counts)]
     edge, starts, live = call(
         edges_kernel,
         [array(cells + (rounds - 1) * slots, LANES)] + own,
@@ -422,8 +425,8 @@
         functools.partial(opening_kernel, early_layers, swaps),
         own + [array(LANES, cells)] + [array(rounds * part, LANES)] * len(swaps),
         [source, assignment, counts, arrival, first_map, starts, live],
-        in_hbm=range(3),
-        scratch=copied + [pltpu.SemaphoreType.DMA((2 + rounds,))],
+        in_hbm=range(1),
+        scratch=[scratch(source), pltpu.SemaphoreType.DMA((rounds,))],
         aliases={5: 0, 6: 1},
     )
     starts, live, edge_cells = opened[:3]
@@ -431,11 +434,11 @@
         send(m, [(layer, layer) for layer in range(early_layers)], swap)
         for m, swap in zip(opened[3:], swaps)
     ]
-    traces, map_ext, band = call(
+    inner, map_ext, band = call(
         functools.partial(inside_kernel, early_layers),
         [array(soon * slots, cells, kind=jnp.float32), whole, array(*band.shape)],
-        [starts, first_map, second_map, edge_cells, band],
-        in_hbm=(4,),
+        [starts, first_map, second_map, edge_cells, damping, band],
+        in_hbm=(5,),
         scratch=[pltpu.SemaphoreType.DMA],
     )
     opened = received
@@ -449,9 +452,17 @@
         going = (chains - 1 if keeps else chains) * slots
         outs = [array(going, cells)] + [array(slots, cells)] * keeps
         outs += [array(chains * part, LANES)] * len(swaps)
-        operands = [starts, live, map_ext, damping, edge_next, traces] + received
+        part_of = functools.partial(takes_part, step, last, early_layers)
+        if step > 0:
+            now = slice(step, step + chains)
+            (inner,) = call(
+                functools.partial(inner_kernel, part_of, now),
+                [array(chains * slots, cells, kind=jnp.float32)],
+                [starts, map_ext, damping, traces],
+            )
+        operands = [live, map_ext, damping, edge_next, inner] + received
         ended = call(
-            functools.partial(step_kernel, swaps, step, chains, keeps, early_layers),
+            functools.partial(step_kernel, swaps, step, chains, keeps, part_of),
             outs,
             operands + (opened if last else []),
         )
@@ -472,12 +483,17 @@
                 [first_map, band, second_map, map_ext],
                 aliases={3: 0},
             )
+    (inner,) = call(
+        functools.partial(inner_kernel, lambda: lax.axis_index("depth") >= 0, slice(rounds - 1, rounds)),
+        [array(slots, cells, kind=jnp.float32)],
+        [starts, map_ext, damping, traces] + kept,
+    )
     (ended,) = call(
-        functools.partial(final_kernel, swaps, picks, len(kept)),
+        functools.partial(final_kernel, swaps, picks),
         [array(slots, cells)],
-        [live, starts, map_ext, damping, traces] + kept + arrived,
+        [live, map_ext, damping, inner] + arrived,
         scratch=[
-            pltpu.VMEM((slots, cells + LANES), jnp.bfloat16),
+            pltpu.VMEM((slots, LANES), jnp.bfloat16),
             scratch(arrival),
             pltpu.SemaphoreType.DMA((2,)),
         ],

time: 46.4 us -> 44.7 us (0.963)
  waiting for transfers between devices: 15.7 us -> 13.1 us
  Pallas kernels: 10.8 us -> 11.7 us
    ppermute x17, waiting for transfers between devices: 15.7 us -> 13.1 us  [send(): return lax.ppermute(x, MESH_AXES, pairs)]
    pallas_call x8 -> x11, Pallas kernels: 10.8 us -> 11.7 us  [call(): pl.pallas_call(kernel, out_shape=out_shape, in_specs=[pl.BlockSpec(memory...]
  transfers between devices with their start and end apart: 17 -> 17, of which waited for: 6 -> 6; matrix products, arithmetic and copies ran while one was open for 0% -> 0% of each run, Pallas kernels for 9% -> 13%
where the time goes in v12:
time: 44.7 us; the launch traced here: 44.3 us
  starting transfers between devices  19 us (43%)
  waiting for transfers between devices  13.1 us (29%)
  Pallas kernels  11.7 us (26%)
  between operations  0.52 us (1%)
    ppermute x17, starting transfers between devices, send(): return lax.ppermute(x, MESH_AXES, pairs)  19 us
    ppermute x17, waiting for transfers between devices, send(): return lax.ppermute(x, MESH_AXES, pairs)  13.1 us
    pallas_call x11, Pallas kernels, call(): pl.pallas_call(kernel, out_shape=out_shape, in_specs=[pl.BlockSpec(memory...  11.7 us
  transfers between devices with their start and end apart: 17, of which 6 were waited for; matrix products, arithmetic and copies ran while one was open for 0% of the time, Pallas kernels for 13%

profile of v12, /device:TPU:1, one launch (start us, length us, event | category | flops | bytes accessed | tf_op | source)
XLA Modules:
  0.0 44.3 jit_solution(1158992394156421154)
XLA Ops:
  0.0 4.0 %shard_map.82 = (bf16[1472,128]{1,0:T(8,128)(2,1)S(1)}, bf16[4,192,896]{2,1,0:T(8,128)(2,1)S(1)}, bf16[4,192,128]{2,1,0:T(8,128)(2,1)S(1)}) custom-call(bf16[4,192,896]{2,1,0:T(8,128)(2,1)} %bitcast.26, s32[4,192]{1,0:T(4,128)} %assignment_in.1, s32[7,1,1,12]{3,2,1,0:T(1,128)} %bitcast.24, bf16[896,896]{1,0:T(8,128)(2,1)} %bitcast.9), custom_call_target="tpu_custom_call" | custom-call | tf_op jit(solution)/shard_map/pallas_call | solution.py:359
  4.1 1.9 %collective-permute-start = (bf16[1472,128]{1,0:T(8,128)(2,1)S(1)}, bf16[1472,128]{1,0:T(8,128)(2,1)S(1)}, u32[]{:S(2)}, u32[]{:S(2)}) collective-permute-start(bf16[1472,128]{1,0:T(8,128)(2,1)S(1)} %get-tuple-element.37), channel_id=1, source_target_pairs={{8,0},{9,1},{10,2},{11,3},{12,4},{13,5},{14,6},{15,7},{16,8},{17,9... | collective-permute-start | bytes 1130504 | tf_op jit(solution)/shard_map/ppermute | solution.py:388
  6.0 0.1 shard_map.83
  6.1 0.8 %collective-permute-start.1 = (bf16[192,128]{1,0:T(8,128)(2,1)S(1)}, bf16[192,128]{1,0:T(8,128)(2,1)S(1)}, u32[]{:S(2)}, u32[]{:S(2)}) collective-permute-start(bf16[192,128]{1,0:T(8,128)(2,1)S(1)} %get-tuple-element.39), channel_id=1, source_target_pairs={{1,2},{2,1},{5,6},{6,5}} | collective-permute-start | bytes 147464 | tf_op jit(solution)/shard_map/ppermute | solution.py:388
  6.9 0.7 %collective-permute-start.2 = (bf16[192,128]{1,0:T(8,128)(2,1)S(1)}, bf16[192,128]{1,0:T(8,128)(2,1)S(1)}, u32[]{:S(2)}, u32[]{:S(2)}) collective-permute-start(bf16[192,128]{1,0:T(8,128)(2,1)S(1)} %get-tuple-element.40), channel_id=1, source_target_pairs={{0,1},{1,0},{2,3},{3,2},{4,5},{5,4},{6,7},{7,6}} | collective-permute-start | bytes 147464 | tf_op jit(solution)/shard_map/ppermute | solution.py:388
  7.6 0.7 %collective-permute-start.3 = (bf16[192,128]{1,0:T(8,128)(2,1)S(1)}, bf16[192,128]{1,0:T(8,128)(2,1)S(1)}, u32[]{:S(2)}, u32[]{:S(2)}) collective-permute-start(bf16[192,128]{1,0:T(8,128)(2,1)S(1)} %get-tuple-element.41), channel_id=1, source_target_pairs={{0,4},{1,5},{2,6},{3,7},{4,0},{5,1},{6,2},{7,3}} | collective-permute-start | bytes 147464 | tf_op jit(solution)/shard_map/ppermute | solution.py:388
  8.3 4.1 %shard_map.84 = (f32[384,896]{1,0:T(8,128)S(1)}, bf16[1024,896]{1,0:T(8,128)(2,1)S(1)}, bf16[4,512,256]{2,1,0:T(8,128)(2,1)S(1)}) custom-call(bf16[4,192,896]{2,1,0:T(8,128)(2,1)S(1)} %get-tuple-element.33.starts, bf16[896,896]{1,0:T(8,128)(2,1)S(1)} %bitcast.11, bf16[896,896]{1,0:T(8,128)(2,1)S(1)} %bitcast.13, ...), custom_call_target="tpu_custom_call" | custom-call | tf_op jit(solution)/shard_map/pallas_call | solution.py:359
  12.4 1.4 %collective-permute-done.refs_3_ = bf16[1472,128]{1,0:T(8,128)(2,1)S(1)} collective-permute-done((bf16[1472,128]{1,0:T(8,128)(2,1)S(1)}, bf16[1472,128]{1,0:T(8,128)(2,1)S(1)}, u32[]{:S(2)}, u32[]{:S(2)}) %collective-permute-start) | collective-permute-done | bytes 376864 | tf_op jit(solution)/shard_map/ppermute | solution.py:388
  13.8 1.3 %collective-permute-start.4 = (bf16[384,896]{1,0:T(8,128)(2,1)S(1)}, bf16[384,896]{1,0:T(8,128)(2,1)S(1)}, u32[]{:S(2)}, u32[]{:S(2)}) collective-permute-start(bf16[384,896]{1,0:T(8,128)(2,1)S(1)} %get-tuple-element.42), channel_id=1, source_target_pairs={{0,8},{1,9},{2,10},{3,11},{4,12},{5,13},{6,14},{7,15}} | collective-permute-start | bytes 2064392 | tf_op jit(solution)/shard_map/ppermute | solution.py:388
  15.1 0.7 %collective-permute-start.5 = (bf16[96,128]{1,0:T(8,128)(2,1)S(1)}, bf16[96,128]{1,0:T(8,128)(2,1)S(1)}, u32[]{:S(2)}, u32[]{:S(2)}) collective-permute-start(bf16[96,128]{1,0:T(8,128)(2,1)S(1)} %get-tuple-element.43), channel_id=1, source_target_pairs={{1,10},{2,9},{5,14},{6,13}} | collective-permute-start | bytes 73736 | tf_op jit(solution)/shard_map/ppermute | solution.py:388
  15.8 1.3 %collective-permute-start.6 = (bf16[96,128]{1,0:T(8,128)(2,1)S(1)}, bf16[96,128]{1,0:T(8,128)(2,1)S(1)}, u32[]{:S(2)}, u32[]{:S(2)}) collective-permute-start(bf16[96,128]{1,0:T(8,128)(2,1)S(1)} %get-tuple-element.44), channel_id=1, source_target_pairs={{0,9},{1,8},{2,11},{3,10},{4,13},{5,12},{6,15},{7,14}} | collective-permute-start | bytes 73736 | tf_op jit(solution)/shard_map/ppermute | solution.py:388
  17.1 1.3 %collective-permute-start.7 = (bf16[96,128]{1,0:T(8,128)(2,1)S(1)}, bf16[96,128]{1,0:T(8,128)(2,1)S(1)}, u32[]{:S(2)}, u32[]{:S(2)}) collective-permute-start(bf16[96,128]{1,0:T(8,128)(2,1)S(1)} %get-tuple-element.45), channel_id=1, source_target_pairs={{0,12},{1,13},{2,14},{3,15},{4,8},{5,9},{6,10},{7,11}} | collective-permute-start | bytes 73736 | tf_op jit(solution)/shard_map/ppermute | solution.py:388
  18.4 0.2 shard_map.85.map_ext.refs_1_
  18.6 4.8 %collective-permute-done.4.refs_0_ = bf16[384,896]{1,0:T(8,128)(2,1)S(1)} collective-permute-done((bf16[384,896]{1,0:T(8,128)(2,1)S(1)}, bf16[384,896]{1,0:T(8,128)(2,1)S(1)}, u32[]{:S(2)}, u32[]{:S(2)}) %collective-permute-start.4) | collective-permute-done | bytes 688160 | tf_op jit(solution)/shard_map/ppermute | solution.py:388
  23.4 1.0 %shard_map.87.refs_4_ = f32[384,896]{1,0:T(8,128)S(1)} custom-call(bf16[4,192,896]{2,1,0:T(8,128)(2,1)S(1)} %get-tuple-element.33.starts, bf16[1024,896]{1,0:T(8,128)(2,1)S(1)} %shard_map.85.map_ext.refs_1_, f32[1,896]{1,0:T(1,128)S(1)} %bitcast.18, bf16[384,896]{1,0:T(8,128)(2,1)S(1)} %collective-permute-done.4.refs_0_), custom_call_target="tpu_custom_call" | custom-call | tf_op jit(solution)/shard_map/pallas_call | solution.py:359
  24.4 1.2 %collective-permute-done.6.refs_6_ = bf16[96,128]{1,0:T(8,128)(2,1)S(1)} collective-permute-done((bf16[96,128]{1,0:T(8,128)(2,1)S(1)}, bf16[96,128]{1,0:T(8,128)(2,1)S(1)}, u32[]{:S(2)}, u32[]{:S(2)}) %collective-permute-start.6) | collective-permute-done | bytes 24608 | tf_op jit(solution)/shard_map/ppermute | solution.py:388
  25.5 1.8 %collective-permute-done.7.refs_7_ = bf16[96,128]{1,0:T(8,128)(2,1)S(1)} collective-permute-done((bf16[96,128]{1,0:T(8,128)(2,1)S(1)}, bf16[96,128]{1,0:T(8,128)(2,1)S(1)}, u32[]{:S(2)}, u32[]{:S(2)}) %collective-permute-start.7) | collective-permute-done | bytes 24608 | tf_op jit(solution)/shard_map/ppermute | solution.py:388
  27.4 0.7 %shard_map.88 = (bf16[192,896]{1,0:T(8,128)(2,1)S(1)}, bf16[192,896]{1,0:T(8,128)(2,1)S(1)}, bf16[96,128]{1,0:T(8,128)(2,1)S(1)}, bf16[96,128]{1,0:T(8,128)(2,1)S(1)}, bf16[96,128]{1,0:T(8,128)(2,1)S(1)}) custom-call(bf16[4,192,128]{2,1,0:T(8,128)(2,1)S(1)} %get-tuple-element.32.refs_0_.live, bf16[1024,896]{1,0:T(8,128)(2,1)S(1)} %shard_map.85.map_ext.refs_1_, ...), custom_call_target="tpu_custom_call" | custom-call | tf_op jit(solution)/shard_map/pallas_call | solution.py:359
  28.1 1.3 %collective-permute-start.8 = (bf16[192,896]{1,0:T(8,128)(2,1)S(1)}, bf16[192,896]{1,0:T(8,128)(2,1)S(1)}, u32[]{:S(2)}, u32[]{:S(2)}) collective-permute-start(bf16[192,896]{1,0:T(8,128)(2,1)S(1)} %get-tuple-element.46), channel_id=1, source_target_pairs={{8,16},{9,17},{10,18},{11,19},{12,20},{13,21},{14,22},{15,23}} | collective-permute-start | bytes 1032200 | tf_op jit(solution)/shard_map/ppermute | solution.py:388
  29.4 0.7 %collective-permute-start.9 = (bf16[96,128]{1,0:T(8,128)(2,1)S(1)}, bf16[96,128]{1,0:T(8,128)(2,1)S(1)}, u32[]{:S(2)}, u32[]{:S(2)}) collective-permute-start(bf16[96,128]{1,0:T(8,128)(2,1)S(1)} %get-tuple-element.47), channel_id=1, source_target_pairs={{9,18},{10,17},{13,22},{14,21}} | collective-permute-start | bytes 73736 | tf_op jit(solution)/shard_map/ppermute | solution.py:388
  30.1 1.3 %collective-permute-start.10 = (bf16[96,128]{1,0:T(8,128)(2,1)S(1)}, bf16[96,128]{1,0:T(8,128)(2,1)S(1)}, u32[]{:S(2)}, u32[]{:S(2)}) collective-permute-start(bf16[96,128]{1,0:T(8,128)(2,1)S(1)} %get-tuple-element.48), channel_id=1, source_target_pairs={{8,17},{9,16},{10,19},{11,18},{12,21},{13,20},{14,23},{15,22}} | collective-permute-start | bytes 73736 | tf_op jit(solution)/shard_map/ppermute | solution.py:388
  31.4 1.3 %collective-permute-start.11 = (bf16[96,128]{1,0:T(8,128)(2,1)S(1)}, bf16[96,128]{1,0:T(8,128)(2,1)S(1)}, u32[]{:S(2)}, u32[]{:S(2)}) collective-permute-start(bf16[96,128]{1,0:T(8,128)(2,1)S(1)} %get-tuple-element.49), channel_id=1, source_target_pairs={{8,20},{9,21},{10,22},{11,23},{12,16},{13,17},{14,18},{15,19}} | collective-permute-start | bytes 73736 | tf_op jit(solution)/shard_map/ppermute | solution.py:388
  32.7 1.3 %collective-permute-start.13 = (bf16[192,896]{1,0:T(8,128)(2,1)S(1)}, bf16[192,896]{1,0:T(8,128)(2,1)S(1)}, u32[]{:S(2)}, u32[]{:S(2)}) collective-permute-start(bf16[192,896]{1,0:T(8,128)(2,1)S(1)} %get-tuple-element.51), channel_id=1, source_target_pairs={{8,16},{9,17},{10,18},{11,19},{12,20},{13,21},{14,22},{15,23}} | collective-permute-start | bytes 1032200 | tf_op jit(solution)/shard_map/ppermute | solution.py:388
  34.1 0.0 collective-permute-done.11.refs_7_.refs_5_
  34.1 1.3 %collective-permute-start.12 = (bf16[192,896]{1,0:T(8,128)(2,1)S(1)}, bf16[192,896]{1,0:T(8,128)(2,1)S(1)}, u32[]{:S(2)}, u32[]{:S(2)}) collective-permute-start(bf16[192,896]{1,0:T(8,128)(2,1)S(1)} %get-tuple-element.50), channel_id=1, source_target_pairs={{16,24},{17,25},{18,26},{19,27},{20,28},{21,29},{22,30},{23,31},{0... | collective-permute-start | bytes 1032200 | tf_op jit(solution)/shard_map/ppermute | solution.py:388
  35.4 0.7 %collective-permute-start.14 = (bf16[48,128]{1,0:T(8,128)(2,1)S(1)}, bf16[48,128]{1,0:T(8,128)(2,1)S(1)}, u32[]{:S(2)}, u32[]{:S(2)}) collective-permute-start(bf16[48,128]{1,0:T(8,128)(2,1)S(1)} %get-tuple-element.52), channel_id=1, source_target_pairs={{17,26},{18,25},{21,30},{22,29},{1,10},{2,9},{5,14},{6,13}} | collective-permute-start | bytes 36872 | tf_op jit(solution)/shard_map/ppermute | solution.py:388
  36.1 1.3 %collective-permute-start.15 = (bf16[48,128]{1,0:T(8,128)(2,1)S(1)}, bf16[48,128]{1,0:T(8,128)(2,1)S(1)}, u32[]{:S(2)}, u32[]{:S(2)}) collective-permute-start(bf16[48,128]{1,0:T(8,128)(2,1)S(1)} %get-tuple-element.53), channel_id=1, source_target_pairs={{16,25},{17,24},{18,27},{19,26},{20,29},{21,28},{22,31},{23,30},{0... | collective-permute-start | bytes 36872 | tf_op jit(solution)/shard_map/ppermute | solution.py:388
  37.4 1.3 %collective-permute-start.16 = (bf16[48,128]{1,0:T(8,128)(2,1)S(1)}, bf16[48,128]{1,0:T(8,128)(2,1)S(1)}, u32[]{:S(2)}, u32[]{:S(2)}) collective-permute-start(bf16[48,128]{1,0:T(8,128)(2,1)S(1)} %get-tuple-element.54), channel_id=1, source_target_pairs={{16,28},{17,29},{18,30},{19,31},{20,24},{21,25},{22,26},{23,27},{0... | collective-permute-start | bytes 36872 | tf_op jit(solution)/shard_map/ppermute | solution.py:388
  38.7 0.6 %shard_map.91.inner = f32[192,896]{1,0:T(8,128)S(1)} custom-call(bf16[4,192,896]{2,1,0:T(8,128)(2,1)S(1)} %get-tuple-element.33.starts, bf16[1024,896]{1,0:T(8,128)(2,1)S(1)} %shard_map.85.map_ext.refs_1_, f32[1,896]{1,0:T(1,128)S(1)} %bitcast.22, bf16[192,896]{1,0:T(8,128)(2,1)S(1)} %collective-permute-done.12.refs_0_, ...), custom_call_target="tpu_custom_call" | custom-call | tf_op jit(solution)/shard_map/pallas_call | solution.py:359
  39.3 2.1 %collective-permute-done.15.refs_7_ = bf16[48,128]{1,0:T(8,128)(2,1)S(1)} collective-permute-done((bf16[48,128]{1,0:T(8,128)(2,1)S(1)}, bf16[48,128]{1,0:T(8,128)(2,1)S(1)}, u32[]{:S(2)}, u32[]{:S(2)}) %collective-permute-start.15) | collective-permute-done | bytes 12320 | tf_op jit(solution)/shard_map/ppermute | solution.py:388
  41.4 1.7 %collective-permute-done.16.refs_8_ = bf16[48,128]{1,0:T(8,128)(2,1)S(1)} collective-permute-done((bf16[48,128]{1,0:T(8,128)(2,1)S(1)}, bf16[48,128]{1,0:T(8,128)(2,1)S(1)}, u32[]{:S(2)}, u32[]{:S(2)}) %collective-permute-start.16) | collective-permute-done | bytes 12320 | tf_op jit(solution)/shard_map/ppermute | solution.py:388
  43.1 1.1 %shard_map.92 = bf16[192,896]{1,0:T(8,128)(2,1)} custom-call(bf16[4,192,128]{2,1,0:T(8,128)(2,1)S(1)} %get-tuple-element.32.refs_0_.live, bf16[1024,896]{1,0:T(8,128)(2,1)S(1)} %shard_map.85.map_ext.refs_1_, f32[1,896]{1,0:T(1,128)S(1)} %bitcast.23, f32[192,896]{1,0:T(8,128)S(1)} %shard_map.91.inner, ...), custom_call_target="tpu_custom_call" | custom-call | tf_op jit(solution)/shard_map/pallas_call | solution.py:359
  (25 shorter events, 0.1 us)
Async XLA Ops:
  0.0 6.0 %copy-start = (bf16[1,1,1,896,896]{4,3,2,1,0:T(8,128)(2,1)S(1)}, bf16[1,1,1,896,896]{4,3,2,1,0:T(8,128)(2,1)}, u32[]{:S(2)}) copy-start(bf16[1,1,1,896,896]{4,3,2,1,0:T(8,128)(2,1)} %param.12) | copy-start | bytes 4816900
  0.0 6.0 %copy-start.2 = (bf16[1,192,1,1,896]{4,1,3,2,0:T(8,128)(2,1)S(1)}, bf16[1,192,1,1,896]{4,1,3,2,0:T(8,128)(2,1)}, u32[]{:S(2)}) copy-start(bf16[1,192,1,1,896]{4,1,3,2,0:T(8,128)(2,1)} %param.8) | copy-start | bytes 1032196
  0.0 6.0 %copy-start.4 = (s32[4,192]{1,0:T(4,128)S(1)}, s32[4,192]{1,0:T(4,128)}, u32[]{:S(2)}) copy-start(s32[4,192]{1,0:T(4,128)} %assignment_in.1) | copy-start | bytes 9220
  0.0 6.0 %copy-start.5 = (s32[7,12,1,1]{1,3,2,0:T(1,128)S(1)}, s32[7,12,1,1]{1,3,2,0:T(1,128)}, u32[]{:S(2)}) copy-start(s32[7,12,1,1]{1,3,2,0:T(1,128)} %param.11) | copy-start | bytes 1012
  4.1 9.8 %collective-permute-start = (bf16[1472,128]{1,0:T(8,128)(2,1)S(1)}, bf16[1472,128]{1,0:T(8,128)(2,1)S(1)}, u32[]{:S(2)}, u32[]{:S(2)}) collective-permute-start(bf16[1472,128]{1,0:T(8,128)(2,1)S(1)} %get-tuple-element.37), channel_id=1, source_target_pairs={{8,0},{9,1},{10,2},{11,3},{12,4},{13,5},{14,6},{15,7},{16,8},{17,9... | collective-permute-start | bytes 1130504 | tf_op jit(solution)/shard_map/ppermute | solution.py:388
  6.0 2.3 %copy-start.1 = (bf16[1,1,1,896,896]{4,3,2,1,0:T(8,128)(2,1)S(1)}, bf16[1,1,1,896,896]{4,3,2,1,0:T(8,128)(2,1)}, u32[]{:S(2)}) copy-start(bf16[1,1,1,896,896]{4,3,2,1,0:T(8,128)(2,1)} %param.13) | copy-start | bytes 4816900
  6.0 2.3 %copy-start.3 = (f32[1,1,1,896]{3,2,1,0:T(1,128)S(1)}, f32[1,1,1,896]{3,2,1,0:T(1,128)}, u32[]{:S(2)}) copy-start(f32[1,1,1,896]{3,2,1,0:T(1,128)} %param.14) | copy-start | bytes 10756
  6.1 6.3 %collective-permute-start.1 = (bf16[192,128]{1,0:T(8,128)(2,1)S(1)}, bf16[192,128]{1,0:T(8,128)(2,1)S(1)}, u32[]{:S(2)}, u32[]{:S(2)}) collective-permute-start(bf16[192,128]{1,0:T(8,128)(2,1)S(1)} %get-tuple-element.39), channel_id=1, source_target_pairs={{1,2},{2,1},{5,6},{6,5}} | collective-permute-start | bytes 147464 | tf_op jit(solution)/shard_map/ppermute | solution.py:388
  6.9 5.5 %collective-permute-start.2 = (bf16[192,128]{1,0:T(8,128)(2,1)S(1)}, bf16[192,128]{1,0:T(8,128)(2,1)S(1)}, u32[]{:S(2)}, u32[]{:S(2)}) collective-permute-start(bf16[192,128]{1,0:T(8,128)(2,1)S(1)} %get-tuple-element.40), channel_id=1, source_target_pairs={{0,1},{1,0},{2,3},{3,2},{4,5},{5,4},{6,7},{7,6}} | collective-permute-start | bytes 147464 | tf_op jit(solution)/shard_map/ppermute | solution.py:388
  7.6 4.8 %collective-permute-start.3 = (bf16[192,128]{1,0:T(8,128)(2,1)S(1)}, bf16[192,128]{1,0:T(8,128)(2,1)S(1)}, u32[]{:S(2)}, u32[]{:S(2)}) collective-permute-start(bf16[192,128]{1,0:T(8,128)(2,1)S(1)} %get-tuple-element.41), channel_id=1, source_target_pairs={{0,4},{1,5},{2,6},{3,7},{4,0},{5,1},{6,2},{7,3}} | collective-permute-start | bytes 147464 | tf_op jit(solution)/shard_map/ppermute | solution.py:388
  13.8 9.6 %collective-permute-start.4 = (bf16[384,896]{1,0:T(8,128)(2,1)S(1)}, bf16[384,896]{1,0:T(8,128)(2,1)S(1)}, u32[]{:S(2)}, u32[]{:S(2)}) collective-permute-start(bf16[384,896]{1,0:T(8,128)(2,1)S(1)} %get-tuple-element.42), channel_id=1, source_target_pairs={{0,8},{1,9},{2,10},{3,11},{4,12},{5,13},{6,14},{7,15}} | collective-permute-start | bytes 2064392 | tf_op jit(solution)/shard_map/ppermute | solution.py:388
  15.1 9.3 %collective-permute-start.5 = (bf16[96,128]{1,0:T(8,128)(2,1)S(1)}, bf16[96,128]{1,0:T(8,128)(2,1)S(1)}, u32[]{:S(2)}, u32[]{:S(2)}) collective-permute-start(bf16[96,128]{1,0:T(8,128)(2,1)S(1)} %get-tuple-element.43), channel_id=1, source_target_pairs={{1,10},{2,9},{5,14},{6,13}} | collective-permute-start | bytes 73736 | tf_op jit(solution)/shard_map/ppermute | solution.py:388
  15.8 9.7 %collective-permute-start.6 = (bf16[96,128]{1,0:T(8,128)(2,1)S(1)}, bf16[96,128]{1,0:T(8,128)(2,1)S(1)}, u32[]{:S(2)}, u32[]{:S(2)}) collective-permute-start(bf16[96,128]{1,0:T(8,128)(2,1)S(1)} %get-tuple-element.44), channel_id=1, source_target_pairs={{0,9},{1,8},{2,11},{3,10},{4,13},{5,12},{6,15},{7,14}} | collective-permute-start | bytes 73736 | tf_op jit(solution)/shard_map/ppermute | solution.py:388
  17.1 10.3 %collective-permute-start.7 = (bf16[96,128]{1,0:T(8,128)(2,1)S(1)}, bf16[96,128]{1,0:T(8,128)(2,1)S(1)}, u32[]{:S(2)}, u32[]{:S(2)}) collective-permute-start(bf16[96,128]{1,0:T(8,128)(2,1)S(1)} %get-tuple-element.45), channel_id=1, source_target_pairs={{0,12},{1,13},{2,14},{3,15},{4,8},{5,9},{6,10},{7,11}} | collective-permute-start | bytes 73736 | tf_op jit(solution)/shard_map/ppermute | solution.py:388
  28.1 5.9 %collective-permute-start.8 = (bf16[192,896]{1,0:T(8,128)(2,1)S(1)}, bf16[192,896]{1,0:T(8,128)(2,1)S(1)}, u32[]{:S(2)}, u32[]{:S(2)}) collective-permute-start(bf16[192,896]{1,0:T(8,128)(2,1)S(1)} %get-tuple-element.46), channel_id=1, source_target_pairs={{8,16},{9,17},{10,18},{11,19},{12,20},{13,21},{14,22},{15,23}} | collective-permute-start | bytes 1032200 | tf_op jit(solution)/shard_map/ppermute | solution.py:388
  29.4 4.6 %collective-permute-start.9 = (bf16[96,128]{1,0:T(8,128)(2,1)S(1)}, bf16[96,128]{1,0:T(8,128)(2,1)S(1)}, u32[]{:S(2)}, u32[]{:S(2)}) collective-permute-start(bf16[96,128]{1,0:T(8,128)(2,1)S(1)} %get-tuple-element.47), channel_id=1, source_target_pairs={{9,18},{10,17},{13,22},{14,21}} | collective-permute-start | bytes 73736 | tf_op jit(solution)/shard_map/ppermute | solution.py:388
  30.1 4.0 %collective-permute-start.10 = (bf16[96,128]{1,0:T(8,128)(2,1)S(1)}, bf16[96,128]{1,0:T(8,128)(2,1)S(1)}, u32[]{:S(2)}, u32[]{:S(2)}) collective-permute-start(bf16[96,128]{1,0:T(8,128)(2,1)S(1)} %get-tuple-element.48), channel_id=1, source_target_pairs={{8,17},{9,16},{10,19},{11,18},{12,21},{13,20},{14,23},{15,22}} | collective-permute-start | bytes 73736 | tf_op jit(solution)/shard_map/ppermute | solution.py:388
  31.4 2.7 %collective-permute-start.11 = (bf16[96,128]{1,0:T(8,128)(2,1)S(1)}, bf16[96,128]{1,0:T(8,128)(2,1)S(1)}, u32[]{:S(2)}, u32[]{:S(2)}) collective-permute-start(bf16[96,128]{1,0:T(8,128)(2,1)S(1)} %get-tuple-element.49), channel_id=1, source_target_pairs={{8,20},{9,21},{10,22},{11,23},{12,16},{13,17},{14,18},{15,19}} | collective-permute-start | bytes 73736 | tf_op jit(solution)/shard_map/ppermute | solution.py:388
  32.7 6.0 %collective-permute-start.13 = (bf16[192,896]{1,0:T(8,128)(2,1)S(1)}, bf16[192,896]{1,0:T(8,128)(2,1)S(1)}, u32[]{:S(2)}, u32[]{:S(2)}) collective-permute-start(bf16[192,896]{1,0:T(8,128)(2,1)S(1)} %get-tuple-element.51), channel_id=1, source_target_pairs={{8,16},{9,17},{10,18},{11,19},{12,20},{13,21},{14,22},{15,23}} | collective-permute-start | bytes 1032200 | tf_op jit(solution)/shard_map/ppermute | solution.py:388
  34.1 4.6 %collective-permute-start.12 = (bf16[192,896]{1,0:T(8,128)(2,1)S(1)}, bf16[192,896]{1,0:T(8,128)(2,1)S(1)}, u32[]{:S(2)}, u32[]{:S(2)}) collective-permute-start(bf16[192,896]{1,0:T(8,128)(2,1)S(1)} %get-tuple-element.50), channel_id=1, source_target_pairs={{16,24},{17,25},{18,26},{19,27},{20,28},{21,29},{22,30},{23,31},{0... | collective-permute-start | bytes 1032200 | tf_op jit(solution)/shard_map/ppermute | solution.py:388
  35.4 3.9 %collective-permute-start.14 = (bf16[48,128]{1,0:T(8,128)(2,1)S(1)}, bf16[48,128]{1,0:T(8,128)(2,1)S(1)}, u32[]{:S(2)}, u32[]{:S(2)}) collective-permute-start(bf16[48,128]{1,0:T(8,128)(2,1)S(1)} %get-tuple-element.52), channel_id=1, source_target_pairs={{17,26},{18,25},{21,30},{22,29},{1,10},{2,9},{5,14},{6,13}} | collective-permute-start | bytes 36872 | tf_op jit(solution)/shard_map/ppermute | solution.py:388
  36.1 5.3 %collective-permute-start.15 = (bf16[48,128]{1,0:T(8,128)(2,1)S(1)}, bf16[48,128]{1,0:T(8,128)(2,1)S(1)}, u32[]{:S(2)}, u32[]{:S(2)}) collective-permute-start(bf16[48,128]{1,0:T(8,128)(2,1)S(1)} %get-tuple-element.53), channel_id=1, source_target_pairs={{16,25},{17,24},{18,27},{19,26},{20,29},{21,28},{22,31},{23,30},{0... | collective-permute-start | bytes 36872 | tf_op jit(solution)/shard_map/ppermute | solution.py:388
  37.4 5.7 %collective-permute-start.16 = (bf16[48,128]{1,0:T(8,128)(2,1)S(1)}, bf16[48,128]{1,0:T(8,128)(2,1)S(1)}, u32[]{:S(2)}, u32[]{:S(2)}) collective-permute-start(bf16[48,128]{1,0:T(8,128)(2,1)S(1)} %get-tuple-element.54), channel_id=1, source_target_pairs={{16,28},{17,29},{18,30},{19,31},{20,24},{21,25},{22,26},{23,27},{0... | collective-permute-start | bytes 36872 | tf_op jit(solution)/shard_map/ppermute | solution.py:388

commit v13 on v12

--- a/solution.py
+++ b/solution.py
@@ -167,10 +167,10 @@
         first_edge = dot(first_map[...], edge_selector(cells)).astype(jnp.bfloat16)
         own = [counts_in[unit + r, 0] for r in range(rounds)]
         fill_live(live_out, own)
+        chosen = [chosen_of(assignment_in[r : r + 1], own[r]) for r in range(rounds)]
         for r in range(rounds):
-            chosen = chosen_of(assignment_in[r : r + 1], own[r])
             copies[r].wait()
-            picked = dot_t(chosen, source_in[r])
+            picked = dot_t(chosen[r], source_in[r])
             if r == 0:
                 live = live_out[0].astype(jnp.float32)
                 live = jnp.concatenate([live] * (cells // LANES), axis=1)
@@ -259,29 +259,29 @@
     return damp * image + (1.0 - damp) * start.astype(jnp.float32)
 
 
-def takes_part(step, last, early_layers):
+def takes_part(step, early_layers):
     layer = lax.axis_index("depth")
-    here = (layer >= step) & (layer < step + early_layers)
-    return here | (layer == 0) if last else here
-
-
-def inner_kernel(part_of, rounds, starts, map_ext, damping, *refs):
-    arrived, out = refs[:-1], refs[-1]
-    cells = out.shape[1]
+    return (layer >= step) & (layer < step + early_layers)
+
+
+def inner_kernel(part_of, rounds, extras, starts, map_ext, damping, traces, *refs):
+    others, out = refs[:-1], refs[-1]
+    rows, cells = out.shape
 
     @pl.when(part_of())
     def _():
         start = starts[rounds].reshape(-1, cells).astype(jnp.float32)
-        for traces in arrived:
-            start = start + traces[...].astype(jnp.float32)
-        start = start.astype(jnp.bfloat16)
+        came = traces[:rows].astype(jnp.float32)
+        for (layer, row), other in zip(extras, others):
+            here = lax.axis_index("depth") == layer
+            came = jnp.where(here, other[row : row + rows].astype(jnp.float32), came)
+        start = (start + came).astype(jnp.bfloat16)
         out[...] = blend(dot(start, map_ext[:cells]), start, damping[...])
 
 
 def step_kernel(swaps, step, chains, keeps, part_of, *refs):
     live, map_ext, damping, edge_next, inner = refs[:5]
     received = refs[5 : 5 + len(swaps)]
-    opened = refs[5 + len(swaps) : -1 - len(swaps) - keeps]
     outs = refs[-1 - len(swaps) - keeps :]
     traces_out, messages = outs[0], outs[1 + keeps :]
     cells = inner.shape[1]
@@ -291,16 +291,9 @@
     @pl.when(part_of())
     def _():
         groups = groups_of(swaps)
-        upper = lax.axis_index("depth") == 0
         halo = []
         for chain in range(chains):
             packed = [ref[chain * part : (chain + 1) * part] for ref in received]
-            if opened:
-                at = (step + chain) * part
-                packed = [
-                    jnp.where(upper, ref[at : at + part].astype(jnp.float32), x)
-                    for ref, x in zip(opened, packed)
-                ]
             halo.append(halo_of(packed, groups, live[step + chain]))
         halo = jnp.concatenate(halo, axis=0)
         ended = inner[...] + damping[...] * dot(halo, map_ext[cells:])
@@ -400,7 +393,7 @@
     damping = damping[0, 0]
     swaps = exchanges()
     early_layers = layers - rounds + 1
-    soon = rounds - 2
+    soon = rounds - 1
 
     def array(*shape, kind=jnp.bfloat16):
         return jax.ShapeDtypeStruct(shape, kind)
@@ -441,22 +434,21 @@
         in_hbm=(5,),
         scratch=[pltpu.SemaphoreType.DMA],
     )
-    opened = received
-    arrived = list(opened)
+    arrived = list(received)
     picks = [(0, 0)]
     kept = []
+    extras = []
     for step in range(rounds - 1):
-        chains = min(rounds - 1 - step, soon)
-        last = step == rounds - 2
-        keeps = step + chains == rounds - 1 and not last
+        chains = soon - step
+        keeps = chains > 1 and step > 0
         going = (chains - 1 if keeps else chains) * slots
         outs = [array(going, cells)] + [array(slots, cells)] * keeps
         outs += [array(chains * part, LANES)] * len(swaps)
-        part_of = functools.partial(takes_part, step, last, early_layers)
+        part_of = functools.partial(takes_part, step, early_layers)
         if step > 0:
             now = slice(step, step + chains)
             (inner,) = call(
-                functools.partial(inner_kernel, part_of, now),
+                functools.partial(inner_kernel, part_of, now, []),
                 [array(chains * slots, cells, kind=jnp.float32)],
                 [starts, map_ext, damping, traces],
             )
@@ -464,18 +456,20 @@
         ended = call(
             functools.partial(step_kernel, swaps, step, chains, keeps, part_of),
             outs,
-            operands + (opened if last else []),
+            operands,
         )
         moves = [(layer, layer + 1) for layer in range(step, step + early_layers)]
-        if last:
-            moves.append((0, 1))
         traces = send(ended[0], moves)
         if keeps:
             kept.append(send(ended[1], [(step, step + 1)]))
+            extras.append((step + 1, 0))
+        elif chains > 1:
+            kept.append(traces)
+            extras.append((step + 1, (chains - 1) * slots))
+        if chains > 1:
             picks.append((step + 1, len(arrived) // len(swaps)))
         received = [send(m, moves, swap) for m, swap in zip(ended[-len(swaps) :], swaps)]
-        if step > 0:
-            arrived += received
+        arrived += received
         if step == 0:
             (map_ext,) = call(
                 functools.partial(whole_map_kernel, early_layers),
@@ -483,8 +477,9 @@
                 [first_map, band, second_map, map_ext],
                 aliases={3: 0},
             )
+    everywhere = functools.partial(takes_part, 0, layers)
     (inner,) = call(
-        functools.partial(inner_kernel, lambda: lax.axis_index("depth") >= 0, slice(rounds - 1, rounds)),
+        functools.partial(inner_kernel, everywhere, slice(soon, rounds), extras),
         [array(slots, cells, kind=jnp.float32)],
         [starts, map_ext, damping, traces] + kept,
     )

time: 44.7 us -> 44.8 us (level)
  the two profiles are of different devices: /device:TPU:1 before, /device:TPU:3 now
where the time goes in v13:
time: 44.8 us; the launch traced here: 44.4 us
  waiting for transfers between devices  18.4 us (41%)
  starting transfers between devices  15.3 us (34%)
  Pallas kernels  10.1 us (23%)
  between operations  0.56 us (1%)
    ppermute x17, waiting for transfers between devices, send(): return lax.ppermute(x, MESH_AXES, pairs)  18.4 us
    ppermute x17, starting transfers between devices, send(): return lax.ppermute(x, MESH_AXES, pairs)  15.3 us
    pallas_call x11, Pallas kernels, call(): pl.pallas_call(kernel, out_shape=out_shape, in_specs=[pl.BlockSpec(memory...  10.1 us
  transfers between devices with their start and end apart: 17, of which 3 were waited for; matrix products, arithmetic and copies ran while one was open for 0% of the time, Pallas kernels for 11%

profile of v13, /device:TPU:3, one launch (start us, length us, event | category | flops | bytes accessed | tf_op | source)
XLA Modules:
  0.0 44.4 jit_solution(14124003633731075666)
XLA Ops:
  0.0 4.0 %shard_map.82 = (bf16[1472,128]{1,0:T(8,128)(2,1)S(1)}, bf16[4,192,896]{2,1,0:T(8,128)(2,1)S(1)}, bf16[4,192,128]{2,1,0:T(8,128)(2,1)S(1)}) custom-call(bf16[4,192,896]{2,1,0:T(8,128)(2,1)} %bitcast.26, s32[4,192]{1,0:T(4,128)} %assignment_in.1, s32[7,1,1,12]{3,2,1,0:T(1,128)} %bitcast.24, bf16[896,896]{1,0:T(8,128)(2,1)} %bitcast.9), custom_call_target="tpu_custom_call" | custom-call | tf_op jit(solution)/shard_map/pallas_call | solution.py:352
  4.1 2.6 %collective-permute-start = (bf16[1472,128]{1,0:T(8,128)(2,1)S(1)}, bf16[1472,128]{1,0:T(8,128)(2,1)S(1)}, u32[]{:S(2)}, u32[]{:S(2)}) collective-permute-start(bf16[1472,128]{1,0:T(8,128)(2,1)S(1)} %get-tuple-element.37), channel_id=1, source_target_pairs={{8,0},{9,1},{10,2},{11,3},{12,4},{13,5},{14,6},{15,7},{16,8},{17,9... | collective-permute-start | bytes 1130504 | tf_op jit(solution)/shard_map/ppermute | solution.py:381
  6.7 0.0 copy-start.1
  6.7 0.0 copy-start.3
  6.7 0.1 shard_map.83
  6.8 0.8 %collective-permute-start.1 = (bf16[192,128]{1,0:T(8,128)(2,1)S(1)}, bf16[192,128]{1,0:T(8,128)(2,1)S(1)}, u32[]{:S(2)}, u32[]{:S(2)}) collective-permute-start(bf16[192,128]{1,0:T(8,128)(2,1)S(1)} %get-tuple-element.39), channel_id=1, source_target_pairs={{1,2},{2,1},{5,6},{6,5}} | collective-permute-start | bytes 147464 | tf_op jit(solution)/shard_map/ppermute | solution.py:381
  7.6 0.7 %collective-permute-start.2 = (bf16[192,128]{1,0:T(8,128)(2,1)S(1)}, bf16[192,128]{1,0:T(8,128)(2,1)S(1)}, u32[]{:S(2)}, u32[]{:S(2)}) collective-permute-start(bf16[192,128]{1,0:T(8,128)(2,1)S(1)} %get-tuple-element.40), channel_id=1, source_target_pairs={{0,1},{1,0},{2,3},{3,2},{4,5},{5,4},{6,7},{7,6}} | collective-permute-start | bytes 147464 | tf_op jit(solution)/shard_map/ppermute | solution.py:381
  8.3 0.7 %collective-permute-start.3 = (bf16[192,128]{1,0:T(8,128)(2,1)S(1)}, bf16[192,128]{1,0:T(8,128)(2,1)S(1)}, u32[]{:S(2)}, u32[]{:S(2)}) collective-permute-start(bf16[192,128]{1,0:T(8,128)(2,1)S(1)} %get-tuple-element.41), channel_id=1, source_target_pairs={{0,4},{1,5},{2,6},{3,7},{4,0},{5,1},{6,2},{7,3}} | collective-permute-start | bytes 147464 | tf_op jit(solution)/shard_map/ppermute | solution.py:381
  9.0 4.1 %shard_map.84 = (f32[576,896]{1,0:T(8,128)S(1)}, bf16[1024,896]{1,0:T(8,128)(2,1)S(1)}, bf16[4,512,256]{2,1,0:T(8,128)(2,1)S(1)}) custom-call(bf16[4,192,896]{2,1,0:T(8,128)(2,1)S(1)} %get-tuple-element.33.starts, bf16[896,896]{1,0:T(8,128)(2,1)S(1)} %bitcast.11, bf16[896,896]{1,0:T(8,128)(2,1)S(1)} %bitcast.13, ...), custom_call_target="tpu_custom_call" | custom-call | tf_op jit(solution)/shard_map/pallas_call | solution.py:352
  13.1 0.0 collective-permute-done.2.refs_6_.refs_1_
  13.1 0.0 collective-permute-done.3.refs_7_.refs_2_
  13.2 0.7 %collective-permute-start.4 = (bf16[576,896]{1,0:T(8,128)(2,1)S(1)}, bf16[576,896]{1,0:T(8,128)(2,1)S(1)}, u32[]{:S(2)}, u32[]{:S(2)}) collective-permute-start(bf16[576,896]{1,0:T(8,128)(2,1)S(1)} %get-tuple-element.42), channel_id=1, source_target_pairs={{0,8},{1,9},{2,10},{3,11},{4,12},{5,13},{6,14},{7,15}} | collective-permute-start | bytes 3096584 | tf_op jit(solution)/shard_map/ppermute | solution.py:381
  13.9 0.7 %collective-permute-start.5 = (bf16[144,128]{1,0:T(8,128)(2,1)S(1)}, bf16[144,128]{1,0:T(8,128)(2,1)S(1)}, u32[]{:S(2)}, u32[]{:S(2)}) collective-permute-start(bf16[144,128]{1,0:T(8,128)(2,1)S(1)} %get-tuple-element.43), channel_id=1, source_target_pairs={{1,10},{2,9},{5,14},{6,13}} | collective-permute-start | bytes 110600 | tf_op jit(solution)/shard_map/ppermute | solution.py:381
  14.6 0.7 %collective-permute-start.6 = (bf16[144,128]{1,0:T(8,128)(2,1)S(1)}, bf16[144,128]{1,0:T(8,128)(2,1)S(1)}, u32[]{:S(2)}, u32[]{:S(2)}) collective-permute-start(bf16[144,128]{1,0:T(8,128)(2,1)S(1)} %get-tuple-element.44), channel_id=1, source_target_pairs={{0,9},{1,8},{2,11},{3,10},{4,13},{5,12},{6,15},{7,14}} | collective-permute-start | bytes 110600 | tf_op jit(solution)/shard_map/ppermute | solution.py:381
  15.2 0.7 %collective-permute-start.7 = (bf16[144,128]{1,0:T(8,128)(2,1)S(1)}, bf16[144,128]{1,0:T(8,128)(2,1)S(1)}, u32[]{:S(2)}, u32[]{:S(2)}) collective-permute-start(bf16[144,128]{1,0:T(8,128)(2,1)S(1)} %get-tuple-element.45), channel_id=1, source_target_pairs={{0,12},{1,13},{2,14},{3,15},{4,8},{5,9},{6,10},{7,11}} | collective-permute-start | bytes 110600 | tf_op jit(solution)/shard_map/ppermute | solution.py:381
  15.9 0.2 shard_map.85.map_ext.refs_1_
  16.2 0.0 collective-permute-done.5.refs_5_.refs_3_
  16.2 0.0 collective-permute-done.6.refs_6_.refs_4_
  16.2 0.7 %collective-permute-start.8 = (bf16[192,896]{1,0:T(8,128)(2,1)S(1)}, bf16[192,896]{1,0:T(8,128)(2,1)S(1)}, u32[]{:S(2)}, u32[]{:S(2)}) collective-permute-start(bf16[192,896]{1,0:T(8,128)(2,1)S(1)} %get-tuple-element.46), channel_id=1, source_target_pairs={{8,16},{9,17},{10,18},{11,19},{12,20},{13,21},{14,22},{15,23}} | collective-permute-start | bytes 1032200 | tf_op jit(solution)/shard_map/ppermute | solution.py:381
  16.9 0.7 %collective-permute-start.9 = (bf16[96,128]{1,0:T(8,128)(2,1)S(1)}, bf16[96,128]{1,0:T(8,128)(2,1)S(1)}, u32[]{:S(2)}, u32[]{:S(2)}) collective-permute-start(bf16[96,128]{1,0:T(8,128)(2,1)S(1)} %get-tuple-element.47), channel_id=1, source_target_pairs={{9,18},{10,17},{13,22},{14,21}} | collective-permute-start | bytes 73736 | tf_op jit(solution)/shard_map/ppermute | solution.py:381
  17.6 0.7 %collective-permute-start.10 = (bf16[96,128]{1,0:T(8,128)(2,1)S(1)}, bf16[96,128]{1,0:T(8,128)(2,1)S(1)}, u32[]{:S(2)}, u32[]{:S(2)}) collective-permute-start(bf16[96,128]{1,0:T(8,128)(2,1)S(1)} %get-tuple-element.48), channel_id=1, source_target_pairs={{8,17},{9,16},{10,19},{11,18},{12,21},{13,20},{14,23},{15,22}} | collective-permute-start | bytes 73736 | tf_op jit(solution)/shard_map/ppermute | solution.py:381
  18.2 0.7 %collective-permute-start.11 = (bf16[96,128]{1,0:T(8,128)(2,1)S(1)}, bf16[96,128]{1,0:T(8,128)(2,1)S(1)}, u32[]{:S(2)}, u32[]{:S(2)}) collective-permute-start(bf16[96,128]{1,0:T(8,128)(2,1)S(1)} %get-tuple-element.49), channel_id=1, source_target_pairs={{8,20},{9,21},{10,22},{11,23},{12,16},{13,17},{14,18},{15,19}} | collective-permute-start | bytes 73736 | tf_op jit(solution)/shard_map/ppermute | solution.py:381
  18.9 0.7 %collective-permute-start.13 = (bf16[192,896]{1,0:T(8,128)(2,1)S(1)}, bf16[192,896]{1,0:T(8,128)(2,1)S(1)}, u32[]{:S(2)}, u32[]{:S(2)}) collective-permute-start(bf16[192,896]{1,0:T(8,128)(2,1)S(1)} %get-tuple-element.51), channel_id=1, source_target_pairs={{8,16},{9,17},{10,18},{11,19},{12,20},{13,21},{14,22},{15,23}} | collective-permute-start | bytes 1032200 | tf_op jit(solution)/shard_map/ppermute | solution.py:381
  19.7 1.3 %collective-permute-start.12 = (bf16[192,896]{1,0:T(8,128)(2,1)S(1)}, bf16[192,896]{1,0:T(8,128)(2,1)S(1)}, u32[]{:S(2)}, u32[]{:S(2)}) collective-permute-start(bf16[192,896]{1,0:T(8,128)(2,1)S(1)} %get-tuple-element.50), channel_id=1, source_target_pairs={{16,24},{17,25},{18,26},{19,27},{20,28},{21,29},{22,30},{23,31}} | collective-permute-start | bytes 1032200 | tf_op jit(solution)/shard_map/ppermute | solution.py:381
  21.0 0.7 %collective-permute-start.14 = (bf16[48,128]{1,0:T(8,128)(2,1)S(1)}, bf16[48,128]{1,0:T(8,128)(2,1)S(1)}, u32[]{:S(2)}, u32[]{:S(2)}) collective-permute-start(bf16[48,128]{1,0:T(8,128)(2,1)S(1)} %get-tuple-element.52), channel_id=1, source_target_pairs={{17,26},{18,25},{21,30},{22,29}} | collective-permute-start | bytes 36872 | tf_op jit(solution)/shard_map/ppermute | solution.py:381
  21.7 1.3 %collective-permute-start.15 = (bf16[48,128]{1,0:T(8,128)(2,1)S(1)}, bf16[48,128]{1,0:T(8,128)(2,1)S(1)}, u32[]{:S(2)}, u32[]{:S(2)}) collective-permute-start(bf16[48,128]{1,0:T(8,128)(2,1)S(1)} %get-tuple-element.53), channel_id=1, source_target_pairs={{16,25},{17,24},{18,27},{19,26},{20,29},{21,28},{22,31},{23,30}} | collective-permute-start | bytes 36872 | tf_op jit(solution)/shard_map/ppermute | solution.py:381
  23.0 1.3 %collective-permute-start.16 = (bf16[48,128]{1,0:T(8,128)(2,1)S(1)}, bf16[48,128]{1,0:T(8,128)(2,1)S(1)}, u32[]{:S(2)}, u32[]{:S(2)}) collective-permute-start(bf16[48,128]{1,0:T(8,128)(2,1)S(1)} %get-tuple-element.54), channel_id=1, source_target_pairs={{16,28},{17,29},{18,30},{19,31},{20,24},{21,25},{22,26},{23,27}} | collective-permute-start | bytes 36872 | tf_op jit(solution)/shard_map/ppermute | solution.py:381
  24.3 14.9 %collective-permute-done.12.traces = bf16[192,896]{1,0:T(8,128)(2,1)S(1)} collective-permute-done((bf16[192,896]{1,0:T(8,128)(2,1)S(1)}, bf16[192,896]{1,0:T(8,128)(2,1)S(1)}, u32[]{:S(2)}, u32[]{:S(2)}) %collective-permute-start.12) | collective-permute-done | bytes 344096 | tf_op jit(solution)/shard_map/ppermute | solution.py:381
  39.2 0.6 %shard_map.91.inner = f32[192,896]{1,0:T(8,128)S(1)} custom-call(bf16[4,192,896]{2,1,0:T(8,128)(2,1)S(1)} %get-tuple-element.33.starts, bf16[1024,896]{1,0:T(8,128)(2,1)S(1)} %shard_map.85.map_ext.refs_1_, f32[1,896]{1,0:T(1,128)S(1)} %bitcast.22, bf16[192,896]{1,0:T(8,128)(2,1)S(1)} %collective-permute-done.12.traces, ...), custom_call_target="tpu_custom_call" | custom-call | tf_op jit(solution)/shard_map/pallas_call | solution.py:352
  39.8 2.8 %collective-permute-done.15.refs_10_ = bf16[48,128]{1,0:T(8,128)(2,1)S(1)} collective-permute-done((bf16[48,128]{1,0:T(8,128)(2,1)S(1)}, bf16[48,128]{1,0:T(8,128)(2,1)S(1)}, u32[]{:S(2)}, u32[]{:S(2)}) %collective-permute-start.15) | collective-permute-done | bytes 12320 | tf_op jit(solution)/shard_map/ppermute | solution.py:381
  42.5 0.7 %collective-permute-done.16.refs_11_ = bf16[48,128]{1,0:T(8,128)(2,1)S(1)} collective-permute-done((bf16[48,128]{1,0:T(8,128)(2,1)S(1)}, bf16[48,128]{1,0:T(8,128)(2,1)S(1)}, u32[]{:S(2)}, u32[]{:S(2)}) %collective-permute-start.16) | collective-permute-done | bytes 12320 | tf_op jit(solution)/shard_map/ppermute | solution.py:381
  43.2 1.1 %shard_map.92 = bf16[192,896]{1,0:T(8,128)(2,1)} custom-call(bf16[4,192,128]{2,1,0:T(8,128)(2,1)S(1)} %get-tuple-element.32.refs_0_.live, bf16[1024,896]{1,0:T(8,128)(2,1)S(1)} %shard_map.85.map_ext.refs_1_, f32[1,896]{1,0:T(1,128)S(1)} %bitcast.23, f32[192,896]{1,0:T(8,128)S(1)} %shard_map.91.inner, ...), custom_call_target="tpu_custom_call" | custom-call | tf_op jit(solution)/shard_map/pallas_call | solution.py:352
  (25 shorter events, 0.1 us)
Async XLA Ops:
  0.0 6.7 %copy-start.4 = (s32[4,192]{1,0:T(4,128)S(1)}, s32[4,192]{1,0:T(4,128)}, u32[]{:S(2)}) copy-start(s32[4,192]{1,0:T(4,128)} %assignment_in.1) | copy-start | bytes 9220
  0.0 6.7 %copy-start = (bf16[1,1,1,896,896]{4,3,2,1,0:T(8,128)(2,1)S(1)}, bf16[1,1,1,896,896]{4,3,2,1,0:T(8,128)(2,1)}, u32[]{:S(2)}) copy-start(bf16[1,1,1,896,896]{4,3,2,1,0:T(8,128)(2,1)} %param.12) | copy-start | bytes 4816900
  0.0 6.7 %copy-start.5 = (s32[7,12,1,1]{1,3,2,0:T(1,128)S(1)}, s32[7,12,1,1]{1,3,2,0:T(1,128)}, u32[]{:S(2)}) copy-start(s32[7,12,1,1]{1,3,2,0:T(1,128)} %param.11) | copy-start | bytes 1012
  0.0 6.7 %copy-start.2 = (bf16[1,192,1,1,896]{4,1,3,2,0:T(8,128)(2,1)S(1)}, bf16[1,192,1,1,896]{4,1,3,2,0:T(8,128)(2,1)}, u32[]{:S(2)}) copy-start(bf16[1,192,1,1,896]{4,1,3,2,0:T(8,128)(2,1)} %param.8) | copy-start | bytes 1032196
  4.1 9.1 %collective-permute-start = (bf16[1472,128]{1,0:T(8,128)(2,1)S(1)}, bf16[1472,128]{1,0:T(8,128)(2,1)S(1)}, u32[]{:S(2)}, u32[]{:S(2)}) collective-permute-start(bf16[1472,128]{1,0:T(8,128)(2,1)S(1)} %get-tuple-element.37), channel_id=1, source_target_pairs={{8,0},{9,1},{10,2},{11,3},{12,4},{13,5},{14,6},{15,7},{16,8},{17,9... | collective-permute-start | bytes 1130504 | tf_op jit(solution)/shard_map/ppermute | solution.py:381
  6.7 2.3 %copy-start.1 = (bf16[1,1,1,896,896]{4,3,2,1,0:T(8,128)(2,1)S(1)}, bf16[1,1,1,896,896]{4,3,2,1,0:T(8,128)(2,1)}, u32[]{:S(2)}) copy-start(bf16[1,1,1,896,896]{4,3,2,1,0:T(8,128)(2,1)} %param.13) | copy-start | bytes 4816900
  6.7 2.3 %copy-start.3 = (f32[1,1,1,896]{3,2,1,0:T(1,128)S(1)}, f32[1,1,1,896]{3,2,1,0:T(1,128)}, u32[]{:S(2)}) copy-start(f32[1,1,1,896]{3,2,1,0:T(1,128)} %param.14) | copy-start | bytes 10756
  6.8 6.3 %collective-permute-start.1 = (bf16[192,128]{1,0:T(8,128)(2,1)S(1)}, bf16[192,128]{1,0:T(8,128)(2,1)S(1)}, u32[]{:S(2)}, u32[]{:S(2)}) collective-permute-start(bf16[192,128]{1,0:T(8,128)(2,1)S(1)} %get-tuple-element.39), channel_id=1, source_target_pairs={{1,2},{2,1},{5,6},{6,5}} | collective-permute-start | bytes 147464 | tf_op jit(solution)/shard_map/ppermute | solution.py:381
  7.6 5.5 %collective-permute-start.2 = (bf16[192,128]{1,0:T(8,128)(2,1)S(1)}, bf16[192,128]{1,0:T(8,128)(2,1)S(1)}, u32[]{:S(2)}, u32[]{:S(2)}) collective-permute-start(bf16[192,128]{1,0:T(8,128)(2,1)S(1)} %get-tuple-element.40), channel_id=1, source_target_pairs={{0,1},{1,0},{2,3},{3,2},{4,5},{5,4},{6,7},{7,6}} | collective-permute-start | bytes 147464 | tf_op jit(solution)/shard_map/ppermute | solution.py:381
  8.3 4.8 %collective-permute-start.3 = (bf16[192,128]{1,0:T(8,128)(2,1)S(1)}, bf16[192,128]{1,0:T(8,128)(2,1)S(1)}, u32[]{:S(2)}, u32[]{:S(2)}) collective-permute-start(bf16[192,128]{1,0:T(8,128)(2,1)S(1)} %get-tuple-element.41), channel_id=1, source_target_pairs={{0,4},{1,5},{2,6},{3,7},{4,0},{5,1},{6,2},{7,3}} | collective-permute-start | bytes 147464 | tf_op jit(solution)/shard_map/ppermute | solution.py:381
  13.2 3.0 %collective-permute-start.4 = (bf16[576,896]{1,0:T(8,128)(2,1)S(1)}, bf16[576,896]{1,0:T(8,128)(2,1)S(1)}, u32[]{:S(2)}, u32[]{:S(2)}) collective-permute-start(bf16[576,896]{1,0:T(8,128)(2,1)S(1)} %get-tuple-element.42), channel_id=1, source_target_pairs={{0,8},{1,9},{2,10},{3,11},{4,12},{5,13},{6,14},{7,15}} | collective-permute-start | bytes 3096584 | tf_op jit(solution)/shard_map/ppermute | solution.py:381
  13.9 2.3 %collective-permute-start.5 = (bf16[144,128]{1,0:T(8,128)(2,1)S(1)}, bf16[144,128]{1,0:T(8,128)(2,1)S(1)}, u32[]{:S(2)}, u32[]{:S(2)}) collective-permute-start(bf16[144,128]{1,0:T(8,128)(2,1)S(1)} %get-tuple-element.43), channel_id=1, source_target_pairs={{1,10},{2,9},{5,14},{6,13}} | collective-permute-start | bytes 110600 | tf_op jit(solution)/shard_map/ppermute | solution.py:381
  14.6 1.6 %collective-permute-start.6 = (bf16[144,128]{1,0:T(8,128)(2,1)S(1)}, bf16[144,128]{1,0:T(8,128)(2,1)S(1)}, u32[]{:S(2)}, u32[]{:S(2)}) collective-permute-start(bf16[144,128]{1,0:T(8,128)(2,1)S(1)} %get-tuple-element.44), channel_id=1, source_target_pairs={{0,9},{1,8},{2,11},{3,10},{4,13},{5,12},{6,15},{7,14}} | collective-permute-start | bytes 110600 | tf_op jit(solution)/shard_map/ppermute | solution.py:381
  15.2 0.9 %collective-permute-start.7 = (bf16[144,128]{1,0:T(8,128)(2,1)S(1)}, bf16[144,128]{1,0:T(8,128)(2,1)S(1)}, u32[]{:S(2)}, u32[]{:S(2)}) collective-permute-start(bf16[144,128]{1,0:T(8,128)(2,1)S(1)} %get-tuple-element.45), channel_id=1, source_target_pairs={{0,12},{1,13},{2,14},{3,15},{4,8},{5,9},{6,10},{7,11}} | collective-permute-start | bytes 110600 | tf_op jit(solution)/shard_map/ppermute | solution.py:381
  16.2 3.4 %collective-permute-start.8 = (bf16[192,896]{1,0:T(8,128)(2,1)S(1)}, bf16[192,896]{1,0:T(8,128)(2,1)S(1)}, u32[]{:S(2)}, u32[]{:S(2)}) collective-permute-start(bf16[192,896]{1,0:T(8,128)(2,1)S(1)} %get-tuple-element.46), channel_id=1, source_target_pairs={{8,16},{9,17},{10,18},{11,19},{12,20},{13,21},{14,22},{15,23}} | collective-permute-start | bytes 1032200 | tf_op jit(solution)/shard_map/ppermute | solution.py:381
  16.9 2.7 %collective-permute-start.9 = (bf16[96,128]{1,0:T(8,128)(2,1)S(1)}, bf16[96,128]{1,0:T(8,128)(2,1)S(1)}, u32[]{:S(2)}, u32[]{:S(2)}) collective-permute-start(bf16[96,128]{1,0:T(8,128)(2,1)S(1)} %get-tuple-element.47), channel_id=1, source_target_pairs={{9,18},{10,17},{13,22},{14,21}} | collective-permute-start | bytes 73736 | tf_op jit(solution)/shard_map/ppermute | solution.py:381
  17.6 2.1 %collective-permute-start.10 = (bf16[96,128]{1,0:T(8,128)(2,1)S(1)}, bf16[96,128]{1,0:T(8,128)(2,1)S(1)}, u32[]{:S(2)}, u32[]{:S(2)}) collective-permute-start(bf16[96,128]{1,0:T(8,128)(2,1)S(1)} %get-tuple-element.48), channel_id=1, source_target_pairs={{8,17},{9,16},{10,19},{11,18},{12,21},{13,20},{14,23},{15,22}} | collective-permute-start | bytes 73736 | tf_op jit(solution)/shard_map/ppermute | solution.py:381
  18.2 1.4 %collective-permute-start.11 = (bf16[96,128]{1,0:T(8,128)(2,1)S(1)}, bf16[96,128]{1,0:T(8,128)(2,1)S(1)}, u32[]{:S(2)}, u32[]{:S(2)}) collective-permute-start(bf16[96,128]{1,0:T(8,128)(2,1)S(1)} %get-tuple-element.49), channel_id=1, source_target_pairs={{8,20},{9,21},{10,22},{11,23},{12,16},{13,17},{14,18},{15,19}} | collective-permute-start | bytes 73736 | tf_op jit(solution)/shard_map/ppermute | solution.py:381
  18.9 5.4 %collective-permute-start.13 = (bf16[192,896]{1,0:T(8,128)(2,1)S(1)}, bf16[192,896]{1,0:T(8,128)(2,1)S(1)}, u32[]{:S(2)}, u32[]{:S(2)}) collective-permute-start(bf16[192,896]{1,0:T(8,128)(2,1)S(1)} %get-tuple-element.51), channel_id=1, source_target_pairs={{8,16},{9,17},{10,18},{11,19},{12,20},{13,21},{14,22},{15,23}} | collective-permute-start | bytes 1032200 | tf_op jit(solution)/shard_map/ppermute | solution.py:381
  19.7 19.5 %collective-permute-start.12 = (bf16[192,896]{1,0:T(8,128)(2,1)S(1)}, bf16[192,896]{1,0:T(8,128)(2,1)S(1)}, u32[]{:S(2)}, u32[]{:S(2)}) collective-permute-start(bf16[192,896]{1,0:T(8,128)(2,1)S(1)} %get-tuple-element.50), channel_id=1, source_target_pairs={{16,24},{17,25},{18,26},{19,27},{20,28},{21,29},{22,30},{23,31}} | collective-permute-start | bytes 1032200 | tf_op jit(solution)/shard_map/ppermute | solution.py:381
  21.0 18.8 %collective-permute-start.14 = (bf16[48,128]{1,0:T(8,128)(2,1)S(1)}, bf16[48,128]{1,0:T(8,128)(2,1)S(1)}, u32[]{:S(2)}, u32[]{:S(2)}) collective-permute-start(bf16[48,128]{1,0:T(8,128)(2,1)S(1)} %get-tuple-element.52), channel_id=1, source_target_pairs={{17,26},{18,25},{21,30},{22,29}} | collective-permute-start | bytes 36872 | tf_op jit(solution)/shard_map/ppermute | solution.py:381
  21.7 20.9 %collective-permute-start.15 = (bf16[48,128]{1,0:T(8,128)(2,1)S(1)}, bf16[48,128]{1,0:T(8,128)(2,1)S(1)}, u32[]{:S(2)}, u32[]{:S(2)}) collective-permute-start(bf16[48,128]{1,0:T(8,128)(2,1)S(1)} %get-tuple-element.53), channel_id=1, source_target_pairs={{16,25},{17,24},{18,27},{19,26},{20,29},{21,28},{22,31},{23,30}} | collective-permute-start | bytes 36872 | tf_op jit(solution)/shard_map/ppermute | solution.py:381
  23.0 20.2 %collective-permute-start.16 = (bf16[48,128]{1,0:T(8,128)(2,1)S(1)}, bf16[48,128]{1,0:T(8,128)(2,1)S(1)}, u32[]{:S(2)}, u32[]{:S(2)}) collective-permute-start(bf16[48,128]{1,0:T(8,128)(2,1)S(1)} %get-tuple-element.54), channel_id=1, source_target_pairs={{16,28},{17,29},{18,30},{19,31},{20,24},{21,25},{22,26},{23,27}} | collective-permute-start | bytes 36872 | tf_op jit(solution)/shard_map/ppermute | solution.py:381

commit v14 on v13

--- a/solution.py
+++ b/solution.py
@@ -223,19 +223,21 @@
     early = lax.axis_index("depth") < early_layers
     copy = pltpu.make_async_copy(band, band_in, sem)
     copy.start()
-    edge_rows = dot(edge_cells[...], second_map[...])
-    whole_ext[cells:] = (coupling_weight * edge_rows).astype(jnp.bfloat16)
 
     @pl.when(early)
     def _():
         start = starts[:chains].reshape(-1, cells)
         mapped = dot(start, first_map[...]).astype(jnp.bfloat16)
         copy.wait()
-        image = dot(coupled(mapped, band_in), second_map[...])
-        traces_out[...] = blend(image, start, damping[...])
+        rows = jnp.concatenate([coupled(mapped, band_in), edge_cells[...]], axis=0)
+        image = dot(rows, second_map[...])
+        traces_out[...] = blend(image[: chains * slots], start, damping[...])
+        whole_ext[cells:] = (coupling_weight * image[chains * slots :]).astype(jnp.bfloat16)
 
     @pl.when(jnp.logical_not(early))
     def _():
+        edge_rows = dot(edge_cells[...], second_map[...])
+        whole_ext[cells:] = (coupling_weight * edge_rows).astype(jnp.bfloat16)
         copy.wait()
         fill_whole_map(first_map, band_in, second_map, whole_ext)
 
@@ -264,25 +266,46 @@
     return (layer >= step) & (layer < step + early_layers)
 
 
-def inner_kernel(part_of, rounds, extras, starts, map_ext, damping, traces, *refs):
+def inner_of(start, map_ext, damping):
+    cells = start.shape[1]
+    return blend(dot(start, map_ext[:cells]), start, damping[...])
+
+
+def inner_kernel(part_of, step, chains, starts, map_ext, damping, edge_next, traces, *outs):
+    inner_out, edges_out, halo_map = outs
+    rows, cells = inner_out.shape
+    slots = rows // chains
+
+    @pl.when(part_of())
+    def _():
+        start = starts[step : step + chains].reshape(-1, cells).astype(jnp.float32)
+        start = (start + traces[:rows].astype(jnp.float32)).astype(jnp.bfloat16)
+        inner = inner_of(start, map_ext, damping)
+        inner_out[...] = inner
+        at = cells + step * slots
+        edges = dot(inner.astype(jnp.bfloat16), edge_next[:cells])
+        edges_out[...] = edges + edge_next[at : at + rows].astype(jnp.float32)
+        brings = (damping[...] * map_ext[cells:].astype(jnp.float32)).astype(jnp.bfloat16)
+        halo_map[:, :cells] = brings
+        halo_map[:, cells:] = dot(brings, edge_next[:cells]).astype(jnp.bfloat16)
+
+
+def last_inner_kernel(extras, starts, map_ext, damping, traces, *refs):
     others, out = refs[:-1], refs[-1]
-    rows, cells = out.shape
-
-    @pl.when(part_of())
-    def _():
-        start = starts[rounds].reshape(-1, cells).astype(jnp.float32)
-        came = traces[:rows].astype(jnp.float32)
-        for (layer, row), other in zip(extras, others):
-            here = lax.axis_index("depth") == layer
-            came = jnp.where(here, other[row : row + rows].astype(jnp.float32), came)
-        start = (start + came).astype(jnp.bfloat16)
-        out[...] = blend(dot(start, map_ext[:cells]), start, damping[...])
-
-
-def step_kernel(swaps, step, chains, keeps, part_of, *refs):
-    live, map_ext, damping, edge_next, inner = refs[:5]
-    received = refs[5 : 5 + len(swaps)]
-    outs = refs[-1 - len(swaps) - keeps :]
+    rows = out.shape[0]
+    came = traces[...].astype(jnp.float32)
+    for (layer, row), other in zip(extras, others):
+        here = lax.axis_index("depth") == layer
+        came = jnp.where(here, other[row : row + rows].astype(jnp.float32), came)
+    start = starts[starts.shape[0] - 1].astype(jnp.float32) + came
+    out[...] = inner_of(start.astype(jnp.bfloat16), map_ext, damping)
+
+
+def step_kernel(swaps, step, chains, keeps, part_of, live, inner, *refs):
+    operands = refs[:3] if step == 0 else refs[:2]
+    refs = refs[len(operands) :]
+    received = refs[: len(swaps)]
+    outs = refs[len(swaps) :]
     traces_out, messages = outs[0], outs[1 + keeps :]
     cells = inner.shape[1]
     slots = inner.shape[0] // chains
@@ -296,15 +319,20 @@
             packed = [ref[chain * part : (chain + 1) * part] for ref in received]
             halo.append(halo_of(packed, groups, live[step + chain]))
         halo = jnp.concatenate(halo, axis=0)
-        ended = inner[...] + damping[...] * dot(halo, map_ext[cells:])
-        ended = ended.astype(jnp.bfloat16)
+        if step == 0:
+            map_ext, damping, edge_next = operands
+            ended = inner[...] + damping[...] * dot(halo, map_ext[cells:])
+            ended = ended.astype(jnp.bfloat16)
+            edges = dot(ended, edge_next[:cells])
+            edges += edge_next[cells : cells + chains * slots].astype(jnp.float32)
+        else:
+            edges_but, halo_map = operands
+            edges = edges_but[...] + dot(halo, halo_map[:, cells:])
+            ended = (inner[...] + dot(halo, halo_map[:, :cells])).astype(jnp.bfloat16)
         going = traces_out.shape[0]
         traces_out[...] = ended[:going]
         if keeps:
             outs[1][...] = ended[going:]
-        at = cells + step * slots
-        edges = dot(ended, edge_next[:cells])
-        edges += edge_next[at : at + chains * slots].astype(jnp.float32)
         for message, group in zip(messages, groups):
             for chain in range(chains):
                 message[chain * part : (chain + 1) * part] = pack(
@@ -314,26 +342,22 @@
 
 def final_kernel(swaps, picks, live, map_ext, damping, inner, *refs):
     slots, cells = inner.shape
-    received = refs[:-4]
-    traces_out, halo, ended, sems = refs[-4:]
+    received = refs[:-3]
+    traces_out, ended, sems = refs[-3:]
     part = slots // 4
     layer = lax.axis_index("depth")
-    groups = groups_of(swaps)
-
-    def take(phase):
-        messages = received[phase * len(swaps) : (phase + 1) * len(swaps)]
-        messages = [ref[ref.shape[0] - part :] for ref in messages]
-        halo[...] = halo_of(messages, groups, live[live.shape[0] - 1])
-
-    by_rule = layer < 0
-    for at, phase in picks:
-        by_rule = by_rule | (layer == at)
-        pl.when(layer == at)(functools.partial(take, phase))
-    pl.when(jnp.logical_not(by_rule))(functools.partial(take, len(received) // len(swaps) - 1))
+    packed = []
+    for at in range(len(swaps)):
+        phases = [ref[ref.shape[0] - part :].astype(jnp.float32) for ref in received[at :: len(swaps)]]
+        message = phases[-1]
+        for own, phase in picks:
+            message = jnp.where(layer == own, phases[phase], message)
+        packed.append(message)
+    halo = halo_of(packed, groups_of(swaps), live[live.shape[0] - 1])
     copies = []
     half = cells // LANES // 2 * LANES
     for at, columns in enumerate([slice(0, half), slice(half, cells)]):
-        image = dot(halo[...], map_ext[cells:, columns])
+        image = dot(halo, map_ext[cells:, columns])
         ended[:, columns] = (inner[:, columns] + damping[:, columns] * image).astype(jnp.bfloat16)
         copies.append(
             pltpu.make_async_copy(ended.at[:, columns], traces_out.at[:, columns], sems.at[at])
@@ -445,14 +469,19 @@
         outs = [array(going, cells)] + [array(slots, cells)] * keeps
         outs += [array(chains * part, LANES)] * len(swaps)
         part_of = functools.partial(takes_part, step, early_layers)
+        operands = [map_ext, damping, edge_next]
         if step > 0:
-            now = slice(step, step + chains)
-            (inner,) = call(
-                functools.partial(inner_kernel, part_of, now, []),
-                [array(chains * slots, cells, kind=jnp.float32)],
-                [starts, map_ext, damping, traces],
+            rows = chains * slots
+            inner, *operands = call(
+                functools.partial(inner_kernel, part_of, step, chains),
+                [
+                    array(rows, cells, kind=jnp.float32),
+                    array(rows, LANES, kind=jnp.float32),
+                    array(LANES, cells + LANES),
+                ],
+                [starts, map_ext, damping, edge_next, traces],
             )
-        operands = [live, map_ext, damping, edge_next, inner] + received
+        operands = [live, inner] + operands + received
         ended = call(
             functools.partial(step_kernel, swaps, step, chains, keeps, part_of),
             outs,
@@ -477,9 +506,8 @@
                 [first_map, band, second_map, map_ext],
                 aliases={3: 0},
             )
-    everywhere = functools.partial(takes_part, 0, layers)
     (inner,) = call(
-        functools.partial(inner_kernel, everywhere, slice(soon, rounds), extras),
+        functools.partial(last_inner_kernel, extras),
         [array(slots, cells, kind=jnp.float32)],
         [starts, map_ext, damping, traces] + kept,
     )
@@ -488,7 +516,6 @@
         [array(slots, cells)],
         [live, map_ext, damping, inner] + arrived,
         scratch=[
-            pltpu.VMEM((slots, LANES), jnp.bfloat16),
             scratch(arrival),
             pltpu.SemaphoreType.DMA((2,)),
         ],

time: 44.8 us -> 44.4 us (level)
  no operation moved by 1% of the time
where the time goes in v14:
time: 44.4 us; the launch traced here: 44 us
  waiting for transfers between devices  18 us (41%)
  starting transfers between devices  15.3 us (34%)
  Pallas kernels  10.1 us (23%)
  between operations  0.56 us (1%)
    ppermute x17, waiting for transfers between devices, send(): return lax.ppermute(x, MESH_AXES, pairs)  18 us
    ppermute x17, starting transfers between devices, send(): return lax.ppermute(x, MESH_AXES, pairs)  15.3 us
    pallas_call x11, Pallas kernels, call(): pl.pallas_call(kernel, out_shape=out_shape, in_specs=[pl.BlockSpec(memory...  10.1 us
  transfers between devices with their start and end apart: 17, of which 3 were waited for; matrix products, arithmetic and copies ran while one was open for 0% of the time, Pallas kernels for 11%

profile of v14, /device:TPU:3, one launch (start us, length us, event | category | flops | bytes accessed | tf_op | source)
XLA Modules:
  0.0 44.0 jit_solution(17199332093939864847)
XLA Ops:
  0.0 4.0 %shard_map.82 = (bf16[1472,128]{1,0:T(8,128)(2,1)S(1)}, bf16[4,192,896]{2,1,0:T(8,128)(2,1)S(1)}, bf16[4,192,128]{2,1,0:T(8,128)(2,1)S(1)}) custom-call(bf16[4,192,896]{2,1,0:T(8,128)(2,1)} %bitcast.24, s32[4,192]{1,0:T(4,128)} %assignment_in.1, s32[7,1,1,12]{3,2,1,0:T(1,128)} %bitcast.22, bf16[896,896]{1,0:T(8,128)(2,1)} %bitcast.9), custom_call_target="tpu_custom_call" | custom-call | tf_op jit(solution)/shard_map/pallas_call | solution.py:376
  4.1 2.6 %collective-permute-start = (bf16[1472,128]{1,0:T(8,128)(2,1)S(1)}, bf16[1472,128]{1,0:T(8,128)(2,1)S(1)}, u32[]{:S(2)}, u32[]{:S(2)}) collective-permute-start(bf16[1472,128]{1,0:T(8,128)(2,1)S(1)} %get-tuple-element.43), channel_id=1, source_target_pairs={{8,0},{9,1},{10,2},{11,3},{12,4},{13,5},{14,6},{15,7},{16,8},{17,9... | collective-permute-start | bytes 1130504 | tf_op jit(solution)/shard_map/ppermute | solution.py:405
  6.7 0.0 copy-start.1
  6.7 0.0 copy-start.3
  6.7 0.1 shard_map.83
  6.8 0.8 %collective-permute-start.1 = (bf16[192,128]{1,0:T(8,128)(2,1)S(1)}, bf16[192,128]{1,0:T(8,128)(2,1)S(1)}, u32[]{:S(2)}, u32[]{:S(2)}) collective-permute-start(bf16[192,128]{1,0:T(8,128)(2,1)S(1)} %get-tuple-element.45), channel_id=1, source_target_pairs={{1,2},{2,1},{5,6},{6,5}} | collective-permute-start | bytes 147464 | tf_op jit(solution)/shard_map/ppermute | solution.py:405
  7.6 0.7 %collective-permute-start.2 = (bf16[192,128]{1,0:T(8,128)(2,1)S(1)}, bf16[192,128]{1,0:T(8,128)(2,1)S(1)}, u32[]{:S(2)}, u32[]{:S(2)}) collective-permute-start(bf16[192,128]{1,0:T(8,128)(2,1)S(1)} %get-tuple-element.46), channel_id=1, source_target_pairs={{0,1},{1,0},{2,3},{3,2},{4,5},{5,4},{6,7},{7,6}} | collective-permute-start | bytes 147464 | tf_op jit(solution)/shard_map/ppermute | solution.py:405
  8.3 0.7 %collective-permute-start.3 = (bf16[192,128]{1,0:T(8,128)(2,1)S(1)}, bf16[192,128]{1,0:T(8,128)(2,1)S(1)}, u32[]{:S(2)}, u32[]{:S(2)}) collective-permute-start(bf16[192,128]{1,0:T(8,128)(2,1)S(1)} %get-tuple-element.47), channel_id=1, source_target_pairs={{0,4},{1,5},{2,6},{3,7},{4,0},{5,1},{6,2},{7,3}} | collective-permute-start | bytes 147464 | tf_op jit(solution)/shard_map/ppermute | solution.py:405
  9.0 4.1 %shard_map.84 = (f32[576,896]{1,0:T(8,128)S(1)}, bf16[1024,896]{1,0:T(8,128)(2,1)S(1)}, bf16[4,512,256]{2,1,0:T(8,128)(2,1)S(1)}) custom-call(bf16[4,192,896]{2,1,0:T(8,128)(2,1)S(1)} %get-tuple-element.39.starts, bf16[896,896]{1,0:T(8,128)(2,1)S(1)} %bitcast.11, bf16[896,896]{1,0:T(8,128)(2,1)S(1)} %bitcast.13, ...), custom_call_target="tpu_custom_call" | custom-call | tf_op jit(solution)/shard_map/pallas_call | solution.py:376
  13.1 0.0 collective-permute-done.1.refs_3_.refs_0_
  13.1 0.0 collective-permute-done.refs_2_.edge_next
  13.1 0.7 %collective-permute-start.4 = (bf16[576,896]{1,0:T(8,128)(2,1)S(1)}, bf16[576,896]{1,0:T(8,128)(2,1)S(1)}, u32[]{:S(2)}, u32[]{:S(2)}) collective-permute-start(bf16[576,896]{1,0:T(8,128)(2,1)S(1)} %get-tuple-element.48), channel_id=1, source_target_pairs={{0,8},{1,9},{2,10},{3,11},{4,12},{5,13},{6,14},{7,15}} | collective-permute-start | bytes 3096584 | tf_op jit(solution)/shard_map/ppermute | solution.py:405
  13.9 0.7 %collective-permute-start.5 = (bf16[144,128]{1,0:T(8,128)(2,1)S(1)}, bf16[144,128]{1,0:T(8,128)(2,1)S(1)}, u32[]{:S(2)}, u32[]{:S(2)}) collective-permute-start(bf16[144,128]{1,0:T(8,128)(2,1)S(1)} %get-tuple-element.52), channel_id=1, source_target_pairs={{1,10},{2,9},{5,14},{6,13}} | collective-permute-start | bytes 110600 | tf_op jit(solution)/shard_map/ppermute | solution.py:405
  14.6 0.7 %collective-permute-start.6 = (bf16[144,128]{1,0:T(8,128)(2,1)S(1)}, bf16[144,128]{1,0:T(8,128)(2,1)S(1)}, u32[]{:S(2)}, u32[]{:S(2)}) collective-permute-start(bf16[144,128]{1,0:T(8,128)(2,1)S(1)} %get-tuple-element.53), channel_id=1, source_target_pairs={{0,9},{1,8},{2,11},{3,10},{4,13},{5,12},{6,15},{7,14}} | collective-permute-start | bytes 110600 | tf_op jit(solution)/shard_map/ppermute | solution.py:405
  15.2 0.7 %collective-permute-start.7 = (bf16[144,128]{1,0:T(8,128)(2,1)S(1)}, bf16[144,128]{1,0:T(8,128)(2,1)S(1)}, u32[]{:S(2)}, u32[]{:S(2)}) collective-permute-start(bf16[144,128]{1,0:T(8,128)(2,1)S(1)} %get-tuple-element.54), channel_id=1, source_target_pairs={{0,12},{1,13},{2,14},{3,15},{4,8},{5,9},{6,10},{7,11}} | collective-permute-start | bytes 110600 | tf_op jit(solution)/shard_map/ppermute | solution.py:405
  15.9 0.2 shard_map.85.map_ext
  16.1 0.0 collective-permute-done.4.traces.refs_0_
  16.1 0.0 collective-permute-done.6.refs_3_.refs_4_
  16.2 0.7 %collective-permute-start.8 = (bf16[192,896]{1,0:T(8,128)(2,1)S(1)}, bf16[192,896]{1,0:T(8,128)(2,1)S(1)}, u32[]{:S(2)}, u32[]{:S(2)}) collective-permute-start(bf16[192,896]{1,0:T(8,128)(2,1)S(1)} %get-tuple-element.55), channel_id=1, source_target_pairs={{8,16},{9,17},{10,18},{11,19},{12,20},{13,21},{14,22},{15,23}} | collective-permute-start | bytes 1032200 | tf_op jit(solution)/shard_map/ppermute | solution.py:405
  16.9 0.7 %collective-permute-start.9 = (bf16[96,128]{1,0:T(8,128)(2,1)S(1)}, bf16[96,128]{1,0:T(8,128)(2,1)S(1)}, u32[]{:S(2)}, u32[]{:S(2)}) collective-permute-start(bf16[96,128]{1,0:T(8,128)(2,1)S(1)} %get-tuple-element.59), channel_id=1, source_target_pairs={{9,18},{10,17},{13,22},{14,21}} | collective-permute-start | bytes 73736 | tf_op jit(solution)/shard_map/ppermute | solution.py:405
  17.6 0.7 %collective-permute-start.10 = (bf16[96,128]{1,0:T(8,128)(2,1)S(1)}, bf16[96,128]{1,0:T(8,128)(2,1)S(1)}, u32[]{:S(2)}, u32[]{:S(2)}) collective-permute-start(bf16[96,128]{1,0:T(8,128)(2,1)S(1)} %get-tuple-element.60), channel_id=1, source_target_pairs={{8,17},{9,16},{10,19},{11,18},{12,21},{13,20},{14,23},{15,22}} | collective-permute-start | bytes 73736 | tf_op jit(solution)/shard_map/ppermute | solution.py:405
  18.2 0.7 %collective-permute-start.11 = (bf16[96,128]{1,0:T(8,128)(2,1)S(1)}, bf16[96,128]{1,0:T(8,128)(2,1)S(1)}, u32[]{:S(2)}, u32[]{:S(2)}) collective-permute-start(bf16[96,128]{1,0:T(8,128)(2,1)S(1)} %get-tuple-element.61), channel_id=1, source_target_pairs={{8,20},{9,21},{10,22},{11,23},{12,16},{13,17},{14,18},{15,19}} | collective-permute-start | bytes 73736 | tf_op jit(solution)/shard_map/ppermute | solution.py:405
  18.9 0.7 %collective-permute-start.13 = (bf16[192,896]{1,0:T(8,128)(2,1)S(1)}, bf16[192,896]{1,0:T(8,128)(2,1)S(1)}, u32[]{:S(2)}, u32[]{:S(2)}) collective-permute-start(bf16[192,896]{1,0:T(8,128)(2,1)S(1)} %get-tuple-element.63), channel_id=1, source_target_pairs={{8,16},{9,17},{10,18},{11,19},{12,20},{13,21},{14,22},{15,23}} | collective-permute-start | bytes 1032200 | tf_op jit(solution)/shard_map/ppermute | solution.py:405
  19.7 1.3 %collective-permute-start.12 = (bf16[192,896]{1,0:T(8,128)(2,1)S(1)}, bf16[192,896]{1,0:T(8,128)(2,1)S(1)}, u32[]{:S(2)}, u32[]{:S(2)}) collective-permute-start(bf16[192,896]{1,0:T(8,128)(2,1)S(1)} %get-tuple-element.62), channel_id=1, source_target_pairs={{16,24},{17,25},{18,26},{19,27},{20,28},{21,29},{22,30},{23,31}} | collective-permute-start | bytes 1032200 | tf_op jit(solution)/shard_map/ppermute | solution.py:405
  21.0 0.7 %collective-permute-start.14 = (bf16[48,128]{1,0:T(8,128)(2,1)S(1)}, bf16[48,128]{1,0:T(8,128)(2,1)S(1)}, u32[]{:S(2)}, u32[]{:S(2)}) collective-permute-start(bf16[48,128]{1,0:T(8,128)(2,1)S(1)} %get-tuple-element.64), channel_id=1, source_target_pairs={{17,26},{18,25},{21,30},{22,29}} | collective-permute-start | bytes 36872 | tf_op jit(solution)/shard_map/ppermute | solution.py:405
  21.7 1.3 %collective-permute-start.15 = (bf16[48,128]{1,0:T(8,128)(2,1)S(1)}, bf16[48,128]{1,0:T(8,128)(2,1)S(1)}, u32[]{:S(2)}, u32[]{:S(2)}) collective-permute-start(bf16[48,128]{1,0:T(8,128)(2,1)S(1)} %get-tuple-element.65), channel_id=1, source_target_pairs={{16,25},{17,24},{18,27},{19,26},{20,29},{21,28},{22,31},{23,30}} | collective-permute-start | bytes 36872 | tf_op jit(solution)/shard_map/ppermute | solution.py:405
  23.0 1.3 %collective-permute-start.16 = (bf16[48,128]{1,0:T(8,128)(2,1)S(1)}, bf16[48,128]{1,0:T(8,128)(2,1)S(1)}, u32[]{:S(2)}, u32[]{:S(2)}) collective-permute-start(bf16[48,128]{1,0:T(8,128)(2,1)S(1)} %get-tuple-element.66), channel_id=1, source_target_pairs={{16,28},{17,29},{18,30},{19,31},{20,24},{21,25},{22,26},{23,27}} | collective-permute-start | bytes 36872 | tf_op jit(solution)/shard_map/ppermute | solution.py:405
  24.3 14.3 %collective-permute-done.12.traces = bf16[192,896]{1,0:T(8,128)(2,1)S(1)} collective-permute-done((bf16[192,896]{1,0:T(8,128)(2,1)S(1)}, bf16[192,896]{1,0:T(8,128)(2,1)S(1)}, u32[]{:S(2)}, u32[]{:S(2)}) %collective-permute-start.12) | collective-permute-done | bytes 344096 | tf_op jit(solution)/shard_map/ppermute | solution.py:405
  38.5 0.6 %shard_map.91.inner = f32[192,896]{1,0:T(8,128)S(1)} custom-call(bf16[4,192,896]{2,1,0:T(8,128)(2,1)S(1)} %get-tuple-element.39.starts, bf16[1024,896]{1,0:T(8,128)(2,1)S(1)} %shard_map.85.map_ext, f32[1,896]{1,0:T(1,128)S(1)} %bitcast.20, bf16[192,896]{1,0:T(8,128)(2,1)S(1)} %collective-permute-done.12.traces, ...), custom_call_target="tpu_custom_call" | custom-call | tf_op jit(solution)/shard_map/pallas_call | solution.py:376
  39.1 2.7 %collective-permute-done.15.refs_10_ = bf16[48,128]{1,0:T(8,128)(2,1)S(1)} collective-permute-done((bf16[48,128]{1,0:T(8,128)(2,1)S(1)}, bf16[48,128]{1,0:T(8,128)(2,1)S(1)}, u32[]{:S(2)}, u32[]{:S(2)}) %collective-permute-start.15) | collective-permute-done | bytes 12320 | tf_op jit(solution)/shard_map/ppermute | solution.py:405
  41.9 0.9 %collective-permute-done.16.refs_11_ = bf16[48,128]{1,0:T(8,128)(2,1)S(1)} collective-permute-done((bf16[48,128]{1,0:T(8,128)(2,1)S(1)}, bf16[48,128]{1,0:T(8,128)(2,1)S(1)}, u32[]{:S(2)}, u32[]{:S(2)}) %collective-permute-start.16) | collective-permute-done | bytes 12320 | tf_op jit(solution)/shard_map/ppermute | solution.py:405
  42.8 1.0 %shard_map.92 = bf16[192,896]{1,0:T(8,128)(2,1)} custom-call(bf16[4,192,128]{2,1,0:T(8,128)(2,1)S(1)} %get-tuple-element.38.live, bf16[1024,896]{1,0:T(8,128)(2,1)S(1)} %shard_map.85.map_ext, f32[1,896]{1,0:T(1,128)S(1)} %bitcast.21, f32[192,896]{1,0:T(8,128)S(1)} %shard_map.91.inner, bf16[192,128]{1,0:T(8,128)(2,1)S(1)} %collective-permute-done.1.refs_3_.refs_0_, ...), custom_call_target="tpu_custom_call" | custom-call | tf_op jit(solution)/shard_map/pallas_call | solution.py:376
  (25 shorter events, 0.1 us)
Async XLA Ops:
  0.0 6.7 %copy-start.4 = (s32[4,192]{1,0:T(4,128)S(1)}, s32[4,192]{1,0:T(4,128)}, u32[]{:S(2)}) copy-start(s32[4,192]{1,0:T(4,128)} %assignment_in.1) | copy-start | bytes 9220
  0.0 6.7 %copy-start = (bf16[1,1,1,896,896]{4,3,2,1,0:T(8,128)(2,1)S(1)}, bf16[1,1,1,896,896]{4,3,2,1,0:T(8,128)(2,1)}, u32[]{:S(2)}) copy-start(bf16[1,1,1,896,896]{4,3,2,1,0:T(8,128)(2,1)} %param.12) | copy-start | bytes 4816900
  0.0 6.7 %copy-start.5 = (s32[7,12,1,1]{1,3,2,0:T(1,128)S(1)}, s32[7,12,1,1]{1,3,2,0:T(1,128)}, u32[]{:S(2)}) copy-start(s32[7,12,1,1]{1,3,2,0:T(1,128)} %param.11) | copy-start | bytes 1012
  0.0 6.7 %copy-start.2 = (bf16[1,192,1,1,896]{4,1,3,2,0:T(8,128)(2,1)S(1)}, bf16[1,192,1,1,896]{4,1,3,2,0:T(8,128)(2,1)}, u32[]{:S(2)}) copy-start(bf16[1,192,1,1,896]{4,1,3,2,0:T(8,128)(2,1)} %param.8) | copy-start | bytes 1032196
  4.1 9.1 %collective-permute-start = (bf16[1472,128]{1,0:T(8,128)(2,1)S(1)}, bf16[1472,128]{1,0:T(8,128)(2,1)S(1)}, u32[]{:S(2)}, u32[]{:S(2)}) collective-permute-start(bf16[1472,128]{1,0:T(8,128)(2,1)S(1)} %get-tuple-element.43), channel_id=1, source_target_pairs={{8,0},{9,1},{10,2},{11,3},{12,4},{13,5},{14,6},{15,7},{16,8},{17,9... | collective-permute-start | bytes 1130504 | tf_op jit(solution)/shard_map/ppermute | solution.py:405
  6.7 2.3 %copy-start.1 = (bf16[1,1,1,896,896]{4,3,2,1,0:T(8,128)(2,1)S(1)}, bf16[1,1,1,896,896]{4,3,2,1,0:T(8,128)(2,1)}, u32[]{:S(2)}) copy-start(bf16[1,1,1,896,896]{4,3,2,1,0:T(8,128)(2,1)} %param.13) | copy-start | bytes 4816900
  6.7 2.3 %copy-start.3 = (f32[1,1,1,896]{3,2,1,0:T(1,128)S(1)}, f32[1,1,1,896]{3,2,1,0:T(1,128)}, u32[]{:S(2)}) copy-start(f32[1,1,1,896]{3,2,1,0:T(1,128)} %param.14) | copy-start | bytes 10756
  6.8 6.2 %collective-permute-start.1 = (bf16[192,128]{1,0:T(8,128)(2,1)S(1)}, bf16[192,128]{1,0:T(8,128)(2,1)S(1)}, u32[]{:S(2)}, u32[]{:S(2)}) collective-permute-start(bf16[192,128]{1,0:T(8,128)(2,1)S(1)} %get-tuple-element.45), channel_id=1, source_target_pairs={{1,2},{2,1},{5,6},{6,5}} | collective-permute-start | bytes 147464 | tf_op jit(solution)/shard_map/ppermute | solution.py:405
  7.6 5.5 %collective-permute-start.2 = (bf16[192,128]{1,0:T(8,128)(2,1)S(1)}, bf16[192,128]{1,0:T(8,128)(2,1)S(1)}, u32[]{:S(2)}, u32[]{:S(2)}) collective-permute-start(bf16[192,128]{1,0:T(8,128)(2,1)S(1)} %get-tuple-element.46), channel_id=1, source_target_pairs={{0,1},{1,0},{2,3},{3,2},{4,5},{5,4},{6,7},{7,6}} | collective-permute-start | bytes 147464 | tf_op jit(solution)/shard_map/ppermute | solution.py:405
  8.3 4.8 %collective-permute-start.3 = (bf16[192,128]{1,0:T(8,128)(2,1)S(1)}, bf16[192,128]{1,0:T(8,128)(2,1)S(1)}, u32[]{:S(2)}, u32[]{:S(2)}) collective-permute-start(bf16[192,128]{1,0:T(8,128)(2,1)S(1)} %get-tuple-element.47), channel_id=1, source_target_pairs={{0,4},{1,5},{2,6},{3,7},{4,0},{5,1},{6,2},{7,3}} | collective-permute-start | bytes 147464 | tf_op jit(solution)/shard_map/ppermute | solution.py:405
  13.1 3.0 %collective-permute-start.4 = (bf16[576,896]{1,0:T(8,128)(2,1)S(1)}, bf16[576,896]{1,0:T(8,128)(2,1)S(1)}, u32[]{:S(2)}, u32[]{:S(2)}) collective-permute-start(bf16[576,896]{1,0:T(8,128)(2,1)S(1)} %get-tuple-element.48), channel_id=1, source_target_pairs={{0,8},{1,9},{2,10},{3,11},{4,12},{5,13},{6,14},{7,15}} | collective-permute-start | bytes 3096584 | tf_op jit(solution)/shard_map/ppermute | solution.py:405
  13.9 2.3 %collective-permute-start.5 = (bf16[144,128]{1,0:T(8,128)(2,1)S(1)}, bf16[144,128]{1,0:T(8,128)(2,1)S(1)}, u32[]{:S(2)}, u32[]{:S(2)}) collective-permute-start(bf16[144,128]{1,0:T(8,128)(2,1)S(1)} %get-tuple-element.52), channel_id=1, source_target_pairs={{1,10},{2,9},{5,14},{6,13}} | collective-permute-start | bytes 110600 | tf_op jit(solution)/shard_map/ppermute | solution.py:405
  14.6 1.6 %collective-permute-start.6 = (bf16[144,128]{1,0:T(8,128)(2,1)S(1)}, bf16[144,128]{1,0:T(8,128)(2,1)S(1)}, u32[]{:S(2)}, u32[]{:S(2)}) collective-permute-start(bf16[144,128]{1,0:T(8,128)(2,1)S(1)} %get-tuple-element.53), channel_id=1, source_target_pairs={{0,9},{1,8},{2,11},{3,10},{4,13},{5,12},{6,15},{7,14}} | collective-permute-start | bytes 110600 | tf_op jit(solution)/shard_map/ppermute | solution.py:405
  15.2 0.9 %collective-permute-start.7 = (bf16[144,128]{1,0:T(8,128)(2,1)S(1)}, bf16[144,128]{1,0:T(8,128)(2,1)S(1)}, u32[]{:S(2)}, u32[]{:S(2)}) collective-permute-start(bf16[144,128]{1,0:T(8,128)(2,1)S(1)} %get-tuple-element.54), channel_id=1, source_target_pairs={{0,12},{1,13},{2,14},{3,15},{4,8},{5,9},{6,10},{7,11}} | collective-permute-start | bytes 110600 | tf_op jit(solution)/shard_map/ppermute | solution.py:405
  16.2 3.4 %collective-permute-start.8 = (bf16[192,896]{1,0:T(8,128)(2,1)S(1)}, bf16[192,896]{1,0:T(8,128)(2,1)S(1)}, u32[]{:S(2)}, u32[]{:S(2)}) collective-permute-start(bf16[192,896]{1,0:T(8,128)(2,1)S(1)} %get-tuple-element.55), channel_id=1, source_target_pairs={{8,16},{9,17},{10,18},{11,19},{12,20},{13,21},{14,22},{15,23}} | collective-permute-start | bytes 1032200 | tf_op jit(solution)/shard_map/ppermute | solution.py:405
  16.9 2.7 %collective-permute-start.9 = (bf16[96,128]{1,0:T(8,128)(2,1)S(1)}, bf16[96,128]{1,0:T(8,128)(2,1)S(1)}, u32[]{:S(2)}, u32[]{:S(2)}) collective-permute-start(bf16[96,128]{1,0:T(8,128)(2,1)S(1)} %get-tuple-element.59), channel_id=1, source_target_pairs={{9,18},{10,17},{13,22},{14,21}} | collective-permute-start | bytes 73736 | tf_op jit(solution)/shard_map/ppermute | solution.py:405
  17.6 2.1 %collective-permute-start.10 = (bf16[96,128]{1,0:T(8,128)(2,1)S(1)}, bf16[96,128]{1,0:T(8,128)(2,1)S(1)}, u32[]{:S(2)}, u32[]{:S(2)}) collective-permute-start(bf16[96,128]{1,0:T(8,128)(2,1)S(1)} %get-tuple-element.60), channel_id=1, source_target_pairs={{8,17},{9,16},{10,19},{11,18},{12,21},{13,20},{14,23},{15,22}} | collective-permute-start | bytes 73736 | tf_op jit(solution)/shard_map/ppermute | solution.py:405
  18.2 1.4 %collective-permute-start.11 = (bf16[96,128]{1,0:T(8,128)(2,1)S(1)}, bf16[96,128]{1,0:T(8,128)(2,1)S(1)}, u32[]{:S(2)}, u32[]{:S(2)}) collective-permute-start(bf16[96,128]{1,0:T(8,128)(2,1)S(1)} %get-tuple-element.61), channel_id=1, source_target_pairs={{8,20},{9,21},{10,22},{11,23},{12,16},{13,17},{14,18},{15,19}} | collective-permute-start | bytes 73736 | tf_op jit(solution)/shard_map/ppermute | solution.py:405
  18.9 5.4 %collective-permute-start.13 = (bf16[192,896]{1,0:T(8,128)(2,1)S(1)}, bf16[192,896]{1,0:T(8,128)(2,1)S(1)}, u32[]{:S(2)}, u32[]{:S(2)}) collective-permute-start(bf16[192,896]{1,0:T(8,128)(2,1)S(1)} %get-tuple-element.63), channel_id=1, source_target_pairs={{8,16},{9,17},{10,18},{11,19},{12,20},{13,21},{14,22},{15,23}} | collective-permute-start | bytes 1032200 | tf_op jit(solution)/shard_map/ppermute | solution.py:405
  19.7 18.8 %collective-permute-start.12 = (bf16[192,896]{1,0:T(8,128)(2,1)S(1)}, bf16[192,896]{1,0:T(8,128)(2,1)S(1)}, u32[]{:S(2)}, u32[]{:S(2)}) collective-permute-start(bf16[192,896]{1,0:T(8,128)(2,1)S(1)} %get-tuple-element.62), channel_id=1, source_target_pairs={{16,24},{17,25},{18,26},{19,27},{20,28},{21,29},{22,30},{23,31}} | collective-permute-start | bytes 1032200 | tf_op jit(solution)/shard_map/ppermute | solution.py:405
  21.0 18.1 %collective-permute-start.14 = (bf16[48,128]{1,0:T(8,128)(2,1)S(1)}, bf16[48,128]{1,0:T(8,128)(2,1)S(1)}, u32[]{:S(2)}, u32[]{:S(2)}) collective-permute-start(bf16[48,128]{1,0:T(8,128)(2,1)S(1)} %get-tuple-element.64), channel_id=1, source_target_pairs={{17,26},{18,25},{21,30},{22,29}} | collective-permute-start | bytes 36872 | tf_op jit(solution)/shard_map/ppermute | solution.py:405
  21.7 20.2 %collective-permute-start.15 = (bf16[48,128]{1,0:T(8,128)(2,1)S(1)}, bf16[48,128]{1,0:T(8,128)(2,1)S(1)}, u32[]{:S(2)}, u32[]{:S(2)}) collective-permute-start(bf16[48,128]{1,0:T(8,128)(2,1)S(1)} %get-tuple-element.65), channel_id=1, source_target_pairs={{16,25},{17,24},{18,27},{19,26},{20,29},{21,28},{22,31},{23,30}} | collective-permute-start | bytes 36872 | tf_op jit(solution)/shard_map/ppermute | solution.py:405
  23.0 19.9 %collective-permute-start.16 = (bf16[48,128]{1,0:T(8,128)(2,1)S(1)}, bf16[48,128]{1,0:T(8,128)(2,1)S(1)}, u32[]{:S(2)}, u32[]{:S(2)}) collective-permute-start(bf16[48,128]{1,0:T(8,128)(2,1)S(1)} %get-tuple-element.66), channel_id=1, source_target_pairs={{16,28},{17,29},{18,30},{19,31},{20,24},{21,25},{22,26},{23,27}} | collective-permute-start | bytes 36872 | tf_op jit(solution)/shard_map/ppermute | solution.py:405

commit v15 on v14

--- a/solution.py
+++ b/solution.py
@@ -242,8 +242,12 @@
         fill_whole_map(first_map, band_in, second_map, whole_ext)
 
 
-def whole_map_kernel(early_layers, first_map, band, second_map, whole_in, whole_ext):
-    del whole_in
+def whole_map_kernel(early_layers, first_map, band, second_map, damping, edge_next, *refs):
+    whole_in, whole_ext, halo_map = refs
+    cells = first_map.shape[0]
+    brings = (damping[...] * whole_in[cells:].astype(jnp.float32)).astype(jnp.bfloat16)
+    halo_map[:, :cells] = brings
+    halo_map[:, cells:] = dot(brings, edge_next[:cells]).astype(jnp.bfloat16)
 
     @pl.when(lax.axis_index("depth") < early_layers)
     def _():
@@ -272,7 +276,7 @@
 
 
 def inner_kernel(part_of, step, chains, starts, map_ext, damping, edge_next, traces, *outs):
-    inner_out, edges_out, halo_map = outs
+    inner_out, edges_out = outs
     rows, cells = inner_out.shape
     slots = rows // chains
 
@@ -285,9 +289,6 @@
         at = cells + step * slots
         edges = dot(inner.astype(jnp.bfloat16), edge_next[:cells])
         edges_out[...] = edges + edge_next[at : at + rows].astype(jnp.float32)
-        brings = (damping[...] * map_ext[cells:].astype(jnp.float32)).astype(jnp.bfloat16)
-        halo_map[:, :cells] = brings
-        halo_map[:, cells:] = dot(brings, edge_next[:cells]).astype(jnp.bfloat16)
 
 
 def last_inner_kernel(extras, starts, map_ext, damping, traces, *refs):
@@ -472,15 +473,15 @@
         operands = [map_ext, damping, edge_next]
         if step > 0:
             rows = chains * slots
-            inner, *operands = call(
+            inner, edges = call(
                 functools.partial(inner_kernel, part_of, step, chains),
                 [
                     array(rows, cells, kind=jnp.float32),
                     array(rows, LANES, kind=jnp.float32),
-                    array(LANES, cells + LANES),
                 ],
                 [starts, map_ext, damping, edge_next, traces],
             )
+            operands = [edges, halo_map]
         operands = [live, inner] + operands + received
         ended = call(
             functools.partial(step_kernel, swaps, step, chains, keeps, part_of),
@@ -500,11 +501,11 @@
         received = [send(m, moves, swap) for m, swap in zip(ended[-len(swaps) :], swaps)]
         arrived += received
         if step == 0:
-            (map_ext,) = call(
+            map_ext, halo_map = call(
                 functools.partial(whole_map_kernel, early_layers),
-                [whole],
-                [first_map, band, second_map, map_ext],
-                aliases={3: 0},
+                [whole, array(LANES, cells + LANES)],
+                [first_map, band, second_map, damping, edge_next, map_ext],
+                aliases={5: 0},
             )
     (inner,) = call(
         functools.partial(last_inner_kernel, extras),

time: 44.4 us -> 44.3 us (level)
  transfers between devices with their start and end apart: 17 -> 17, of which waited for: 3 -> 3; matrix products, arithmetic and copies ran while one was open for 0% -> 0% of each run, Pallas kernels for 11% -> 12%
where the time goes in v15:
time: 44.3 us; the launch traced here: 43.9 us
  waiting for transfers between devices  17.7 us (40%)
  starting transfers between devices  15.3 us (35%)
  Pallas kernels  10.3 us (23%)
  between operations  0.56 us (1%)
    ppermute x17, waiting for transfers between devices, send(): return lax.ppermute(x, MESH_AXES, pairs)  17.7 us
    ppermute x17, starting transfers between devices, send(): return lax.ppermute(x, MESH_AXES, pairs)  15.3 us
    pallas_call x11, Pallas kernels, call(): pl.pallas_call(kernel, out_shape=out_shape, in_specs=[pl.BlockSpec(memory...  10.3 us
  transfers between devices with their start and end apart: 17, of which 3 were waited for; matrix products, arithmetic and copies ran while one was open for 0% of the time, Pallas kernels for 12%

profile of v15, /device:TPU:3, one launch (start us, length us, event | category | flops | bytes accessed | tf_op | source)
XLA Modules:
  0.0 43.9 jit_solution(1628147720887552181)
XLA Ops:
  0.0 4.0 %shard_map.82 = (bf16[1472,128]{1,0:T(8,128)(2,1)S(1)}, bf16[4,192,896]{2,1,0:T(8,128)(2,1)S(1)}, bf16[4,192,128]{2,1,0:T(8,128)(2,1)S(1)}) custom-call(bf16[4,192,896]{2,1,0:T(8,128)(2,1)} %bitcast.25, s32[4,192]{1,0:T(4,128)} %assignment_in.1, s32[7,1,1,12]{3,2,1,0:T(1,128)} %bitcast.23, bf16[896,896]{1,0:T(8,128)(2,1)} %bitcast.9), custom_call_target="tpu_custom_call" | custom-call | tf_op jit(solution)/shard_map/pallas_call | solution.py:377
  4.1 2.6 %collective-permute-start = (bf16[1472,128]{1,0:T(8,128)(2,1)S(1)}, bf16[1472,128]{1,0:T(8,128)(2,1)S(1)}, u32[]{:S(2)}, u32[]{:S(2)}) collective-permute-start(bf16[1472,128]{1,0:T(8,128)(2,1)S(1)} %get-tuple-element.42), channel_id=1, source_target_pairs={{8,0},{9,1},{10,2},{11,3},{12,4},{13,5},{14,6},{15,7},{16,8},{17,9... | collective-permute-start | bytes 1130504 | tf_op jit(solution)/shard_map/ppermute | solution.py:406
  6.7 0.0 copy-start.1
  6.7 0.0 copy-start.3
  6.7 0.1 shard_map.83
  6.8 0.8 %collective-permute-start.1 = (bf16[192,128]{1,0:T(8,128)(2,1)S(1)}, bf16[192,128]{1,0:T(8,128)(2,1)S(1)}, u32[]{:S(2)}, u32[]{:S(2)}) collective-permute-start(bf16[192,128]{1,0:T(8,128)(2,1)S(1)} %get-tuple-element.46), channel_id=1, source_target_pairs={{1,2},{2,1},{5,6},{6,5}} | collective-permute-start | bytes 147464 | tf_op jit(solution)/shard_map/ppermute | solution.py:406
  7.6 0.7 %collective-permute-start.2 = (bf16[192,128]{1,0:T(8,128)(2,1)S(1)}, bf16[192,128]{1,0:T(8,128)(2,1)S(1)}, u32[]{:S(2)}, u32[]{:S(2)}) collective-permute-start(bf16[192,128]{1,0:T(8,128)(2,1)S(1)} %get-tuple-element.47), channel_id=1, source_target_pairs={{0,1},{1,0},{2,3},{3,2},{4,5},{5,4},{6,7},{7,6}} | collective-permute-start | bytes 147464 | tf_op jit(solution)/shard_map/ppermute | solution.py:406
  8.3 0.7 %collective-permute-start.3 = (bf16[192,128]{1,0:T(8,128)(2,1)S(1)}, bf16[192,128]{1,0:T(8,128)(2,1)S(1)}, u32[]{:S(2)}, u32[]{:S(2)}) collective-permute-start(bf16[192,128]{1,0:T(8,128)(2,1)S(1)} %get-tuple-element.48), channel_id=1, source_target_pairs={{0,4},{1,5},{2,6},{3,7},{4,0},{5,1},{6,2},{7,3}} | collective-permute-start | bytes 147464 | tf_op jit(solution)/shard_map/ppermute | solution.py:406
  9.0 4.1 %shard_map.84 = (f32[576,896]{1,0:T(8,128)S(1)}, bf16[1024,896]{1,0:T(8,128)(2,1)S(1)}, bf16[4,512,256]{2,1,0:T(8,128)(2,1)S(1)}) custom-call(bf16[4,192,896]{2,1,0:T(8,128)(2,1)S(1)} %get-tuple-element.39.starts, bf16[896,896]{1,0:T(8,128)(2,1)S(1)} %bitcast.11, bf16[896,896]{1,0:T(8,128)(2,1)S(1)} %bitcast.13, ...), custom_call_target="tpu_custom_call" | custom-call | tf_op jit(solution)/shard_map/pallas_call | solution.py:377
  13.1 0.0 collective-permute-done.1.refs_3_.refs_0_
  13.1 0.0 collective-permute-done.2.refs_4_.refs_1_
  13.1 0.0 collective-permute-done.edge_next.refs_2_
  13.1 0.7 %collective-permute-start.4 = (bf16[576,896]{1,0:T(8,128)(2,1)S(1)}, bf16[576,896]{1,0:T(8,128)(2,1)S(1)}, u32[]{:S(2)}, u32[]{:S(2)}) collective-permute-start(bf16[576,896]{1,0:T(8,128)(2,1)S(1)} %get-tuple-element.49), channel_id=1, source_target_pairs={{0,8},{1,9},{2,10},{3,11},{4,12},{5,13},{6,14},{7,15}} | collective-permute-start | bytes 3096584 | tf_op jit(solution)/shard_map/ppermute | solution.py:406
  13.9 0.7 %collective-permute-start.5 = (bf16[144,128]{1,0:T(8,128)(2,1)S(1)}, bf16[144,128]{1,0:T(8,128)(2,1)S(1)}, u32[]{:S(2)}, u32[]{:S(2)}) collective-permute-start(bf16[144,128]{1,0:T(8,128)(2,1)S(1)} %get-tuple-element.53), channel_id=1, source_target_pairs={{1,10},{2,9},{5,14},{6,13}} | collective-permute-start | bytes 110600 | tf_op jit(solution)/shard_map/ppermute | solution.py:406
  14.5 0.7 %collective-permute-start.6 = (bf16[144,128]{1,0:T(8,128)(2,1)S(1)}, bf16[144,128]{1,0:T(8,128)(2,1)S(1)}, u32[]{:S(2)}, u32[]{:S(2)}) collective-permute-start(bf16[144,128]{1,0:T(8,128)(2,1)S(1)} %get-tuple-element.54), channel_id=1, source_target_pairs={{0,9},{1,8},{2,11},{3,10},{4,13},{5,12},{6,15},{7,14}} | collective-permute-start | bytes 110600 | tf_op jit(solution)/shard_map/ppermute | solution.py:406
  15.2 0.7 %collective-permute-start.7 = (bf16[144,128]{1,0:T(8,128)(2,1)S(1)}, bf16[144,128]{1,0:T(8,128)(2,1)S(1)}, u32[]{:S(2)}, u32[]{:S(2)}) collective-permute-start(bf16[144,128]{1,0:T(8,128)(2,1)S(1)} %get-tuple-element.55), channel_id=1, source_target_pairs={{0,12},{1,13},{2,14},{3,15},{4,8},{5,9},{6,10},{7,11}} | collective-permute-start | bytes 110600 | tf_op jit(solution)/shard_map/ppermute | solution.py:406
  15.9 0.4 shard_map.85
  16.3 0.0 collective-permute-done.5.refs_2_.refs_3_
  16.4 0.7 %collective-permute-start.8 = (bf16[192,896]{1,0:T(8,128)(2,1)S(1)}, bf16[192,896]{1,0:T(8,128)(2,1)S(1)}, u32[]{:S(2)}, u32[]{:S(2)}) collective-permute-start(bf16[192,896]{1,0:T(8,128)(2,1)S(1)} %get-tuple-element.56), channel_id=1, source_target_pairs={{8,16},{9,17},{10,18},{11,19},{12,20},{13,21},{14,22},{15,23}} | collective-permute-start | bytes 1032200 | tf_op jit(solution)/shard_map/ppermute | solution.py:406
  17.1 0.7 %collective-permute-start.9 = (bf16[96,128]{1,0:T(8,128)(2,1)S(1)}, bf16[96,128]{1,0:T(8,128)(2,1)S(1)}, u32[]{:S(2)}, u32[]{:S(2)}) collective-permute-start(bf16[96,128]{1,0:T(8,128)(2,1)S(1)} %get-tuple-element.59), channel_id=1, source_target_pairs={{9,18},{10,17},{13,22},{14,21}} | collective-permute-start | bytes 73736 | tf_op jit(solution)/shard_map/ppermute | solution.py:406
  17.7 0.7 %collective-permute-start.10 = (bf16[96,128]{1,0:T(8,128)(2,1)S(1)}, bf16[96,128]{1,0:T(8,128)(2,1)S(1)}, u32[]{:S(2)}, u32[]{:S(2)}) collective-permute-start(bf16[96,128]{1,0:T(8,128)(2,1)S(1)} %get-tuple-element.60), channel_id=1, source_target_pairs={{8,17},{9,16},{10,19},{11,18},{12,21},{13,20},{14,23},{15,22}} | collective-permute-start | bytes 73736 | tf_op jit(solution)/shard_map/ppermute | solution.py:406
  18.4 0.7 %collective-permute-start.11 = (bf16[96,128]{1,0:T(8,128)(2,1)S(1)}, bf16[96,128]{1,0:T(8,128)(2,1)S(1)}, u32[]{:S(2)}, u32[]{:S(2)}) collective-permute-start(bf16[96,128]{1,0:T(8,128)(2,1)S(1)} %get-tuple-element.61), channel_id=1, source_target_pairs={{8,20},{9,21},{10,22},{11,23},{12,16},{13,17},{14,18},{15,19}} | collective-permute-start | bytes 73736 | tf_op jit(solution)/shard_map/ppermute | solution.py:406
  19.1 0.7 %collective-permute-start.13 = (bf16[192,896]{1,0:T(8,128)(2,1)S(1)}, bf16[192,896]{1,0:T(8,128)(2,1)S(1)}, u32[]{:S(2)}, u32[]{:S(2)}) collective-permute-start(bf16[192,896]{1,0:T(8,128)(2,1)S(1)} %get-tuple-element.63), channel_id=1, source_target_pairs={{8,16},{9,17},{10,18},{11,19},{12,20},{13,21},{14,22},{15,23}} | collective-permute-start | bytes 1032200 | tf_op jit(solution)/shard_map/ppermute | solution.py:406
  19.9 1.3 %collective-permute-start.12 = (bf16[192,896]{1,0:T(8,128)(2,1)S(1)}, bf16[192,896]{1,0:T(8,128)(2,1)S(1)}, u32[]{:S(2)}, u32[]{:S(2)}) collective-permute-start(bf16[192,896]{1,0:T(8,128)(2,1)S(1)} %get-tuple-element.62), channel_id=1, source_target_pairs={{16,24},{17,25},{18,26},{19,27},{20,28},{21,29},{22,30},{23,31}} | collective-permute-start | bytes 1032200 | tf_op jit(solution)/shard_map/ppermute | solution.py:406
  21.2 0.7 %collective-permute-start.14 = (bf16[48,128]{1,0:T(8,128)(2,1)S(1)}, bf16[48,128]{1,0:T(8,128)(2,1)S(1)}, u32[]{:S(2)}, u32[]{:S(2)}) collective-permute-start(bf16[48,128]{1,0:T(8,128)(2,1)S(1)} %get-tuple-element.64), channel_id=1, source_target_pairs={{17,26},{18,25},{21,30},{22,29}} | collective-permute-start | bytes 36872 | tf_op jit(solution)/shard_map/ppermute | solution.py:406
  21.8 1.3 %collective-permute-start.15 = (bf16[48,128]{1,0:T(8,128)(2,1)S(1)}, bf16[48,128]{1,0:T(8,128)(2,1)S(1)}, u32[]{:S(2)}, u32[]{:S(2)}) collective-permute-start(bf16[48,128]{1,0:T(8,128)(2,1)S(1)} %get-tuple-element.65), channel_id=1, source_target_pairs={{16,25},{17,24},{18,27},{19,26},{20,29},{21,28},{22,31},{23,30}} | collective-permute-start | bytes 36872 | tf_op jit(solution)/shard_map/ppermute | solution.py:406
  23.1 1.3 %collective-permute-start.16 = (bf16[48,128]{1,0:T(8,128)(2,1)S(1)}, bf16[48,128]{1,0:T(8,128)(2,1)S(1)}, u32[]{:S(2)}, u32[]{:S(2)}) collective-permute-start(bf16[48,128]{1,0:T(8,128)(2,1)S(1)} %get-tuple-element.66), channel_id=1, source_target_pairs={{16,28},{17,29},{18,30},{19,31},{20,24},{21,25},{22,26},{23,27}} | collective-permute-start | bytes 36872 | tf_op jit(solution)/shard_map/ppermute | solution.py:406
  24.5 14.1 %collective-permute-done.12.traces = bf16[192,896]{1,0:T(8,128)(2,1)S(1)} collective-permute-done((bf16[192,896]{1,0:T(8,128)(2,1)S(1)}, bf16[192,896]{1,0:T(8,128)(2,1)S(1)}, u32[]{:S(2)}, u32[]{:S(2)}) %collective-permute-start.12) | collective-permute-done | bytes 344096 | tf_op jit(solution)/shard_map/ppermute | solution.py:406
  38.5 0.6 %shard_map.91.inner = f32[192,896]{1,0:T(8,128)S(1)} custom-call(bf16[4,192,896]{2,1,0:T(8,128)(2,1)S(1)} %get-tuple-element.39.starts, bf16[1024,896]{1,0:T(8,128)(2,1)S(1)} %get-tuple-element.44.map_ext, f32[1,896]{1,0:T(1,128)S(1)} %bitcast.21, bf16[192,896]{1,0:T(8,128)(2,1)S(1)} %collective-permute-done.12.traces, ...), custom_call_target="tpu_custom_call" | custom-call | tf_op jit(solution)/shard_map/pallas_call | solution.py:377
  39.1 2.8 %collective-permute-done.15.refs_10_ = bf16[48,128]{1,0:T(8,128)(2,1)S(1)} collective-permute-done((bf16[48,128]{1,0:T(8,128)(2,1)S(1)}, bf16[48,128]{1,0:T(8,128)(2,1)S(1)}, u32[]{:S(2)}, u32[]{:S(2)}) %collective-permute-start.15) | collective-permute-done | bytes 12320 | tf_op jit(solution)/shard_map/ppermute | solution.py:406
  41.9 0.8 %collective-permute-done.16.refs_11_ = bf16[48,128]{1,0:T(8,128)(2,1)S(1)} collective-permute-done((bf16[48,128]{1,0:T(8,128)(2,1)S(1)}, bf16[48,128]{1,0:T(8,128)(2,1)S(1)}, u32[]{:S(2)}, u32[]{:S(2)}) %collective-permute-start.16) | collective-permute-done | bytes 12320 | tf_op jit(solution)/shard_map/ppermute | solution.py:406
  42.7 1.0 %shard_map.92 = bf16[192,896]{1,0:T(8,128)(2,1)} custom-call(bf16[4,192,128]{2,1,0:T(8,128)(2,1)S(1)} %get-tuple-element.38.live, bf16[1024,896]{1,0:T(8,128)(2,1)S(1)} %get-tuple-element.44.map_ext, f32[1,896]{1,0:T(1,128)S(1)} %bitcast.22, f32[192,896]{1,0:T(8,128)S(1)} %shard_map.91.inner, bf16[192,128]{1,0:T(8,128)(2,1)S(1)} %collective-permute-done.1.refs_3_.refs_0_, ...), custom_call_target="tpu_custom_call" | custom-call | tf_op jit(solution)/shard_map/pallas_call | solution.py:377
  (25 shorter events, 0.1 us)
Async XLA Ops:
  0.0 6.7 %copy-start.4 = (s32[4,192]{1,0:T(4,128)S(1)}, s32[4,192]{1,0:T(4,128)}, u32[]{:S(2)}) copy-start(s32[4,192]{1,0:T(4,128)} %assignment_in.1) | copy-start | bytes 9220
  0.0 6.7 %copy-start = (bf16[1,1,1,896,896]{4,3,2,1,0:T(8,128)(2,1)S(1)}, bf16[1,1,1,896,896]{4,3,2,1,0:T(8,128)(2,1)}, u32[]{:S(2)}) copy-start(bf16[1,1,1,896,896]{4,3,2,1,0:T(8,128)(2,1)} %param.12) | copy-start | bytes 4816900
  0.0 6.7 %copy-start.5 = (s32[7,12,1,1]{1,3,2,0:T(1,128)S(1)}, s32[7,12,1,1]{1,3,2,0:T(1,128)}, u32[]{:S(2)}) copy-start(s32[7,12,1,1]{1,3,2,0:T(1,128)} %param.11) | copy-start | bytes 1012
  0.0 6.7 %copy-start.2 = (bf16[1,192,1,1,896]{4,1,3,2,0:T(8,128)(2,1)S(1)}, bf16[1,192,1,1,896]{4,1,3,2,0:T(8,128)(2,1)}, u32[]{:S(2)}) copy-start(bf16[1,192,1,1,896]{4,1,3,2,0:T(8,128)(2,1)} %param.8) | copy-start | bytes 1032196
  4.1 9.1 %collective-permute-start = (bf16[1472,128]{1,0:T(8,128)(2,1)S(1)}, bf16[1472,128]{1,0:T(8,128)(2,1)S(1)}, u32[]{:S(2)}, u32[]{:S(2)}) collective-permute-start(bf16[1472,128]{1,0:T(8,128)(2,1)S(1)} %get-tuple-element.42), channel_id=1, source_target_pairs={{8,0},{9,1},{10,2},{11,3},{12,4},{13,5},{14,6},{15,7},{16,8},{17,9... | collective-permute-start | bytes 1130504 | tf_op jit(solution)/shard_map/ppermute | solution.py:406
  6.7 2.3 %copy-start.1 = (bf16[1,1,1,896,896]{4,3,2,1,0:T(8,128)(2,1)S(1)}, bf16[1,1,1,896,896]{4,3,2,1,0:T(8,128)(2,1)}, u32[]{:S(2)}) copy-start(bf16[1,1,1,896,896]{4,3,2,1,0:T(8,128)(2,1)} %param.13) | copy-start | bytes 4816900
  6.7 2.3 %copy-start.3 = (f32[1,1,1,896]{3,2,1,0:T(1,128)S(1)}, f32[1,1,1,896]{3,2,1,0:T(1,128)}, u32[]{:S(2)}) copy-start(f32[1,1,1,896]{3,2,1,0:T(1,128)} %param.14) | copy-start | bytes 10756
  6.8 6.2 %collective-permute-start.1 = (bf16[192,128]{1,0:T(8,128)(2,1)S(1)}, bf16[192,128]{1,0:T(8,128)(2,1)S(1)}, u32[]{:S(2)}, u32[]{:S(2)}) collective-permute-start(bf16[192,128]{1,0:T(8,128)(2,1)S(1)} %get-tuple-element.46), channel_id=1, source_target_pairs={{1,2},{2,1},{5,6},{6,5}} | collective-permute-start | bytes 147464 | tf_op jit(solution)/shard_map/ppermute | solution.py:406
  7.6 5.5 %collective-permute-start.2 = (bf16[192,128]{1,0:T(8,128)(2,1)S(1)}, bf16[192,128]{1,0:T(8,128)(2,1)S(1)}, u32[]{:S(2)}, u32[]{:S(2)}) collective-permute-start(bf16[192,128]{1,0:T(8,128)(2,1)S(1)} %get-tuple-element.47), channel_id=1, source_target_pairs={{0,1},{1,0},{2,3},{3,2},{4,5},{5,4},{6,7},{7,6}} | collective-permute-start | bytes 147464 | tf_op jit(solution)/shard_map/ppermute | solution.py:406
  8.3 4.8 %collective-permute-start.3 = (bf16[192,128]{1,0:T(8,128)(2,1)S(1)}, bf16[192,128]{1,0:T(8,128)(2,1)S(1)}, u32[]{:S(2)}, u32[]{:S(2)}) collective-permute-start(bf16[192,128]{1,0:T(8,128)(2,1)S(1)} %get-tuple-element.48), channel_id=1, source_target_pairs={{0,4},{1,5},{2,6},{3,7},{4,0},{5,1},{6,2},{7,3}} | collective-permute-start | bytes 147464 | tf_op jit(solution)/shard_map/ppermute | solution.py:406
  13.1 3.2 %collective-permute-start.4 = (bf16[576,896]{1,0:T(8,128)(2,1)S(1)}, bf16[576,896]{1,0:T(8,128)(2,1)S(1)}, u32[]{:S(2)}, u32[]{:S(2)}) collective-permute-start(bf16[576,896]{1,0:T(8,128)(2,1)S(1)} %get-tuple-element.49), channel_id=1, source_target_pairs={{0,8},{1,9},{2,10},{3,11},{4,12},{5,13},{6,14},{7,15}} | collective-permute-start | bytes 3096584 | tf_op jit(solution)/shard_map/ppermute | solution.py:406
  13.9 2.5 %collective-permute-start.5 = (bf16[144,128]{1,0:T(8,128)(2,1)S(1)}, bf16[144,128]{1,0:T(8,128)(2,1)S(1)}, u32[]{:S(2)}, u32[]{:S(2)}) collective-permute-start(bf16[144,128]{1,0:T(8,128)(2,1)S(1)} %get-tuple-element.53), channel_id=1, source_target_pairs={{1,10},{2,9},{5,14},{6,13}} | collective-permute-start | bytes 110600 | tf_op jit(solution)/shard_map/ppermute | solution.py:406
  14.5 1.8 %collective-permute-start.6 = (bf16[144,128]{1,0:T(8,128)(2,1)S(1)}, bf16[144,128]{1,0:T(8,128)(2,1)S(1)}, u32[]{:S(2)}, u32[]{:S(2)}) collective-permute-start(bf16[144,128]{1,0:T(8,128)(2,1)S(1)} %get-tuple-element.54), channel_id=1, source_target_pairs={{0,9},{1,8},{2,11},{3,10},{4,13},{5,12},{6,15},{7,14}} | collective-permute-start | bytes 110600 | tf_op jit(solution)/shard_map/ppermute | solution.py:406
  15.2 1.1 %collective-permute-start.7 = (bf16[144,128]{1,0:T(8,128)(2,1)S(1)}, bf16[144,128]{1,0:T(8,128)(2,1)S(1)}, u32[]{:S(2)}, u32[]{:S(2)}) collective-permute-start(bf16[144,128]{1,0:T(8,128)(2,1)S(1)} %get-tuple-element.55), channel_id=1, source_target_pairs={{0,12},{1,13},{2,14},{3,15},{4,8},{5,9},{6,10},{7,11}} | collective-permute-start | bytes 110600 | tf_op jit(solution)/shard_map/ppermute | solution.py:406
  16.4 3.4 %collective-permute-start.8 = (bf16[192,896]{1,0:T(8,128)(2,1)S(1)}, bf16[192,896]{1,0:T(8,128)(2,1)S(1)}, u32[]{:S(2)}, u32[]{:S(2)}) collective-permute-start(bf16[192,896]{1,0:T(8,128)(2,1)S(1)} %get-tuple-element.56), channel_id=1, source_target_pairs={{8,16},{9,17},{10,18},{11,19},{12,20},{13,21},{14,22},{15,23}} | collective-permute-start | bytes 1032200 | tf_op jit(solution)/shard_map/ppermute | solution.py:406
  17.1 2.7 %collective-permute-start.9 = (bf16[96,128]{1,0:T(8,128)(2,1)S(1)}, bf16[96,128]{1,0:T(8,128)(2,1)S(1)}, u32[]{:S(2)}, u32[]{:S(2)}) collective-permute-start(bf16[96,128]{1,0:T(8,128)(2,1)S(1)} %get-tuple-element.59), channel_id=1, source_target_pairs={{9,18},{10,17},{13,22},{14,21}} | collective-permute-start | bytes 73736 | tf_op jit(solution)/shard_map/ppermute | solution.py:406
  17.7 2.1 %collective-permute-start.10 = (bf16[96,128]{1,0:T(8,128)(2,1)S(1)}, bf16[96,128]{1,0:T(8,128)(2,1)S(1)}, u32[]{:S(2)}, u32[]{:S(2)}) collective-permute-start(bf16[96,128]{1,0:T(8,128)(2,1)S(1)} %get-tuple-element.60), channel_id=1, source_target_pairs={{8,17},{9,16},{10,19},{11,18},{12,21},{13,20},{14,23},{15,22}} | collective-permute-start | bytes 73736 | tf_op jit(solution)/shard_map/ppermute | solution.py:406
  18.4 1.4 %collective-permute-start.11 = (bf16[96,128]{1,0:T(8,128)(2,1)S(1)}, bf16[96,128]{1,0:T(8,128)(2,1)S(1)}, u32[]{:S(2)}, u32[]{:S(2)}) collective-permute-start(bf16[96,128]{1,0:T(8,128)(2,1)S(1)} %get-tuple-element.61), channel_id=1, source_target_pairs={{8,20},{9,21},{10,22},{11,23},{12,16},{13,17},{14,18},{15,19}} | collective-permute-start | bytes 73736 | tf_op jit(solution)/shard_map/ppermute | solution.py:406
  19.1 5.4 %collective-permute-start.13 = (bf16[192,896]{1,0:T(8,128)(2,1)S(1)}, bf16[192,896]{1,0:T(8,128)(2,1)S(1)}, u32[]{:S(2)}, u32[]{:S(2)}) collective-permute-start(bf16[192,896]{1,0:T(8,128)(2,1)S(1)} %get-tuple-element.63), channel_id=1, source_target_pairs={{8,16},{9,17},{10,18},{11,19},{12,20},{13,21},{14,22},{15,23}} | collective-permute-start | bytes 1032200 | tf_op jit(solution)/shard_map/ppermute | solution.py:406
  19.9 18.6 %collective-permute-start.12 = (bf16[192,896]{1,0:T(8,128)(2,1)S(1)}, bf16[192,896]{1,0:T(8,128)(2,1)S(1)}, u32[]{:S(2)}, u32[]{:S(2)}) collective-permute-start(bf16[192,896]{1,0:T(8,128)(2,1)S(1)} %get-tuple-element.62), channel_id=1, source_target_pairs={{16,24},{17,25},{18,26},{19,27},{20,28},{21,29},{22,30},{23,31}} | collective-permute-start | bytes 1032200 | tf_op jit(solution)/shard_map/ppermute | solution.py:406
  21.2 17.9 %collective-permute-start.14 = (bf16[48,128]{1,0:T(8,128)(2,1)S(1)}, bf16[48,128]{1,0:T(8,128)(2,1)S(1)}, u32[]{:S(2)}, u32[]{:S(2)}) collective-permute-start(bf16[48,128]{1,0:T(8,128)(2,1)S(1)} %get-tuple-element.64), channel_id=1, source_target_pairs={{17,26},{18,25},{21,30},{22,29}} | collective-permute-start | bytes 36872 | tf_op jit(solution)/shard_map/ppermute | solution.py:406
  21.8 20.0 %collective-permute-start.15 = (bf16[48,128]{1,0:T(8,128)(2,1)S(1)}, bf16[48,128]{1,0:T(8,128)(2,1)S(1)}, u32[]{:S(2)}, u32[]{:S(2)}) collective-permute-start(bf16[48,128]{1,0:T(8,128)(2,1)S(1)} %get-tuple-element.65), channel_id=1, source_target_pairs={{16,25},{17,24},{18,27},{19,26},{20,29},{21,28},{22,31},{23,30}} | collective-permute-start | bytes 36872 | tf_op jit(solution)/shard_map/ppermute | solution.py:406
  23.1 19.6 %collective-permute-start.16 = (bf16[48,128]{1,0:T(8,128)(2,1)S(1)}, bf16[48,128]{1,0:T(8,128)(2,1)S(1)}, u32[]{:S(2)}, u32[]{:S(2)}) collective-permute-start(bf16[48,128]{1,0:T(8,128)(2,1)S(1)} %get-tuple-element.66), channel_id=1, source_target_pairs={{16,28},{17,29},{18,30},{19,31},{20,24},{21,25},{22,26},{23,27}} | collective-permute-start | bytes 36872 | tf_op jit(solution)/shard_map/ppermute | solution.py:406
